TPU v7x, 32 devices: a whole 2x2x4 slice. The times are simulated.
32 devices in a mesh: groups: 2 (over y), blk: 4 (over z), head: 4 (over x, core).
Axes of the slice: x: 2, y: 2, z: 4, core: 2. Of those that a mesh axis runs over, the one named last changes fastest.
Arguments:
- ctx_query: bfloat16 [4096, 8192], P(('groups', 'blk'), 'head'), parts along dimension 0, may hold values from -5 to 5
- ctx_key: bfloat16 [4096, 1024], P(('groups', 'blk'), 'head'), parts along dimension 0, may hold values from -5 to 5
- ctx_value: bfloat16 [4096, 1024], P(('groups', 'blk'), 'head'), parts along dimension 0, may hold values from -4.5 to 4.5
- opt_query: bfloat16 [128, 8192], P(('groups', 'blk'), 'head'), parts along dimension 0, may hold values from -5 to 5
- opt_owner: int32 [128], P('groups'), parts along dimension 0, may hold values from 0 to 3, as said below
- opt_slot: int32 [128], P('groups'), parts along dimension 0, may hold values from 0 to 31, as said below
- opt_length: int32 [128], P('groups'), parts along dimension 0, may hold values from 512 to 2048
Outputs:
- ctx_out: bfloat16 [4096, 8192], P(('groups', 'blk'), 'head'), parts along dimension 0
- opt_out: bfloat16 [256, 8192], P(('groups', 'blk'), 'head'), parts along dimension 0
There are 2 independent parts, one for each index of `groups`. A program takes and returns all parts, laid end to end along the dimension named above; each array names one. Nothing has to cross between parts.
Inputs may be any that keep to these rules, and one draw needn't show every extreme that they name: `opt_owner`: each option token has its own pair of owner block and slot; no block owns more than 32 option tokens, and one block owns exactly 32. `opt_slot`: slots of one owner are distinct.
All inputs are finite; a program needn't handle non-finite values.
Results may differ from a plain program's by a relative error of at most 0.017.
Values may be sent and summed in bfloat16 or wider, within the bound.
No kernel may reach another device: no remote copies, remote signals or barrier semaphores. Data moves between devices by JAX's collectives and lax.ppermute only.
A program may use at most 64 MiB of HBM per device.

v0:
```python
import jax
import jax.numpy as jnp
from jax import lax
from jax.sharding import PartitionSpec as P

HD = 128
HQ = 64
KVH = 8
CAP = 32


def from_root(value, axis, root):
    mine = lax.axis_index(axis) == root
    return lax.psum(jnp.where(mine, value, jnp.zeros_like(value)), axis)


def soft_parts(query_head, keys, values, masks, scale):
    scores = []
    for key_part, mask_part in zip(keys, masks):
        raw = (
            jnp.einsum("td,sd->ts", query_head, key_part, preferred_element_type=jnp.float32)
            * scale
        )
        scores.append(jnp.where(mask_part, raw, -1e30))
    top = jnp.max(scores[0], axis=1)
    for extra in scores[1:]:
        top = jnp.maximum(top, jnp.max(extra, axis=1))
    total = jnp.zeros_like(top)
    accum = jnp.zeros((query_head.shape[0], values[0].shape[1]), jnp.float32)
    for score_part, value_part in zip(scores, values):
        expo = jnp.exp(score_part - top[:, None])
        total = total + jnp.sum(expo, axis=1)
        accum = accum + jnp.dot(
            expo.astype(jnp.bfloat16), value_part, preferred_element_type=jnp.float32
        )
    return (accum / total[:, None], top, total)


def body(ctx_query, ctx_key, ctx_value, opt_query, opt_owner, opt_slot, opt_length):
    group_size = HQ // KVH
    scale = HD ** (-0.5)
    block_index = lax.axis_index("blk")
    block_count = lax.axis_size("blk")
    rows = ctx_query.shape[0]
    local_heads = ctx_query.shape[1] // HD
    anchor_key, anchor_value = (from_root(ctx_key, "blk", 0), from_root(ctx_value, "blk", 0))
    spots = jnp.arange(rows, dtype=jnp.int32)
    causal = spots[:, None] >= spots[None, :]
    anchor_mask = jnp.broadcast_to(block_index > 0, (rows, rows))

    def phase_one(head_id, result):
        group = head_id // group_size
        query_head = lax.dynamic_slice_in_dim(ctx_query, head_id * HD, HD, 1)
        key_local = lax.dynamic_slice_in_dim(ctx_key, group * HD, HD, 1)
        value_local = lax.dynamic_slice_in_dim(ctx_value, group * HD, HD, 1)
        key_anchor = lax.dynamic_slice_in_dim(anchor_key, group * HD, HD, 1)
        value_anchor = lax.dynamic_slice_in_dim(anchor_value, group * HD, HD, 1)
        output, top, total = soft_parts(
            query_head,
            (key_anchor, key_local),
            (value_anchor, value_local),
            (anchor_mask, causal),
            scale,
        )
        return lax.dynamic_update_slice_in_dim(result, output.astype(jnp.bfloat16), head_id * HD, 1)

    ctx_out = lax.fori_loop(0, local_heads, phase_one, jnp.zeros(ctx_query.shape, jnp.bfloat16))
    all_queries = lax.all_gather(opt_query, "blk", axis=0, tiled=True)
    options = all_queries.shape[0]
    count = jnp.clip(opt_length - block_index * rows, 0, rows)
    live = count > 0
    visible = spots[None, :] < count[:, None]

    def phase_two(head_id, carry):
        partial_value, stats = carry
        group = head_id // group_size
        query_head = lax.dynamic_slice_in_dim(all_queries, head_id * HD, HD, 1)
        key_local = lax.dynamic_slice_in_dim(ctx_key, group * HD, HD, 1)
        value_local = lax.dynamic_slice_in_dim(ctx_value, group * HD, HD, 1)
        output, top, total = soft_parts(query_head, (key_local,), (value_local,), (visible,), scale)
        output = jnp.where(live[:, None], output, 0.0).astype(jnp.bfloat16)
        stat = jnp.where(live, top + jnp.log(total), -1e30)
        partial_value = lax.dynamic_update_slice_in_dim(partial_value, output, head_id * HD, 1)
        stats = lax.dynamic_update_slice_in_dim(stats, stat[:, None], head_id, 1)
        return (partial_value, stats)

    start = (
        jnp.zeros((options, local_heads * HD), jnp.bfloat16),
        jnp.zeros((options, local_heads), jnp.float32),
    )
    partial_value, stats = lax.fori_loop(0, local_heads, phase_two, start)
    slot_total = CAP * block_count
    where_to = opt_owner * CAP + opt_slot
    top_all = lax.pmax(stats, "blk")
    weight = jnp.exp(stats - top_all)
    weight_sum = lax.psum(weight, "blk")
    share = weight / weight_sum
    term = (
        partial_value.reshape(options, local_heads, HD).astype(jnp.float32) * share[:, :, None]
    ).reshape(options, local_heads * HD)
    buffer = jnp.zeros((slot_total, local_heads * HD), jnp.float32).at[where_to].set(term)
    opt_out = lax.psum_scatter(buffer.astype(jnp.bfloat16), "blk", scatter_dimension=0, tiled=True)
    return (ctx_out, opt_out)


def solution(mesh):
    return jax.shard_map(
        body,
        mesh=mesh,
        in_specs=(
            P(("groups", "blk"), "head"),
            P(("groups", "blk"), "head"),
            P(("groups", "blk"), "head"),
            P(("groups", "blk"), "head"),
            P("groups"),
            P("groups"),
            P("groups"),
        ),
        out_specs=(P(("groups", "blk"), "head"), P(("groups", "blk"), "head")),
        check_vma=False,
    )
```

profile of v0, /device:TPU:12, one launch (start us, length us, event | category | flops | bytes accessed | tf_op | source)
XLA Modules:
  0.0 126.8 jit_solution(5371850114910661687)
XLA Ops:
  8.2 14.9 %all_gather.3 = bf16[64,2048]{1,0:T(8,128)(2,1)S(1)} all-gather(bf16[16,2048]{1,0:T(8,128)(2,1)} %param.14), channel_id=1, replica_groups=mesh['groups'=2,'blk'=4,'head'=4] {'blk'}, dimensions={0}, use_global_device_ids=true | all-gather | bytes 327680 | tf_op jit(solution)/shard_map/all_gather | solution.py:68
  23.9 12.9 %while.35 = (s32[]{:T(128)}, bf16[64,2048]{1,0:T(8,128)(2,1)S(1)}, f32[64,16]{0,1:T(8,128)S(1)}, pred[64]{0:T(512)(128)(4,1)S(1)}, bf16[64,2048]{1,0:T(8,128)(2,...) while((s32[]{:T(128)}, bf16[64,2048]{1,0:T(8,128)(2,1)S(1)}, ...), condition=%wide.region_11.12_spmd.clone, body=%wide.region_8.11_spmd.clone.sunk | while | flops 17063952 | bytes 692635 | solution.py:91
  36.8 10.1 %pmax.7 = f32[64,16]{0,1:T(8,128)S(1)} all-reduce(f32[64,16]{0,1:T(8,128)S(1)} %get-tuple-element.425), channel_id=1, replica_groups=mesh['groups'=2,'blk'=4,'head'=4] {'blk'}, use_global_device_ids=true, to_apply=%region_12.13 | all-reduce | flops 1024 | bytes 8192 | tf_op jit(solution)/shard_map/pmax | solution.py:94
  46.8 10.9 %psum.23 = f32[64,16]{0,1:T(8,128)S(1)} all-reduce(f32[64,16]{0,1:T(8,128)S(1)} %subtract_exponential_fusion.3), channel_id=1, replica_groups=mesh['groups'=2,'blk'=4,'head'=4] {'blk'}, use_global_device_ids=true, to_apply=%region_13.14 | all-reduce | flops 1024 | bytes 8192 | tf_op jit(solution)/shard_map/psum | solution.py:96
  58.1 1.3 %scatter_custom_fusion = f32[128,2048]{1,0:T(8,128)S(1)} fusion(s32[64]{0:T(128)S(1)} %compare_select_fusion, f32[8,8,16,128]{3,2,1,0:T(8,128)S(1)} %bitcast.8, bf16[64,2048]{1,0:T(8,128)(2,1)S(1)} %get-tuple-element.424, f32[]{:T(128)} %constant.275.clone.1), kind=kCustom, calls=%fused_computation.50 | custom fusion | flops 262144 | bytes 1835012 | tf_op jit(solution)/shard_map/scatter | solution.py:101
  61.4 57.1 %while.34 = (s32[]{:T(128)}, bf16[512,2048]{1,0:T(8,128)(2,1)S(1)}, bf16[512,2048]{1,0:T(8,128)(2,1)}, bf16[512,256]{1,0:T(8,128)(2,1)S(1)}, bf16[512,256]{1,0:T...) while((s32[]{:T(128)}, bf16[512,2048]{1,0:T(8,128)(2,1)S(1)}, ...), condition=%wide.region_7.8_spmd.clone, body=%wide.region_2.7_spmd.clone.sunk | while | flops 272563200 | bytes 7762787 | solution.py:67
  65.0 1.2 fusion.68
  66.2 1.2 fusion.69
  68.6 1.2 fusion.68
  69.8 1.2 fusion.69
  73.4 1.2 fusion.69
  77.0 1.2 fusion.69
  80.5 1.2 fusion.69
  84.1 1.2 fusion.69
  87.7 1.2 fusion.69
  91.3 1.2 fusion.69
  94.8 1.2 fusion.69
  98.4 1.2 fusion.69
  102.0 1.2 fusion.69
  105.6 1.2 fusion.69
  109.1 1.2 fusion.69
  111.5 1.2 fusion.68
  112.7 1.2 fusion.69
  118.6 1.3 %copy-done.1 = bf16[512,2048]{1,0:T(8,128)(2,1)} copy-done((bf16[512,2048]{1,0:T(8,128)(2,1)}, bf16[512,2048]{1,0:T(8,128)(2,1)S(1)}, u32[]{:S(2)}) %copy-start.1) | copy-done | bytes 2097176
  (207 shorter events, 51.4 us)
Async XLA Ops:
  7.2 16.7 %copy-start.4 = (bf16[512,256]{1,0:T(8,128)(2,1)S(1)}, bf16[512,256]{1,0:T(8,128)(2,1)}, u32[]{:S(2)}) copy-start(bf16[512,256]{1,0:T(8,128)(2,1)} %param.13) | copy-start | bytes 786436
  7.2 16.7 %copy-start = (bf16[512,256]{1,0:T(8,128)(2,1)S(1)}, bf16[512,256]{1,0:T(8,128)(2,1)}, u32[]{:S(2)}) copy-start(bf16[512,256]{1,0:T(8,128)(2,1)} %param.12) | copy-start | bytes 786436
  7.2 53.2 %all-reduce.3.cloned.1.call-start = ((), (), s32[]{:S(2)}) async-start(), calls=%async_computation.2 | async-start | bytes 1048576 | tf_op jit(solution)/shard_map/psum | solution.py:14
  8.1 110.5 %reduce-scatter.2.cloned.1.call-start = ((), (), s32[]{:S(2)}) async-start(), calls=%async_computation.1 | async-start | bytes 655360 | tf_op jit(solution)/shard_map/reduce_scatter | solution.py:102
  23.8 34.1 %copy-start.6 = (s32[64]{0:T(128)S(1)}, s32[64]{0:T(128)}, u32[]{:S(2)}) copy-start(s32[64]{0:T(128)} %param.16) | copy-start | bytes 772
  23.8 34.1 %copy-start.7 = (s32[64]{0:T(128)S(1)}, s32[64]{0:T(128)}, u32[]{:S(2)}) copy-start(s32[64]{0:T(128)} %param.15) | copy-start | bytes 772
  60.3 0.9 copy-start.5
  60.4 1.0 copy-start.2
  60.4 1.1 copy-start.3
  118.6 1.3 %copy-start.1 = (bf16[512,2048]{1,0:T(8,128)(2,1)}, bf16[512,2048]{1,0:T(8,128)(2,1)S(1)}, u32[]{:S(2)}) copy-start(bf16[512,2048]{1,0:T(8,128)(2,1)S(1)} %get-tuple-element.421) | copy-start | bytes 6291460
Sparse Core Ops, SparseCore 0:
  11.0 40.9 all-reduce.2
  60.5 17.6 reduce-scatter.1
where the time goes:
time: 128 us; the launch traced here: 127 us
  matrix products  59.5 us (46%)
  blocking collectives  36 us (28%)
  between operations  14.2 us (11%)
  other arithmetic  12 us (9%)
  local copies, waits for them, and re-layouts  3.25 us (3%)
  loops' own time  1.72 us (1%)
    dot_general x48, matrix products, soft_parts(): jnp.einsum('td,sd->ts', query_head, key_part, preferred_element_type=jnp....  43.6 us
    dot_general x48, matrix products, soft_parts(): jnp.dot(expo.astype(jnp.bfloat16), value_part, preferred_element_type=jnp...  15.9 us
    all_gather x1, blocking collectives, body(): all_queries = lax.all_gather(opt_query, 'blk', axis=0, tiled=True)  14.9 us
    psum x1, blocking collectives, body(): weight_sum = lax.psum(weight, 'blk')  10.9 us
    pmax x1, blocking collectives, body(): top_all = lax.pmax(stats, 'blk')  10.1 us
    reduce_sum x32, other arithmetic, soft_parts(): total = total + jnp.sum(expo, axis=1)  7.92 us
  transfers between devices with their start and end apart: 2, of which 0 were waited for; matrix products, arithmetic and copies ran while one was open for 57% of the time, Pallas kernels for 0%

commit v1 on v0

v1 whole, which is shorter than its diff:
```python
import functools
import math

import jax
import jax.numpy as jnp
from jax import lax
from jax.experimental import pallas as pl
from jax.experimental.pallas import tpu as pltpu
from jax.sharding import PartitionSpec as P

HD = 128
HQ = 64
KVH = 8
CAP = 32
GROUP = HQ // KVH
SCALE = HD ** (-0.5)
LOG2E = math.log2(math.e)
NEG = -1e30
TILE = 256
VMEM = pl.BlockSpec(memory_space=pltpu.VMEM)
SMEM = pl.BlockSpec(memory_space=pltpu.SMEM)


def nt(a, b):
    return lax.dot_general(a, b, (((1,), (1,)), ((), ())), preferred_element_type=jnp.float32)


def nn(a, b):
    return jnp.dot(a, b, preferred_element_type=jnp.float32)


def params(mib):
    return pltpu.CompilerParams(vmem_limit_bytes=mib * 1024 * 1024)


def split_kernel(heads, k_ref, v_ref, *outs):
    for g in range(heads):
        outs[2 * g][...] = k_ref[:, g * HD : (g + 1) * HD]
        outs[2 * g + 1][...] = v_ref[:, g * HD : (g + 1) * HD]


def split_heads(key, value):
    rows, heads = key.shape[0], key.shape[1] // HD
    shape = jax.ShapeDtypeStruct((rows, HD), key.dtype)
    outs = pl.pallas_call(
        functools.partial(split_kernel, heads),
        out_shape=[shape] * (2 * heads),
        in_specs=[VMEM] * 2,
        out_specs=[VMEM] * (2 * heads),
        compiler_params=params(16),
        name="split_heads",
    )(key, value)
    return [(outs[2 * g], outs[2 * g + 1]) for g in range(heads)]


def ctx_kernel(count, blk_ref, q_ref, k_ref, v_ref, *refs):
    cand = refs[:count]
    o_ref = refs[-4]
    ve, ka, vae = refs[-3:]
    rows = q_ref.shape[0]
    blk = blk_ref[0]

    @pl.when(pl.program_id(0) == 0)
    def _():
        ve[:, :HD] = v_ref[...]
        ve[:, HD:] = jnp.ones((rows, HD), jnp.bfloat16)
        vae[:, HD:] = jnp.ones((rows, HD), jnp.bfloat16)
        if count == 2:
            ka[...] = cand[0][...]
            vae[:, :HD] = cand[1][...]
        else:
            first_k, first_v, up, down = cand

            @pl.when(blk == 1)
            def _():
                ka[...] = down[...]
                vae[:, :HD] = up[...]

            @pl.when(blk == 2)
            def _():
                ka[...] = first_k[...]
                vae[:, :HD] = down[...]

            @pl.when(blk == 3)
            def _():
                ka[...] = up[...]
                vae[:, :HD] = first_v[...]

    row = lax.broadcasted_iota(jnp.int32, (TILE, TILE), 0)
    col = lax.broadcasted_iota(jnp.int32, (TILE, TILE), 1)

    def attend(anchor):
        for at in range(0, rows, TILE):
            q = q_ref[at : at + TILE, :]
            diag = jnp.where(row >= col, nt(q, k_ref[at : at + TILE, :]), NEG)
            scores = [(diag, ve[at : at + TILE, :])]
            if at:
                scores.append((nt(q, k_ref[:at, :]), ve[:at, :]))
            if anchor:
                scores.append((nt(q, ka[...]), vae[...]))
            top = functools.reduce(jnp.maximum, [jnp.max(s, axis=1, keepdims=True) for s, _ in scores])
            total = None
            for s, v in scores:
                p = jnp.exp2((s - top) * (SCALE * LOG2E)).astype(jnp.bfloat16)
                part = nn(p, v)
                total = part if total is None else total + part
            o_ref[at : at + TILE, :] = (total[:, :HD] / total[:, HD:]).astype(jnp.bfloat16)

    pl.when(blk == 0)(lambda: attend(False))
    pl.when(blk > 0)(lambda: attend(True))


def ctx_attention(blk, query, key, value, anchors, g, prior):
    rows = query.shape[0]
    whole = pl.BlockSpec((rows, HD), lambda h: (0, 0))
    column = pl.BlockSpec((rows, HD), lambda h: (0, g * GROUP + h))
    args = [blk, query, key, value, *anchors]
    specs = [SMEM, column] + [whole] * (2 + len(anchors))
    alias = {}
    if prior is not None:
        alias = {len(args): 0}
        args.append(prior)
        specs.append(pl.BlockSpec(memory_space=pl.ANY))
    flops = 4 * GROUP * rows * rows * HD * 2
    return pl.pallas_call(
        functools.partial(ctx_kernel, len(anchors)),
        grid=(GROUP,),
        out_shape=jax.ShapeDtypeStruct(query.shape, query.dtype),
        in_specs=specs,
        out_specs=column,
        scratch_shapes=[
            pltpu.VMEM((rows, 2 * HD), jnp.bfloat16),
            pltpu.VMEM((rows, HD), jnp.bfloat16),
            pltpu.VMEM((rows, 2 * HD), jnp.bfloat16),
        ],
        input_output_aliases=alias,
        compiler_params=params(32),
        cost_estimate=pl.CostEstimate(flops=flops, bytes_accessed=4 * GROUP * rows * HD, transcendentals=2 * GROUP * rows * rows),
        name="ctx_attention",
    )(*args)


def option_kernel(n, heads, blk_ref, owner_ref, slot_ref, length_ref, k_ref, v_ref, *refs):
    queries, outs, (q_all, part) = refs[:n], refs[n : 2 * n], refs[2 * n :]
    blk = blk_ref[0]
    rows = k_ref.shape[0]
    each = queries[0].shape[0]
    options = n * each
    for d in range(n):
        at = lax.rem(blk + n - d, n) * each
        q_all[pl.ds(pl.multiple_of(at, each), each), :] = queries[d][...]
    eye = lax.broadcasted_iota(jnp.int32, (options, options), 0) == lax.broadcasted_iota(jnp.int32, (options, options), 1)
    length = jnp.sum(jnp.where(eye, length_ref[...].astype(jnp.float32), 0.0), axis=1, keepdims=True)
    seen = length - (blk * rows).astype(jnp.float32)
    lane = lax.broadcasted_iota(jnp.int32, (options, HD), 1)
    logs = jnp.zeros((options, HD), jnp.float32)
    stack = max(1, min(GROUP, 512 // options))
    spots = lax.broadcasted_iota(jnp.int32, (options * stack, rows), 1).astype(jnp.float32)
    seen_all = jnp.concatenate([seen] * stack, axis=0)
    for first in range(0, heads, stack):
        g = first // GROUP
        q = jnp.concatenate([q_all[:, h * HD : (h + 1) * HD] for h in range(first, first + stack)], axis=0)
        s = nt(q, k_ref[:, g * HD : (g + 1) * HD])
        s = jnp.where(spots < seen_all, s, NEG)
        top = jnp.max(s, axis=1, keepdims=True)
        e = jnp.exp2((s - top) * (SCALE * LOG2E))
        z = jnp.sum(e, axis=1, keepdims=True)
        o = nn(e.astype(jnp.bfloat16), v_ref[:, g * HD : (g + 1) * HD]) / z
        live = seen_all > 0
        o = jnp.where(live, o, 0.0).astype(jnp.bfloat16)
        log = jnp.where(live, top * SCALE + jnp.log(z), NEG)
        for j in range(stack):
            h = first + j
            part[:, h * HD : (h + 1) * HD] = o[j * options : (j + 1) * options]
            logs = jnp.where(lax.rem(lane, heads) == h, log[j * options : (j + 1) * options], logs)
    high = logs.astype(jnp.bfloat16)
    rest = logs - high.astype(jnp.float32)
    mid = rest.astype(jnp.bfloat16)
    low = (rest - mid.astype(jnp.float32)).astype(jnp.bfloat16)
    part[:, heads * HD :] = jnp.where(
        lane < heads,
        high.astype(jnp.float32),
        jnp.where(lane < 2 * heads, mid.astype(jnp.float32), jnp.where(lane < 3 * heads, low.astype(jnp.float32), 0.0)),
    ).astype(jnp.bfloat16)
    slot = lax.broadcasted_iota(jnp.int32, (CAP, options), 0)
    for d in range(n):
        target = lax.rem(blk + d, n)
        pick = (owner_ref[...] == target) & (slot_ref[...] == slot)
        outs[d][...] = nn(jnp.where(pick, 1.0, 0.0).astype(jnp.bfloat16), part[...]).astype(jnp.bfloat16)


def option_partials(blk, owner, slot, length, key, value, queries):
    n, heads = len(queries), queries[0].shape[1] // HD
    options = n * queries[0].shape[0]
    width = (heads + 1) * HD
    row = lambda x: x.reshape(1, options)
    return pl.pallas_call(
        functools.partial(option_kernel, n, heads),
        out_shape=[jax.ShapeDtypeStruct((CAP, width), jnp.bfloat16)] * n,
        in_specs=[SMEM] + [VMEM] * (5 + n),
        out_specs=[VMEM] * n,
        scratch_shapes=[
            pltpu.VMEM((options, heads * HD), jnp.bfloat16),
            pltpu.VMEM((options, width), jnp.bfloat16),
        ],
        compiler_params=params(32),
        cost_estimate=pl.CostEstimate(
            flops=4 * options * heads * key.shape[0] * HD, bytes_accessed=1 << 20, transcendentals=options * heads * key.shape[0]
        ),
        name="option_partials",
    )(blk, row(owner), row(slot), row(length), key, value, *queries)


def merge_kernel(heads, *refs):
    parts, o_ref = refs[:-1], refs[-1]
    width = heads * HD
    lane = lax.broadcasted_iota(jnp.int32, (HD, width), 0)
    head = lax.broadcasted_iota(jnp.int32, (HD, width), 1) // HD
    pick = jnp.where((lax.rem(lane, heads) == head) & (lane < 3 * heads), 1.0, 0.0).astype(jnp.bfloat16)
    logs = [nn(p[:, width:], pick) for p in parts]
    top = functools.reduce(jnp.maximum, logs)
    weights = [jnp.exp(log - top) for log in logs]
    total = sum(weights[1:], weights[0])
    merged = sum(w * p[:, :width].astype(jnp.float32) for w, p in zip(weights, parts))
    o_ref[...] = (merged / total).astype(jnp.bfloat16)


def merge(parts):
    heads = parts[0].shape[1] // HD - 1
    return pl.pallas_call(
        functools.partial(merge_kernel, heads),
        out_shape=jax.ShapeDtypeStruct((CAP, heads * HD), jnp.bfloat16),
        in_specs=[VMEM] * len(parts),
        out_specs=VMEM,
        compiler_params=params(32),
        name="merge",
    )(*parts)


def shifted(x, n, d):
    return lax.ppermute(x, "blk", [(i, (i + d) % n) for i in range(n)])


def from_root(x, blk):
    return lax.psum(jnp.where(blk == 0, x, jnp.zeros_like(x)), "blk")


def body(ctx_query, ctx_key, ctx_value, opt_query, opt_owner, opt_slot, opt_length):
    n = lax.axis_size("blk")
    blk = lax.axis_index("blk")
    blk_arr = blk.astype(jnp.int32).reshape(1)
    queries = [opt_query] + [shifted(opt_query, n, d) for d in range(1, n)]
    local = split_heads(ctx_key, ctx_value)
    if n == 4:
        anchors = []
        for key, value in local:
            first_k = lax.ppermute(key, "blk", [(0, 2)])
            first_v = lax.ppermute(value, "blk", [(0, 3)])
            held = jnp.where(blk == 2, first_k, first_v)
            up = lax.ppermute(held, "blk", [(2, 3), (3, 1)])
            down = lax.ppermute(held, "blk", [(2, 1), (3, 2)])
            anchors.append((first_k, first_v, up, down))
    else:
        anchors = [(from_root(key, blk), from_root(value, blk)) for key, value in local]
    sends = option_partials(blk_arr, opt_owner, opt_slot, opt_length, ctx_key, ctx_value, queries)
    parts = [sends[0]] + [shifted(sends[d], n, d) for d in range(1, n)]
    ctx_out = None
    for g, (key, value) in enumerate(local):
        ctx_out = ctx_attention(blk_arr, ctx_query, key, value, anchors[g], g, ctx_out)
    opt_out = merge(parts)
    return (ctx_out, opt_out)


def solution(mesh):
    spread = P(("groups", "blk"), "head")
    return jax.shard_map(
        body,
        mesh=mesh,
        in_specs=(spread, spread, spread, spread, P("groups"), P("groups"), P("groups")),
        out_specs=(spread, spread),
        check_vma=False,
    )
```

time: 128 us -> 75.9 us (0.59)
  matrix products: 59.5 us -> 0 us
  blocking collectives: 36 us -> 0 us
  Pallas kernels: 0 us -> 24.7 us
  waiting for transfers between devices: 0.07 us -> 22.3 us
  starting transfers between devices: 0.08 us -> 20.9 us
  between operations: 14.2 us -> 0.76 us
  other arithmetic: 12 us -> 0.03 us
  local copies, waits for them, and re-layouts: 3.25 us -> 6.6 us
  loops' own time: 1.72 us -> 0 us
    dot_general x96 -> x0, matrix products: 59.5 us -> none  [the longest x48 43.6 us: soft_parts(): jnp.einsum('td,sd->ts', query_head, key_part, preferred_element_type=jnp....]
    pallas_call x0 -> x5, Pallas kernels: none -> 24.7 us  [the longest x2 21.4 us: ctx_attention(): pl.pallas_call(functools.partial(ctx_kernel, len(anchors)), grid=(GROUP,)...]
    ppermute x0 -> x14, waiting for transfers between devices: none -> 22.3 us  [the longest x6 20.1 us: shifted(): return lax.ppermute(x, 'blk', [(i, (i + d) % n) for i in range(n)])]
    ppermute x0 -> x14, starting transfers between devices: none -> 20.9 us  [the longest x6 13.1 us: shifted(): return lax.ppermute(x, 'blk', [(i, (i + d) % n) for i in range(n)])]
    all_gather x1 -> x0, blocking collectives: 14.9 us -> none  [body(): all_queries = lax.all_gather(opt_query, 'blk', axis=0, tiled=True)]
    psum x1 -> x0, blocking collectives: 10.9 us -> none  [body(): weight_sum = lax.psum(weight, 'blk')]
    pmax x1 -> x0, blocking collectives: 10.1 us -> none  [body(): top_all = lax.pmax(stats, 'blk')]
    reduce_sum x32 -> x0, other arithmetic: 7.92 us -> none  [soft_parts(): total = total + jnp.sum(expo, axis=1)]
  transfers between devices with their start and end apart: 2 -> 14, of which waited for: 0 -> 5; matrix products, arithmetic and copies ran while one was open for 57% -> 0% of each run, Pallas kernels for 0% -> 18%
where the time goes in v1:
time: 75.9 us; the launch traced here: 75.3 us
  Pallas kernels  24.7 us (33%)
  waiting for transfers between devices  22.3 us (29%)
  starting transfers between devices  20.9 us (28%)
  local copies, waits for them, and re-layouts  6.6 us (9%)
  between operations  0.76 us (1%)
    pallas_call x2, Pallas kernels, ctx_attention(): pl.pallas_call(functools.partial(ctx_kernel, len(anchors)), grid=(GROUP,)...  21.4 us
    ppermute x6, waiting for transfers between devices, shifted(): return lax.ppermute(x, 'blk', [(i, (i + d) % n) for i in range(n)])  20.1 us
    ppermute x6, starting transfers between devices, shifted(): return lax.ppermute(x, 'blk', [(i, (i + d) % n) for i in range(n)])  13.1 us
    unnamed x18, local copies, waits for them, and re-layouts  6.6 us
    ppermute x2, starting transfers between devices, body(): up = lax.ppermute(held, 'blk', [(2, 3), (3, 1)])  2.58 us
    ppermute x2, starting transfers between devices, body(): down = lax.ppermute(held, 'blk', [(2, 1), (3, 2)])  2.57 us
    ppermute x2, waiting for transfers between devices, body(): down = lax.ppermute(held, 'blk', [(2, 1), (3, 2)])  2.12 us
    pallas_call x1, Pallas kernels, option_partials(): pl.pallas_call(functools.partial(option_kernel, n, heads), out_shape=[jax...  2.02 us
  transfers between devices with their start and end apart: 14, of which 5 were waited for; matrix products, arithmetic and copies ran while one was open for 0% of the time, Pallas kernels for 18%

profile of v1, /device:TPU:12, one launch (start us, length us, event | category | flops | bytes accessed | tf_op | source)
XLA Modules:
  0.0 75.3 jit_solution(18440423702704995960)
XLA Ops:
  0.6 0.9 %copy-done = bf16[512,256]{1,0:T(8,128)(2,1)S(1)} copy-done((bf16[512,256]{1,0:T(8,128)(2,1)S(1)}, bf16[512,256]{1,0:T(8,128)(2,1)}, u32[]{:S(2)}) %copy-start) | copy-done | bytes 262168
  1.6 0.9 %copy-done.2 = bf16[512,256]{1,0:T(8,128)(2,1)S(1)} copy-done((bf16[512,256]{1,0:T(8,128)(2,1)S(1)}, bf16[512,256]{1,0:T(8,128)(2,1)}, u32[]{:S(2)}) %copy-start.2) | copy-done | bytes 262168
  2.6 0.7 collective-permute-start.4
  3.3 0.7 collective-permute-start.5
  4.0 5.3 %collective-permute-start.10 = (bf16[16,2048]{1,0:T(8,128)(2,1)}, bf16[16,2048]{1,0:T(8,128)(2,1)S(1)}, u32[]{:S(2)}, u32[]{:S(2)}) collective-permute-start(bf16[16,2048]{1,0:T(8,128)(2,1)} %refs_0_.1), channel_id=1, source_target_pairs={{0,12},{4,0},{8,4},{12,8},{1,13},{5,1},{9,5},{13,9},{2,14},{6,2},{... | collective-permute-start | bytes 196616 | tf_op jit(solution)/shard_map/ppermute | solution.py:241
  9.3 2.4 %collective-permute-start.9 = (bf16[16,2048]{1,0:T(8,128)(2,1)}, bf16[16,2048]{1,0:T(8,128)(2,1)S(1)}, u32[]{:S(2)}, u32[]{:S(2)}) collective-permute-start(bf16[16,2048]{1,0:T(8,128)(2,1)} %refs_0_.1), channel_id=1, source_target_pairs={{0,8},{4,12},{8,0},{12,4},{1,9},{5,13},{9,1},{13,5},{2,10},{6,14},... | collective-permute-start | bytes 196616 | tf_op jit(solution)/shard_map/ppermute | solution.py:241
  12.4 5.1 %collective-permute-done.8.refs_1_ = bf16[16,2048]{1,0:T(8,128)(2,1)S(1)} collective-permute-done((bf16[16,2048]{1,0:T(8,128)(2,1)}, bf16[16,2048]{1,0:T(8,128)(2,1)S(1)}, u32[]{:S(2)}, u32[]{:S(2)}) %collective-permute-start.8) | collective-permute-done | bytes 65568 | tf_op jit(solution)/shard_map/ppermute | solution.py:241
  18.2 4.3 %collective-permute-done.9.refs_2_ = bf16[16,2048]{1,0:T(8,128)(2,1)S(1)} collective-permute-done((bf16[16,2048]{1,0:T(8,128)(2,1)}, bf16[16,2048]{1,0:T(8,128)(2,1)S(1)}, u32[]{:S(2)}, u32[]{:S(2)}) %collective-permute-start.9) | collective-permute-done | bytes 65568 | tf_op jit(solution)/shard_map/ppermute | solution.py:241
  22.5 0.9 %copy-done.1 = bf16[512,256]{1,0:T(8,128)(2,1)S(1)} copy-done((bf16[512,256]{1,0:T(8,128)(2,1)S(1)}, bf16[512,256]{1,0:T(8,128)(2,1)}, u32[]{:S(2)}) %copy-start.1) | copy-done | bytes 262168
  23.4 0.9 %copy-done.3 = bf16[512,256]{1,0:T(8,128)(2,1)S(1)} copy-done((bf16[512,256]{1,0:T(8,128)(2,1)S(1)}, bf16[512,256]{1,0:T(8,128)(2,1)}, u32[]{:S(2)}) %copy-start.3) | copy-done | bytes 262168
  24.4 0.8 %copy-done.5 = bf16[16,2048]{1,0:T(8,128)(2,1)S(1)} copy-done((bf16[16,2048]{1,0:T(8,128)(2,1)S(1)}, bf16[16,2048]{1,0:T(8,128)(2,1)}, u32[]{:S(2)}) %copy-start.5) | copy-done | bytes 65560
  27.2 2.0 %option_partials.1 = (bf16[32,2176]{1,0:T(8,128)(2,1)S(1)}, bf16[32,2176]{1,0:T(8,128)(2,1)S(1)}, bf16[32,2176]{1,0:T(8,128)(2,1)S(1)}, bf16[32,2176]{1,0:T(8,128)(2,1)S(1)}) custom-call(s32[1]{0:T(128)} %bitcast.blk_ref, s32[1,64]{1,0:T(1,128)S(1)} %bitcast.4, s32[1,64]{1,0:T(1,128)S(1)} %bitcast.5, s32[1,64]{1,0:T(1,128)S(1)} %bitcast.6, ...), custom_call_target="tpu_custom_call" | custom-call | flops 268435456 | bytes 1048576 | tf_op jit(solution)/shard_map/option_partials/pallas_call | solution.py:197
  29.6 3.0 %collective-permute-start.12 = (bf16[32,2176]{1,0:T(8,128)(2,1)S(1)}, bf16[32,2176]{1,0:T(8,128)(2,1)S(1)}, u32[]{:S(2)}, u32[]{:S(2)}) collective-permute-start(bf16[32,2176]{1,0:T(8,128)(2,1)S(1)} %get-tuple-element.16), channel_id=1, source_target_pairs={{0,8},{4,12},{8,0},{12,4},{1,9},{5,13},{9,1},{13,5},{2,10},{6,14},... | collective-permute-start | bytes 417800 | tf_op jit(solution)/shard_map/ppermute | solution.py:241
  32.7 1.9 %collective-permute-start.13 = (bf16[32,2176]{1,0:T(8,128)(2,1)S(1)}, bf16[32,2176]{1,0:T(8,128)(2,1)S(1)}, u32[]{:S(2)}, u32[]{:S(2)}) collective-permute-start(bf16[32,2176]{1,0:T(8,128)(2,1)S(1)} %get-tuple-element.17), channel_id=1, source_target_pairs={{0,12},{4,0},{8,4},{12,8},{1,13},{5,1},{9,5},{13,9},{2,14},{6,2},{... | collective-permute-start | bytes 417800 | tf_op jit(solution)/shard_map/ppermute | solution.py:241
  34.6 1.3 %collective-permute-start.6 = (bf16[512,128]{1,0:T(8,128)(2,1)S(1)}, bf16[512,128]{1,0:T(8,128)(2,1)S(1)}, u32[]{:S(2)}, u32[]{:S(2)}) collective-permute-start(bf16[512,128]{1,0:T(8,128)(2,1)S(1)} %broadcast_select_fusion), channel_id=1, source_target_pairs={{8,12},{12,4},{9,13},{13,5},{10,14},{14,6},{11,15},{15,7},{24,28},... | collective-permute-start | bytes 393224 | tf_op jit(solution)/shard_map/ppermute | solution.py:260
  35.9 1.3 %collective-permute-start.7 = (bf16[512,128]{1,0:T(8,128)(2,1)S(1)}, bf16[512,128]{1,0:T(8,128)(2,1)S(1)}, u32[]{:S(2)}, u32[]{:S(2)}) collective-permute-start(bf16[512,128]{1,0:T(8,128)(2,1)S(1)} %broadcast_select_fusion), channel_id=1, source_target_pairs={{8,4},{12,8},{9,5},{13,9},{10,6},{14,10},{11,7},{15,11},{24,20},{2... | collective-permute-start | bytes 393224 | tf_op jit(solution)/shard_map/ppermute | solution.py:261
  37.3 1.3 %collective-permute-start.2 = (bf16[512,128]{1,0:T(8,128)(2,1)S(1)}, bf16[512,128]{1,0:T(8,128)(2,1)S(1)}, u32[]{:S(2)}, u32[]{:S(2)}) collective-permute-start(bf16[512,128]{1,0:T(8,128)(2,1)S(1)} %broadcast_select_fusion.1), channel_id=1, source_target_pairs={{8,12},{12,4},{9,13},{13,5},{10,14},{14,6},{11,15},{15,7},{24,28},... | collective-permute-start | bytes 393224 | tf_op jit(solution)/shard_map/ppermute | solution.py:260
  38.6 3.3 %collective-permute-done.12.refs_2_ = bf16[32,2176]{1,0:T(8,128)(2,1)S(1)} collective-permute-done((bf16[32,2176]{1,0:T(8,128)(2,1)S(1)}, bf16[32,2176]{1,0:T(8,128)(2,1)S(1)}, u32[]{:S(2)}, u32[]{:S(2)}) %collective-permute-start.12) | collective-permute-done | bytes 139296 | tf_op jit(solution)/shard_map/ppermute | solution.py:241
  41.8 1.3 %collective-permute-start.3 = (bf16[512,128]{1,0:T(8,128)(2,1)S(1)}, bf16[512,128]{1,0:T(8,128)(2,1)S(1)}, u32[]{:S(2)}, u32[]{:S(2)}) collective-permute-start(bf16[512,128]{1,0:T(8,128)(2,1)S(1)} %broadcast_select_fusion.1), channel_id=1, source_target_pairs={{8,4},{12,8},{9,5},{13,9},{10,6},{14,10},{11,7},{15,11},{24,20},{2... | collective-permute-start | bytes 393224 | tf_op jit(solution)/shard_map/ppermute | solution.py:261
  43.1 7.5 %collective-permute-done.13.refs_3_ = bf16[32,2176]{1,0:T(8,128)(2,1)S(1)} collective-permute-done((bf16[32,2176]{1,0:T(8,128)(2,1)S(1)}, bf16[32,2176]{1,0:T(8,128)(2,1)S(1)}, u32[]{:S(2)}, u32[]{:S(2)}) %collective-permute-start.13) | collective-permute-done | bytes 139296 | tf_op jit(solution)/shard_map/ppermute | solution.py:241
  50.6 1.2 %merge.1 = bf16[32,2048]{1,0:T(8,128)(2,1)} custom-call(bf16[32,2176]{1,0:T(8,128)(2,1)S(1)} %get-tuple-element.14.refs_0_, bf16[32,2176]{1,0:T(8,128)(2,1)S(1)} %collective-permute-done.11.refs_1_, bf16[32,2176]{1,0:T(8,128)(2,1)S(1)} %collective-permute-done.12.refs_2_, bf16[32,2176]{1,0:T(8,128)(2,1)S(1)} %collective-permute-done.13.refs_3_), custom_call_target="tpu_custom_call" | custom-call | tf_op jit(solution)/shard_map/merge/pallas_call | solution.py:230
  51.8 2.1 %collective-permute-done.7.refs_3_ = bf16[512,128]{1,0:T(8,128)(2,1)S(1)} collective-permute-done((bf16[512,128]{1,0:T(8,128)(2,1)S(1)}, bf16[512,128]{1,0:T(8,128)(2,1)S(1)}, u32[]{:S(2)}, u32[]{:S(2)}) %collective-permute-start.7) | collective-permute-done | bytes 131104 | tf_op jit(solution)/shard_map/ppermute | solution.py:261
  53.9 10.7 %ctx_attention.2.refs_4_ = bf16[512,2048]{1,0:T(8,128)(2,1)} custom-call(s32[1]{0:T(128)} %bitcast.blk_ref, bf16[512,2048]{1,0:T(8,128)(2,1)S(1)} %copy-done.4, bf16[512,128]{1,0:T(8,128)(2,1)S(1)} %get-tuple-element.12.k_ref, bf16[512,128]{1,0:T(8,128)(2,1)S(1)} %get-tuple-element.13.v_ref, bf16[512,128]{1,0:T(8,128)(2,1)S(1)} %collective-permute-done.4.refs_0_, ...), custom_call_target="tpu_custom_call" | custom-call | flops 2147483648 | bytes 2097152 | tf_op jit(solution)/shard_map/ctx_attention/pallas_call | solution.py:125
  64.6 10.7 %ctx_attention.3 = bf16[512,2048]{1,0:T(8,128)(2,1)} custom-call(s32[1]{0:T(128)} %bitcast.blk_ref, bf16[512,2048]{1,0:T(8,128)(2,1)S(1)} %copy-done.4, bf16[512,128]{1,0:T(8,128)(2,1)S(1)} %get-tuple-element.10.k_ref, bf16[512,128]{1,0:T(8,128)(2,1)S(1)} %get-tuple-element.11.v_ref, ...), custom_call_target="tpu_custom_call", output_to_operand_aliasing={{}: (8, {})} | custom-call | flops 2147483648 | bytes 2097152 | tf_op jit(solution)/shard_map/ctx_attention/pallas_call | solution.py:125
  (29 shorter events, 3.8 us)
Async XLA Ops:
  0.6 1.0 %copy-start = (bf16[512,256]{1,0:T(8,128)(2,1)S(1)}, bf16[512,256]{1,0:T(8,128)(2,1)}, u32[]{:S(2)}) copy-start(bf16[512,256]{1,0:T(8,128)(2,1)} %k_ref.3) | copy-start | bytes 786436
  1.6 0.9 %copy-start.2 = (bf16[512,256]{1,0:T(8,128)(2,1)S(1)}, bf16[512,256]{1,0:T(8,128)(2,1)}, u32[]{:S(2)}) copy-start(bf16[512,256]{1,0:T(8,128)(2,1)} %v_ref.3) | copy-start | bytes 786436
  2.6 27.0 %collective-permute-start.4 = (bf16[512,128]{1,0:T(8,128)(2,1)S(1)}, bf16[512,128]{1,0:T(8,128)(2,1)S(1)}, u32[]{:S(2)}, u32[]{:S(2)}) collective-permute-start(bf16[512,128]{1,0:T(8,128)(2,1)S(1)} %get-tuple-element.12.k_ref), channel_id=1, source_target_pairs={{0,8},{1,9},{2,10},{3,11},{16,24},{17,25},{18,26},{19,27}} | collective-permute-start | bytes 393224 | tf_op jit(solution)/shard_map/ppermute | solution.py:257
  3.3 29.4 %collective-permute-start.5 = (bf16[512,128]{1,0:T(8,128)(2,1)S(1)}, bf16[512,128]{1,0:T(8,128)(2,1)S(1)}, u32[]{:S(2)}, u32[]{:S(2)}) collective-permute-start(bf16[512,128]{1,0:T(8,128)(2,1)S(1)} %get-tuple-element.13.v_ref), channel_id=1, source_target_pairs={{0,12},{1,13},{2,14},{3,15},{16,28},{17,29},{18,30},{19,31}} | collective-permute-start | bytes 393224 | tf_op jit(solution)/shard_map/ppermute | solution.py:258
  4.0 7.8 %collective-permute-start.10 = (bf16[16,2048]{1,0:T(8,128)(2,1)}, bf16[16,2048]{1,0:T(8,128)(2,1)S(1)}, u32[]{:S(2)}, u32[]{:S(2)}) collective-permute-start(bf16[16,2048]{1,0:T(8,128)(2,1)} %refs_0_.1), channel_id=1, source_target_pairs={{0,12},{4,0},{8,4},{12,8},{1,13},{5,1},{9,5},{13,9},{2,14},{6,2},{... | collective-permute-start | bytes 196616 | tf_op jit(solution)/shard_map/ppermute | solution.py:241
  9.3 8.2 %collective-permute-start.8 = (bf16[16,2048]{1,0:T(8,128)(2,1)}, bf16[16,2048]{1,0:T(8,128)(2,1)S(1)}, u32[]{:S(2)}, u32[]{:S(2)}) collective-permute-start(bf16[16,2048]{1,0:T(8,128)(2,1)} %refs_0_.1), channel_id=1, source_target_pairs={{0,4},{4,8},{8,12},{12,0},{1,5},{5,9},{9,13},{13,1},{2,6},{6,10},{... | collective-permute-start | bytes 196616 | tf_op jit(solution)/shard_map/ppermute | solution.py:241
  9.3 13.2 %collective-permute-start.9 = (bf16[16,2048]{1,0:T(8,128)(2,1)}, bf16[16,2048]{1,0:T(8,128)(2,1)S(1)}, u32[]{:S(2)}, u32[]{:S(2)}) collective-permute-start(bf16[16,2048]{1,0:T(8,128)(2,1)} %refs_0_.1), channel_id=1, source_target_pairs={{0,8},{4,12},{8,0},{12,4},{1,9},{5,13},{9,1},{13,5},{2,10},{6,14},... | collective-permute-start | bytes 196616 | tf_op jit(solution)/shard_map/ppermute | solution.py:241
  11.8 22.9 %collective-permute-start = (bf16[512,128]{1,0:T(8,128)(2,1)S(1)}, bf16[512,128]{1,0:T(8,128)(2,1)S(1)}, u32[]{:S(2)}, u32[]{:S(2)}) collective-permute-start(bf16[512,128]{1,0:T(8,128)(2,1)S(1)} %get-tuple-element.10.k_ref), channel_id=1, source_target_pairs={{0,8},{1,9},{2,10},{3,11},{16,24},{17,25},{18,26},{19,27}} | collective-permute-start | bytes 393224 | tf_op jit(solution)/shard_map/ppermute | solution.py:257
  17.6 18.4 %collective-permute-start.1 = (bf16[512,128]{1,0:T(8,128)(2,1)S(1)}, bf16[512,128]{1,0:T(8,128)(2,1)S(1)}, u32[]{:S(2)}, u32[]{:S(2)}) collective-permute-start(bf16[512,128]{1,0:T(8,128)(2,1)S(1)} %get-tuple-element.11.v_ref), channel_id=1, source_target_pairs={{0,12},{1,13},{2,14},{3,15},{16,28},{17,29},{18,30},{19,31}} | collective-permute-start | bytes 393224 | tf_op jit(solution)/shard_map/ppermute | solution.py:258
  22.5 0.9 %copy-start.1 = (bf16[512,256]{1,0:T(8,128)(2,1)S(1)}, bf16[512,256]{1,0:T(8,128)(2,1)}, u32[]{:S(2)}) copy-start(bf16[512,256]{1,0:T(8,128)(2,1)} %k_ref.3) | copy-start | bytes 786436
  23.4 0.9 %copy-start.3 = (bf16[512,256]{1,0:T(8,128)(2,1)S(1)}, bf16[512,256]{1,0:T(8,128)(2,1)}, u32[]{:S(2)}) copy-start(bf16[512,256]{1,0:T(8,128)(2,1)} %v_ref.3) | copy-start | bytes 786436
  24.4 0.8 %copy-start.5 = (bf16[16,2048]{1,0:T(8,128)(2,1)S(1)}, bf16[16,2048]{1,0:T(8,128)(2,1)}, u32[]{:S(2)}) copy-start(bf16[16,2048]{1,0:T(8,128)(2,1)} %refs_0_.1) | copy-start | bytes 196612
  25.2 0.7 copy-start.6
  25.9 0.7 copy-start.7
  26.5 0.7 copy-start.8
  27.2 26.7 %copy-start.4 = (bf16[512,2048]{1,0:T(8,128)(2,1)S(1)}, bf16[512,2048]{1,0:T(8,128)(2,1)}, u32[]{:S(2)}) copy-start(bf16[512,2048]{1,0:T(8,128)(2,1)} %q_ref.3) | copy-start | bytes 6291460
  29.2 8.0 %collective-permute-start.11 = (bf16[32,2176]{1,0:T(8,128)(2,1)S(1)}, bf16[32,2176]{1,0:T(8,128)(2,1)S(1)}, u32[]{:S(2)}, u32[]{:S(2)}) collective-permute-start(bf16[32,2176]{1,0:T(8,128)(2,1)S(1)} %get-tuple-element.15), channel_id=1, source_target_pairs={{0,4},{4,8},{8,12},{12,0},{1,5},{5,9},{9,13},{13,1},{2,6},{6,10},{... | collective-permute-start | bytes 417800 | tf_op jit(solution)/shard_map/ppermute | solution.py:241
  29.6 12.2 %collective-permute-start.12 = (bf16[32,2176]{1,0:T(8,128)(2,1)S(1)}, bf16[32,2176]{1,0:T(8,128)(2,1)S(1)}, u32[]{:S(2)}, u32[]{:S(2)}) collective-permute-start(bf16[32,2176]{1,0:T(8,128)(2,1)S(1)} %get-tuple-element.16), channel_id=1, source_target_pairs={{0,8},{4,12},{8,0},{12,4},{1,9},{5,13},{9,1},{13,5},{2,10},{6,14},... | collective-permute-start | bytes 417800 | tf_op jit(solution)/shard_map/ppermute | solution.py:241
  32.7 17.9 %collective-permute-start.13 = (bf16[32,2176]{1,0:T(8,128)(2,1)S(1)}, bf16[32,2176]{1,0:T(8,128)(2,1)S(1)}, u32[]{:S(2)}, u32[]{:S(2)}) collective-permute-start(bf16[32,2176]{1,0:T(8,128)(2,1)S(1)} %get-tuple-element.17), channel_id=1, source_target_pairs={{0,12},{4,0},{8,4},{12,8},{1,13},{5,1},{9,5},{13,9},{2,14},{6,2},{... | collective-permute-start | bytes 417800 | tf_op jit(solution)/shard_map/ppermute | solution.py:241
  34.6 17.1 %collective-permute-start.6 = (bf16[512,128]{1,0:T(8,128)(2,1)S(1)}, bf16[512,128]{1,0:T(8,128)(2,1)S(1)}, u32[]{:S(2)}, u32[]{:S(2)}) collective-permute-start(bf16[512,128]{1,0:T(8,128)(2,1)S(1)} %broadcast_select_fusion), channel_id=1, source_target_pairs={{8,12},{12,4},{9,13},{13,5},{10,14},{14,6},{11,15},{15,7},{24,28},... | collective-permute-start | bytes 393224 | tf_op jit(solution)/shard_map/ppermute | solution.py:260
  35.9 18.0 %collective-permute-start.7 = (bf16[512,128]{1,0:T(8,128)(2,1)S(1)}, bf16[512,128]{1,0:T(8,128)(2,1)S(1)}, u32[]{:S(2)}, u32[]{:S(2)}) collective-permute-start(bf16[512,128]{1,0:T(8,128)(2,1)S(1)} %broadcast_select_fusion), channel_id=1, source_target_pairs={{8,4},{12,8},{9,5},{13,9},{10,6},{14,10},{11,7},{15,11},{24,20},{2... | collective-permute-start | bytes 393224 | tf_op jit(solution)/shard_map/ppermute | solution.py:261
  37.3 27.3 %collective-permute-start.2 = (bf16[512,128]{1,0:T(8,128)(2,1)S(1)}, bf16[512,128]{1,0:T(8,128)(2,1)S(1)}, u32[]{:S(2)}, u32[]{:S(2)}) collective-permute-start(bf16[512,128]{1,0:T(8,128)(2,1)S(1)} %broadcast_select_fusion.1), channel_id=1, source_target_pairs={{8,12},{12,4},{9,13},{13,5},{10,14},{14,6},{11,15},{15,7},{24,28},... | collective-permute-start | bytes 393224 | tf_op jit(solution)/shard_map/ppermute | solution.py:260
  41.8 22.8 %collective-permute-start.3 = (bf16[512,128]{1,0:T(8,128)(2,1)S(1)}, bf16[512,128]{1,0:T(8,128)(2,1)S(1)}, u32[]{:S(2)}, u32[]{:S(2)}) collective-permute-start(bf16[512,128]{1,0:T(8,128)(2,1)S(1)} %broadcast_select_fusion.1), channel_id=1, source_target_pairs={{8,4},{12,8},{9,5},{13,9},{10,6},{14,10},{11,7},{15,11},{24,20},{2... | collective-permute-start | bytes 393224 | tf_op jit(solution)/shard_map/ppermute | solution.py:261

commit v2 on v1

v2 whole, which is shorter than its diff:
```python
import functools
import math

import jax
import jax.numpy as jnp
from jax import lax
from jax.experimental import pallas as pl
from jax.experimental.pallas import tpu as pltpu
from jax.sharding import PartitionSpec as P

HD = 128
HQ = 64
KVH = 8
CAP = 32
GROUP = HQ // KVH
SCALE = HD ** (-0.5)
C2 = SCALE * math.log2(math.e)
NEG = -1e30
TILE = 256
PAIR = 2
VMEM = pl.BlockSpec(memory_space=pltpu.VMEM)
SMEM = pl.BlockSpec(memory_space=pltpu.SMEM)
HBM = pl.BlockSpec(memory_space=pltpu.HBM)
ANY = pl.BlockSpec(memory_space=pl.ANY)


def nt(a, b):
    return lax.dot_general(a, b, (((1,), (1,)), ((), ())), preferred_element_type=jnp.float32)


def nn(a, b):
    return jnp.dot(a, b, preferred_element_type=jnp.float32)


def params(mib):
    return pltpu.CompilerParams(vmem_limit_bytes=mib * 1024 * 1024)


def fold(op, items):
    return functools.reduce(op, items)


def prep_kernel(heads, k_ref, v_ref, *refs):
    smalls = (len(refs) - heads - 1) // 2
    small_in, kv = refs[:smalls], refs[smalls : smalls + heads]
    small_out, sem = refs[smalls + heads : -1], refs[-1]
    copies = []
    for g in range(heads):
        for ref, at in ((k_ref, 0), (v_ref, HD)):
            copies.append((ref.at[:, g * HD : (g + 1) * HD], kv[g].at[:, at : at + HD]))
    copies += list(zip(small_in, small_out))
    started = [pltpu.make_async_copy(a, b, sem.at[i]) for i, (a, b) in enumerate(copies)]
    for copy in started:
        copy.start()
    for copy in started:
        copy.wait()


def prep(key, value, smalls):
    rows, heads = key.shape[0], key.shape[1] // HD
    outs = pl.pallas_call(
        functools.partial(prep_kernel, heads),
        out_shape=[jax.ShapeDtypeStruct((rows, 2 * HD), key.dtype)] * heads
        + [jax.ShapeDtypeStruct(s.shape, s.dtype) for s in smalls],
        in_specs=[HBM] * (2 + len(smalls)),
        out_specs=[VMEM] * (heads + len(smalls)),
        scratch_shapes=[pltpu.SemaphoreType.DMA((2 * heads + len(smalls),))],
        compiler_params=params(16),
        name="prep",
    )(key, value, *smalls)
    return outs[:heads], outs[heads:]


def pipelined(tasks, scores, finish):
    ahead = scores(tasks[0])
    for i, task in enumerate(tasks):
        now = ahead
        if i + 1 < len(tasks):
            ahead = scores(tasks[i + 1])
        finish(task, now)


def local_kernel(q_ref, kv_ref, o_ref, l_ref, ve):
    step = pl.program_id(0)
    rows = q_ref.shape[0]

    @pl.when(step == 0)
    def _():
        ve[:, :HD] = kv_ref[:, HD:]
        ve[:, HD:] = jnp.ones((rows, HD), jnp.bfloat16)
        l_ref[...] = jnp.zeros(l_ref.shape, jnp.float32)

    lane = lax.broadcasted_iota(jnp.int32, (TILE, HD), 1)
    seen = lax.broadcasted_iota(jnp.int32, (TILE, TILE), 0) >= lax.broadcasted_iota(jnp.int32, (TILE, TILE), 1)

    def scores(task):
        j, at = task
        q = q_ref[at : at + TILE, j * HD : (j + 1) * HD]
        parts = [nt(q, kv_ref[:at, :HD])] if at else []
        parts.append(jnp.where(seen, nt(q, kv_ref[at : at + TILE, :HD]), NEG))
        return parts

    def finish(task, parts):
        j, at = task
        top = fold(jnp.maximum, [jnp.max(s, axis=1, keepdims=True) for s in parts])
        total = None
        for s, start in zip(parts, [0, at] if at else [at]):
            p = jnp.exp2((s - top) * C2).astype(jnp.bfloat16)
            part = nn(p, ve[start : start + s.shape[1], :])
            total = part if total is None else total + part
        z = total[:, HD:]
        o_ref[at : at + TILE, j * HD : (j + 1) * HD] = total[:, :HD] / z
        log = top * C2 + jnp.log2(z)
        l_ref[at : at + TILE, :] = jnp.where(lane == step * PAIR + j, log, l_ref[at : at + TILE, :])

    pipelined([(j, at) for j in range(PAIR) for at in range(0, rows, TILE)], scores, finish)


def local_attention(query, kv, g):
    rows = query.shape[0]
    steps = GROUP // PAIR
    whole = pl.BlockSpec((rows, 2 * HD), lambda h: (0, 0))
    return pl.pallas_call(
        local_kernel,
        grid=(steps,),
        out_shape=[
            jax.ShapeDtypeStruct((rows, GROUP * HD), jnp.float32),
            jax.ShapeDtypeStruct((rows, HD), jnp.float32),
        ],
        in_specs=[pl.BlockSpec((rows, PAIR * HD), lambda h: (0, g * steps + h)), whole],
        out_specs=[
            pl.BlockSpec((rows, PAIR * HD), lambda h: (0, h)),
            pl.BlockSpec((rows, HD), lambda h: (0, 0)),
        ],
        scratch_shapes=[pltpu.VMEM((rows, 2 * HD), jnp.bfloat16)],
        compiler_params=params(24),
        cost_estimate=pl.CostEstimate(
            flops=8 * GROUP * rows * rows * HD, bytes_accessed=6 * GROUP * rows * HD, transcendentals=GROUP * rows * rows
        ),
        name="local_attention",
    )(query, kv)


def anchor_kernel(count, blk_ref, q_ref, o_in, l_ref, *refs):
    cand, (o_ref, ka, vae) = refs[:count], refs[-3:]
    step = pl.program_id(0)
    rows = q_ref.shape[0]
    blk = blk_ref[0]

    @pl.when(step == 0)
    def _():
        vae[:, HD:] = jnp.ones((rows, HD), jnp.bfloat16)

        def take(ref):
            ka[...] = ref[:, :HD]
            vae[:, :HD] = ref[:, HD:]

        if count == 1:
            take(cand[0])
        else:
            pl.when(blk == 1)(lambda: take(cand[1]))
            pl.when(blk == 2)(lambda: take(cand[0]))
            pl.when(blk == 3)(lambda: take(cand[2]))

    lane = lax.broadcasted_iota(jnp.int32, (TILE, HD), 1)

    def scores(task):
        j, at = task
        return nt(q_ref[at : at + TILE, j * HD : (j + 1) * HD], ka[...])

    def finish(task, s):
        j, at = task
        log = jnp.sum(jnp.where(lane == step * PAIR + j, l_ref[at : at + TILE, :], 0.0), axis=1, keepdims=True)
        top = jnp.maximum(jnp.max(s, axis=1, keepdims=True) * C2, log)
        p = jnp.exp2(s * C2 - top).astype(jnp.bfloat16)
        total = nn(p, vae[...])
        w = jnp.exp2(log - top)
        o = o_in[at : at + TILE, j * HD : (j + 1) * HD]
        out = (total[:, :HD] + w * o) / (total[:, HD:] + w)
        o_ref[at : at + TILE, j * HD : (j + 1) * HD] = out.astype(jnp.bfloat16)

    @pl.when(blk > 0)
    def _():
        pipelined([(j, at) for j in range(PAIR) for at in range(0, rows, TILE)], scores, finish)

    @pl.when(blk == 0)
    def _():
        o_ref[...] = o_in[...].astype(jnp.bfloat16)


def anchor_attention(blk, query, state, cands, g, prior):
    rows = query.shape[0]
    steps = GROUP // PAIR
    block = (rows, PAIR * HD)
    column = pl.BlockSpec(block, lambda h: (0, g * steps + h))
    args = [blk, query, *state, *cands]
    specs = [SMEM, column, pl.BlockSpec(block, lambda h: (0, h)), pl.BlockSpec((rows, HD), lambda h: (0, 0))]
    specs += [pl.BlockSpec((rows, 2 * HD), lambda h: (0, 0))] * len(cands)
    alias = {}
    if prior is not None:
        alias = {len(args): 0}
        args.append(prior)
        specs.append(ANY)
    return pl.pallas_call(
        functools.partial(anchor_kernel, len(cands)),
        grid=(steps,),
        out_shape=jax.ShapeDtypeStruct(query.shape, query.dtype),
        in_specs=specs,
        out_specs=column,
        scratch_shapes=[pltpu.VMEM((rows, HD), jnp.bfloat16), pltpu.VMEM((rows, 2 * HD), jnp.bfloat16)],
        input_output_aliases=alias,
        compiler_params=params(24),
        cost_estimate=pl.CostEstimate(
            flops=8 * GROUP * rows * rows * HD, bytes_accessed=8 * GROUP * rows * HD, transcendentals=GROUP * rows * rows
        ),
        name="anchor_attention",
    )(*args)


def fold_order(n):
    bits = n.bit_length() - 1
    return sorted(range(n), key=lambda x: int(format(x, "0%db" % bits)[::-1], 2))


def option_kernel(masks, heads, blk_ref, owner_ref, slot_ref, length_ref, *refs):
    n = len(masks)
    kv_heads = heads // GROUP
    kv, queries = refs[:kv_heads], refs[kv_heads : kv_heads + n]
    keep, send, q_all, part = refs[kv_heads + n :]
    blk = blk_ref[0]
    rows = kv[0].shape[0]
    each = queries[0].shape[0]
    options = n * each
    for mask, query in zip(masks, queries):
        at = jnp.bitwise_xor(blk, mask) * each
        q_all[pl.ds(pl.multiple_of(at, each), each), :] = query[...]
    eye = lax.broadcasted_iota(jnp.int32, (options, options), 0) == lax.broadcasted_iota(jnp.int32, (options, options), 1)
    length = jnp.sum(jnp.where(eye, length_ref[...].astype(jnp.float32), 0.0), axis=1, keepdims=True)
    seen = length - (blk * rows).astype(jnp.float32)
    lane = lax.broadcasted_iota(jnp.int32, (options, HD), 1)
    logs = jnp.zeros((options, HD), jnp.float32)
    stack = max(1, min(GROUP, 512 // options))
    spots = lax.broadcasted_iota(jnp.int32, (options * stack, rows), 1).astype(jnp.float32)
    seen_all = jnp.concatenate([seen] * stack, axis=0)
    for first in range(0, heads, stack):
        g = first // GROUP
        q = jnp.concatenate([q_all[:, h * HD : (h + 1) * HD] for h in range(first, first + stack)], axis=0)
        s = nt(q, kv[g][:, :HD])
        s = jnp.where(spots < seen_all, s, NEG)
        top = jnp.max(s, axis=1, keepdims=True)
        e = jnp.exp2((s - top) * C2)
        z = jnp.sum(e, axis=1, keepdims=True)
        o = nn(e.astype(jnp.bfloat16), kv[g][:, HD:]) / z
        live = seen_all > 0
        o = jnp.where(live, o, 0.0).astype(jnp.bfloat16)
        log = jnp.where(live, top * SCALE + jnp.log(z), NEG)
        for j in range(stack):
            h = first + j
            part[:, h * HD : (h + 1) * HD] = o[j * options : (j + 1) * options]
            logs = jnp.where(lax.rem(lane, heads) == h, log[j * options : (j + 1) * options], logs)
    part[:, heads * HD :] = summands(logs, heads)
    slot = lax.broadcasted_iota(jnp.int32, (CAP, options), 0)
    order = fold_order(n)
    for half, out in ((order[: n // 2], keep), (order[n // 2 :], send)):
        for i, mask in enumerate(half):
            pick = (owner_ref[...] == jnp.bitwise_xor(blk, mask)) & (slot_ref[...] == slot)
            pick = jnp.where(pick, 1.0, 0.0).astype(jnp.bfloat16)
            out[i * CAP : (i + 1) * CAP, :] = nn(pick, part[...]).astype(jnp.bfloat16)


def summands(logs, heads):
    lane = lax.broadcasted_iota(jnp.int32, logs.shape, 1)
    high = logs.astype(jnp.bfloat16).astype(jnp.float32)
    rest = logs - high
    mid = rest.astype(jnp.bfloat16).astype(jnp.float32)
    low = rest - mid
    low = jnp.where(lane < 3 * heads, low, 0.0)
    return jnp.where(lane < heads, high, jnp.where(lane < 2 * heads, mid, low)).astype(jnp.bfloat16)


def option_partials(blk, owner, slot, length, kvs, masks, queries):
    n, heads = len(queries), queries[0].shape[1] // HD
    options = n * queries[0].shape[0]
    width = (heads + 1) * HD
    rows = kvs[0].shape[0]
    return pl.pallas_call(
        functools.partial(option_kernel, masks, heads),
        out_shape=[jax.ShapeDtypeStruct((n // 2 * CAP, width), jnp.bfloat16)] * 2,
        in_specs=[SMEM] + [VMEM] * (3 + len(kvs) + n),
        out_specs=[VMEM] * 2,
        scratch_shapes=[
            pltpu.VMEM((options, heads * HD), jnp.bfloat16),
            pltpu.VMEM((options, width), jnp.bfloat16),
        ],
        compiler_params=params(32),
        cost_estimate=pl.CostEstimate(
            flops=4 * options * heads * rows * HD, bytes_accessed=1 << 20, transcendentals=options * heads * rows
        ),
        name="option_partials",
    )(blk, owner, slot, length, *kvs, *queries)


def merge_kernel(heads, a, b, *outs):
    width = heads * HD
    lane = lax.broadcasted_iota(jnp.int32, (HD, width), 0)
    head = lax.broadcasted_iota(jnp.int32, (HD, width), 1) // HD
    pick = jnp.where((lax.rem(lane, heads) == head) & (lane < 3 * heads), 1.0, 0.0).astype(jnp.bfloat16)
    logs = [nn(x[:, width:], pick) for x in (a, b)]
    top = jnp.maximum(*logs)
    weights = [jnp.exp(log - top) for log in logs]
    total = weights[0] + weights[1]
    merged = (weights[0] * a[:, :width].astype(jnp.float32) + weights[1] * b[:, :width].astype(jnp.float32)) / total
    merged = merged.astype(jnp.bfloat16)
    if len(outs) == 1:
        outs[0][...] = merged
        return
    log = top + jnp.log(total)
    lane = lax.broadcasted_iota(jnp.int32, (a.shape[0], HD), 1)
    packed = jnp.zeros((a.shape[0], HD), jnp.float32)
    for h in range(heads):
        packed = jnp.where(lax.rem(lane, heads) == h, log[:, h * HD : (h + 1) * HD], packed)
    packed = summands(packed, heads)
    half = a.shape[0] // 2
    for i, out in enumerate(outs):
        out[:, :width] = merged[i * half : (i + 1) * half]
        out[:, width:] = packed[i * half : (i + 1) * half]


def merge(a, b, last):
    rows, width = a.shape
    heads = width // HD - 1
    if last:
        shapes = [jax.ShapeDtypeStruct((rows, heads * HD), jnp.bfloat16)]
    else:
        shapes = [jax.ShapeDtypeStruct((rows // 2, width), jnp.bfloat16)] * 2
    return pl.pallas_call(
        functools.partial(merge_kernel, heads),
        out_shape=shapes,
        in_specs=[VMEM] * 2,
        out_specs=[VMEM] * len(shapes),
        compiler_params=params(32),
        name="merge",
    )(a, b)


def swap(x, n, mask):
    return lax.ppermute(x, "blk", [(i, i ^ mask) for i in range(n)])


def from_root(x, blk):
    return lax.psum(jnp.where(blk == 0, x, jnp.zeros_like(x)), "blk")


def body(ctx_query, ctx_key, ctx_value, opt_query, opt_owner, opt_slot, opt_length):
    n = lax.axis_size("blk")
    blk = lax.axis_index("blk")
    blk_arr = blk.astype(jnp.int32).reshape(1)
    options = opt_owner.shape[0]
    rounds = n.bit_length() - 1

    masks, queries = [0], [opt_query]
    for bit in reversed(range(rounds)):
        queries = queries + [swap(q, n, 1 << bit) for q in queries]
        masks = masks + [m | (1 << bit) for m in masks]
    row = lambda x: x.reshape(1, options)
    kvs, smalls = prep(ctx_key, ctx_value, [row(opt_owner), row(opt_slot), row(opt_length), opt_query])
    queries[0] = smalls[3]

    if n == 4:
        first = [lax.ppermute(kv, "blk", [(0, 2)]) for kv in kvs]
        anchors = [(x, lax.ppermute(x, "blk", [(2, 1)]), lax.ppermute(x, "blk", [(2, 3)])) for x in first]
    else:
        anchors = [(from_root(kv, blk),) for kv in kvs]

    states = [local_attention(ctx_query, kv, g) for g, kv in enumerate(kvs)]
    keep, send = option_partials(blk_arr, *smalls[:3], kvs, masks, queries)
    for bit in range(rounds):
        got = swap(send, n, 1 << bit)
        last = bit == rounds - 1
        outs = merge(keep, got, last)
        if last:
            opt_out = outs[0]
        else:
            keep, send = outs
    ctx_out = None
    for g, state in enumerate(states):
        ctx_out = anchor_attention(blk_arr, ctx_query, state, anchors[g], g, ctx_out)
    return (ctx_out, opt_out)


def solution(mesh):
    spread = P(("groups", "blk"), "head")
    return jax.shard_map(
        body,
        mesh=mesh,
        in_specs=(spread, spread, spread, spread, P("groups"), P("groups"), P("groups")),
        out_specs=(spread, spread),
        check_vma=False,
    )
```

time: 75.9 us -> 53.5 us (0.70)
  waiting for transfers between devices: 22.3 us -> 8.81 us
  starting transfers between devices: 20.9 us -> 16.6 us
  Pallas kernels: 24.7 us -> 21.4 us
  local copies, waits for them, and re-layouts: 6.6 us -> 5.45 us
    ppermute x14 -> x11, waiting for transfers between devices: 22.3 us -> 8.81 us  [the longest x5 8.3 us: swap(): return lax.ppermute(x, 'blk', [(i, i ^ mask) for i in range(n)])]
    ppermute x14 -> x11, starting transfers between devices: 20.9 us -> 16.6 us  [the longest x5 11.2 us: swap(): return lax.ppermute(x, 'blk', [(i, i ^ mask) for i in range(n)])]
    pallas_call x5 -> x8, Pallas kernels: 24.7 us -> 21.4 us  [the longest x2 9.94 us: anchor_attention(): pl.pallas_call(functools.partial(anchor_kernel, len(cands)), grid=(steps,...]
    unnamed x18 -> x14, local copies, waits for them, and re-layouts: 6.6 us -> 5.45 us
  transfers between devices with their start and end apart: 14 -> 11, of which waited for: 5 -> 4; matrix products, arithmetic and copies ran while one was open for 0% -> 0% of each run, Pallas kernels for 18% -> 37%
where the time goes in v2:
time: 53.5 us; the launch traced here: 53 us
  Pallas kernels  21.4 us (40%)
  starting transfers between devices  16.6 us (31%)
  waiting for transfers between devices  8.81 us (16%)
  local copies, waits for them, and re-layouts  5.45 us (10%)
  between operations  0.78 us (1%)
    ppermute x5, starting transfers between devices, swap(): return lax.ppermute(x, 'blk', [(i, i ^ mask) for i in range(n)])  11.2 us
    pallas_call x2, Pallas kernels, anchor_attention(): pl.pallas_call(functools.partial(anchor_kernel, len(cands)), grid=(steps,...  9.94 us
    ppermute x5, waiting for transfers between devices, swap(): return lax.ppermute(x, 'blk', [(i, i ^ mask) for i in range(n)])  8.3 us
    pallas_call x2, Pallas kernels, local_attention(): pl.pallas_call(local_kernel, grid=(steps,), out_shape=[jax.ShapeDtypeStru...  6.87 us
    unnamed x14, local copies, waits for them, and re-layouts  5.45 us
    ppermute x2, starting transfers between devices, body(): lax.ppermute(x, 'blk', [(2, 1)])  2.7 us
    pallas_call x1, Pallas kernels, option_partials(): pl.pallas_call(functools.partial(option_kernel, masks, heads), out_shape=...  2.02 us
    pallas_call x2, Pallas kernels, merge(): pl.pallas_call(functools.partial(merge_kernel, heads), out_shape=shapes,...  1.55 us
  transfers between devices with their start and end apart: 11, of which 4 were waited for; matrix products, arithmetic and copies ran while one was open for 0% of the time, Pallas kernels for 37%

profile of v2, /device:TPU:12, one launch (start us, length us, event | category | flops | bytes accessed | tf_op | source)
XLA Modules:
  0.0 53.0 jit_solution(14575370367077853644)
XLA Ops:
  0.6 0.9 %copy-done.2 = bf16[512,256]{1,0:T(8,128)(2,1)S(1)} copy-done((bf16[512,256]{1,0:T(8,128)(2,1)S(1)}, bf16[512,256]{1,0:T(8,128)(2,1)}, u32[]{:S(2)}) %copy-start.2) | copy-done | bytes 262168
  1.6 0.9 %copy-done.3 = bf16[512,256]{1,0:T(8,128)(2,1)S(1)} copy-done((bf16[512,256]{1,0:T(8,128)(2,1)S(1)}, bf16[512,256]{1,0:T(8,128)(2,1)}, u32[]{:S(2)}) %copy-start.3) | copy-done | bytes 262168
  2.5 0.7 %copy-done.4 = s32[64]{0:T(128)S(1)} copy-done((s32[64]{0:T(128)S(1)}, s32[64]{0:T(128)}, u32[]{:S(2)}) %copy-start.4) | copy-done | bytes 280
  4.5 1.0 %prep.1 = (bf16[512,256]{1,0:T(8,128)(2,1)S(1)}, bf16[512,256]{1,0:T(8,128)(2,1)S(1)}, s32[1,64]{1,0:T(1,128)S(1)}, s32[1,64]{1,0:T(1,128)S(1)}, s32[1,64]{1,0:T(1,128)S(1)}, /*index=5*/bf16[16,2048]{1,0:T(8,128)(2,1)S(1)}) custom-call(bf16[512,256]{1,0:T(8,128)(2,1)S(1)} %copy-done.2, bf16[512,256]{1,0:T(8,128)(2,1)S(1)} %copy-done.3, s32[1,64]{1,0:T(1,128)S(1)} %bitcast.4, ...), custom_call_target="tpu_custom_call" | custom-call | tf_op jit(solution)/shard_map/prep/pallas_call | solution.py:61
  5.5 0.7 %collective-permute-start.3 = (bf16[512,256]{1,0:T(8,128)(2,1)S(1)}, bf16[512,256]{1,0:T(8,128)(2,1)S(1)}, u32[]{:S(2)}, u32[]{:S(2)}) collective-permute-start(bf16[512,256]{1,0:T(8,128)(2,1)S(1)} %get-tuple-element.19.kv_ref.refs_0_), channel_id=1, source_target_pairs={{0,8},{1,9},{2,10},{3,11},{16,24},{17,25},{18,26},{19,27}} | collective-permute-start | bytes 786440 | tf_op jit(solution)/shard_map/ppermute | solution.py:370
  6.2 2.7 %collective-permute-start.6 = (bf16[16,2048]{1,0:T(8,128)(2,1)}, bf16[16,2048]{1,0:T(8,128)(2,1)S(1)}, u32[]{:S(2)}, u32[]{:S(2)}) collective-permute-start(bf16[16,2048]{1,0:T(8,128)(2,1)} %refs_3_.1), channel_id=1, source_target_pairs={{0,8},{4,12},{8,0},{12,4},{1,9},{5,13},{9,1},{13,5},{2,10},{6,14},... | collective-permute-start | bytes 196616 | tf_op jit(solution)/shard_map/ppermute | solution.py:347
  8.9 1.8 %collective-permute-start.7 = (bf16[16,2048]{1,0:T(8,128)(2,1)}, bf16[16,2048]{1,0:T(8,128)(2,1)S(1)}, u32[]{:S(2)}, u32[]{:S(2)}) collective-permute-start(bf16[16,2048]{1,0:T(8,128)(2,1)} %refs_3_.1), channel_id=1, source_target_pairs={{0,4},{4,0},{8,12},{12,8},{1,5},{5,1},{9,13},{13,9},{2,6},{6,2},{1... | collective-permute-start | bytes 196616 | tf_op jit(solution)/shard_map/ppermute | solution.py:347
  10.6 6.4 %collective-permute-done.6.refs_3_ = bf16[16,2048]{1,0:T(8,128)(2,1)S(1)} collective-permute-done((bf16[16,2048]{1,0:T(8,128)(2,1)}, bf16[16,2048]{1,0:T(8,128)(2,1)S(1)}, u32[]{:S(2)}, u32[]{:S(2)}) %collective-permute-start.6) | collective-permute-done | bytes 65568 | tf_op jit(solution)/shard_map/ppermute | solution.py:347
  17.0 1.7 %collective-permute-start.8 = (bf16[16,2048]{1,0:T(8,128)(2,1)S(1)}, bf16[16,2048]{1,0:T(8,128)(2,1)S(1)}, u32[]{:S(2)}, u32[]{:S(2)}) collective-permute-start(bf16[16,2048]{1,0:T(8,128)(2,1)S(1)} %collective-permute-done.6.refs_3_), channel_id=1, source_target_pairs={{0,4},{4,0},{8,12},{12,8},{1,5},{5,1},{9,13},{13,9},{2,6},{6,2},{1... | collective-permute-start | bytes 196616 | tf_op jit(solution)/shard_map/ppermute | solution.py:347
  18.7 0.7 %collective-permute-start = (bf16[512,256]{1,0:T(8,128)(2,1)S(1)}, bf16[512,256]{1,0:T(8,128)(2,1)S(1)}, u32[]{:S(2)}, u32[]{:S(2)}) collective-permute-start(bf16[512,256]{1,0:T(8,128)(2,1)S(1)} %get-tuple-element.16.kv_ref.refs_1_), channel_id=1, source_target_pairs={{0,8},{1,9},{2,10},{3,11},{16,24},{17,25},{18,26},{19,27}} | collective-permute-start | bytes 786440 | tf_op jit(solution)/shard_map/ppermute | solution.py:370
  20.0 1.3 %collective-permute-done.8.refs_5_ = bf16[16,2048]{1,0:T(8,128)(2,1)S(1)} collective-permute-done((bf16[16,2048]{1,0:T(8,128)(2,1)S(1)}, bf16[16,2048]{1,0:T(8,128)(2,1)S(1)}, u32[]{:S(2)}, u32[]{:S(2)}) %collective-permute-start.8) | collective-permute-done | bytes 65568 | tf_op jit(solution)/shard_map/ppermute | solution.py:347
  21.3 2.0 %option_partials.1 = (bf16[64,2176]{1,0:T(8,128)(2,1)S(1)}, bf16[64,2176]{1,0:T(8,128)(2,1)S(1)}) custom-call(s32[1]{0:T(128)} %bitcast.blk_ref, s32[1,64]{1,0:T(1,128)S(1)} %get-tuple-element.22.owner_ref, s32[1,64]{1,0:T(1,128)S(1)} %get-tuple-element.23.slot_ref, s32[1,64]{1,0:T(1,128)S(1)} %get-tuple-element.24.length_ref, ...), custom_call_target="tpu_custom_call" | custom-call | flops 268435456 | bytes 1048576 | tf_op jit(solution)/shard_map/option_partials/pallas_call | solution.py:286
  23.3 3.2 %collective-permute-start.9 = (bf16[64,2176]{1,0:T(8,128)(2,1)S(1)}, bf16[64,2176]{1,0:T(8,128)(2,1)S(1)}, u32[]{:S(2)}, u32[]{:S(2)}) collective-permute-start(bf16[64,2176]{1,0:T(8,128)(2,1)S(1)} %get-tuple-element.27), channel_id=1, source_target_pairs={{0,4},{4,0},{8,12},{12,8},{1,5},{5,1},{9,13},{13,9},{2,6},{6,2},{1... | collective-permute-start | bytes 835592 | tf_op jit(solution)/shard_map/ppermute | solution.py:347
  26.5 1.3 %collective-permute-start.4 = (bf16[512,256]{1,0:T(8,128)(2,1)S(1)}, bf16[512,256]{1,0:T(8,128)(2,1)S(1)}, u32[]{:S(2)}, u32[]{:S(2)}) collective-permute-start(bf16[512,256]{1,0:T(8,128)(2,1)S(1)} %collective-permute-done.3.refs_0_), channel_id=1, source_target_pairs={{8,4},{9,5},{10,6},{11,7},{24,20},{25,21},{26,22},{27,23}} | collective-permute-start | bytes 786440 | tf_op jit(solution)/shard_map/ppermute | solution.py:371
  27.8 0.7 %collective-permute-start.5 = (bf16[512,256]{1,0:T(8,128)(2,1)S(1)}, bf16[512,256]{1,0:T(8,128)(2,1)S(1)}, u32[]{:S(2)}, u32[]{:S(2)}) collective-permute-start(bf16[512,256]{1,0:T(8,128)(2,1)S(1)} %collective-permute-done.3.refs_0_), channel_id=1, source_target_pairs={{8,12},{9,13},{10,14},{11,15},{24,28},{25,29},{26,30},{27,31}} | collective-permute-start | bytes 786440 | tf_op jit(solution)/shard_map/ppermute | solution.py:371
  28.5 1.6 %copy-done = bf16[512,2048]{1,0:T(8,128)(2,1)S(1)} copy-done((bf16[512,2048]{1,0:T(8,128)(2,1)S(1)}, bf16[512,2048]{1,0:T(8,128)(2,1)}, u32[]{:S(2)}) %copy-start) | copy-done | bytes 2097176
  30.1 3.4 %local_attention.3 = (f32[512,1024]{1,0:T(8,128)S(1)}, f32[512,128]{1,0:T(8,128)S(1)}) custom-call(bf16[512,2048]{1,0:T(8,128)(2,1)S(1)} %copy-done, bf16[512,256]{1,0:T(8,128)(2,1)S(1)} %get-tuple-element.19.kv_ref.refs_0_), custom_call_target="tpu_custom_call" | custom-call | flops 2147483648 | bytes 3145728 | tf_op jit(solution)/shard_map/local_attention/pallas_call | solution.py:123
  33.5 1.4 %collective-permute-start.1 = (bf16[512,256]{1,0:T(8,128)(2,1)S(1)}, bf16[512,256]{1,0:T(8,128)(2,1)S(1)}, u32[]{:S(2)}, u32[]{:S(2)}) collective-permute-start(bf16[512,256]{1,0:T(8,128)(2,1)S(1)} %collective-permute-done.refs_0_), channel_id=1, source_target_pairs={{8,4},{9,5},{10,6},{11,7},{24,20},{25,21},{26,22},{27,23}} | collective-permute-start | bytes 786440 | tf_op jit(solution)/shard_map/ppermute | solution.py:371
  35.0 0.7 %collective-permute-start.2 = (bf16[512,256]{1,0:T(8,128)(2,1)S(1)}, bf16[512,256]{1,0:T(8,128)(2,1)S(1)}, u32[]{:S(2)}, u32[]{:S(2)}) collective-permute-start(bf16[512,256]{1,0:T(8,128)(2,1)S(1)} %collective-permute-done.refs_0_), channel_id=1, source_target_pairs={{8,12},{9,13},{10,14},{11,15},{24,28},{25,29},{26,30},{27,31}} | collective-permute-start | bytes 786440 | tf_op jit(solution)/shard_map/ppermute | solution.py:371
  35.6 3.5 %local_attention.2 = (f32[512,1024]{1,0:T(8,128)S(1)}, f32[512,128]{1,0:T(8,128)S(1)}) custom-call(bf16[512,2048]{1,0:T(8,128)(2,1)S(1)} %copy-done, bf16[512,256]{1,0:T(8,128)(2,1)S(1)} %get-tuple-element.16.kv_ref.refs_1_), custom_call_target="tpu_custom_call" | custom-call | flops 2147483648 | bytes 3145728 | tf_op jit(solution)/shard_map/local_attention/pallas_call | solution.py:123
  39.7 1.9 %collective-permute-start.10 = (bf16[32,2176]{1,0:T(8,128)(2,1)S(1)}, bf16[32,2176]{1,0:T(8,128)(2,1)S(1)}, u32[]{:S(2)}, u32[]{:S(2)}) collective-permute-start(bf16[32,2176]{1,0:T(8,128)(2,1)S(1)} %get-tuple-element.29), channel_id=1, source_target_pairs={{0,8},{4,12},{8,0},{12,4},{1,9},{5,13},{9,1},{13,5},{2,10},{6,14},... | collective-permute-start | bytes 417800 | tf_op jit(solution)/shard_map/ppermute | solution.py:347
  41.6 5.0 %anchor_attention.2.refs_3_ = bf16[512,2048]{1,0:T(8,128)(2,1)} custom-call(s32[1]{0:T(128)} %bitcast.blk_ref, bf16[512,2048]{1,0:T(8,128)(2,1)S(1)} %copy-done.1, f32[512,1024]{1,0:T(8,128)S(1)} %get-tuple-element.20.o_in, f32[512,128]{1,0:T(8,128)S(1)} %get-tuple-element.21.l_ref, bf16[512,256]{1,0:T(8,128)(2,1)S(1)} %collective-permute-done.3.refs_0_, ...), custom_call_target="tpu_custom_call" | custom-call | flops 2147483648 | bytes 4194304 | tf_op jit(solution)/shard_map/anchor_attention/pallas_call | solution.py:204
  47.0 5.0 %anchor_attention.3 = bf16[512,2048]{1,0:T(8,128)(2,1)} custom-call(s32[1]{0:T(128)} %bitcast.blk_ref, bf16[512,2048]{1,0:T(8,128)(2,1)S(1)} %copy-done.1, f32[512,1024]{1,0:T(8,128)S(1)} %get-tuple-element.17.o_in, f32[512,128]{1,0:T(8,128)S(1)} %get-tuple-element.18.l_ref, ...), custom_call_target="tpu_custom_call", output_to_operand_aliasing={{}: (7, {})} | custom-call | flops 2147483648 | bytes 4194304 | tf_op jit(solution)/shard_map/anchor_attention/pallas_call | solution.py:204
  52.0 1.0 %merge.3 = bf16[32,2048]{1,0:T(8,128)(2,1)} custom-call(bf16[32,2176]{1,0:T(8,128)(2,1)S(1)} %get-tuple-element.28.a, bf16[32,2176]{1,0:T(8,128)(2,1)S(1)} %collective-permute-done.10.b), custom_call_target="tpu_custom_call" | custom-call | tf_op jit(solution)/shard_map/merge/pallas_call | solution.py:336
  (20 shorter events, 3.0 us)
Async XLA Ops:
  0.6 1.0 %copy-start.2 = (bf16[512,256]{1,0:T(8,128)(2,1)S(1)}, bf16[512,256]{1,0:T(8,128)(2,1)}, u32[]{:S(2)}) copy-start(bf16[512,256]{1,0:T(8,128)(2,1)} %k_ref.1) | copy-start | bytes 786436
  1.6 0.9 %copy-start.3 = (bf16[512,256]{1,0:T(8,128)(2,1)S(1)}, bf16[512,256]{1,0:T(8,128)(2,1)}, u32[]{:S(2)}) copy-start(bf16[512,256]{1,0:T(8,128)(2,1)} %v_ref.1) | copy-start | bytes 786436
  2.5 0.7 %copy-start.4 = (s32[64]{0:T(128)S(1)}, s32[64]{0:T(128)}, u32[]{:S(2)}) copy-start(s32[64]{0:T(128)} %param.11) | copy-start | bytes 772
  3.2 0.7 %copy-start.5 = (s32[64]{0:T(128)S(1)}, s32[64]{0:T(128)}, u32[]{:S(2)}) copy-start(s32[64]{0:T(128)} %param.12) | copy-start | bytes 772
  3.8 0.7 %copy-start.6 = (s32[64]{0:T(128)S(1)}, s32[64]{0:T(128)}, u32[]{:S(2)}) copy-start(s32[64]{0:T(128)} %param.13) | copy-start | bytes 772
  5.5 21.0 %collective-permute-start.3 = (bf16[512,256]{1,0:T(8,128)(2,1)S(1)}, bf16[512,256]{1,0:T(8,128)(2,1)S(1)}, u32[]{:S(2)}, u32[]{:S(2)}) collective-permute-start(bf16[512,256]{1,0:T(8,128)(2,1)S(1)} %get-tuple-element.19.kv_ref.refs_0_), channel_id=1, source_target_pairs={{0,8},{1,9},{2,10},{3,11},{16,24},{17,25},{18,26},{19,27}} | collective-permute-start | bytes 786440 | tf_op jit(solution)/shard_map/ppermute | solution.py:370
  6.2 10.8 %collective-permute-start.6 = (bf16[16,2048]{1,0:T(8,128)(2,1)}, bf16[16,2048]{1,0:T(8,128)(2,1)S(1)}, u32[]{:S(2)}, u32[]{:S(2)}) collective-permute-start(bf16[16,2048]{1,0:T(8,128)(2,1)} %refs_3_.1), channel_id=1, source_target_pairs={{0,8},{4,12},{8,0},{12,4},{1,9},{5,13},{9,1},{13,5},{2,10},{6,14},... | collective-permute-start | bytes 196616 | tf_op jit(solution)/shard_map/ppermute | solution.py:347
  8.9 11.2 %collective-permute-start.7 = (bf16[16,2048]{1,0:T(8,128)(2,1)}, bf16[16,2048]{1,0:T(8,128)(2,1)S(1)}, u32[]{:S(2)}, u32[]{:S(2)}) collective-permute-start(bf16[16,2048]{1,0:T(8,128)(2,1)} %refs_3_.1), channel_id=1, source_target_pairs={{0,4},{4,0},{8,12},{12,8},{1,5},{5,1},{9,13},{13,9},{2,6},{6,2},{1... | collective-permute-start | bytes 196616 | tf_op jit(solution)/shard_map/ppermute | solution.py:347
  17.0 4.3 %collective-permute-start.8 = (bf16[16,2048]{1,0:T(8,128)(2,1)S(1)}, bf16[16,2048]{1,0:T(8,128)(2,1)S(1)}, u32[]{:S(2)}, u32[]{:S(2)}) collective-permute-start(bf16[16,2048]{1,0:T(8,128)(2,1)S(1)} %collective-permute-done.6.refs_3_), channel_id=1, source_target_pairs={{0,4},{4,0},{8,12},{12,8},{1,5},{5,1},{9,13},{13,9},{2,6},{6,2},{1... | collective-permute-start | bytes 196616 | tf_op jit(solution)/shard_map/ppermute | solution.py:347
  18.7 14.8 %collective-permute-start = (bf16[512,256]{1,0:T(8,128)(2,1)S(1)}, bf16[512,256]{1,0:T(8,128)(2,1)S(1)}, u32[]{:S(2)}, u32[]{:S(2)}) collective-permute-start(bf16[512,256]{1,0:T(8,128)(2,1)S(1)} %get-tuple-element.16.kv_ref.refs_1_), channel_id=1, source_target_pairs={{0,8},{1,9},{2,10},{3,11},{16,24},{17,25},{18,26},{19,27}} | collective-permute-start | bytes 786440 | tf_op jit(solution)/shard_map/ppermute | solution.py:370
  23.3 15.8 %collective-permute-start.9 = (bf16[64,2176]{1,0:T(8,128)(2,1)S(1)}, bf16[64,2176]{1,0:T(8,128)(2,1)S(1)}, u32[]{:S(2)}, u32[]{:S(2)}) collective-permute-start(bf16[64,2176]{1,0:T(8,128)(2,1)S(1)} %get-tuple-element.27), channel_id=1, source_target_pairs={{0,4},{4,0},{8,12},{12,8},{1,5},{5,1},{9,13},{13,9},{2,6},{6,2},{1... | collective-permute-start | bytes 835592 | tf_op jit(solution)/shard_map/ppermute | solution.py:347
  26.5 15.1 %collective-permute-start.4 = (bf16[512,256]{1,0:T(8,128)(2,1)S(1)}, bf16[512,256]{1,0:T(8,128)(2,1)S(1)}, u32[]{:S(2)}, u32[]{:S(2)}) collective-permute-start(bf16[512,256]{1,0:T(8,128)(2,1)S(1)} %collective-permute-done.3.refs_0_), channel_id=1, source_target_pairs={{8,4},{9,5},{10,6},{11,7},{24,20},{25,21},{26,22},{27,23}} | collective-permute-start | bytes 786440 | tf_op jit(solution)/shard_map/ppermute | solution.py:371
  27.8 13.8 %collective-permute-start.5 = (bf16[512,256]{1,0:T(8,128)(2,1)S(1)}, bf16[512,256]{1,0:T(8,128)(2,1)S(1)}, u32[]{:S(2)}, u32[]{:S(2)}) collective-permute-start(bf16[512,256]{1,0:T(8,128)(2,1)S(1)} %collective-permute-done.3.refs_0_), channel_id=1, source_target_pairs={{8,12},{9,13},{10,14},{11,15},{24,28},{25,29},{26,30},{27,31}} | collective-permute-start | bytes 786440 | tf_op jit(solution)/shard_map/ppermute | solution.py:371
  28.5 1.6 %copy-start = (bf16[512,2048]{1,0:T(8,128)(2,1)S(1)}, bf16[512,2048]{1,0:T(8,128)(2,1)}, u32[]{:S(2)}) copy-start(bf16[512,2048]{1,0:T(8,128)(2,1)} %q_ref.7) | copy-start | bytes 6291460
  33.5 8.1 %copy-start.1 = (bf16[512,2048]{1,0:T(8,128)(2,1)S(1)}, bf16[512,2048]{1,0:T(8,128)(2,1)}, u32[]{:S(2)}) copy-start(bf16[512,2048]{1,0:T(8,128)(2,1)} %q_ref.7) | copy-start | bytes 6291460
  33.5 13.5 %collective-permute-start.1 = (bf16[512,256]{1,0:T(8,128)(2,1)S(1)}, bf16[512,256]{1,0:T(8,128)(2,1)S(1)}, u32[]{:S(2)}, u32[]{:S(2)}) collective-permute-start(bf16[512,256]{1,0:T(8,128)(2,1)S(1)} %collective-permute-done.refs_0_), channel_id=1, source_target_pairs={{8,4},{9,5},{10,6},{11,7},{24,20},{25,21},{26,22},{27,23}} | collective-permute-start | bytes 786440 | tf_op jit(solution)/shard_map/ppermute | solution.py:371
  35.0 12.1 %collective-permute-start.2 = (bf16[512,256]{1,0:T(8,128)(2,1)S(1)}, bf16[512,256]{1,0:T(8,128)(2,1)S(1)}, u32[]{:S(2)}, u32[]{:S(2)}) collective-permute-start(bf16[512,256]{1,0:T(8,128)(2,1)S(1)} %collective-permute-done.refs_0_), channel_id=1, source_target_pairs={{8,12},{9,13},{10,14},{11,15},{24,28},{25,29},{26,30},{27,31}} | collective-permute-start | bytes 786440 | tf_op jit(solution)/shard_map/ppermute | solution.py:371
  39.7 12.3 %collective-permute-start.10 = (bf16[32,2176]{1,0:T(8,128)(2,1)S(1)}, bf16[32,2176]{1,0:T(8,128)(2,1)S(1)}, u32[]{:S(2)}, u32[]{:S(2)}) collective-permute-start(bf16[32,2176]{1,0:T(8,128)(2,1)S(1)} %get-tuple-element.29), channel_id=1, source_target_pairs={{0,8},{4,12},{8,0},{12,4},{1,9},{5,13},{9,1},{13,5},{2,10},{6,14},... | collective-permute-start | bytes 417800 | tf_op jit(solution)/shard_map/ppermute | solution.py:347

commit v3 on v2

--- a/solution.py
+++ b/solution.py
@@ -22,6 +22,7 @@
 SMEM = pl.BlockSpec(memory_space=pltpu.SMEM)
 HBM = pl.BlockSpec(memory_space=pltpu.HBM)
 ANY = pl.BlockSpec(memory_space=pl.ANY)
+BRIEF = pl.CostEstimate(flops=1, bytes_accessed=1, transcendentals=0)
 
 
 def nt(a, b):
@@ -66,8 +67,9 @@
         out_specs=[VMEM] * (heads + len(smalls)),
         scratch_shapes=[pltpu.SemaphoreType.DMA((2 * heads + len(smalls),))],
         compiler_params=params(16),
+        cost_estimate=BRIEF,
         name="prep",
-    )(key, value, *smalls)
+    )(*[pltpu.with_memory_space_constraint(x, pltpu.HBM) for x in (key, value, *smalls)])
     return outs[:heads], outs[heads:]
 
 
@@ -134,11 +136,9 @@
         ],
         scratch_shapes=[pltpu.VMEM((rows, 2 * HD), jnp.bfloat16)],
         compiler_params=params(24),
-        cost_estimate=pl.CostEstimate(
-            flops=8 * GROUP * rows * rows * HD, bytes_accessed=6 * GROUP * rows * HD, transcendentals=GROUP * rows * rows
-        ),
+        cost_estimate=BRIEF,
         name="local_attention",
-    )(query, kv)
+    )(pltpu.with_memory_space_constraint(query, pltpu.HBM), kv)
 
 
 def anchor_kernel(count, blk_ref, q_ref, o_in, l_ref, *refs):
@@ -210,9 +210,7 @@
         scratch_shapes=[pltpu.VMEM((rows, HD), jnp.bfloat16), pltpu.VMEM((rows, 2 * HD), jnp.bfloat16)],
         input_output_aliases=alias,
         compiler_params=params(24),
-        cost_estimate=pl.CostEstimate(
-            flops=8 * GROUP * rows * rows * HD, bytes_accessed=8 * GROUP * rows * HD, transcendentals=GROUP * rows * rows
-        ),
+        cost_estimate=BRIEF,
         name="anchor_attention",
     )(*args)
 
@@ -222,16 +220,15 @@
     return sorted(range(n), key=lambda x: int(format(x, "0%db" % bits)[::-1], 2))
 
 
-def option_kernel(masks, heads, blk_ref, owner_ref, slot_ref, length_ref, *refs):
-    n = len(masks)
+def option_kernel(n, heads, blk_ref, owner_ref, slot_ref, length_ref, *refs):
     kv_heads = heads // GROUP
     kv, queries = refs[:kv_heads], refs[kv_heads : kv_heads + n]
-    keep, send, q_all, part = refs[kv_heads + n :]
+    keep, send, q_all, part = refs[kv_heads + n + 1 :]
     blk = blk_ref[0]
     rows = kv[0].shape[0]
     each = queries[0].shape[0]
     options = n * each
-    for mask, query in zip(masks, queries):
+    for mask, query in enumerate(queries):
         at = jnp.bitwise_xor(blk, mask) * each
         q_all[pl.ds(pl.multiple_of(at, each), each), :] = query[...]
     eye = lax.broadcasted_iota(jnp.int32, (options, options), 0) == lax.broadcasted_iota(jnp.int32, (options, options), 1)
@@ -278,29 +275,27 @@
     return jnp.where(lane < heads, high, jnp.where(lane < 2 * heads, mid, low)).astype(jnp.bfloat16)
 
 
-def option_partials(blk, owner, slot, length, kvs, masks, queries):
+def option_partials(blk, owner, slot, length, kvs, queries, after):
     n, heads = len(queries), queries[0].shape[1] // HD
     options = n * queries[0].shape[0]
     width = (heads + 1) * HD
     rows = kvs[0].shape[0]
     return pl.pallas_call(
-        functools.partial(option_kernel, masks, heads),
+        functools.partial(option_kernel, n, heads),
         out_shape=[jax.ShapeDtypeStruct((n // 2 * CAP, width), jnp.bfloat16)] * 2,
-        in_specs=[SMEM] + [VMEM] * (3 + len(kvs) + n),
+        in_specs=[SMEM] + [VMEM] * (3 + len(kvs) + n) + [ANY],
         out_specs=[VMEM] * 2,
         scratch_shapes=[
             pltpu.VMEM((options, heads * HD), jnp.bfloat16),
             pltpu.VMEM((options, width), jnp.bfloat16),
         ],
         compiler_params=params(32),
-        cost_estimate=pl.CostEstimate(
-            flops=4 * options * heads * rows * HD, bytes_accessed=1 << 20, transcendentals=options * heads * rows
-        ),
+        cost_estimate=BRIEF,
         name="option_partials",
-    )(blk, owner, slot, length, *kvs, *queries)
-
-
-def merge_kernel(heads, a, b, *outs):
+    )(blk, owner, slot, length, *kvs, *queries, after)
+
+
+def merge_kernel(heads, a, b, after, *outs):
     width = heads * HD
     lane = lax.broadcasted_iota(jnp.int32, (HD, width), 0)
     head = lax.broadcasted_iota(jnp.int32, (HD, width), 1) // HD
@@ -326,7 +321,7 @@
         out[:, width:] = packed[i * half : (i + 1) * half]
 
 
-def merge(a, b, last):
+def merge(a, b, last, after):
     rows, width = a.shape
     heads = width // HD - 1
     if last:
@@ -336,11 +331,12 @@
     return pl.pallas_call(
         functools.partial(merge_kernel, heads),
         out_shape=shapes,
-        in_specs=[VMEM] * 2,
+        in_specs=[VMEM] * 2 + [ANY],
         out_specs=[VMEM] * len(shapes),
         compiler_params=params(32),
+        cost_estimate=BRIEF,
         name="merge",
-    )(a, b)
+    )(a, b, after)
 
 
 def swap(x, n, mask):
@@ -358,26 +354,26 @@
     options = opt_owner.shape[0]
     rounds = n.bit_length() - 1
 
-    masks, queries = [0], [opt_query]
-    for bit in reversed(range(rounds)):
-        queries = queries + [swap(q, n, 1 << bit) for q in queries]
-        masks = masks + [m | (1 << bit) for m in masks]
+    queries = [opt_query] + [swap(opt_query, n, mask) for mask in range(1, n)]
     row = lambda x: x.reshape(1, options)
     kvs, smalls = prep(ctx_key, ctx_value, [row(opt_owner), row(opt_slot), row(opt_length), opt_query])
     queries[0] = smalls[3]
 
+    states = [local_attention(ctx_query, kvs[0], 0)]
+    queries, kvs, states = lax.optimization_barrier((queries, kvs, states))
+    states += [local_attention(ctx_query, kv, g) for g, kv in enumerate(kvs) if g]
     if n == 4:
         first = [lax.ppermute(kv, "blk", [(0, 2)]) for kv in kvs]
+        first[1:], states = lax.optimization_barrier((first[1:], states))
         anchors = [(x, lax.ppermute(x, "blk", [(2, 1)]), lax.ppermute(x, "blk", [(2, 3)])) for x in first]
     else:
         anchors = [(from_root(kv, blk),) for kv in kvs]
 
-    states = [local_attention(ctx_query, kv, g) for g, kv in enumerate(kvs)]
-    keep, send = option_partials(blk_arr, *smalls[:3], kvs, masks, queries)
+    keep, send = option_partials(blk_arr, *smalls[:3], kvs, queries, states[0][1])
     for bit in range(rounds):
         got = swap(send, n, 1 << bit)
         last = bit == rounds - 1
-        outs = merge(keep, got, last)
+        outs = merge(keep, got, last, states[-1][1])
         if last:
             opt_out = outs[0]
         else:

time: 53.5 us -> 52.7 us (0.985)
  local copies, waits for them, and re-layouts: 5.45 us -> 1.27 us
  Pallas kernels: 21.4 us -> 23.6 us
  waiting for transfers between devices: 8.81 us -> 10.4 us
    ppermute x2, waiting for transfers between devices: 0.49 us -> 6.44 us  [body(): lax.ppermute(x, 'blk', [(2, 1)])]
    ppermute x5, waiting for transfers between devices: 8.3 us -> 3.95 us  [swap(): return lax.ppermute(x, 'blk', [(i, i ^ mask) for i in range(n)])]
    unnamed x14 -> x10, local copies, waits for them, and re-layouts: 5.45 us -> 1.27 us
    pallas_call x2, Pallas kernels: 6.87 us -> 8.92 us  [local_attention(): pl.pallas_call(local_kernel, grid=(steps,), out_shape=[jax.ShapeDtypeStru...]
  transfers between devices with their start and end apart: 11 -> 11, of which waited for: 4 -> 2; matrix products, arithmetic and copies ran while one was open for 0% -> 0% of each run, Pallas kernels for 37% -> 43%
where the time goes in v3:
time: 52.7 us; the launch traced here: 52.3 us
  Pallas kernels  23.6 us (45%)
  starting transfers between devices  16.2 us (31%)
  waiting for transfers between devices  10.4 us (20%)
  local copies, waits for them, and re-layouts  1.27 us (2%)
  between operations  0.82 us (2%)
    ppermute x5, starting transfers between devices, swap(): return lax.ppermute(x, 'blk', [(i, i ^ mask) for i in range(n)])  10.9 us
    pallas_call x2, Pallas kernels, anchor_attention(): pl.pallas_call(functools.partial(anchor_kernel, len(cands)), grid=(steps,...  9.93 us
    pallas_call x2, Pallas kernels, local_attention(): pl.pallas_call(local_kernel, grid=(steps,), out_shape=[jax.ShapeDtypeStru...  8.92 us
    ppermute x2, waiting for transfers between devices, body(): lax.ppermute(x, 'blk', [(2, 1)])  6.44 us
    ppermute x5, waiting for transfers between devices, swap(): return lax.ppermute(x, 'blk', [(i, i ^ mask) for i in range(n)])  3.95 us
    ppermute x2, starting transfers between devices, body(): lax.ppermute(x, 'blk', [(2, 1)])  2.57 us
    pallas_call x1, Pallas kernels, option_partials(): pl.pallas_call(functools.partial(option_kernel, n, heads), out_shape=[jax...  2.02 us
    pallas_call x2, Pallas kernels, merge(): pl.pallas_call(functools.partial(merge_kernel, heads), out_shape=shapes,...  1.55 us
  transfers between devices with their start and end apart: 11, of which 2 were waited for; matrix products, arithmetic and copies ran while one was open for 0% of the time, Pallas kernels for 43%

profile of v3, /device:TPU:12, one launch (start us, length us, event | category | flops | bytes accessed | tf_op | source)
XLA Modules:
  0.0 52.3 jit_solution(8055913692078085190)
XLA Ops:
  0.6 0.5 collective-permute-start
  1.1 2.6 %collective-permute-start.1 = (bf16[16,2048]{1,0:T(8,128)(2,1)}, bf16[16,2048]{1,0:T(8,128)(2,1)S(1)}, u32[]{:S(2)}, u32[]{:S(2)}) collective-permute-start(bf16[16,2048]{1,0:T(8,128)(2,1)} %refs_3_.1), channel_id=1, source_target_pairs={{0,8},{4,12},{8,0},{12,4},{1,9},{5,13},{9,1},{13,5},{2,10},{6,14},... | collective-permute-start | bytes 196616 | tf_op jit(solution)/shard_map/ppermute | solution.py:343
  3.7 0.5 collective-permute-start.2
  4.2 1.2 %prep.1 = (bf16[512,256]{1,0:T(8,128)(2,1)S(1)}, bf16[512,256]{1,0:T(8,128)(2,1)S(1)}, s32[1,64]{1,0:T(1,128)S(1)}, s32[1,64]{1,0:T(1,128)S(1)}, s32[1,64]{1,0:T(1,128)S(1)}, /*index=5*/bf16[16,2048]{1,0:T(8,128)(2,1)S(1)}) custom-call(bf16[512,256]{1,0:T(8,128)(2,1)} %k_ref.1, bf16[512,256]{1,0:T(8,128)(2,1)} %v_ref.1, s32[1,64]{1,0:T(1,128)} %bitcast.4, ...), custom_call_target="tpu_custom_call" | custom-call | flops 1 | bytes 1 | tf_op jit(solution)/shard_map/prep/pallas_call | solution.py:62
  5.4 0.6 %copy-done.3 = bf16[16,2048]{1,0:T(8,128)(2,1)} copy-done((bf16[16,2048]{1,0:T(8,128)(2,1)}, bf16[16,2048]{1,0:T(8,128)(2,1)S(1)}, u32[]{:S(2)}) %copy-start.3) | copy-done | bytes 65560
  6.0 4.4 %local_attention.2 = (f32[512,1024]{1,0:T(8,128)S(1)}, f32[512,128]{1,0:T(8,128)S(1)}) custom-call(bf16[512,2048]{1,0:T(8,128)(2,1)} %q_ref.7, bf16[512,256]{1,0:T(8,128)(2,1)S(1)} %get-tuple-element.44.kv_ref.refs_0_), custom_call_target="tpu_custom_call" | custom-call | flops 1 | bytes 1 | tf_op jit(solution)/shard_map/local_attention/pallas_call | solution.py:125
  10.5 0.6 %copy-done.1 = bf16[16,2048]{1,0:T(8,128)(2,1)} copy-done((bf16[16,2048]{1,0:T(8,128)(2,1)}, bf16[16,2048]{1,0:T(8,128)(2,1)S(1)}, u32[]{:S(2)}) %copy-start.1) | copy-done | bytes 65560
  11.1 0.7 %collective-permute-start.3 = (bf16[512,256]{1,0:T(8,128)(2,1)S(1)}, bf16[512,256]{1,0:T(8,128)(2,1)S(1)}, u32[]{:S(2)}, u32[]{:S(2)}) collective-permute-start(bf16[512,256]{1,0:T(8,128)(2,1)S(1)} %get-tuple-element.34.kv_ref.refs_1_), channel_id=1, source_target_pairs={{0,8},{1,9},{2,10},{3,11},{16,24},{17,25},{18,26},{19,27}} | collective-permute-start | bytes 786440 | tf_op jit(solution)/shard_map/ppermute | solution.py:366
  11.8 0.7 %collective-permute-start.6 = (bf16[512,256]{1,0:T(8,128)(2,1)S(1)}, bf16[512,256]{1,0:T(8,128)(2,1)S(1)}, u32[]{:S(2)}, u32[]{:S(2)}) collective-permute-start(bf16[512,256]{1,0:T(8,128)(2,1)S(1)} %get-tuple-element.44.kv_ref.refs_0_), channel_id=1, source_target_pairs={{0,8},{1,9},{2,10},{3,11},{16,24},{17,25},{18,26},{19,27}} | collective-permute-start | bytes 786440 | tf_op jit(solution)/shard_map/ppermute | solution.py:366
  12.4 0.0 copy-start.2
  12.5 4.5 %local_attention.3 = (f32[512,1024]{1,0:T(8,128)S(1)}, f32[512,128]{1,0:T(8,128)S(1)}) custom-call(bf16[512,2048]{1,0:T(8,128)(2,1)} %q_ref.7, bf16[512,256]{1,0:T(8,128)(2,1)S(1)} %get-tuple-element.34.kv_ref.refs_1_), custom_call_target="tpu_custom_call" | custom-call | flops 1 | bytes 1 | tf_op jit(solution)/shard_map/local_attention/pallas_call | solution.py:125
  17.1 2.0 %option_partials.1 = (bf16[64,2176]{1,0:T(8,128)(2,1)S(1)}, bf16[64,2176]{1,0:T(8,128)(2,1)S(1)}) custom-call(s32[1]{0:T(128)} %bitcast.blk_ref, s32[1,64]{1,0:T(1,128)S(1)} %get-tuple-element.45.owner_ref, s32[1,64]{1,0:T(1,128)S(1)} %get-tuple-element.46.slot_ref, s32[1,64]{1,0:T(1,128)S(1)} %get-tuple-element.47.length_ref, ...), custom_call_target="tpu_custom_call" | custom-call | flops 1 | bytes 1 | tf_op jit(solution)/shard_map/option_partials/pallas_call | solution.py:283
  19.1 5.8 %collective-permute-start.9 = (bf16[64,2176]{1,0:T(8,128)(2,1)S(1)}, bf16[64,2176]{1,0:T(8,128)(2,1)S(1)}, u32[]{:S(2)}, u32[]{:S(2)}) collective-permute-start(bf16[64,2176]{1,0:T(8,128)(2,1)S(1)} %get-tuple-element.53), channel_id=1, source_target_pairs={{0,4},{4,0},{8,12},{12,8},{1,5},{5,1},{9,13},{13,9},{2,6},{6,2},{1... | collective-permute-start | bytes 835592 | tf_op jit(solution)/shard_map/ppermute | solution.py:343
  24.9 1.3 %collective-permute-start.7 = (bf16[512,256]{1,0:T(8,128)(2,1)S(1)}, bf16[512,256]{1,0:T(8,128)(2,1)S(1)}, u32[]{:S(2)}, u32[]{:S(2)}) collective-permute-start(bf16[512,256]{1,0:T(8,128)(2,1)S(1)} %collective-permute-done.6.refs_0_), channel_id=1, source_target_pairs={{8,4},{9,5},{10,6},{11,7},{24,20},{25,21},{26,22},{27,23}} | collective-permute-start | bytes 786440 | tf_op jit(solution)/shard_map/ppermute | solution.py:368
  26.2 0.7 %collective-permute-start.8 = (bf16[512,256]{1,0:T(8,128)(2,1)S(1)}, bf16[512,256]{1,0:T(8,128)(2,1)S(1)}, u32[]{:S(2)}, u32[]{:S(2)}) collective-permute-start(bf16[512,256]{1,0:T(8,128)(2,1)S(1)} %collective-permute-done.6.refs_0_), channel_id=1, source_target_pairs={{8,12},{9,13},{10,14},{11,15},{24,28},{25,29},{26,30},{27,31}} | collective-permute-start | bytes 786440 | tf_op jit(solution)/shard_map/ppermute | solution.py:368
  26.8 1.3 %collective-permute-start.4 = (bf16[512,256]{1,0:T(8,128)(2,1)S(1)}, bf16[512,256]{1,0:T(8,128)(2,1)S(1)}, u32[]{:S(2)}, u32[]{:S(2)}) collective-permute-start(bf16[512,256]{1,0:T(8,128)(2,1)S(1)} %collective-permute-done.3.refs_0_), channel_id=1, source_target_pairs={{8,4},{9,5},{10,6},{11,7},{24,20},{25,21},{26,22},{27,23}} | collective-permute-start | bytes 786440 | tf_op jit(solution)/shard_map/ppermute | solution.py:368
  28.1 0.7 %collective-permute-start.5 = (bf16[512,256]{1,0:T(8,128)(2,1)S(1)}, bf16[512,256]{1,0:T(8,128)(2,1)S(1)}, u32[]{:S(2)}, u32[]{:S(2)}) collective-permute-start(bf16[512,256]{1,0:T(8,128)(2,1)S(1)} %collective-permute-done.3.refs_0_), channel_id=1, source_target_pairs={{8,12},{9,13},{10,14},{11,15},{24,28},{25,29},{26,30},{27,31}} | collective-permute-start | bytes 786440 | tf_op jit(solution)/shard_map/ppermute | solution.py:368
  28.8 3.9 %collective-permute-done.9.b = bf16[64,2176]{1,0:T(8,128)(2,1)S(1)} collective-permute-done((bf16[64,2176]{1,0:T(8,128)(2,1)S(1)}, bf16[64,2176]{1,0:T(8,128)(2,1)S(1)}, u32[]{:S(2)}, u32[]{:S(2)}) %collective-permute-start.9) | collective-permute-done | bytes 278560 | tf_op jit(solution)/shard_map/ppermute | solution.py:343
  32.8 0.6 %merge.2 = (bf16[32,2176]{1,0:T(8,128)(2,1)S(1)}, bf16[32,2176]{1,0:T(8,128)(2,1)S(1)}) custom-call(bf16[64,2176]{1,0:T(8,128)(2,1)S(1)} %get-tuple-element.52.a, bf16[64,2176]{1,0:T(8,128)(2,1)S(1)} %collective-permute-done.9.b, f32[512,128]{1,0:T(8,128)S(1)} %get-tuple-element.40.l_ref.after), custom_call_target="tpu_custom_call" | custom-call | flops 1 | bytes 1 | tf_op jit(solution)/shard_map/merge/pallas_call | solution.py:331
  33.3 1.6 %collective-permute-start.10 = (bf16[32,2176]{1,0:T(8,128)(2,1)S(1)}, bf16[32,2176]{1,0:T(8,128)(2,1)S(1)}, u32[]{:S(2)}, u32[]{:S(2)}) collective-permute-start(bf16[32,2176]{1,0:T(8,128)(2,1)S(1)} %get-tuple-element.55), channel_id=1, source_target_pairs={{0,8},{4,12},{8,0},{12,4},{1,9},{5,13},{9,1},{13,5},{2,10},{6,14},... | collective-permute-start | bytes 417800 | tf_op jit(solution)/shard_map/ppermute | solution.py:343
  34.9 6.4 %collective-permute-done.7.refs_1_ = bf16[512,256]{1,0:T(8,128)(2,1)S(1)} collective-permute-done((bf16[512,256]{1,0:T(8,128)(2,1)S(1)}, bf16[512,256]{1,0:T(8,128)(2,1)S(1)}, u32[]{:S(2)}, u32[]{:S(2)}) %collective-permute-start.7) | collective-permute-done | bytes 262176 | tf_op jit(solution)/shard_map/ppermute | solution.py:368
  41.4 4.9 %anchor_attention.2.refs_3_ = bf16[512,2048]{1,0:T(8,128)(2,1)} custom-call(s32[1]{0:T(128)} %bitcast.blk_ref, bf16[512,2048]{1,0:T(8,128)(2,1)S(1)} %copy-done, f32[512,1024]{1,0:T(8,128)S(1)} %get-tuple-element.42.o_in, f32[512,128]{1,0:T(8,128)S(1)} %get-tuple-element.43.l_ref.refs_6_, bf16[512,256]{1,0:T(8,128)(2,1)S(1)} %collective-permute-done.6.refs_0_, ...), custom_call_target="tpu_custom_call" | custom-call | flops 1 | bytes 1 | tf_op jit(solution)/shard_map/anchor_attention/pallas_call | solution.py:204
  46.3 5.0 %anchor_attention.3 = bf16[512,2048]{1,0:T(8,128)(2,1)} custom-call(s32[1]{0:T(128)} %bitcast.blk_ref, bf16[512,2048]{1,0:T(8,128)(2,1)S(1)} %copy-done, f32[512,1024]{1,0:T(8,128)S(1)} %get-tuple-element.39.o_in, f32[512,128]{1,0:T(8,128)S(1)} %get-tuple-element.40.l_ref.after, ...), custom_call_target="tpu_custom_call", output_to_operand_aliasing={{}: (7, {})} | custom-call | flops 1 | bytes 1 | tf_op jit(solution)/shard_map/anchor_attention/pallas_call | solution.py:204
  51.3 1.0 %merge.3 = bf16[32,2048]{1,0:T(8,128)(2,1)} custom-call(bf16[32,2176]{1,0:T(8,128)(2,1)S(1)} %get-tuple-element.54.a, bf16[32,2176]{1,0:T(8,128)(2,1)S(1)} %collective-permute-done.10.b, f32[512,128]{1,0:T(8,128)S(1)} %get-tuple-element.40.l_ref.after), custom_call_target="tpu_custom_call" | custom-call | flops 1 | bytes 1 | tf_op jit(solution)/shard_map/merge/pallas_call | solution.py:331
  (16 shorter events, 0.0 us)
Async XLA Ops:
  0.6 9.8 %collective-permute-start = (bf16[16,2048]{1,0:T(8,128)(2,1)}, bf16[16,2048]{1,0:T(8,128)(2,1)S(1)}, u32[]{:S(2)}, u32[]{:S(2)}) collective-permute-start(bf16[16,2048]{1,0:T(8,128)(2,1)} %refs_3_.1), channel_id=1, source_target_pairs={{0,4},{4,0},{8,12},{12,8},{1,5},{5,1},{9,13},{13,9},{2,6},{6,2},{1... | collective-permute-start | bytes 196616 | tf_op jit(solution)/shard_map/ppermute | solution.py:343
  1.1 9.3 %collective-permute-start.1 = (bf16[16,2048]{1,0:T(8,128)(2,1)}, bf16[16,2048]{1,0:T(8,128)(2,1)S(1)}, u32[]{:S(2)}, u32[]{:S(2)}) collective-permute-start(bf16[16,2048]{1,0:T(8,128)(2,1)} %refs_3_.1), channel_id=1, source_target_pairs={{0,8},{4,12},{8,0},{12,4},{1,9},{5,13},{9,1},{13,5},{2,10},{6,14},... | collective-permute-start | bytes 196616 | tf_op jit(solution)/shard_map/ppermute | solution.py:343
  3.7 6.7 %collective-permute-start.2 = (bf16[16,2048]{1,0:T(8,128)(2,1)}, bf16[16,2048]{1,0:T(8,128)(2,1)S(1)}, u32[]{:S(2)}, u32[]{:S(2)}) collective-permute-start(bf16[16,2048]{1,0:T(8,128)(2,1)} %refs_3_.1), channel_id=1, source_target_pairs={{0,12},{4,8},{8,4},{12,0},{1,13},{5,9},{9,5},{13,1},{2,14},{6,10},... | collective-permute-start | bytes 196616 | tf_op jit(solution)/shard_map/ppermute | solution.py:343
  5.4 0.6 %copy-start.3 = (bf16[16,2048]{1,0:T(8,128)(2,1)}, bf16[16,2048]{1,0:T(8,128)(2,1)S(1)}, u32[]{:S(2)}) copy-start(bf16[16,2048]{1,0:T(8,128)(2,1)S(1)} %get-tuple-element.48.refs_2_) | copy-start | bytes 196612
  10.4 0.6 %copy-start.1 = (bf16[16,2048]{1,0:T(8,128)(2,1)}, bf16[16,2048]{1,0:T(8,128)(2,1)S(1)}, u32[]{:S(2)}) copy-start(bf16[16,2048]{1,0:T(8,128)(2,1)S(1)} %collective-permute-done.2.refs_5_) | copy-start | bytes 196612
  11.1 6.0 %collective-permute-start.3 = (bf16[512,256]{1,0:T(8,128)(2,1)S(1)}, bf16[512,256]{1,0:T(8,128)(2,1)S(1)}, u32[]{:S(2)}, u32[]{:S(2)}) collective-permute-start(bf16[512,256]{1,0:T(8,128)(2,1)S(1)} %get-tuple-element.34.kv_ref.refs_1_), channel_id=1, source_target_pairs={{0,8},{1,9},{2,10},{3,11},{16,24},{17,25},{18,26},{19,27}} | collective-permute-start | bytes 786440 | tf_op jit(solution)/shard_map/ppermute | solution.py:366
  11.8 13.1 %collective-permute-start.6 = (bf16[512,256]{1,0:T(8,128)(2,1)S(1)}, bf16[512,256]{1,0:T(8,128)(2,1)S(1)}, u32[]{:S(2)}, u32[]{:S(2)}) collective-permute-start(bf16[512,256]{1,0:T(8,128)(2,1)S(1)} %get-tuple-element.44.kv_ref.refs_0_), channel_id=1, source_target_pairs={{0,8},{1,9},{2,10},{3,11},{16,24},{17,25},{18,26},{19,27}} | collective-permute-start | bytes 786440 | tf_op jit(solution)/shard_map/ppermute | solution.py:366
  12.4 4.6 %copy-start.2 = (bf16[16,2048]{1,0:T(8,128)(2,1)S(1)}, bf16[16,2048]{1,0:T(8,128)(2,1)}, u32[]{:S(2)}) copy-start(bf16[16,2048]{1,0:T(8,128)(2,1)} %copy-done.1) | copy-start | bytes 196612
  12.5 4.6 %copy-start.4 = (bf16[16,2048]{1,0:T(8,128)(2,1)S(1)}, bf16[16,2048]{1,0:T(8,128)(2,1)}, u32[]{:S(2)}) copy-start(bf16[16,2048]{1,0:T(8,128)(2,1)} %copy-done.3) | copy-start | bytes 196612
  12.5 28.9 %copy-start = (bf16[512,2048]{1,0:T(8,128)(2,1)S(1)}, bf16[512,2048]{1,0:T(8,128)(2,1)}, u32[]{:S(2)}) copy-start(bf16[512,2048]{1,0:T(8,128)(2,1)} %q_ref.7) | copy-start | bytes 6291460
  19.1 13.7 %collective-permute-start.9 = (bf16[64,2176]{1,0:T(8,128)(2,1)S(1)}, bf16[64,2176]{1,0:T(8,128)(2,1)S(1)}, u32[]{:S(2)}, u32[]{:S(2)}) collective-permute-start(bf16[64,2176]{1,0:T(8,128)(2,1)S(1)} %get-tuple-element.53), channel_id=1, source_target_pairs={{0,4},{4,0},{8,12},{12,8},{1,5},{5,1},{9,13},{13,9},{2,6},{6,2},{1... | collective-permute-start | bytes 835592 | tf_op jit(solution)/shard_map/ppermute | solution.py:343
  24.9 16.5 %collective-permute-start.7 = (bf16[512,256]{1,0:T(8,128)(2,1)S(1)}, bf16[512,256]{1,0:T(8,128)(2,1)S(1)}, u32[]{:S(2)}, u32[]{:S(2)}) collective-permute-start(bf16[512,256]{1,0:T(8,128)(2,1)S(1)} %collective-permute-done.6.refs_0_), channel_id=1, source_target_pairs={{8,4},{9,5},{10,6},{11,7},{24,20},{25,21},{26,22},{27,23}} | collective-permute-start | bytes 786440 | tf_op jit(solution)/shard_map/ppermute | solution.py:368
  26.2 15.2 %collective-permute-start.8 = (bf16[512,256]{1,0:T(8,128)(2,1)S(1)}, bf16[512,256]{1,0:T(8,128)(2,1)S(1)}, u32[]{:S(2)}, u32[]{:S(2)}) collective-permute-start(bf16[512,256]{1,0:T(8,128)(2,1)S(1)} %collective-permute-done.6.refs_0_), channel_id=1, source_target_pairs={{8,12},{9,13},{10,14},{11,15},{24,28},{25,29},{26,30},{27,31}} | collective-permute-start | bytes 786440 | tf_op jit(solution)/shard_map/ppermute | solution.py:368
  26.8 19.5 %collective-permute-start.4 = (bf16[512,256]{1,0:T(8,128)(2,1)S(1)}, bf16[512,256]{1,0:T(8,128)(2,1)S(1)}, u32[]{:S(2)}, u32[]{:S(2)}) collective-permute-start(bf16[512,256]{1,0:T(8,128)(2,1)S(1)} %collective-permute-done.3.refs_0_), channel_id=1, source_target_pairs={{8,4},{9,5},{10,6},{11,7},{24,20},{25,21},{26,22},{27,23}} | collective-permute-start | bytes 786440 | tf_op jit(solution)/shard_map/ppermute | solution.py:368
  28.1 18.2 %collective-permute-start.5 = (bf16[512,256]{1,0:T(8,128)(2,1)S(1)}, bf16[512,256]{1,0:T(8,128)(2,1)S(1)}, u32[]{:S(2)}, u32[]{:S(2)}) collective-permute-start(bf16[512,256]{1,0:T(8,128)(2,1)S(1)} %collective-permute-done.3.refs_0_), channel_id=1, source_target_pairs={{8,12},{9,13},{10,14},{11,15},{24,28},{25,29},{26,30},{27,31}} | collective-permute-start | bytes 786440 | tf_op jit(solution)/shard_map/ppermute | solution.py:368
  33.3 18.0 %collective-permute-start.10 = (bf16[32,2176]{1,0:T(8,128)(2,1)S(1)}, bf16[32,2176]{1,0:T(8,128)(2,1)S(1)}, u32[]{:S(2)}, u32[]{:S(2)}) collective-permute-start(bf16[32,2176]{1,0:T(8,128)(2,1)S(1)} %get-tuple-element.55), channel_id=1, source_target_pairs={{0,8},{4,12},{8,0},{12,4},{1,9},{5,13},{9,1},{13,5},{2,10},{6,14},... | collective-permute-start | bytes 417800 | tf_op jit(solution)/shard_map/ppermute | solution.py:343

commit v4 on v3

--- a/solution.py
+++ b/solution.py
@@ -70,7 +70,7 @@
         cost_estimate=BRIEF,
         name="prep",
     )(*[pltpu.with_memory_space_constraint(x, pltpu.HBM) for x in (key, value, *smalls)])
-    return outs[:heads], outs[heads:]
+    return list(outs[:heads]), list(outs[heads:])
 
 
 def pipelined(tasks, scores, finish):
@@ -138,7 +138,7 @@
         compiler_params=params(24),
         cost_estimate=BRIEF,
         name="local_attention",
-    )(pltpu.with_memory_space_constraint(query, pltpu.HBM), kv)
+    )(query, kv)
 
 
 def anchor_kernel(count, blk_ref, q_ref, o_in, l_ref, *refs):
@@ -356,20 +356,21 @@
 
     queries = [opt_query] + [swap(opt_query, n, mask) for mask in range(1, n)]
     row = lambda x: x.reshape(1, options)
-    kvs, smalls = prep(ctx_key, ctx_value, [row(opt_owner), row(opt_slot), row(opt_length), opt_query])
-    queries[0] = smalls[3]
+    kvs, smalls = prep(ctx_key, ctx_value, [row(opt_owner), row(opt_slot), row(opt_length), opt_query, ctx_query])
+    queries[0], ctx_query = smalls[3:]
 
     states = [local_attention(ctx_query, kvs[0], 0)]
-    queries, kvs, states = lax.optimization_barrier((queries, kvs, states))
+    keep, send = option_partials(blk_arr, *smalls[:3], kvs, queries, states[0][1])
+    if n == 4:
+        first = [lax.ppermute(kv, "blk", [(0, 2)]) for kv in kvs]
+        first[0], kvs[1:] = lax.optimization_barrier((first[0], kvs[1:]))
     states += [local_attention(ctx_query, kv, g) for g, kv in enumerate(kvs) if g]
     if n == 4:
-        first = [lax.ppermute(kv, "blk", [(0, 2)]) for kv in kvs]
         first[1:], states = lax.optimization_barrier((first[1:], states))
         anchors = [(x, lax.ppermute(x, "blk", [(2, 1)]), lax.ppermute(x, "blk", [(2, 3)])) for x in first]
     else:
         anchors = [(from_root(kv, blk),) for kv in kvs]
 
-    keep, send = option_partials(blk_arr, *smalls[:3], kvs, queries, states[0][1])
     for bit in range(rounds):
         got = swap(send, n, 1 << bit)
         last = bit == rounds - 1

time: 52.7 us -> 59.9 us (1.14)
  the two profiles are of different devices: /device:TPU:12 before, /device:TPU:22 now
where the time goes in v4:
time: 59.9 us; the launch traced here: 59.6 us
  Pallas kernels  23.3 us (39%)
  waiting for transfers between devices  20.1 us (34%)
  starting transfers between devices  14.1 us (24%)
  local copies, waits for them, and re-layouts  1.32 us (2%)
  between operations  0.77 us (1%)
    ppermute x5, waiting for transfers between devices, swap(): return lax.ppermute(x, 'blk', [(i, i ^ mask) for i in range(n)])  20.1 us
    pallas_call x2, Pallas kernels, anchor_attention(): pl.pallas_call(functools.partial(anchor_kernel, len(cands)), grid=(steps,...  9.94 us
    pallas_call x2, Pallas kernels, local_attention(): pl.pallas_call(local_kernel, grid=(steps,), out_shape=[jax.ShapeDtypeStru...  6.87 us
    ppermute x5, starting transfers between devices, swap(): return lax.ppermute(x, 'blk', [(i, i ^ mask) for i in range(n)])  4.48 us
    ppermute x2, starting transfers between devices, body(): lax.ppermute(x, 'blk', [(2, 3)])  4.3 us
    pallas_call x1, Pallas kernels, option_partials(): pl.pallas_call(functools.partial(option_kernel, n, heads), out_shape=[jax...  2.9 us
    ppermute x2, starting transfers between devices, body(): lax.ppermute(x, 'blk', [(2, 1)])  2.77 us
    ppermute x2, starting transfers between devices, body(): first = [lax.ppermute(kv, 'blk', [(0, 2)]) for kv in kvs]  2.58 us
  transfers between devices with their start and end apart: 11, of which 3 were waited for; matrix products, arithmetic and copies ran while one was open for 0% of the time, Pallas kernels for 27%

profile of v4, /device:TPU:22, one launch (start us, length us, event | category | flops | bytes accessed | tf_op | source)
XLA Modules:
  0.0 59.6 jit_solution(10890781535852725685)
XLA Ops:
  0.6 2.0 %prep.1 = (bf16[512,256]{1,0:T(8,128)(2,1)S(1)}, bf16[512,256]{1,0:T(8,128)(2,1)S(1)}, s32[1,64]{1,0:T(1,128)S(1)}, s32[1,64]{1,0:T(1,128)S(1)}, s32[1,64]{1,0:T...) custom-call(bf16[512,256]{1,0:T(8,128)(2,1)} %k_ref.1, bf16[512,256]{1,0:T(8,128)(2,1)} %v_ref.1, ...), custom_call_target="tpu_custom_call" | custom-call | flops 1 | bytes 1 | tf_op jit(solution)/shard_map/prep/pallas_call | solution.py:62
  2.7 1.3 %collective-permute-start.1 = (bf16[512,256]{1,0:T(8,128)(2,1)S(1)}, bf16[512,256]{1,0:T(8,128)(2,1)S(1)}, u32[]{:S(2)}, u32[]{:S(2)}) collective-permute-start(bf16[512,256]{1,0:T(8,128)(2,1)S(1)} %get-tuple-element.26.kv_ref.refs_0_), channel_id=1, source_target_pairs={{0,8},{1,9},{2,10},{3,11},{16,24},{17,25},{18,26},{19,27}} | collective-permute-start | bytes 786440 | tf_op jit(solution)/shard_map/ppermute | solution.py:365
  4.0 1.3 %collective-permute-start = (bf16[512,256]{1,0:T(8,128)(2,1)S(1)}, bf16[512,256]{1,0:T(8,128)(2,1)S(1)}, u32[]{:S(2)}, u32[]{:S(2)}) collective-permute-start(bf16[512,256]{1,0:T(8,128)(2,1)S(1)} %get-tuple-element.29.kv_ref.refs_1_), channel_id=1, source_target_pairs={{0,8},{1,9},{2,10},{3,11},{16,24},{17,25},{18,26},{19,27}} | collective-permute-start | bytes 786440 | tf_op jit(solution)/shard_map/ppermute | solution.py:365
  5.3 0.4 collective-permute-start.6
  5.7 3.3 %collective-permute-start.7 = (bf16[16,2048]{1,0:T(8,128)(2,1)}, bf16[16,2048]{1,0:T(8,128)(2,1)}, u32[]{:S(2)}, u32[]{:S(2)}) collective-permute-start(bf16[16,2048]{1,0:T(8,128)(2,1)} %refs_3_.1), channel_id=1, source_target_pairs={{0,8},{4,12},{8,0},{12,4},{1,9},{5,13},{9,1},{13,5},{2,10},{6,14},... | collective-permute-start | bytes 196616 | tf_op jit(solution)/shard_map/ppermute | solution.py:343
  9.0 0.5 collective-permute-start.8
  9.5 3.4 %local_attention.2 = (f32[512,1024]{1,0:T(8,128)S(1)}, f32[512,128]{1,0:T(8,128)S(1)}) custom-call(bf16[512,2048]{1,0:T(8,128)(2,1)S(1)} %get-tuple-element.24.q_ref, bf16[512,256]{1,0:T(8,128)(2,1)S(1)} %get-tuple-element.26.kv_ref.refs_0_), custom_call_target="tpu_custom_call" | custom-call | flops 1 | bytes 1 | tf_op jit(solution)/shard_map/local_attention/pallas_call | solution.py:125
  12.9 1.3 %copy-done = f32[512,1024]{1,0:T(8,128)} copy-done((f32[512,1024]{1,0:T(8,128)}, f32[512,1024]{1,0:T(8,128)S(1)}, u32[]{:S(2)}) %copy-start) | copy-done | bytes 2097176
  14.2 8.6 %collective-permute-done.7.refs_4_ = bf16[16,2048]{1,0:T(8,128)(2,1)} collective-permute-done((bf16[16,2048]{1,0:T(8,128)(2,1)}, bf16[16,2048]{1,0:T(8,128)(2,1)}, u32[]{:S(2)}, u32[]{:S(2)}) %collective-permute-start.7) | collective-permute-done | bytes 65568 | tf_op jit(solution)/shard_map/ppermute | solution.py:343
  22.8 2.1 %collective-permute-done.8.refs_5_ = bf16[16,2048]{1,0:T(8,128)(2,1)} collective-permute-done((bf16[16,2048]{1,0:T(8,128)(2,1)}, bf16[16,2048]{1,0:T(8,128)(2,1)}, u32[]{:S(2)}, u32[]{:S(2)}) %collective-permute-start.8) | collective-permute-done | bytes 65568 | tf_op jit(solution)/shard_map/ppermute | solution.py:343
  24.8 2.9 %option_partials.1 = (bf16[64,2176]{1,0:T(8,128)(2,1)S(1)}, bf16[64,2176]{1,0:T(8,128)(2,1)S(1)}) custom-call(s32[1]{0:T(128)} %bitcast.blk_ref, s32[1,64]{1,0:T(1,128)S(1)} %get-tuple-element.38.owner_ref, s32[1,64]{1,0:T(1,128)S(1)} %get-tuple-element.39.slot_ref, s32[1,64]{1,0:T(1,128)S(1)} %get-tuple-element.40.length_ref, ...), custom_call_target="tpu_custom_call" | custom-call | flops 1 | bytes 1 | tf_op jit(solution)/shard_map/option_partials/pallas_call | solution.py:283
  27.7 0.0 copy-start.1
  27.8 0.2 collective-permute-start.9
  28.0 1.5 %collective-permute-start.4 = (bf16[512,256]{1,0:T(8,128)(2,1)S(1)}, bf16[512,256]{1,0:T(8,128)(2,1)S(1)}, u32[]{:S(2)}, u32[]{:S(2)}) collective-permute-start(bf16[512,256]{1,0:T(8,128)(2,1)S(1)} %collective-permute-done.1.refs_0_), channel_id=1, source_target_pairs={{8,4},{9,5},{10,6},{11,7},{24,20},{25,21},{26,22},{27,23}} | collective-permute-start | bytes 786440 | tf_op jit(solution)/shard_map/ppermute | solution.py:370
  29.5 3.0 %collective-permute-start.5 = (bf16[512,256]{1,0:T(8,128)(2,1)S(1)}, bf16[512,256]{1,0:T(8,128)(2,1)S(1)}, u32[]{:S(2)}, u32[]{:S(2)}) collective-permute-start(bf16[512,256]{1,0:T(8,128)(2,1)S(1)} %collective-permute-done.1.refs_0_), channel_id=1, source_target_pairs={{8,12},{9,13},{10,14},{11,15},{24,28},{25,29},{26,30},{27,31}} | collective-permute-start | bytes 786440 | tf_op jit(solution)/shard_map/ppermute | solution.py:370
  32.5 3.5 %local_attention.3 = (f32[512,1024]{1,0:T(8,128)S(1)}, f32[512,128]{1,0:T(8,128)S(1)}) custom-call(bf16[512,2048]{1,0:T(8,128)(2,1)S(1)} %get-tuple-element.24.q_ref, bf16[512,256]{1,0:T(8,128)(2,1)S(1)} %get-tuple-element.29.kv_ref.refs_1_), custom_call_target="tpu_custom_call" | custom-call | flops 1 | bytes 1 | tf_op jit(solution)/shard_map/local_attention/pallas_call | solution.py:125
  35.9 1.3 %collective-permute-start.2 = (bf16[512,256]{1,0:T(8,128)(2,1)S(1)}, bf16[512,256]{1,0:T(8,128)(2,1)S(1)}, u32[]{:S(2)}, u32[]{:S(2)}) collective-permute-start(bf16[512,256]{1,0:T(8,128)(2,1)S(1)} %collective-permute-done.refs_0_), channel_id=1, source_target_pairs={{8,4},{9,5},{10,6},{11,7},{24,20},{25,21},{26,22},{27,23}} | collective-permute-start | bytes 786440 | tf_op jit(solution)/shard_map/ppermute | solution.py:370
  37.2 1.3 %collective-permute-start.3 = (bf16[512,256]{1,0:T(8,128)(2,1)S(1)}, bf16[512,256]{1,0:T(8,128)(2,1)S(1)}, u32[]{:S(2)}, u32[]{:S(2)}) collective-permute-start(bf16[512,256]{1,0:T(8,128)(2,1)S(1)} %collective-permute-done.refs_0_), channel_id=1, source_target_pairs={{8,12},{9,13},{10,14},{11,15},{24,28},{25,29},{26,30},{27,31}} | collective-permute-start | bytes 786440 | tf_op jit(solution)/shard_map/ppermute | solution.py:370
  38.6 0.6 merge.2
  39.1 0.1 collective-permute-start.10
  39.2 9.4 %collective-permute-done.10.b = bf16[32,2176]{1,0:T(8,128)(2,1)S(1)} collective-permute-done((bf16[32,2176]{1,0:T(8,128)(2,1)S(1)}, bf16[32,2176]{1,0:T(8,128)(2,1)S(1)}, u32[]{:S(2)}, u32[]{:S(2)}) %collective-permute-start.10) | collective-permute-done | bytes 139296 | tf_op jit(solution)/shard_map/ppermute | solution.py:343
  48.6 1.0 %merge.3 = bf16[32,2048]{1,0:T(8,128)(2,1)} custom-call(bf16[32,2176]{1,0:T(8,128)(2,1)S(1)} %get-tuple-element.44.a, bf16[32,2176]{1,0:T(8,128)(2,1)S(1)} %collective-permute-done.10.b, f32[512,128]{1,0:T(8,128)S(1)} %get-tuple-element.33.l_ref.after), custom_call_target="tpu_custom_call" | custom-call | flops 1 | bytes 1 | tf_op jit(solution)/shard_map/merge/pallas_call | solution.py:331
  49.6 5.0 %anchor_attention.2.refs_3_ = bf16[512,2048]{1,0:T(8,128)(2,1)} custom-call(s32[1]{0:T(128)} %bitcast.blk_ref, bf16[512,2048]{1,0:T(8,128)(2,1)S(1)} %get-tuple-element.24.q_ref, f32[512,1024]{1,0:T(8,128)S(1)} %copy-done.1, f32[512,128]{1,0:T(8,128)S(1)} %get-tuple-element.36.l_ref.refs_6_, bf16[512,256]{1,0:T(8,128)(2,1)S(1)} %collective-permute-done.1.refs_0_, ...), custom_call_target="tpu_custom_call" | custom-call | flops 1 | bytes 1 | tf_op jit(solution)/shard_map/anchor_attention/pallas_call | solution.py:204
  54.6 5.0 %anchor_attention.3 = bf16[512,2048]{1,0:T(8,128)(2,1)} custom-call(s32[1]{0:T(128)} %bitcast.blk_ref, bf16[512,2048]{1,0:T(8,128)(2,1)S(1)} %get-tuple-element.24.q_ref, f32[512,1024]{1,0:T(8,128)S(1)} %get-tuple-element.32.o_in, f32[512,128]{1,0:T(8,128)S(1)} %get-tuple-element.33.l_ref.after, ...), custom_call_target="tpu_custom_call", output_to_operand_aliasing={{}: (7, {})} | custom-call | flops 1 | bytes 1 | tf_op jit(solution)/shard_map/anchor_attention/pallas_call | solution.py:204
  (10 shorter events, 0.0 us)
Async XLA Ops:
  2.7 25.3 %collective-permute-start.1 = (bf16[512,256]{1,0:T(8,128)(2,1)S(1)}, bf16[512,256]{1,0:T(8,128)(2,1)S(1)}, u32[]{:S(2)}, u32[]{:S(2)}) collective-permute-start(bf16[512,256]{1,0:T(8,128)(2,1)S(1)} %get-tuple-element.26.kv_ref.refs_0_), channel_id=1, source_target_pairs={{0,8},{1,9},{2,10},{3,11},{16,24},{17,25},{18,26},{19,27}} | collective-permute-start | bytes 786440 | tf_op jit(solution)/shard_map/ppermute | solution.py:365
  4.0 32.0 %collective-permute-start = (bf16[512,256]{1,0:T(8,128)(2,1)S(1)}, bf16[512,256]{1,0:T(8,128)(2,1)S(1)}, u32[]{:S(2)}, u32[]{:S(2)}) collective-permute-start(bf16[512,256]{1,0:T(8,128)(2,1)S(1)} %get-tuple-element.29.kv_ref.refs_1_), channel_id=1, source_target_pairs={{0,8},{1,9},{2,10},{3,11},{16,24},{17,25},{18,26},{19,27}} | collective-permute-start | bytes 786440 | tf_op jit(solution)/shard_map/ppermute | solution.py:365
  5.3 8.9 %collective-permute-start.6 = (bf16[16,2048]{1,0:T(8,128)(2,1)}, bf16[16,2048]{1,0:T(8,128)(2,1)S(1)}, u32[]{:S(2)}, u32[]{:S(2)}) collective-permute-start(bf16[16,2048]{1,0:T(8,128)(2,1)} %refs_3_.1), channel_id=1, source_target_pairs={{0,4},{4,0},{8,12},{12,8},{1,5},{5,1},{9,13},{13,9},{2,6},{6,2},{1... | collective-permute-start | bytes 196616 | tf_op jit(solution)/shard_map/ppermute | solution.py:343
  5.7 17.1 %collective-permute-start.7 = (bf16[16,2048]{1,0:T(8,128)(2,1)}, bf16[16,2048]{1,0:T(8,128)(2,1)}, u32[]{:S(2)}, u32[]{:S(2)}) collective-permute-start(bf16[16,2048]{1,0:T(8,128)(2,1)} %refs_3_.1), channel_id=1, source_target_pairs={{0,8},{4,12},{8,0},{12,4},{1,9},{5,13},{9,1},{13,5},{2,10},{6,14},... | collective-permute-start | bytes 196616 | tf_op jit(solution)/shard_map/ppermute | solution.py:343
  9.0 15.9 %collective-permute-start.8 = (bf16[16,2048]{1,0:T(8,128)(2,1)}, bf16[16,2048]{1,0:T(8,128)(2,1)}, u32[]{:S(2)}, u32[]{:S(2)}) collective-permute-start(bf16[16,2048]{1,0:T(8,128)(2,1)} %refs_3_.1), channel_id=1, source_target_pairs={{0,12},{4,8},{8,4},{12,0},{1,13},{5,9},{9,5},{13,1},{2,14},{6,10},... | collective-permute-start | bytes 196616 | tf_op jit(solution)/shard_map/ppermute | solution.py:343
  12.9 1.3 %copy-start = (f32[512,1024]{1,0:T(8,128)}, f32[512,1024]{1,0:T(8,128)S(1)}, u32[]{:S(2)}) copy-start(f32[512,1024]{1,0:T(8,128)S(1)} %get-tuple-element.35.o_in) | copy-start | bytes 6291460
  27.7 21.9 %copy-start.1 = (f32[512,1024]{1,0:T(8,128)S(1)}, f32[512,1024]{1,0:T(8,128)}, u32[]{:S(2)}) copy-start(f32[512,1024]{1,0:T(8,128)} %copy-done) | copy-start | bytes 6291460
  27.8 10.8 %collective-permute-start.9 = (bf16[64,2176]{1,0:T(8,128)(2,1)S(1)}, bf16[64,2176]{1,0:T(8,128)(2,1)S(1)}, u32[]{:S(2)}, u32[]{:S(2)}) collective-permute-start(bf16[64,2176]{1,0:T(8,128)(2,1)S(1)} %get-tuple-element.43), channel_id=1, source_target_pairs={{0,4},{4,0},{8,12},{12,8},{1,5},{5,1},{9,13},{13,9},{2,6},{6,2},{1... | collective-permute-start | bytes 835592 | tf_op jit(solution)/shard_map/ppermute | solution.py:343
  28.0 21.6 %collective-permute-start.4 = (bf16[512,256]{1,0:T(8,128)(2,1)S(1)}, bf16[512,256]{1,0:T(8,128)(2,1)S(1)}, u32[]{:S(2)}, u32[]{:S(2)}) collective-permute-start(bf16[512,256]{1,0:T(8,128)(2,1)S(1)} %collective-permute-done.1.refs_0_), channel_id=1, source_target_pairs={{8,4},{9,5},{10,6},{11,7},{24,20},{25,21},{26,22},{27,23}} | collective-permute-start | bytes 786440 | tf_op jit(solution)/shard_map/ppermute | solution.py:370
  29.5 20.2 %collective-permute-start.5 = (bf16[512,256]{1,0:T(8,128)(2,1)S(1)}, bf16[512,256]{1,0:T(8,128)(2,1)S(1)}, u32[]{:S(2)}, u32[]{:S(2)}) collective-permute-start(bf16[512,256]{1,0:T(8,128)(2,1)S(1)} %collective-permute-done.1.refs_0_), channel_id=1, source_target_pairs={{8,12},{9,13},{10,14},{11,15},{24,28},{25,29},{26,30},{27,31}} | collective-permute-start | bytes 786440 | tf_op jit(solution)/shard_map/ppermute | solution.py:370
  35.9 18.7 %collective-permute-start.2 = (bf16[512,256]{1,0:T(8,128)(2,1)S(1)}, bf16[512,256]{1,0:T(8,128)(2,1)S(1)}, u32[]{:S(2)}, u32[]{:S(2)}) collective-permute-start(bf16[512,256]{1,0:T(8,128)(2,1)S(1)} %collective-permute-done.refs_0_), channel_id=1, source_target_pairs={{8,4},{9,5},{10,6},{11,7},{24,20},{25,21},{26,22},{27,23}} | collective-permute-start | bytes 786440 | tf_op jit(solution)/shard_map/ppermute | solution.py:370
  37.2 17.3 %collective-permute-start.3 = (bf16[512,256]{1,0:T(8,128)(2,1)S(1)}, bf16[512,256]{1,0:T(8,128)(2,1)S(1)}, u32[]{:S(2)}, u32[]{:S(2)}) collective-permute-start(bf16[512,256]{1,0:T(8,128)(2,1)S(1)} %collective-permute-done.refs_0_), channel_id=1, source_target_pairs={{8,12},{9,13},{10,14},{11,15},{24,28},{25,29},{26,30},{27,31}} | collective-permute-start | bytes 786440 | tf_op jit(solution)/shard_map/ppermute | solution.py:370
  39.1 9.5 %collective-permute-start.10 = (bf16[32,2176]{1,0:T(8,128)(2,1)S(1)}, bf16[32,2176]{1,0:T(8,128)(2,1)S(1)}, u32[]{:S(2)}, u32[]{:S(2)}) collective-permute-start(bf16[32,2176]{1,0:T(8,128)(2,1)S(1)} %get-tuple-element.45), channel_id=1, source_target_pairs={{0,8},{4,12},{8,0},{12,4},{1,9},{5,13},{9,1},{13,5},{2,10},{6,14},... | collective-permute-start | bytes 417800 | tf_op jit(solution)/shard_map/ppermute | solution.py:343

commit v5 on v4

--- a/solution.py
+++ b/solution.py
@@ -22,6 +22,7 @@
 SMEM = pl.BlockSpec(memory_space=pltpu.SMEM)
 HBM = pl.BlockSpec(memory_space=pltpu.HBM)
 ANY = pl.BlockSpec(memory_space=pl.ANY)
+LONG = pl.CostEstimate(flops=10**11, bytes_accessed=1, transcendentals=0)
 BRIEF = pl.CostEstimate(flops=1, bytes_accessed=1, transcendentals=0)
 
 
@@ -82,134 +83,133 @@
         finish(task, now)
 
 
-def local_kernel(q_ref, kv_ref, o_ref, l_ref, ve):
-    step = pl.program_id(0)
+def head_columns(h):
+    return slice(h * HD, (h + 1) * HD)
+
+
+def local_kernel(g, q_ref, kv_ref, acc_ref, top_ref, sum_ref, ve):
     rows = q_ref.shape[0]
-
-    @pl.when(step == 0)
-    def _():
-        ve[:, :HD] = kv_ref[:, HD:]
-        ve[:, HD:] = jnp.ones((rows, HD), jnp.bfloat16)
-        l_ref[...] = jnp.zeros(l_ref.shape, jnp.float32)
-
-    lane = lax.broadcasted_iota(jnp.int32, (TILE, HD), 1)
-    seen = lax.broadcasted_iota(jnp.int32, (TILE, TILE), 0) >= lax.broadcasted_iota(jnp.int32, (TILE, TILE), 1)
+    ve[:, :HD] = kv_ref[:, HD:]
+    ve[:, HD:] = jnp.ones((rows, HD), jnp.bfloat16)
+    row = lax.broadcasted_iota(jnp.int32, (PAIR * TILE, TILE), 0)
+    seen = lax.rem(row, TILE) >= lax.broadcasted_iota(jnp.int32, (PAIR * TILE, TILE), 1)
 
     def scores(task):
-        j, at = task
-        q = q_ref[at : at + TILE, j * HD : (j + 1) * HD]
+        first, at = task
+        q = jnp.concatenate([q_ref[at : at + TILE, head_columns(g * GROUP + first + j)] for j in range(PAIR)], axis=0)
         parts = [nt(q, kv_ref[:at, :HD])] if at else []
         parts.append(jnp.where(seen, nt(q, kv_ref[at : at + TILE, :HD]), NEG))
         return parts
 
     def finish(task, parts):
-        j, at = task
+        first, at = task
         top = fold(jnp.maximum, [jnp.max(s, axis=1, keepdims=True) for s in parts])
         total = None
         for s, start in zip(parts, [0, at] if at else [at]):
             p = jnp.exp2((s - top) * C2).astype(jnp.bfloat16)
             part = nn(p, ve[start : start + s.shape[1], :])
             total = part if total is None else total + part
-        z = total[:, HD:]
-        o_ref[at : at + TILE, j * HD : (j + 1) * HD] = total[:, :HD] / z
-        log = top * C2 + jnp.log2(z)
-        l_ref[at : at + TILE, :] = jnp.where(lane == step * PAIR + j, log, l_ref[at : at + TILE, :])
-
-    pipelined([(j, at) for j in range(PAIR) for at in range(0, rows, TILE)], scores, finish)
+        top = jnp.broadcast_to(top * C2, (PAIR * TILE, HD))
+        for j in range(PAIR):
+            here, at_j = (slice(at, at + TILE), head_columns(first + j)), slice(j * TILE, (j + 1) * TILE)
+            acc_ref[here] = total[at_j, :HD]
+            sum_ref[here] = total[at_j, HD:]
+            top_ref[here] = top[at_j]
+
+    pipelined([(h, at) for h in range(0, GROUP, PAIR) for at in range(0, rows, TILE)], scores, finish)
 
 
 def local_attention(query, kv, g):
     rows = query.shape[0]
-    steps = GROUP // PAIR
-    whole = pl.BlockSpec((rows, 2 * HD), lambda h: (0, 0))
     return pl.pallas_call(
-        local_kernel,
-        grid=(steps,),
-        out_shape=[
-            jax.ShapeDtypeStruct((rows, GROUP * HD), jnp.float32),
-            jax.ShapeDtypeStruct((rows, HD), jnp.float32),
-        ],
-        in_specs=[pl.BlockSpec((rows, PAIR * HD), lambda h: (0, g * steps + h)), whole],
-        out_specs=[
-            pl.BlockSpec((rows, PAIR * HD), lambda h: (0, h)),
-            pl.BlockSpec((rows, HD), lambda h: (0, 0)),
-        ],
+        functools.partial(local_kernel, g),
+        out_shape=[jax.ShapeDtypeStruct((rows, GROUP * HD), jnp.float32)] * 3,
+        in_specs=[VMEM] * 2,
+        out_specs=[VMEM] * 3,
         scratch_shapes=[pltpu.VMEM((rows, 2 * HD), jnp.bfloat16)],
-        compiler_params=params(24),
-        cost_estimate=BRIEF,
+        compiler_params=params(16),
+        cost_estimate=LONG,
         name="local_attention",
     )(query, kv)
 
 
-def anchor_kernel(count, blk_ref, q_ref, o_in, l_ref, *refs):
-    cand, (o_ref, ka, vae) = refs[:count], refs[-3:]
-    step = pl.program_id(0)
+def anchor_kernel(g, count, prior, blk_ref, q_ref, acc_ref, top_ref, sum_ref, *refs):
+    cand, (o_ref, token, ka, vae, out, sem) = refs[:count], refs[count + prior :]
     rows = q_ref.shape[0]
     blk = blk_ref[0]
-
-    @pl.when(step == 0)
+    token[...] = jnp.zeros(token.shape, jnp.float32)
+
+    def leave(h):
+        return pltpu.make_async_copy(out.at[h], o_ref.at[:, head_columns(g * GROUP + h)], sem.at[h])
+
+    def take(ref):
+        ka[...] = ref[:, :HD]
+        vae[:, :HD] = ref[:, HD:]
+
+    if count == 1:
+        take(cand[0])
+    else:
+        pl.when(blk == 1)(lambda: take(cand[1]))
+        pl.when(blk == 2)(lambda: take(cand[0]))
+        pl.when(blk == 3)(lambda: take(cand[2]))
+
+    def scores(h):
+        return nt(q_ref[:, head_columns(g * GROUP + h)], ka[...])
+
+    def finish(h, s):
+        held = (slice(None), head_columns(h))
+        before = top_ref[held]
+        top = jnp.maximum(jnp.max(s, axis=1, keepdims=True) * C2, before)
+        p = [jnp.exp2(s[:, at : at + HD] * C2 - top).astype(jnp.bfloat16) for at in range(0, rows, HD)]
+        total = nn(jnp.concatenate(p, axis=1), vae[...])
+        w = jnp.exp2(before - top)
+        o = (total[:, :HD] + w * acc_ref[held]) * inverse(total[:, HD:] + w * sum_ref[held])
+        out[h] = o.astype(jnp.bfloat16)
+        leave(h).start()
+
+    @pl.when(blk > 0)
     def _():
         vae[:, HD:] = jnp.ones((rows, HD), jnp.bfloat16)
-
-        def take(ref):
-            ka[...] = ref[:, :HD]
-            vae[:, :HD] = ref[:, HD:]
-
-        if count == 1:
-            take(cand[0])
-        else:
-            pl.when(blk == 1)(lambda: take(cand[1]))
-            pl.when(blk == 2)(lambda: take(cand[0]))
-            pl.when(blk == 3)(lambda: take(cand[2]))
-
-    lane = lax.broadcasted_iota(jnp.int32, (TILE, HD), 1)
-
-    def scores(task):
-        j, at = task
-        return nt(q_ref[at : at + TILE, j * HD : (j + 1) * HD], ka[...])
-
-    def finish(task, s):
-        j, at = task
-        log = jnp.sum(jnp.where(lane == step * PAIR + j, l_ref[at : at + TILE, :], 0.0), axis=1, keepdims=True)
-        top = jnp.maximum(jnp.max(s, axis=1, keepdims=True) * C2, log)
-        p = jnp.exp2(s * C2 - top).astype(jnp.bfloat16)
-        total = nn(p, vae[...])
-        w = jnp.exp2(log - top)
-        o = o_in[at : at + TILE, j * HD : (j + 1) * HD]
-        out = (total[:, :HD] + w * o) / (total[:, HD:] + w)
-        o_ref[at : at + TILE, j * HD : (j + 1) * HD] = out.astype(jnp.bfloat16)
-
-    @pl.when(blk > 0)
-    def _():
-        pipelined([(j, at) for j in range(PAIR) for at in range(0, rows, TILE)], scores, finish)
+        pipelined(list(range(GROUP)), scores, finish)
 
     @pl.when(blk == 0)
     def _():
-        o_ref[...] = o_in[...].astype(jnp.bfloat16)
+        for h in range(GROUP):
+            held = (slice(None), head_columns(h))
+            out[h] = (acc_ref[held] * inverse(sum_ref[held])).astype(jnp.bfloat16)
+            leave(h).start()
+
+    for h in range(GROUP):
+        leave(h).wait()
+
+
+def inverse(x):
+    guess = pl.reciprocal(x, approx=True)
+    return guess * (2.0 - x * guess)
 
 
 def anchor_attention(blk, query, state, cands, g, prior):
     rows = query.shape[0]
-    steps = GROUP // PAIR
-    block = (rows, PAIR * HD)
-    column = pl.BlockSpec(block, lambda h: (0, g * steps + h))
     args = [blk, query, *state, *cands]
-    specs = [SMEM, column, pl.BlockSpec(block, lambda h: (0, h)), pl.BlockSpec((rows, HD), lambda h: (0, 0))]
-    specs += [pl.BlockSpec((rows, 2 * HD), lambda h: (0, 0))] * len(cands)
+    specs = [SMEM] + [VMEM] * (4 + len(cands))
     alias = {}
     if prior is not None:
         alias = {len(args): 0}
         args.append(prior)
         specs.append(ANY)
     return pl.pallas_call(
-        functools.partial(anchor_kernel, len(cands)),
-        grid=(steps,),
-        out_shape=jax.ShapeDtypeStruct(query.shape, query.dtype),
+        functools.partial(anchor_kernel, g, len(cands), len(alias)),
+        out_shape=[jax.ShapeDtypeStruct(query.shape, query.dtype), jax.ShapeDtypeStruct((8, HD), jnp.float32)],
         in_specs=specs,
-        out_specs=column,
-        scratch_shapes=[pltpu.VMEM((rows, HD), jnp.bfloat16), pltpu.VMEM((rows, 2 * HD), jnp.bfloat16)],
+        out_specs=[ANY, VMEM],
+        scratch_shapes=[
+            pltpu.VMEM((rows, HD), jnp.bfloat16),
+            pltpu.VMEM((rows, 2 * HD), jnp.bfloat16),
+            pltpu.VMEM((GROUP, rows, HD), jnp.bfloat16),
+            pltpu.SemaphoreType.DMA((GROUP,)),
+        ],
         input_output_aliases=alias,
-        compiler_params=params(24),
+        compiler_params=params(16),
         cost_estimate=BRIEF,
         name="anchor_attention",
     )(*args)
@@ -289,7 +289,7 @@
             pltpu.VMEM((options, heads * HD), jnp.bfloat16),
             pltpu.VMEM((options, width), jnp.bfloat16),
         ],
-        compiler_params=params(32),
+        compiler_params=params(16),
         cost_estimate=BRIEF,
         name="option_partials",
     )(blk, owner, slot, length, *kvs, *queries, after)
@@ -333,7 +333,7 @@
         out_shape=shapes,
         in_specs=[VMEM] * 2 + [ANY],
         out_specs=[VMEM] * len(shapes),
-        compiler_params=params(32),
+        compiler_params=params(16),
         cost_estimate=BRIEF,
         name="merge",
     )(a, b, after)
@@ -359,29 +359,31 @@
     kvs, smalls = prep(ctx_key, ctx_value, [row(opt_owner), row(opt_slot), row(opt_length), opt_query, ctx_query])
     queries[0], ctx_query = smalls[3:]
 
+    hold = lax.optimization_barrier
     states = [local_attention(ctx_query, kvs[0], 0)]
     keep, send = option_partials(blk_arr, *smalls[:3], kvs, queries, states[0][1])
     if n == 4:
         first = [lax.ppermute(kv, "blk", [(0, 2)]) for kv in kvs]
-        first[0], kvs[1:] = lax.optimization_barrier((first[0], kvs[1:]))
+        first[0], keep, kvs[1:] = hold((first[0], keep, kvs[1:]))
     states += [local_attention(ctx_query, kv, g) for g, kv in enumerate(kvs) if g]
     if n == 4:
-        first[1:], states = lax.optimization_barrier((first[1:], states))
-        anchors = [(x, lax.ppermute(x, "blk", [(2, 1)]), lax.ppermute(x, "blk", [(2, 3)])) for x in first]
+        first[1:], states = hold((first[1:], states))
+        anchors = [[x, lax.ppermute(x, "blk", [(2, 1)]), lax.ppermute(x, "blk", [(2, 3)])] for x in first]
+        anchors[0], first[1:] = hold((anchors[0], first[1:]))
     else:
-        anchors = [(from_root(kv, blk),) for kv in kvs]
-
+        anchors = [[from_root(kv, blk)] for kv in kvs]
+    ctx_out, tokens = None, []
+    for g, state in enumerate(states):
+        ctx_out, token = anchor_attention(blk_arr, ctx_query, state, anchors[g], g, ctx_out)
+        tokens.append(token)
     for bit in range(rounds):
         got = swap(send, n, 1 << bit)
         last = bit == rounds - 1
-        outs = merge(keep, got, last, states[-1][1])
+        outs = merge(keep, got, last, tokens[-1 if last else 0])
         if last:
             opt_out = outs[0]
         else:
             keep, send = outs
-    ctx_out = None
-    for g, state in enumerate(states):
-        ctx_out = anchor_attention(blk_arr, ctx_query, state, anchors[g], g, ctx_out)
     return (ctx_out, opt_out)
 
 

time: 59.9 us -> 49.5 us (0.83)
  the two profiles are of different devices: /device:TPU:22 before, /device:TPU:12 now
where the time goes in v5:
time: 49.5 us; the launch traced here: 48.9 us
  Pallas kernels  22 us (44%)
  starting transfers between devices  15.9 us (32%)
  waiting for transfers between devices  7.56 us (15%)
  local copies, waits for them, and re-layouts  2.63 us (5%)
  between operations  0.8 us (2%)
    ppermute x5, starting transfers between devices, swap(): return lax.ppermute(x, 'blk', [(i, i ^ mask) for i in range(n)])  9.67 us
    pallas_call x2, Pallas kernels, anchor_attention(): pl.pallas_call(functools.partial(anchor_kernel, g, len(cands), len(alias)...  9.17 us
    ppermute x2, waiting for transfers between devices, body(): lax.ppermute(x, 'blk', [(2, 1)])  7.54 us
    pallas_call x2, Pallas kernels, local_attention(): pl.pallas_call(functools.partial(local_kernel, g), out_shape=[jax.ShapeDt...  5.44 us
    pallas_call x1, Pallas kernels, option_partials(): pl.pallas_call(functools.partial(option_kernel, n, heads), out_shape=[jax...  3.11 us
    pallas_call x1, Pallas kernels, prep(): pl.pallas_call(functools.partial(prep_kernel, heads), out_shape=[jax.Shap...  2.74 us
    ppermute x2, starting transfers between devices, body(): lax.ppermute(x, 'blk', [(2, 1)])  2.72 us
    unnamed x12, local copies, waits for them, and re-layouts  2.63 us
  transfers between devices with their start and end apart: 11, of which 2 were waited for; matrix products, arithmetic and copies ran while one was open for 0% of the time, Pallas kernels for 43%

profile of v5, /device:TPU:12, one launch (start us, length us, event | category | flops | bytes accessed | tf_op | source)
XLA Modules:
  0.0 48.9 jit_solution(14717670538589751077)
XLA Ops:
  0.6 0.5 %collective-permute-start.2 = (bf16[16,2048]{1,0:T(8,128)(2,1)}, bf16[16,2048]{1,0:T(8,128)(2,1)S(1)}, u32[]{:S(2)}, u32[]{:S(2)}) collective-permute-start(bf16[16,2048]{1,0:T(8,128)(2,1)} %refs_3_.1), channel_id=1, source_target_pairs={{0,4},{4,0},{8,12},{12,8},{1,5},{5,1},{9,13},{13,9},{2,6},{6,2},{1... | collective-permute-start | bytes 196616 | tf_op jit(solution)/shard_map/ppermute | solution.py:343
  1.1 2.7 %collective-permute-start.4 = (bf16[16,2048]{1,0:T(8,128)(2,1)}, bf16[16,2048]{1,0:T(8,128)(2,1)S(1)}, u32[]{:S(2)}, u32[]{:S(2)}) collective-permute-start(bf16[16,2048]{1,0:T(8,128)(2,1)} %refs_3_.1), channel_id=1, source_target_pairs={{0,12},{4,8},{8,4},{12,0},{1,13},{5,9},{9,5},{13,1},{2,14},{6,10},... | collective-permute-start | bytes 196616 | tf_op jit(solution)/shard_map/ppermute | solution.py:343
  3.9 1.2 %collective-permute-start.3 = (bf16[16,2048]{1,0:T(8,128)(2,1)}, bf16[16,2048]{1,0:T(8,128)(2,1)S(1)}, u32[]{:S(2)}, u32[]{:S(2)}) collective-permute-start(bf16[16,2048]{1,0:T(8,128)(2,1)} %refs_3_.1), channel_id=1, source_target_pairs={{0,8},{4,12},{8,0},{12,4},{1,9},{5,13},{9,1},{13,5},{2,10},{6,14},... | collective-permute-start | bytes 196616 | tf_op jit(solution)/shard_map/ppermute | solution.py:343
  5.1 2.7 %prep.1 = (bf16[512,256]{1,0:T(8,128)(2,1)S(1)}, bf16[512,256]{1,0:T(8,128)(2,1)}, s32[1,64]{1,0:T(1,128)S(1)}, s32[1,64]{1,0:T(1,128)S(1)}, s32[1,64]{1,0:T(1,1...) custom-call(bf16[512,256]{1,0:T(8,128)(2,1)} %k_ref.1, bf16[512,256]{1,0:T(8,128)(2,1)} %v_ref.1, ...), custom_call_target="tpu_custom_call" | custom-call | flops 1 | bytes 1 | tf_op jit(solution)/shard_map/prep/pallas_call | solution.py:63
  7.8 0.0 copy-start
  7.8 1.4 %collective-permute-start = (bf16[512,256]{1,0:T(8,128)(2,1)}, bf16[512,256]{1,0:T(8,128)(2,1)}, u32[]{:S(2)}, u32[]{:S(2)}) collective-permute-start(bf16[512,256]{1,0:T(8,128)(2,1)} %get-tuple-element.47.refs_1_.kv_ref), channel_id=1, source_target_pairs={{0,8},{1,9},{2,10},{3,11},{16,24},{17,25},{18,26},{19,27}} | collective-permute-start | bytes 786440 | tf_op jit(solution)/shard_map/ppermute | solution.py:366
  9.2 0.7 %collective-permute-start.1 = (bf16[512,256]{1,0:T(8,128)(2,1)S(1)}, bf16[512,256]{1,0:T(8,128)(2,1)S(1)}, u32[]{:S(2)}, u32[]{:S(2)}) collective-permute-start(bf16[512,256]{1,0:T(8,128)(2,1)S(1)} %get-tuple-element.38.kv_ref.refs_0_), channel_id=1, source_target_pairs={{0,8},{1,9},{2,10},{3,11},{16,24},{17,25},{18,26},{19,27}} | collective-permute-start | bytes 786440 | tf_op jit(solution)/shard_map/ppermute | solution.py:366
  9.9 2.2 %local_attention.2 = (f32[512,1024]{1,0:T(8,128)S(1)}, f32[512,1024]{1,0:T(8,128)S(1)}, f32[512,1024]{1,0:T(8,128)S(1)}) custom-call(bf16[512,2048]{1,0:T(8,128)(2,1)S(1)} %get-tuple-element.36.q_ref, bf16[512,256]{1,0:T(8,128)(2,1)S(1)} %get-tuple-element.38.kv_ref.refs_0_), custom_call_target="tpu_custom_call" | custom-call | flops 99999997952 | bytes 1 | tf_op jit(solution)/shard_map/local_attention/pallas_call | solution.py:124
  12.2 1.3 %copy-done.2 = f32[512,1024]{1,0:T(8,128)} copy-done((f32[512,1024]{1,0:T(8,128)}, f32[512,1024]{1,0:T(8,128)S(1)}, u32[]{:S(2)}) %copy-start.2) | copy-done | bytes 2097176
  13.5 1.3 %copy-done.4 = f32[512,1024]{1,0:T(8,128)} copy-done((f32[512,1024]{1,0:T(8,128)}, f32[512,1024]{1,0:T(8,128)S(1)}, u32[]{:S(2)}) %copy-start.4) | copy-done | bytes 2097176
  14.8 3.1 %option_partials.1 = (bf16[64,2176]{1,0:T(8,128)(2,1)S(1)}, bf16[64,2176]{1,0:T(8,128)(2,1)S(1)}) custom-call(s32[1]{0:T(128)} %bitcast.blk_ref, s32[1,64]{1,0:T(1,128)S(1)} %get-tuple-element.42.owner_ref, s32[1,64]{1,0:T(1,128)S(1)} %get-tuple-element.43.slot_ref, s32[1,64]{1,0:T(1,128)S(1)} %get-tuple-element.44.length_ref, ...), custom_call_target="tpu_custom_call" | custom-call | flops 1 | bytes 1 | tf_op jit(solution)/shard_map/option_partials/pallas_call | solution.py:283
  17.9 5.0 %collective-permute-start.9 = (bf16[64,2176]{1,0:T(8,128)(2,1)S(1)}, bf16[64,2176]{1,0:T(8,128)(2,1)S(1)}, u32[]{:S(2)}, u32[]{:S(2)}) collective-permute-start(bf16[64,2176]{1,0:T(8,128)(2,1)S(1)} %get-tuple-element.65), channel_id=1, source_target_pairs={{0,4},{4,0},{8,12},{12,8},{1,5},{5,1},{9,13},{13,9},{2,6},{6,2},{1... | collective-permute-start | bytes 835592 | tf_op jit(solution)/shard_map/ppermute | solution.py:343
  22.9 0.8 %collective-permute-start.8 = (bf16[512,256]{1,0:T(8,128)(2,1)S(1)}, bf16[512,256]{1,0:T(8,128)(2,1)S(1)}, u32[]{:S(2)}, u32[]{:S(2)}) collective-permute-start(bf16[512,256]{1,0:T(8,128)(2,1)S(1)} %collective-permute-done.1.refs_0_), channel_id=1, source_target_pairs={{8,12},{9,13},{10,14},{11,15},{24,28},{25,29},{26,30},{27,31}} | collective-permute-start | bytes 786440 | tf_op jit(solution)/shard_map/ppermute | solution.py:371
  23.7 1.4 %collective-permute-start.7 = (bf16[512,256]{1,0:T(8,128)(2,1)S(1)}, bf16[512,256]{1,0:T(8,128)(2,1)S(1)}, u32[]{:S(2)}, u32[]{:S(2)}) collective-permute-start(bf16[512,256]{1,0:T(8,128)(2,1)S(1)} %collective-permute-done.1.refs_0_), channel_id=1, source_target_pairs={{8,4},{9,5},{10,6},{11,7},{24,20},{25,21},{26,22},{27,23}} | collective-permute-start | bytes 786440 | tf_op jit(solution)/shard_map/ppermute | solution.py:371
  25.2 3.2 %local_attention.3 = (f32[512,1024]{1,0:T(8,128)S(1)}, f32[512,1024]{1,0:T(8,128)S(1)}, f32[512,1024]{1,0:T(8,128)S(1)}) custom-call(bf16[512,2048]{1,0:T(8,128)(2,1)S(1)} %copy-done.1, bf16[512,256]{1,0:T(8,128)(2,1)} %get-tuple-element.47.refs_1_.kv_ref), custom_call_target="tpu_custom_call" | custom-call | flops 99999997952 | bytes 1 | tf_op jit(solution)/shard_map/local_attention/pallas_call | solution.py:124
  28.4 0.7 %collective-permute-start.6 = (bf16[512,256]{1,0:T(8,128)(2,1)}, bf16[512,256]{1,0:T(8,128)(2,1)S(1)}, u32[]{:S(2)}, u32[]{:S(2)}) collective-permute-start(bf16[512,256]{1,0:T(8,128)(2,1)} %collective-permute-done.refs_0_), channel_id=1, source_target_pairs={{8,12},{9,13},{10,14},{11,15},{24,28},{25,29},{26,30},{27,31}} | collective-permute-start | bytes 786440 | tf_op jit(solution)/shard_map/ppermute | solution.py:371
  29.1 1.3 %collective-permute-start.5 = (bf16[512,256]{1,0:T(8,128)(2,1)}, bf16[512,256]{1,0:T(8,128)(2,1)S(1)}, u32[]{:S(2)}, u32[]{:S(2)}) collective-permute-start(bf16[512,256]{1,0:T(8,128)(2,1)} %collective-permute-done.refs_0_), channel_id=1, source_target_pairs={{8,4},{9,5},{10,6},{11,7},{24,20},{25,21},{26,22},{27,23}} | collective-permute-start | bytes 786440 | tf_op jit(solution)/shard_map/ppermute | solution.py:371
  30.4 3.9 %collective-permute-done.7.refs_1_ = bf16[512,256]{1,0:T(8,128)(2,1)S(1)} collective-permute-done((bf16[512,256]{1,0:T(8,128)(2,1)S(1)}, bf16[512,256]{1,0:T(8,128)(2,1)S(1)}, u32[]{:S(2)}, u32[]{:S(2)}) %collective-permute-start.7) | collective-permute-done | bytes 262176 | tf_op jit(solution)/shard_map/ppermute | solution.py:371
  34.3 4.0 %anchor_attention.2 = (bf16[512,2048]{1,0:T(8,128)(2,1)}, f32[8,128]{1,0:T(8,128)S(1)}) custom-call(s32[1]{0:T(128)} %bitcast.blk_ref, bf16[512,2048]{1,0:T(8,128)(2,1)S(1)} %copy-done.1, f32[512,1024]{1,0:T(8,128)S(1)} %copy-done.3, f32[512,1024]{1,0:T(8,128)S(1)} %get-tuple-element.56.refs_6_.top_ref, f32[512,1024]{1,0:T(8,128)S(1)} %copy-done.5, ...), custom_call_target="tpu_custom_call" | custom-call | flops 1 | bytes 1 | tf_op jit(solution)/shard_map/anchor_attention/pallas_call | solution.py:200
  38.3 0.6 %merge.2 = (bf16[32,2176]{1,0:T(8,128)(2,1)S(1)}, bf16[32,2176]{1,0:T(8,128)(2,1)S(1)}) custom-call(bf16[64,2176]{1,0:T(8,128)(2,1)S(1)} %get-tuple-element.64.a, bf16[64,2176]{1,0:T(8,128)(2,1)S(1)} %collective-permute-done.9.b, f32[8,128]{1,0:T(8,128)S(1)} %get-tuple-element.66.after), custom_call_target="tpu_custom_call" | custom-call | flops 1 | bytes 1 | tf_op jit(solution)/shard_map/merge/pallas_call | solution.py:331
  38.9 0.2 collective-permute-start.10
  39.1 3.6 %collective-permute-done.5.refs_1_ = bf16[512,256]{1,0:T(8,128)(2,1)S(1)} collective-permute-done((bf16[512,256]{1,0:T(8,128)(2,1)}, bf16[512,256]{1,0:T(8,128)(2,1)S(1)}, u32[]{:S(2)}, u32[]{:S(2)}) %collective-permute-start.5) | collective-permute-done | bytes 262176 | tf_op jit(solution)/shard_map/ppermute | solution.py:371
  42.8 5.1 %anchor_attention.3 = (bf16[512,2048]{1,0:T(8,128)(2,1)}, f32[8,128]{1,0:T(8,128)S(1)}) custom-call(s32[1]{0:T(128)} %bitcast.blk_ref, bf16[512,2048]{1,0:T(8,128)(2,1)S(1)} %copy-done.1, f32[512,1024]{1,0:T(8,128)S(1)} %get-tuple-element.51.acc_ref, f32[512,1024]{1,0:T(8,128)S(1)} %get-tuple-element.52.top_ref, ...), custom_call_target="tpu_custom_call", output_to_operand_aliasing={{0}: (8, {})} | custom-call | flops 1 | bytes 1 | tf_op jit(solution)/shard_map/anchor_attention/pallas_call | solution.py:200
  47.9 1.0 %merge.3 = bf16[32,2048]{1,0:T(8,128)(2,1)} custom-call(bf16[32,2176]{1,0:T(8,128)(2,1)S(1)} %get-tuple-element.67.a, bf16[32,2176]{1,0:T(8,128)(2,1)S(1)} %collective-permute-done.10.b, f32[8,128]{1,0:T(8,128)S(1)} %get-tuple-element.69.after), custom_call_target="tpu_custom_call" | custom-call | flops 1 | bytes 1 | tf_op jit(solution)/shard_map/merge/pallas_call | solution.py:331
  (18 shorter events, 0.0 us)
Async XLA Ops:
  0.6 14.1 %collective-permute-start.2 = (bf16[16,2048]{1,0:T(8,128)(2,1)}, bf16[16,2048]{1,0:T(8,128)(2,1)S(1)}, u32[]{:S(2)}, u32[]{:S(2)}) collective-permute-start(bf16[16,2048]{1,0:T(8,128)(2,1)} %refs_3_.1), channel_id=1, source_target_pairs={{0,4},{4,0},{8,12},{12,8},{1,5},{5,1},{9,13},{13,9},{2,6},{6,2},{1... | collective-permute-start | bytes 196616 | tf_op jit(solution)/shard_map/ppermute | solution.py:343
  1.1 13.6 %collective-permute-start.4 = (bf16[16,2048]{1,0:T(8,128)(2,1)}, bf16[16,2048]{1,0:T(8,128)(2,1)S(1)}, u32[]{:S(2)}, u32[]{:S(2)}) collective-permute-start(bf16[16,2048]{1,0:T(8,128)(2,1)} %refs_3_.1), channel_id=1, source_target_pairs={{0,12},{4,8},{8,4},{12,0},{1,13},{5,9},{9,5},{13,1},{2,14},{6,10},... | collective-permute-start | bytes 196616 | tf_op jit(solution)/shard_map/ppermute | solution.py:343
  3.9 10.9 %collective-permute-start.3 = (bf16[16,2048]{1,0:T(8,128)(2,1)}, bf16[16,2048]{1,0:T(8,128)(2,1)S(1)}, u32[]{:S(2)}, u32[]{:S(2)}) collective-permute-start(bf16[16,2048]{1,0:T(8,128)(2,1)} %refs_3_.1), channel_id=1, source_target_pairs={{0,8},{4,12},{8,0},{12,4},{1,9},{5,13},{9,1},{13,5},{2,10},{6,14},... | collective-permute-start | bytes 196616 | tf_op jit(solution)/shard_map/ppermute | solution.py:343
  7.8 4.3 %copy-start = (bf16[512,2048]{1,0:T(8,128)(2,1)}, bf16[512,2048]{1,0:T(8,128)(2,1)S(1)}, u32[]{:S(2)}) copy-start(bf16[512,2048]{1,0:T(8,128)(2,1)S(1)} %get-tuple-element.36.q_ref) | copy-start | bytes 6291460
  7.8 20.5 %collective-permute-start = (bf16[512,256]{1,0:T(8,128)(2,1)}, bf16[512,256]{1,0:T(8,128)(2,1)}, u32[]{:S(2)}, u32[]{:S(2)}) collective-permute-start(bf16[512,256]{1,0:T(8,128)(2,1)} %get-tuple-element.47.refs_1_.kv_ref), channel_id=1, source_target_pairs={{0,8},{1,9},{2,10},{3,11},{16,24},{17,25},{18,26},{19,27}} | collective-permute-start | bytes 786440 | tf_op jit(solution)/shard_map/ppermute | solution.py:366
  9.2 13.7 %collective-permute-start.1 = (bf16[512,256]{1,0:T(8,128)(2,1)S(1)}, bf16[512,256]{1,0:T(8,128)(2,1)S(1)}, u32[]{:S(2)}, u32[]{:S(2)}) collective-permute-start(bf16[512,256]{1,0:T(8,128)(2,1)S(1)} %get-tuple-element.38.kv_ref.refs_0_), channel_id=1, source_target_pairs={{0,8},{1,9},{2,10},{3,11},{16,24},{17,25},{18,26},{19,27}} | collective-permute-start | bytes 786440 | tf_op jit(solution)/shard_map/ppermute | solution.py:366
  12.1 1.3 %copy-start.2 = (f32[512,1024]{1,0:T(8,128)}, f32[512,1024]{1,0:T(8,128)S(1)}, u32[]{:S(2)}) copy-start(f32[512,1024]{1,0:T(8,128)S(1)} %get-tuple-element.55.acc_ref) | copy-start | bytes 6291460
  13.5 1.3 %copy-start.4 = (f32[512,1024]{1,0:T(8,128)}, f32[512,1024]{1,0:T(8,128)S(1)}, u32[]{:S(2)}) copy-start(f32[512,1024]{1,0:T(8,128)S(1)} %get-tuple-element.57.sum_ref) | copy-start | bytes 6291460
  14.8 10.4 %copy-start.1 = (bf16[512,2048]{1,0:T(8,128)(2,1)S(1)}, bf16[512,2048]{1,0:T(8,128)(2,1)}, u32[]{:S(2)}) copy-start(bf16[512,2048]{1,0:T(8,128)(2,1)} %copy-done) | copy-start | bytes 6291460
  17.9 20.4 %collective-permute-start.9 = (bf16[64,2176]{1,0:T(8,128)(2,1)S(1)}, bf16[64,2176]{1,0:T(8,128)(2,1)S(1)}, u32[]{:S(2)}, u32[]{:S(2)}) collective-permute-start(bf16[64,2176]{1,0:T(8,128)(2,1)S(1)} %get-tuple-element.65), channel_id=1, source_target_pairs={{0,4},{4,0},{8,12},{12,8},{1,5},{5,1},{9,13},{13,9},{2,6},{6,2},{1... | collective-permute-start | bytes 835592 | tf_op jit(solution)/shard_map/ppermute | solution.py:343
  22.9 11.4 %copy-start.3 = (f32[512,1024]{1,0:T(8,128)S(1)}, f32[512,1024]{1,0:T(8,128)}, u32[]{:S(2)}) copy-start(f32[512,1024]{1,0:T(8,128)} %copy-done.2) | copy-start | bytes 6291460
  22.9 11.4 %copy-start.5 = (f32[512,1024]{1,0:T(8,128)S(1)}, f32[512,1024]{1,0:T(8,128)}, u32[]{:S(2)}) copy-start(f32[512,1024]{1,0:T(8,128)} %copy-done.4) | copy-start | bytes 6291460
  22.9 7.5 %collective-permute-start.8 = (bf16[512,256]{1,0:T(8,128)(2,1)S(1)}, bf16[512,256]{1,0:T(8,128)(2,1)S(1)}, u32[]{:S(2)}, u32[]{:S(2)}) collective-permute-start(bf16[512,256]{1,0:T(8,128)(2,1)S(1)} %collective-permute-done.1.refs_0_), channel_id=1, source_target_pairs={{8,12},{9,13},{10,14},{11,15},{24,28},{25,29},{26,30},{27,31}} | collective-permute-start | bytes 786440 | tf_op jit(solution)/shard_map/ppermute | solution.py:371
  23.7 10.6 %collective-permute-start.7 = (bf16[512,256]{1,0:T(8,128)(2,1)S(1)}, bf16[512,256]{1,0:T(8,128)(2,1)S(1)}, u32[]{:S(2)}, u32[]{:S(2)}) collective-permute-start(bf16[512,256]{1,0:T(8,128)(2,1)S(1)} %collective-permute-done.1.refs_0_), channel_id=1, source_target_pairs={{8,4},{9,5},{10,6},{11,7},{24,20},{25,21},{26,22},{27,23}} | collective-permute-start | bytes 786440 | tf_op jit(solution)/shard_map/ppermute | solution.py:371
  28.4 10.8 %collective-permute-start.6 = (bf16[512,256]{1,0:T(8,128)(2,1)}, bf16[512,256]{1,0:T(8,128)(2,1)S(1)}, u32[]{:S(2)}, u32[]{:S(2)}) collective-permute-start(bf16[512,256]{1,0:T(8,128)(2,1)} %collective-permute-done.refs_0_), channel_id=1, source_target_pairs={{8,12},{9,13},{10,14},{11,15},{24,28},{25,29},{26,30},{27,31}} | collective-permute-start | bytes 786440 | tf_op jit(solution)/shard_map/ppermute | solution.py:371
  29.1 13.7 %collective-permute-start.5 = (bf16[512,256]{1,0:T(8,128)(2,1)}, bf16[512,256]{1,0:T(8,128)(2,1)S(1)}, u32[]{:S(2)}, u32[]{:S(2)}) collective-permute-start(bf16[512,256]{1,0:T(8,128)(2,1)} %collective-permute-done.refs_0_), channel_id=1, source_target_pairs={{8,4},{9,5},{10,6},{11,7},{24,20},{25,21},{26,22},{27,23}} | collective-permute-start | bytes 786440 | tf_op jit(solution)/shard_map/ppermute | solution.py:371
  38.9 9.0 %collective-permute-start.10 = (bf16[32,2176]{1,0:T(8,128)(2,1)S(1)}, bf16[32,2176]{1,0:T(8,128)(2,1)S(1)}, u32[]{:S(2)}, u32[]{:S(2)}) collective-permute-start(bf16[32,2176]{1,0:T(8,128)(2,1)S(1)} %get-tuple-element.68), channel_id=1, source_target_pairs={{0,8},{4,12},{8,0},{12,4},{1,9},{5,13},{9,1},{13,5},{2,10},{6,14},... | collective-permute-start | bytes 417800 | tf_op jit(solution)/shard_map/ppermute | solution.py:343

commit v6 on v5

--- a/solution.py
+++ b/solution.py
@@ -42,15 +42,7 @@
     return functools.reduce(op, items)
 
 
-def prep_kernel(heads, k_ref, v_ref, *refs):
-    smalls = (len(refs) - heads - 1) // 2
-    small_in, kv = refs[:smalls], refs[smalls : smalls + heads]
-    small_out, sem = refs[smalls + heads : -1], refs[-1]
-    copies = []
-    for g in range(heads):
-        for ref, at in ((k_ref, 0), (v_ref, HD)):
-            copies.append((ref.at[:, g * HD : (g + 1) * HD], kv[g].at[:, at : at + HD]))
-    copies += list(zip(small_in, small_out))
+def copy_all(copies, sem):
     started = [pltpu.make_async_copy(a, b, sem.at[i]) for i, (a, b) in enumerate(copies)]
     for copy in started:
         copy.start()
@@ -58,19 +50,33 @@
         copy.wait()
 
 
-def prep(key, value, smalls):
+def in_hbm(x):
+    return pltpu.with_memory_space_constraint(x, pltpu.HBM)
+
+
+def gather_kernel(heads, k_ref, v_ref, *refs):
+    others = (len(refs) - heads - 1) // 2
+    plain, kv, outs, sem = refs[:others], refs[others : others + heads], refs[others + heads : -1], refs[-1]
+    copies = []
+    for g in range(heads):
+        for ref, at in ((k_ref, 0), (v_ref, HD)):
+            copies.append((ref.at[:, g * HD : (g + 1) * HD], kv[g].at[:, at : at + HD]))
+    copy_all(copies + list(zip(plain, outs)), sem)
+
+
+def gather(key, value, others, name):
     rows, heads = key.shape[0], key.shape[1] // HD
+    shapes = [((rows, 2 * HD), key.dtype)] * heads + [(x.shape, x.dtype) for x in others]
     outs = pl.pallas_call(
-        functools.partial(prep_kernel, heads),
-        out_shape=[jax.ShapeDtypeStruct((rows, 2 * HD), key.dtype)] * heads
-        + [jax.ShapeDtypeStruct(s.shape, s.dtype) for s in smalls],
-        in_specs=[HBM] * (2 + len(smalls)),
-        out_specs=[VMEM] * (heads + len(smalls)),
-        scratch_shapes=[pltpu.SemaphoreType.DMA((2 * heads + len(smalls),))],
-        compiler_params=params(16),
+        functools.partial(gather_kernel, heads),
+        out_shape=[pltpu.VMEM(*x) if others else jax.ShapeDtypeStruct(*x) for x in shapes],
+        in_specs=[HBM] * (2 + len(others)),
+        out_specs=[VMEM if others else ANY] * len(shapes),
+        scratch_shapes=[pltpu.SemaphoreType.DMA((2 * heads + len(others),))],
+        compiler_params=params(2),
         cost_estimate=BRIEF,
-        name="prep",
-    )(*[pltpu.with_memory_space_constraint(x, pltpu.HBM) for x in (key, value, *smalls)])
+        name=name,
+    )(*[in_hbm(x) for x in (key, value, *others)])
     return list(outs[:heads]), list(outs[heads:])
 
 
@@ -123,11 +129,11 @@
     rows = query.shape[0]
     return pl.pallas_call(
         functools.partial(local_kernel, g),
-        out_shape=[jax.ShapeDtypeStruct((rows, GROUP * HD), jnp.float32)] * 3,
+        out_shape=[pltpu.VMEM((rows, GROUP * HD), jnp.float32)] * 3,
         in_specs=[VMEM] * 2,
         out_specs=[VMEM] * 3,
         scratch_shapes=[pltpu.VMEM((rows, 2 * HD), jnp.bfloat16)],
-        compiler_params=params(16),
+        compiler_params=params(6),
         cost_estimate=LONG,
         name="local_attention",
     )(query, kv)
@@ -149,8 +155,8 @@
     if count == 1:
         take(cand[0])
     else:
-        pl.when(blk == 1)(lambda: take(cand[1]))
-        pl.when(blk == 2)(lambda: take(cand[0]))
+        pl.when(blk == 1)(lambda: take(cand[0]))
+        pl.when(blk == 2)(lambda: take(cand[1]))
         pl.when(blk == 3)(lambda: take(cand[2]))
 
     def scores(h):
@@ -209,7 +215,7 @@
             pltpu.SemaphoreType.DMA((GROUP,)),
         ],
         input_output_aliases=alias,
-        compiler_params=params(16),
+        compiler_params=params(6),
         cost_estimate=BRIEF,
         name="anchor_attention",
     )(*args)
@@ -289,8 +295,8 @@
             pltpu.VMEM((options, heads * HD), jnp.bfloat16),
             pltpu.VMEM((options, width), jnp.bfloat16),
         ],
-        compiler_params=params(16),
-        cost_estimate=BRIEF,
+        compiler_params=params(4 + options // 32),
+        cost_estimate=LONG,
         name="option_partials",
     )(blk, owner, slot, length, *kvs, *queries, after)
 
@@ -333,7 +339,7 @@
         out_shape=shapes,
         in_specs=[VMEM] * 2 + [ANY],
         out_specs=[VMEM] * len(shapes),
-        compiler_params=params(16),
+        compiler_params=params(6),
         cost_estimate=BRIEF,
         name="merge",
     )(a, b, after)
@@ -354,24 +360,33 @@
     options = opt_owner.shape[0]
     rounds = n.bit_length() - 1
 
+    hold = lax.optimization_barrier
+    row = lambda x: x.reshape(1, options)
+
     queries = [opt_query] + [swap(opt_query, n, mask) for mask in range(1, n)]
-    row = lambda x: x.reshape(1, options)
-    kvs, smalls = prep(ctx_key, ctx_value, [row(opt_owner), row(opt_slot), row(opt_length), opt_query, ctx_query])
-    queries[0], ctx_query = smalls[3:]
-
-    hold = lax.optimization_barrier
+    sent, _ = gather(ctx_key, ctx_value, [], "anchor_parts")
+    if n == 4:
+        on = lambda x: lax.ppermute(x, "blk", [(0, 2), (2, 1), (1, 0), (3, 3)])
+        up = lambda x: lax.ppermute(x, "blk", [(2, 3), (3, 2), (0, 0), (1, 1)])
+        got = on(sent[0])
+    plain = [row(opt_owner), row(opt_slot), row(opt_length), opt_query, ctx_query]
+    kvs, (*smalls, queries[0], ctx_query) = gather(ctx_key, ctx_value, plain, "load")
+
     states = [local_attention(ctx_query, kvs[0], 0)]
-    keep, send = option_partials(blk_arr, *smalls[:3], kvs, queries, states[0][1])
+    keep, send = option_partials(blk_arr, *smalls, kvs, queries, states[0][1])
     if n == 4:
-        first = [lax.ppermute(kv, "blk", [(0, 2)]) for kv in kvs]
-        first[0], keep, kvs[1:] = hold((first[0], keep, kvs[1:]))
-    states += [local_attention(ctx_query, kv, g) for g, kv in enumerate(kvs) if g]
-    if n == 4:
-        first[1:], states = hold((first[1:], states))
-        anchors = [[x, lax.ppermute(x, "blk", [(2, 1)]), lax.ppermute(x, "blk", [(2, 3)])] for x in first]
-        anchors[0], first[1:] = hold((anchors[0], first[1:]))
+        anchors = []
+        got, keep, kvs[1:] = hold((got, keep, kvs[1:]))
+        for g in range(len(kvs)):
+            after = on(jnp.where(blk == 0, sent[g + 1], got) if g + 1 < len(kvs) else got)
+            anchors.append([after, got, up(got)])
+            if g + 1 < len(kvs):
+                states.append(local_attention(ctx_query, kvs[g + 1], g + 1))
+                after, states = hold((after, states))
+            got = after
     else:
-        anchors = [[from_root(kv, blk)] for kv in kvs]
+        states += [local_attention(ctx_query, kv, g) for g, kv in enumerate(kvs) if g]
+        anchors = [[from_root(kv, blk)] for kv in sent]
     ctx_out, tokens = None, []
     for g, state in enumerate(states):
         ctx_out, token = anchor_attention(blk_arr, ctx_query, state, anchors[g], g, ctx_out)

time: 49.5 us -> 63.9 us (1.29)
  the two profiles are of different devices: /device:TPU:12 before, /device:TPU:0 now
where the time goes in v6:
time: 63.9 us; the launch traced here: 63.5 us
  starting transfers between devices  29 us (45%)
  Pallas kernels  22.6 us (35%)
  waiting for transfers between devices  5.59 us (9%)
  local copies, waits for them, and re-layouts  5.56 us (9%)
  between operations  0.81 us (1%)
    ppermute x3, starting transfers between devices, body(): on = lambda x: lax.ppermute(x, 'blk', [(0, 2), (2, 1), (1, 0), (3, 3)])  16.6 us
    pallas_call x2, Pallas kernels, gather(): pl.pallas_call(functools.partial(gather_kernel, heads), out_shape=[pltpu....  11.1 us
    ppermute x5, starting transfers between devices, swap(): return lax.ppermute(x, 'blk', [(i, i ^ mask) for i in range(n)])  10.1 us
    unnamed x14, local copies, waits for them, and re-layouts  5.56 us
    pallas_call x2, Pallas kernels, local_attention(): pl.pallas_call(functools.partial(local_kernel, g), out_shape=[pltpu.VMEM(...  4.44 us
    pallas_call x2, Pallas kernels, anchor_attention(): pl.pallas_call(functools.partial(anchor_kernel, g, len(cands), len(alias)...  3.43 us
    ppermute x5, waiting for transfers between devices, swap(): return lax.ppermute(x, 'blk', [(i, i ^ mask) for i in range(n)])  3.37 us
    ppermute x2, starting transfers between devices, body(): up = lambda x: lax.ppermute(x, 'blk', [(2, 3), (3, 2), (0, 0), (1, 1)])  2.27 us
  transfers between devices with their start and end apart: 10, of which 2 were waited for; matrix products, arithmetic and copies ran while one was open for 0% of the time, Pallas kernels for 34%

profile of v6, /device:TPU:0, one launch (start us, length us, event | category | flops | bytes accessed | tf_op | source)
XLA Modules:
  0.0 63.5 jit_solution(1682610076113660122)
XLA Ops:
  0.6 3.1 %collective-permute-start.1 = (bf16[16,2048]{1,0:T(8,128)(2,1)}, bf16[16,2048]{1,0:T(8,128)(2,1)S(1)}, u32[]{:S(2)}, u32[]{:S(2)}) collective-permute-start(bf16[16,2048]{1,0:T(8,128)(2,1)} %refs_3_.1), channel_id=1, source_target_pairs={{0,4},{4,0},{8,12},{12,8},{1,5},{5,1},{9,13},{13,9},{2,6},{6,2},{1... | collective-permute-start | bytes 196616 | tf_op jit(solution)/shard_map/ppermute | solution.py:349
  3.7 2.6 %collective-permute-start.2 = (bf16[16,2048]{1,0:T(8,128)(2,1)}, bf16[16,2048]{1,0:T(8,128)(2,1)S(1)}, u32[]{:S(2)}, u32[]{:S(2)}) collective-permute-start(bf16[16,2048]{1,0:T(8,128)(2,1)} %refs_3_.1), channel_id=1, source_target_pairs={{0,8},{4,12},{8,0},{12,4},{1,9},{5,13},{9,1},{13,5},{2,10},{6,14},... | collective-permute-start | bytes 196616 | tf_op jit(solution)/shard_map/ppermute | solution.py:349
  6.3 9.1 %anchor_parts.1 = (bf16[512,256]{1,0:T(8,128)(2,1)}, bf16[512,256]{1,0:T(8,128)(2,1)S(1)}) custom-call(bf16[512,256]{1,0:T(8,128)(2,1)} %k_ref.3, bf16[512,256]{1,0:T(8,128)(2,1)} %v_ref.3), custom_call_target="tpu_custom_call" | custom-call | flops 1 | bytes 1 | tf_op jit(solution)/shard_map/anchor_parts/pallas_call | solution.py:70
  15.4 3.8 %collective-permute-start = (bf16[512,256]{1,0:T(8,128)(2,1)}, bf16[512,256]{1,0:T(8,128)(2,1)}, u32[]{:S(2)}, u32[]{:S(2)}) collective-permute-start(bf16[512,256]{1,0:T(8,128)(2,1)} %get-tuple-element.37), channel_id=1, source_target_pairs={{0,8},{8,4},{4,0},{12,12},{1,9},{9,5},{5,1},{13,13},{2,10},{10,6},... | collective-permute-start | bytes 786440 | tf_op jit(solution)/shard_map/ppermute | solution.py:369
  19.2 2.0 %load.1 = (bf16[512,256]{1,0:T(8,128)(2,1)S(1)}, bf16[512,256]{1,0:T(8,128)(2,1)S(1)}, s32[1,64]{1,0:T(1,128)S(1)}, s32[1,64]{1,0:T(1,128)S(1)}, s32[1,64]{1,0:T...) custom-call(bf16[512,256]{1,0:T(8,128)(2,1)} %k_ref.3, bf16[512,256]{1,0:T(8,128)(2,1)} %v_ref.3, ...), custom_call_target="tpu_custom_call" | custom-call | flops 1 | bytes 1 | tf_op jit(solution)/shard_map/load/pallas_call | solution.py:70
  21.3 2.2 %local_attention.2 = (f32[512,1024]{1,0:T(8,128)S(1)}, f32[512,1024]{1,0:T(8,128)S(1)}, f32[512,1024]{1,0:T(8,128)S(1)}) custom-call(bf16[512,2048]{1,0:T(8,128)(2,1)S(1)} %get-tuple-element.35.q_ref, bf16[512,256]{1,0:T(8,128)(2,1)S(1)} %get-tuple-element.41.kv_ref.refs_0_), custom_call_target="tpu_custom_call" | custom-call | flops 99999997952 | bytes 1 | tf_op jit(solution)/shard_map/local_attention/pallas_call | solution.py:130
  23.5 1.3 %copy-done = f32[512,1024]{1,0:T(8,128)} copy-done((f32[512,1024]{1,0:T(8,128)}, f32[512,1024]{1,0:T(8,128)S(1)}, u32[]{:S(2)}) %copy-start) | copy-done | bytes 2097176
  24.8 1.3 %copy-done.2 = f32[512,1024]{1,0:T(8,128)} copy-done((f32[512,1024]{1,0:T(8,128)}, f32[512,1024]{1,0:T(8,128)S(1)}, u32[]{:S(2)}) %copy-start.2) | copy-done | bytes 2097176
  26.2 1.3 %copy-done.5 = f32[512,1024]{1,0:T(8,128)} copy-done((f32[512,1024]{1,0:T(8,128)}, f32[512,1024]{1,0:T(8,128)S(1)}, u32[]{:S(2)}) %copy-start.5) | copy-done | bytes 2097176
  27.5 1.6 %copy-done.3 = f32[512,1024]{1,0:T(8,128)S(1)} copy-done((f32[512,1024]{1,0:T(8,128)S(1)}, f32[512,1024]{1,0:T(8,128)}, u32[]{:S(2)}) %copy-start.3) | copy-done | bytes 2097176
  29.1 2.0 %option_partials.1 = (bf16[64,2176]{1,0:T(8,128)(2,1)S(1)}, bf16[64,2176]{1,0:T(8,128)(2,1)S(1)}) custom-call(s32[1]{0:T(128)} %bitcast.blk_ref, s32[1,64]{1,0:T(1,128)S(1)} %get-tuple-element.38.owner_ref, s32[1,64]{1,0:T(1,128)S(1)} %get-tuple-element.39.slot_ref, s32[1,64]{1,0:T(1,128)S(1)} %get-tuple-element.40.length_ref, ...), custom_call_target="tpu_custom_call" | custom-call | flops 99999997952 | bytes 1 | tf_op jit(solution)/shard_map/option_partials/pallas_call | solution.py:289
  31.1 0.2 collective-permute-start.8
  31.3 1.6 %collective-permute-start.7 = (bf16[512,256]{1,0:T(8,128)(2,1)}, bf16[512,256]{1,0:T(8,128)(2,1)S(1)}, u32[]{:S(2)}, u32[]{:S(2)}) collective-permute-start(bf16[512,256]{1,0:T(8,128)(2,1)} %collective-permute-done.refs_1_), channel_id=1, source_target_pairs={{8,12},{12,8},{0,0},{4,4},{9,13},{13,9},{1,1},{5,5},{10,14},{14,10... | collective-permute-start | bytes 786440 | tf_op jit(solution)/shard_map/ppermute | solution.py:370
  33.0 7.5 %collective-permute-start.4 = (bf16[512,256]{1,0:T(8,128)(2,1)S(1)}, bf16[512,256]{1,0:T(8,128)(2,1)S(1)}, u32[]{:S(2)}, u32[]{:S(2)}) collective-permute-start(bf16[512,256]{1,0:T(8,128)(2,1)S(1)} %broadcast_select_fusion), channel_id=1, source_target_pairs={{0,8},{8,4},{4,0},{12,12},{1,9},{9,5},{5,1},{13,13},{2,10},{10,6},... | collective-permute-start | bytes 786440 | tf_op jit(solution)/shard_map/ppermute | solution.py:369
  40.5 2.2 %local_attention.3 = (f32[512,1024]{1,0:T(8,128)S(1)}, f32[512,1024]{1,0:T(8,128)S(1)}, f32[512,1024]{1,0:T(8,128)S(1)}) custom-call(bf16[512,2048]{1,0:T(8,128)(2,1)S(1)} %get-tuple-element.35.q_ref, bf16[512,256]{1,0:T(8,128)(2,1)S(1)} %get-tuple-element.49.refs_1_.kv_ref), custom_call_target="tpu_custom_call" | custom-call | flops 99999997952 | bytes 1 | tf_op jit(solution)/shard_map/local_attention/pallas_call | solution.py:130
  42.7 2.2 %collective-permute-done.4.refs_0_.refs_1_ = bf16[512,256]{1,0:T(8,128)(2,1)S(1)} collective-permute-done((bf16[512,256]{1,0:T(8,128)(2,1)S(1)}, bf16[512,256]{1,0:T(8,128)(2,1)S(1)}, u32[]{:S(2)}, u32[]{:S(2)}) %collective-permute-start.4) | collective-permute-done | bytes 262176 | tf_op jit(solution)/shard_map/ppermute | solution.py:369
  44.9 5.3 %collective-permute-start.5 = (bf16[512,256]{1,0:T(8,128)(2,1)S(1)}, bf16[512,256]{1,0:T(8,128)(2,1)S(1)}, u32[]{:S(2)}, u32[]{:S(2)}) collective-permute-start(bf16[512,256]{1,0:T(8,128)(2,1)S(1)} %collective-permute-done.4.refs_0_.refs_1_), channel_id=1, source_target_pairs={{0,8},{8,4},{4,0},{12,12},{1,9},{9,5},{5,1},{13,13},{2,10},{10,6},... | collective-permute-start | bytes 786440 | tf_op jit(solution)/shard_map/ppermute | solution.py:369
  50.2 0.7 %collective-permute-start.6 = (bf16[512,256]{1,0:T(8,128)(2,1)S(1)}, bf16[512,256]{1,0:T(8,128)(2,1)S(1)}, u32[]{:S(2)}, u32[]{:S(2)}) collective-permute-start(bf16[512,256]{1,0:T(8,128)(2,1)S(1)} %collective-permute-done.4.refs_0_.refs_1_), channel_id=1, source_target_pairs={{8,12},{12,8},{0,0},{4,4},{9,13},{13,9},{1,1},{5,5},{10,14},{14,10... | collective-permute-start | bytes 786440 | tf_op jit(solution)/shard_map/ppermute | solution.py:370
  50.9 2.2 %anchor_attention.2 = (bf16[512,2048]{1,0:T(8,128)(2,1)}, f32[8,128]{1,0:T(8,128)S(1)}) custom-call(s32[1]{0:T(128)} %bitcast.blk_ref, bf16[512,2048]{1,0:T(8,128)(2,1)S(1)} %get-tuple-element.35.q_ref, f32[512,1024]{1,0:T(8,128)S(1)} %copy-done.1, f32[512,1024]{1,0:T(8,128)S(1)} %copy-done.4, f32[512,1024]{1,0:T(8,128)S(1)} %copy-done.6, ...), custom_call_target="tpu_custom_call" | custom-call | flops 1 | bytes 1 | tf_op jit(solution)/shard_map/anchor_attention/pallas_call | solution.py:206
  53.1 0.6 merge.2
  53.7 4.2 %collective-permute-start.9 = (bf16[32,2176]{1,0:T(8,128)(2,1)S(1)}, bf16[32,2176]{1,0:T(8,128)(2,1)S(1)}, u32[]{:S(2)}, u32[]{:S(2)}) collective-permute-start(bf16[32,2176]{1,0:T(8,128)(2,1)S(1)} %get-tuple-element.66), channel_id=1, source_target_pairs={{0,8},{4,12},{8,0},{12,4},{1,9},{5,13},{9,1},{13,5},{2,10},{6,14},... | collective-permute-start | bytes 417800 | tf_op jit(solution)/shard_map/ppermute | solution.py:349
  57.9 1.2 %anchor_attention.3 = (bf16[512,2048]{1,0:T(8,128)(2,1)}, f32[8,128]{1,0:T(8,128)S(1)}) custom-call(s32[1]{0:T(128)} %bitcast.blk_ref, bf16[512,2048]{1,0:T(8,128)(2,1)S(1)} %get-tuple-element.35.q_ref, f32[512,1024]{1,0:T(8,128)S(1)} %get-tuple-element.53.acc_ref, f32[512,1024]{1,0:T(8,128)S(1)} %get-tuple-element.54.top_ref, ...), custom_call_target="tpu_custom_call", output_to_operand_aliasing={{0}: (8, {})} | custom-call | flops 1 | bytes 1 | tf_op jit(solution)/shard_map/anchor_attention/pallas_call | solution.py:206
  59.2 3.4 %collective-permute-done.9.b = bf16[32,2176]{1,0:T(8,128)(2,1)S(1)} collective-permute-done((bf16[32,2176]{1,0:T(8,128)(2,1)S(1)}, bf16[32,2176]{1,0:T(8,128)(2,1)S(1)}, u32[]{:S(2)}, u32[]{:S(2)}) %collective-permute-start.9) | collective-permute-done | bytes 139296 | tf_op jit(solution)/shard_map/ppermute | solution.py:349
  62.5 1.0 %merge.3 = bf16[32,2048]{1,0:T(8,128)(2,1)} custom-call(bf16[32,2176]{1,0:T(8,128)(2,1)S(1)} %get-tuple-element.65.a, bf16[32,2176]{1,0:T(8,128)(2,1)S(1)} %collective-permute-done.9.b, f32[8,128]{1,0:T(8,128)S(1)} %get-tuple-element.67.after), custom_call_target="tpu_custom_call" | custom-call | flops 1 | bytes 1 | tf_op jit(solution)/shard_map/merge/pallas_call | solution.py:337
  (20 shorter events, 0.1 us)
Async XLA Ops:
  0.6 26.8 %collective-permute-start.1 = (bf16[16,2048]{1,0:T(8,128)(2,1)}, bf16[16,2048]{1,0:T(8,128)(2,1)S(1)}, u32[]{:S(2)}, u32[]{:S(2)}) collective-permute-start(bf16[16,2048]{1,0:T(8,128)(2,1)} %refs_3_.1), channel_id=1, source_target_pairs={{0,4},{4,0},{8,12},{12,8},{1,5},{5,1},{9,13},{13,9},{2,6},{6,2},{1... | collective-permute-start | bytes 196616 | tf_op jit(solution)/shard_map/ppermute | solution.py:349
  3.7 23.8 %collective-permute-start.2 = (bf16[16,2048]{1,0:T(8,128)(2,1)}, bf16[16,2048]{1,0:T(8,128)(2,1)S(1)}, u32[]{:S(2)}, u32[]{:S(2)}) collective-permute-start(bf16[16,2048]{1,0:T(8,128)(2,1)} %refs_3_.1), channel_id=1, source_target_pairs={{0,8},{4,12},{8,0},{12,4},{1,9},{5,13},{9,1},{13,5},{2,10},{6,14},... | collective-permute-start | bytes 196616 | tf_op jit(solution)/shard_map/ppermute | solution.py:349
  6.3 21.2 %collective-permute-start.3 = (bf16[16,2048]{1,0:T(8,128)(2,1)}, bf16[16,2048]{1,0:T(8,128)(2,1)S(1)}, u32[]{:S(2)}, u32[]{:S(2)}) collective-permute-start(bf16[16,2048]{1,0:T(8,128)(2,1)} %refs_3_.1), channel_id=1, source_target_pairs={{0,12},{4,8},{8,4},{12,0},{1,13},{5,9},{9,5},{13,1},{2,14},{6,10},... | collective-permute-start | bytes 196616 | tf_op jit(solution)/shard_map/ppermute | solution.py:349
  15.4 15.9 %collective-permute-start = (bf16[512,256]{1,0:T(8,128)(2,1)}, bf16[512,256]{1,0:T(8,128)(2,1)}, u32[]{:S(2)}, u32[]{:S(2)}) collective-permute-start(bf16[512,256]{1,0:T(8,128)(2,1)} %get-tuple-element.37), channel_id=1, source_target_pairs={{0,8},{8,4},{4,0},{12,12},{1,9},{9,5},{5,1},{13,13},{2,10},{10,6},... | collective-permute-start | bytes 786440 | tf_op jit(solution)/shard_map/ppermute | solution.py:369
  23.5 1.3 %copy-start = (f32[512,1024]{1,0:T(8,128)}, f32[512,1024]{1,0:T(8,128)S(1)}, u32[]{:S(2)}) copy-start(f32[512,1024]{1,0:T(8,128)S(1)} %get-tuple-element.57.acc_ref) | copy-start | bytes 6291460
  24.8 1.3 %copy-start.2 = (f32[512,1024]{1,0:T(8,128)}, f32[512,1024]{1,0:T(8,128)S(1)}, u32[]{:S(2)}) copy-start(f32[512,1024]{1,0:T(8,128)S(1)} %get-tuple-element.58.refs_6_.top_ref) | copy-start | bytes 6291460
  26.2 1.3 %copy-start.5 = (f32[512,1024]{1,0:T(8,128)}, f32[512,1024]{1,0:T(8,128)S(1)}, u32[]{:S(2)}) copy-start(f32[512,1024]{1,0:T(8,128)S(1)} %get-tuple-element.59.sum_ref) | copy-start | bytes 6291460
  27.5 1.6 %copy-start.3 = (f32[512,1024]{1,0:T(8,128)S(1)}, f32[512,1024]{1,0:T(8,128)}, u32[]{:S(2)}) copy-start(f32[512,1024]{1,0:T(8,128)} %copy-done.2) | copy-start | bytes 6291460
  31.1 22.0 %collective-permute-start.8 = (bf16[64,2176]{1,0:T(8,128)(2,1)S(1)}, bf16[64,2176]{1,0:T(8,128)(2,1)S(1)}, u32[]{:S(2)}, u32[]{:S(2)}) collective-permute-start(bf16[64,2176]{1,0:T(8,128)(2,1)S(1)} %get-tuple-element.63), channel_id=1, source_target_pairs={{0,4},{4,0},{8,12},{12,8},{1,5},{5,1},{9,13},{13,9},{2,6},{6,2},{1... | collective-permute-start | bytes 835592 | tf_op jit(solution)/shard_map/ppermute | solution.py:349
  31.3 19.6 %collective-permute-start.7 = (bf16[512,256]{1,0:T(8,128)(2,1)}, bf16[512,256]{1,0:T(8,128)(2,1)S(1)}, u32[]{:S(2)}, u32[]{:S(2)}) collective-permute-start(bf16[512,256]{1,0:T(8,128)(2,1)} %collective-permute-done.refs_1_), channel_id=1, source_target_pairs={{8,12},{12,8},{0,0},{4,4},{9,13},{13,9},{1,1},{5,5},{10,14},{14,10... | collective-permute-start | bytes 786440 | tf_op jit(solution)/shard_map/ppermute | solution.py:370
  32.9 18.0 %copy-start.1 = (f32[512,1024]{1,0:T(8,128)S(1)}, f32[512,1024]{1,0:T(8,128)}, u32[]{:S(2)}) copy-start(f32[512,1024]{1,0:T(8,128)} %copy-done) | copy-start | bytes 6291460
  32.9 18.0 %copy-start.4 = (f32[512,1024]{1,0:T(8,128)S(1)}, f32[512,1024]{1,0:T(8,128)}, u32[]{:S(2)}) copy-start(f32[512,1024]{1,0:T(8,128)} %copy-done.2) | copy-start | bytes 6291460
  32.9 18.0 %copy-start.6 = (f32[512,1024]{1,0:T(8,128)S(1)}, f32[512,1024]{1,0:T(8,128)}, u32[]{:S(2)}) copy-start(f32[512,1024]{1,0:T(8,128)} %copy-done.5) | copy-start | bytes 6291460
  33.0 11.9 %collective-permute-start.4 = (bf16[512,256]{1,0:T(8,128)(2,1)S(1)}, bf16[512,256]{1,0:T(8,128)(2,1)S(1)}, u32[]{:S(2)}, u32[]{:S(2)}) collective-permute-start(bf16[512,256]{1,0:T(8,128)(2,1)S(1)} %broadcast_select_fusion), channel_id=1, source_target_pairs={{0,8},{8,4},{4,0},{12,12},{1,9},{9,5},{5,1},{13,13},{2,10},{10,6},... | collective-permute-start | bytes 786440 | tf_op jit(solution)/shard_map/ppermute | solution.py:369
  44.9 13.0 %collective-permute-start.5 = (bf16[512,256]{1,0:T(8,128)(2,1)S(1)}, bf16[512,256]{1,0:T(8,128)(2,1)S(1)}, u32[]{:S(2)}, u32[]{:S(2)}) collective-permute-start(bf16[512,256]{1,0:T(8,128)(2,1)S(1)} %collective-permute-done.4.refs_0_.refs_1_), channel_id=1, source_target_pairs={{0,8},{8,4},{4,0},{12,12},{1,9},{9,5},{5,1},{13,13},{2,10},{10,6},... | collective-permute-start | bytes 786440 | tf_op jit(solution)/shard_map/ppermute | solution.py:369
  50.2 7.7 %collective-permute-start.6 = (bf16[512,256]{1,0:T(8,128)(2,1)S(1)}, bf16[512,256]{1,0:T(8,128)(2,1)S(1)}, u32[]{:S(2)}, u32[]{:S(2)}) collective-permute-start(bf16[512,256]{1,0:T(8,128)(2,1)S(1)} %collective-permute-done.4.refs_0_.refs_1_), channel_id=1, source_target_pairs={{8,12},{12,8},{0,0},{4,4},{9,13},{13,9},{1,1},{5,5},{10,14},{14,10... | collective-permute-start | bytes 786440 | tf_op jit(solution)/shard_map/ppermute | solution.py:370
  53.7 8.8 %collective-permute-start.9 = (bf16[32,2176]{1,0:T(8,128)(2,1)S(1)}, bf16[32,2176]{1,0:T(8,128)(2,1)S(1)}, u32[]{:S(2)}, u32[]{:S(2)}) collective-permute-start(bf16[32,2176]{1,0:T(8,128)(2,1)S(1)} %get-tuple-element.66), channel_id=1, source_target_pairs={{0,8},{4,12},{8,0},{12,4},{1,9},{5,13},{9,1},{13,5},{2,10},{6,14},... | collective-permute-start | bytes 417800 | tf_op jit(solution)/shard_map/ppermute | solution.py:349

commit v7 on v6

--- a/solution.py
+++ b/solution.py
@@ -42,42 +42,40 @@
     return functools.reduce(op, items)
 
 
-def copy_all(copies, sem):
+def start_all(copies, sem):
     started = [pltpu.make_async_copy(a, b, sem.at[i]) for i, (a, b) in enumerate(copies)]
     for copy in started:
         copy.start()
-    for copy in started:
-        copy.wait()
+    return started
 
 
 def in_hbm(x):
     return pltpu.with_memory_space_constraint(x, pltpu.HBM)
 
 
-def gather_kernel(heads, k_ref, v_ref, *refs):
-    others = (len(refs) - heads - 1) // 2
-    plain, kv, outs, sem = refs[:others], refs[others : others + heads], refs[others + heads : -1], refs[-1]
+def parts_kernel(heads, k_ref, v_ref, *refs):
+    kv, sem = refs[:heads], refs[heads]
     copies = []
     for g in range(heads):
         for ref, at in ((k_ref, 0), (v_ref, HD)):
             copies.append((ref.at[:, g * HD : (g + 1) * HD], kv[g].at[:, at : at + HD]))
-    copy_all(copies + list(zip(plain, outs)), sem)
-
-
-def gather(key, value, others, name):
+    for copy in start_all(copies, sem):
+        copy.wait()
+
+
+def parts(key, value):
     rows, heads = key.shape[0], key.shape[1] // HD
-    shapes = [((rows, 2 * HD), key.dtype)] * heads + [(x.shape, x.dtype) for x in others]
     outs = pl.pallas_call(
-        functools.partial(gather_kernel, heads),
-        out_shape=[pltpu.VMEM(*x) if others else jax.ShapeDtypeStruct(*x) for x in shapes],
-        in_specs=[HBM] * (2 + len(others)),
-        out_specs=[VMEM if others else ANY] * len(shapes),
-        scratch_shapes=[pltpu.SemaphoreType.DMA((2 * heads + len(others),))],
+        functools.partial(parts_kernel, heads),
+        out_shape=[pltpu.VMEM((rows, 2 * HD), key.dtype)] * heads,
+        in_specs=[HBM] * 2,
+        out_specs=[VMEM] * heads,
+        scratch_shapes=[pltpu.SemaphoreType.DMA((2 * heads,))],
         compiler_params=params(2),
         cost_estimate=BRIEF,
-        name=name,
-    )(*[in_hbm(x) for x in (key, value, *others)])
-    return list(outs[:heads]), list(outs[heads:])
+        name="parts",
+    )(in_hbm(key), in_hbm(value))
+    return list(outs)
 
 
 def pipelined(tasks, scores, finish):
@@ -93,8 +91,21 @@
     return slice(h * HD, (h + 1) * HD)
 
 
-def local_kernel(g, q_ref, kv_ref, acc_ref, top_ref, sum_ref, ve):
-    rows = q_ref.shape[0]
+def local_kernel(g, loads, kv_ref, *refs):
+    ins = max(loads, 1)
+    sources, (acc_ref, top_ref, sum_ref) = refs[:ins], refs[ins : ins + 3]
+    held, ve = refs[ins + 3 : ins + 3 + loads] or sources, refs[ins + 3 + loads]
+    q_ref, rows = held[0], kv_ref.shape[0]
+    queries, others = {}, []
+    if loads:
+        sem = refs[-1]
+        order = list(range(g * GROUP, g * GROUP + GROUP)) + [h for h in range(q_ref.shape[1] // HD) if h // GROUP != g]
+        spots = [slice(h * HD, (h + PAIR) * HD) for h in order[::PAIR]]
+        copies = [(sources[0].at[:, spot], q_ref.at[:, spot]) for spot in spots]
+        copies += list(zip(sources[1:], held[1:]))
+        copies = start_all(copies, sem)
+        queries = dict(zip(order[:GROUP:PAIR], copies))
+        others = copies[GROUP // PAIR :]
     ve[:, :HD] = kv_ref[:, HD:]
     ve[:, HD:] = jnp.ones((rows, HD), jnp.bfloat16)
     row = lax.broadcasted_iota(jnp.int32, (PAIR * TILE, TILE), 0)
@@ -102,6 +113,8 @@
 
     def scores(task):
         first, at = task
+        if at == 0 and loads:
+            queries[g * GROUP + first].wait()
         q = jnp.concatenate([q_ref[at : at + TILE, head_columns(g * GROUP + first + j)] for j in range(PAIR)], axis=0)
         parts = [nt(q, kv_ref[:at, :HD])] if at else []
         parts.append(jnp.where(seen, nt(q, kv_ref[at : at + TILE, :HD]), NEG))
@@ -123,20 +136,27 @@
             top_ref[here] = top[at_j]
 
     pipelined([(h, at) for h in range(0, GROUP, PAIR) for at in range(0, rows, TILE)], scores, finish)
-
-
-def local_attention(query, kv, g):
-    rows = query.shape[0]
-    return pl.pallas_call(
-        functools.partial(local_kernel, g),
-        out_shape=[pltpu.VMEM((rows, GROUP * HD), jnp.float32)] * 3,
-        in_specs=[VMEM] * 2,
-        out_specs=[VMEM] * 3,
-        scratch_shapes=[pltpu.VMEM((rows, 2 * HD), jnp.bfloat16)],
+    for copy in others:
+        copy.wait()
+
+
+def local_attention(kv, g, query, loads=()):
+    rows = kv.shape[0]
+    sources = [in_hbm(x) for x in (query, *loads)] if loads else [query]
+    held = [pltpu.VMEM(x.shape, x.dtype) for x in sources] if loads else []
+    count = len(held)
+    outs = pl.pallas_call(
+        functools.partial(local_kernel, g, count),
+        out_shape=[pltpu.VMEM((rows, GROUP * HD), jnp.float32)] * 3 + held,
+        in_specs=[VMEM] + [HBM if loads else VMEM] * len(sources),
+        out_specs=[VMEM] * (3 + count),
+        scratch_shapes=[pltpu.VMEM((rows, 2 * HD), jnp.bfloat16)]
+        + ([pltpu.SemaphoreType.DMA((query.shape[1] // HD // PAIR + len(loads),))] if loads else []),
         compiler_params=params(6),
-        cost_estimate=LONG,
+        cost_estimate=LONG if loads else BRIEF,
         name="local_attention",
-    )(query, kv)
+    )(kv, *sources)
+    return list(outs[:3]), list(outs[3:])
 
 
 def anchor_kernel(g, count, prior, blk_ref, q_ref, acc_ref, top_ref, sum_ref, *refs):
@@ -363,30 +383,29 @@
     hold = lax.optimization_barrier
     row = lambda x: x.reshape(1, options)
 
+    blk_arr, ctx_key = hold((blk_arr, ctx_key))
+    kvs = parts(ctx_key, ctx_value)
     queries = [opt_query] + [swap(opt_query, n, mask) for mask in range(1, n)]
-    sent, _ = gather(ctx_key, ctx_value, [], "anchor_parts")
-    if n == 4:
-        on = lambda x: lax.ppermute(x, "blk", [(0, 2), (2, 1), (1, 0), (3, 3)])
-        up = lambda x: lax.ppermute(x, "blk", [(2, 3), (3, 2), (0, 0), (1, 1)])
-        got = on(sent[0])
-    plain = [row(opt_owner), row(opt_slot), row(opt_length), opt_query, ctx_query]
-    kvs, (*smalls, queries[0], ctx_query) = gather(ctx_key, ctx_value, plain, "load")
-
-    states = [local_attention(ctx_query, kvs[0], 0)]
-    keep, send = option_partials(blk_arr, *smalls, kvs, queries, states[0][1])
+    state, (ctx_query, *smalls, queries[0]) = local_attention(
+        kvs[0], 0, ctx_query, [row(opt_owner), row(opt_slot), row(opt_length), opt_query]
+    )
+    states = [state]
+    keep, send = option_partials(blk_arr, *smalls, kvs, queries, state[1])
     if n == 4:
         anchors = []
-        got, keep, kvs[1:] = hold((got, keep, kvs[1:]))
-        for g in range(len(kvs)):
-            after = on(jnp.where(blk == 0, sent[g + 1], got) if g + 1 < len(kvs) else got)
-            anchors.append([after, got, up(got)])
+        first = [lax.ppermute(kvs[0], "blk", [(0, 2)])]
+        kvs, states = hold((kvs, states))
+        first += [lax.ppermute(kv, "blk", [(0, 2)]) for kv in kvs[1:]]
+        first[0], keep, kvs = hold((first[0], keep, kvs))
+        for g, got in enumerate(first):
+            anchors.append([lax.ppermute(got, "blk", [(2, 1)]), got, lax.ppermute(got, "blk", [(2, 3)])])
             if g + 1 < len(kvs):
-                states.append(local_attention(ctx_query, kvs[g + 1], g + 1))
-                after, states = hold((after, states))
-            got = after
+                states.append(local_attention(kvs[g + 1], g + 1, ctx_query)[0])
+                first[g + 1], states = hold((first[g + 1], states))
+        anchors[0], first = hold((anchors[0], first))
     else:
-        states += [local_attention(ctx_query, kv, g) for g, kv in enumerate(kvs) if g]
-        anchors = [[from_root(kv, blk)] for kv in sent]
+        states += [local_attention(kv, g, ctx_query)[0] for g, kv in enumerate(kvs) if g]
+        anchors = [[from_root(kv, blk)] for kv in kvs]
     ctx_out, tokens = None, []
     for g, state in enumerate(states):
         ctx_out, token = anchor_attention(blk_arr, ctx_query, state, anchors[g], g, ctx_out)

time: 63.9 us -> 45.2 us (0.71)
  the two profiles are of different devices: /device:TPU:0 before, /device:TPU:12 now
where the time goes in v7:
time: 45.2 us; the launch traced here: 44.9 us
  Pallas kernels  22.9 us (51%)
  starting transfers between devices  16.7 us (37%)
  waiting for transfers between devices  4.47 us (10%)
  between operations  0.77 us (2%)
    ppermute x5, starting transfers between devices, swap(): return lax.ppermute(x, 'blk', [(i, i ^ mask) for i in range(n)])  10.7 us
    pallas_call x2, Pallas kernels, anchor_attention(): pl.pallas_call(functools.partial(anchor_kernel, g, len(cands), len(alias)...  9.46 us
    pallas_call x2, Pallas kernels, local_attention(): pl.pallas_call(functools.partial(local_kernel, g, count), out_shape=[pltp...  7.12 us
    ppermute x2, waiting for transfers between devices, body(): lax.ppermute(got, 'blk', [(2, 1)])  4.02 us
    pallas_call x1, Pallas kernels, option_partials(): pl.pallas_call(functools.partial(option_kernel, n, heads), out_shape=[jax...  2.98 us
    ppermute x2, starting transfers between devices, body(): lax.ppermute(got, 'blk', [(2, 1)])  2.58 us
    pallas_call x1, Pallas kernels, parts(): pl.pallas_call(functools.partial(parts_kernel, heads), out_shape=[pltpu.V...  1.83 us
    pallas_call x2, Pallas kernels, merge(): pl.pallas_call(functools.partial(merge_kernel, heads), out_shape=shapes,...  1.55 us
  transfers between devices with their start and end apart: 11, of which 2 were waited for; matrix products, arithmetic and copies ran while one was open for 0% of the time, Pallas kernels for 49%

profile of v7, /device:TPU:12, one launch (start us, length us, event | category | flops | bytes accessed | tf_op | source)
XLA Modules:
  0.0 44.9 jit_solution(1286245056675828)
XLA Ops:
  0.6 0.5 %collective-permute-start.2 = (bf16[16,2048]{1,0:T(8,128)(2,1)}, bf16[16,2048]{1,0:T(8,128)(2,1)S(1)}, u32[]{:S(2)}, u32[]{:S(2)}) collective-permute-start(bf16[16,2048]{1,0:T(8,128)(2,1)} %refs_4_.1), channel_id=1, source_target_pairs={{0,4},{4,0},{8,12},{12,8},{1,5},{5,1},{9,13},{13,9},{2,6},{6,2},{1... | collective-permute-start | bytes 196616 | tf_op jit(solution)/shard_map/ppermute | solution.py:369
  1.1 2.7 %collective-permute-start.4 = (bf16[16,2048]{1,0:T(8,128)(2,1)}, bf16[16,2048]{1,0:T(8,128)(2,1)S(1)}, u32[]{:S(2)}, u32[]{:S(2)}) collective-permute-start(bf16[16,2048]{1,0:T(8,128)(2,1)} %refs_4_.1), channel_id=1, source_target_pairs={{0,12},{4,8},{8,4},{12,0},{1,13},{5,9},{9,5},{13,1},{2,14},{6,10},... | collective-permute-start | bytes 196616 | tf_op jit(solution)/shard_map/ppermute | solution.py:369
  3.8 1.2 %collective-permute-start.3 = (bf16[16,2048]{1,0:T(8,128)(2,1)}, bf16[16,2048]{1,0:T(8,128)(2,1)S(1)}, u32[]{:S(2)}, u32[]{:S(2)}) collective-permute-start(bf16[16,2048]{1,0:T(8,128)(2,1)} %refs_4_.1), channel_id=1, source_target_pairs={{0,8},{4,12},{8,0},{12,4},{1,9},{5,13},{9,1},{13,5},{2,10},{6,14},... | collective-permute-start | bytes 196616 | tf_op jit(solution)/shard_map/ppermute | solution.py:369
  5.1 1.8 %parts.1 = (bf16[512,256]{1,0:T(8,128)(2,1)}, bf16[512,256]{1,0:T(8,128)(2,1)S(1)}) custom-call(bf16[512,256]{1,0:T(8,128)(2,1)} %k_ref, bf16[512,256]{1,0:T(8,128)(2,1)} %v_ref.1), custom_call_target="tpu_custom_call" | custom-call | flops 1 | bytes 1 | tf_op jit(solution)/shard_map/parts/pallas_call | solution.py:68
  6.9 1.4 %collective-permute-start.1 = (bf16[512,256]{1,0:T(8,128)(2,1)}, bf16[512,256]{1,0:T(8,128)(2,1)}, u32[]{:S(2)}, u32[]{:S(2)}) collective-permute-start(bf16[512,256]{1,0:T(8,128)(2,1)} %get-tuple-element.44.kv_ref.refs_0_), channel_id=1, source_target_pairs={{0,8},{1,9},{2,10},{3,11},{16,24},{17,25},{18,26},{19,27}} | collective-permute-start | bytes 786440 | tf_op jit(solution)/shard_map/ppermute | solution.py:396
  8.3 4.8 %local_attention.2 = (f32[512,1024]{1,0:T(8,128)S(1)}, f32[512,1024]{1,0:T(8,128)S(1)}, f32[512,1024]{1,0:T(8,128)S(1)}, bf16[512,2048]{1,0:T(8,128)(2,1)S(1)}, ...) custom-call(bf16[512,256]{1,0:T(8,128)(2,1)} %get-tuple-element.44.kv_ref.refs_0_, ...), custom_call_target="tpu_custom_call" | custom-call | flops 99999997952 | bytes 1 | tf_op jit(solution)/shard_map/local_attention/pallas_call | solution.py:148
  13.1 0.7 %collective-permute-start = (bf16[512,256]{1,0:T(8,128)(2,1)S(1)}, bf16[512,256]{1,0:T(8,128)(2,1)S(1)}, u32[]{:S(2)}, u32[]{:S(2)}) collective-permute-start(bf16[512,256]{1,0:T(8,128)(2,1)S(1)} %get-tuple-element.59.refs_1_.kv_ref), channel_id=1, source_target_pairs={{0,8},{1,9},{2,10},{3,11},{16,24},{17,25},{18,26},{19,27}} | collective-permute-start | bytes 786440 | tf_op jit(solution)/shard_map/ppermute | solution.py:398
  13.8 0.0 collective-permute-done.4.refs_5_
  13.8 0.0 collective-permute-done.3.refs_4_
  13.9 3.0 %option_partials.1 = (bf16[64,2176]{1,0:T(8,128)(2,1)S(1)}, bf16[64,2176]{1,0:T(8,128)(2,1)S(1)}) custom-call(s32[1]{0:T(128)} %bitcast.blk_ref, s32[1,64]{1,0:T(1,128)S(1)} %get-tuple-element.54.owner_ref, s32[1,64]{1,0:T(1,128)S(1)} %get-tuple-element.55.slot_ref, s32[1,64]{1,0:T(1,128)S(1)} %get-tuple-element.56.length_ref, ...), custom_call_target="tpu_custom_call" | custom-call | flops 99999997952 | bytes 1 | tf_op jit(solution)/shard_map/option_partials/pallas_call | solution.py:309
  16.8 5.0 %collective-permute-start.9 = (bf16[64,2176]{1,0:T(8,128)(2,1)S(1)}, bf16[64,2176]{1,0:T(8,128)(2,1)S(1)}, u32[]{:S(2)}, u32[]{:S(2)}) collective-permute-start(bf16[64,2176]{1,0:T(8,128)(2,1)S(1)} %get-tuple-element.77), channel_id=1, source_target_pairs={{0,4},{4,0},{8,12},{12,8},{1,5},{5,1},{9,13},{13,9},{2,6},{6,2},{1... | collective-permute-start | bytes 835592 | tf_op jit(solution)/shard_map/ppermute | solution.py:369
  21.8 0.0 collective-permute-done.1.refs_1_
  21.8 0.7 %collective-permute-start.8 = (bf16[512,256]{1,0:T(8,128)(2,1)}, bf16[512,256]{1,0:T(8,128)(2,1)S(1)}, u32[]{:S(2)}, u32[]{:S(2)}) collective-permute-start(bf16[512,256]{1,0:T(8,128)(2,1)} %collective-permute-done.1.refs_1_), channel_id=1, source_target_pairs={{8,12},{9,13},{10,14},{11,15},{24,28},{25,29},{26,30},{27,31}} | collective-permute-start | bytes 786440 | tf_op jit(solution)/shard_map/ppermute | solution.py:401
  22.5 1.3 %collective-permute-start.7 = (bf16[512,256]{1,0:T(8,128)(2,1)}, bf16[512,256]{1,0:T(8,128)(2,1)S(1)}, u32[]{:S(2)}, u32[]{:S(2)}) collective-permute-start(bf16[512,256]{1,0:T(8,128)(2,1)} %collective-permute-done.1.refs_1_), channel_id=1, source_target_pairs={{8,4},{9,5},{10,6},{11,7},{24,20},{25,21},{26,22},{27,23}} | collective-permute-start | bytes 786440 | tf_op jit(solution)/shard_map/ppermute | solution.py:401
  23.8 2.3 %local_attention.3 = (f32[512,1024]{1,0:T(8,128)S(1)}, f32[512,1024]{1,0:T(8,128)S(1)}, f32[512,1024]{1,0:T(8,128)S(1)}) custom-call(bf16[512,256]{1,0:T(8,128)(2,1)S(1)} %get-tuple-element.59.refs_1_.kv_ref, bf16[512,2048]{1,0:T(8,128)(2,1)S(1)} %get-tuple-element.45.refs_0_.q_ref), custom_call_target="tpu_custom_call" | custom-call | flops 1 | bytes 1 | tf_op jit(solution)/shard_map/local_attention/pallas_call | solution.py:148
  26.1 0.7 %collective-permute-start.6 = (bf16[512,256]{1,0:T(8,128)(2,1)S(1)}, bf16[512,256]{1,0:T(8,128)(2,1)S(1)}, u32[]{:S(2)}, u32[]{:S(2)}) collective-permute-start(bf16[512,256]{1,0:T(8,128)(2,1)S(1)} %collective-permute-done.refs_1_), channel_id=1, source_target_pairs={{8,12},{9,13},{10,14},{11,15},{24,28},{25,29},{26,30},{27,31}} | collective-permute-start | bytes 786440 | tf_op jit(solution)/shard_map/ppermute | solution.py:401
  26.8 1.3 %collective-permute-start.5 = (bf16[512,256]{1,0:T(8,128)(2,1)S(1)}, bf16[512,256]{1,0:T(8,128)(2,1)S(1)}, u32[]{:S(2)}, u32[]{:S(2)}) collective-permute-start(bf16[512,256]{1,0:T(8,128)(2,1)S(1)} %collective-permute-done.refs_1_), channel_id=1, source_target_pairs={{8,4},{9,5},{10,6},{11,7},{24,20},{25,21},{26,22},{27,23}} | collective-permute-start | bytes 786440 | tf_op jit(solution)/shard_map/ppermute | solution.py:401
  28.1 4.0 %collective-permute-done.7.refs_0_ = bf16[512,256]{1,0:T(8,128)(2,1)S(1)} collective-permute-done((bf16[512,256]{1,0:T(8,128)(2,1)}, bf16[512,256]{1,0:T(8,128)(2,1)S(1)}, u32[]{:S(2)}, u32[]{:S(2)}) %collective-permute-start.7) | collective-permute-done | bytes 262176 | tf_op jit(solution)/shard_map/ppermute | solution.py:401
  32.1 5.2 %anchor_attention.2 = (bf16[512,2048]{1,0:T(8,128)(2,1)}, f32[8,128]{1,0:T(8,128)S(1)}) custom-call(s32[1]{0:T(128)} %bitcast.blk_ref, bf16[512,2048]{1,0:T(8,128)(2,1)S(1)} %get-tuple-element.45.refs_0_.q_ref, f32[512,1024]{1,0:T(8,128)S(1)} %get-tuple-element.67.acc_ref, f32[512,1024]{1,0:T(8,128)S(1)} %get-tuple-element.68.refs_6_.top_ref, ...), custom_call_target="tpu_custom_call" | custom-call | flops 1 | bytes 1 | tf_op jit(solution)/shard_map/anchor_attention/pallas_call | solution.py:226
  37.3 0.6 %merge.2 = (bf16[32,2176]{1,0:T(8,128)(2,1)S(1)}, bf16[32,2176]{1,0:T(8,128)(2,1)S(1)}) custom-call(bf16[64,2176]{1,0:T(8,128)(2,1)S(1)} %get-tuple-element.76.a, bf16[64,2176]{1,0:T(8,128)(2,1)S(1)} %collective-permute-done.9.b, f32[8,128]{1,0:T(8,128)S(1)} %get-tuple-element.78.after), custom_call_target="tpu_custom_call" | custom-call | flops 1 | bytes 1 | tf_op jit(solution)/shard_map/merge/pallas_call | solution.py:357
  37.9 1.3 %collective-permute-start.10 = (bf16[32,2176]{1,0:T(8,128)(2,1)S(1)}, bf16[32,2176]{1,0:T(8,128)(2,1)S(1)}, u32[]{:S(2)}, u32[]{:S(2)}) collective-permute-start(bf16[32,2176]{1,0:T(8,128)(2,1)S(1)} %get-tuple-element.80), channel_id=1, source_target_pairs={{0,8},{4,12},{8,0},{12,4},{1,9},{5,13},{9,1},{13,5},{2,10},{6,14},... | collective-permute-start | bytes 417800 | tf_op jit(solution)/shard_map/ppermute | solution.py:369
  39.2 4.3 %anchor_attention.3 = (bf16[512,2048]{1,0:T(8,128)(2,1)}, f32[8,128]{1,0:T(8,128)S(1)}) custom-call(s32[1]{0:T(128)} %bitcast.blk_ref, bf16[512,2048]{1,0:T(8,128)(2,1)S(1)} %get-tuple-element.45.refs_0_.q_ref, f32[512,1024]{1,0:T(8,128)S(1)} %get-tuple-element.63.acc_ref, ...), custom_call_target="tpu_custom_call", output_to_operand_aliasing={{0}: (8, {})} | custom-call | flops 1 | bytes 1 | tf_op jit(solution)/shard_map/anchor_attention/pallas_call | solution.py:226
  43.5 0.4 collective-permute-done.10.b
  43.9 1.0 %merge.3 = bf16[32,2048]{1,0:T(8,128)(2,1)} custom-call(bf16[32,2176]{1,0:T(8,128)(2,1)S(1)} %get-tuple-element.79.a, bf16[32,2176]{1,0:T(8,128)(2,1)S(1)} %collective-permute-done.10.b, f32[8,128]{1,0:T(8,128)S(1)} %get-tuple-element.81.after), custom_call_target="tpu_custom_call" | custom-call | flops 1 | bytes 1 | tf_op jit(solution)/shard_map/merge/pallas_call | solution.py:357
  (6 shorter events, 0.0 us)
Async XLA Ops:
  0.6 13.2 %collective-permute-start.2 = (bf16[16,2048]{1,0:T(8,128)(2,1)}, bf16[16,2048]{1,0:T(8,128)(2,1)S(1)}, u32[]{:S(2)}, u32[]{:S(2)}) collective-permute-start(bf16[16,2048]{1,0:T(8,128)(2,1)} %refs_4_.1), channel_id=1, source_target_pairs={{0,4},{4,0},{8,12},{12,8},{1,5},{5,1},{9,13},{13,9},{2,6},{6,2},{1... | collective-permute-start | bytes 196616 | tf_op jit(solution)/shard_map/ppermute | solution.py:369
  1.1 12.7 %collective-permute-start.4 = (bf16[16,2048]{1,0:T(8,128)(2,1)}, bf16[16,2048]{1,0:T(8,128)(2,1)S(1)}, u32[]{:S(2)}, u32[]{:S(2)}) collective-permute-start(bf16[16,2048]{1,0:T(8,128)(2,1)} %refs_4_.1), channel_id=1, source_target_pairs={{0,12},{4,8},{8,4},{12,0},{1,13},{5,9},{9,5},{13,1},{2,14},{6,10},... | collective-permute-start | bytes 196616 | tf_op jit(solution)/shard_map/ppermute | solution.py:369
  3.8 10.0 %collective-permute-start.3 = (bf16[16,2048]{1,0:T(8,128)(2,1)}, bf16[16,2048]{1,0:T(8,128)(2,1)S(1)}, u32[]{:S(2)}, u32[]{:S(2)}) collective-permute-start(bf16[16,2048]{1,0:T(8,128)(2,1)} %refs_4_.1), channel_id=1, source_target_pairs={{0,8},{4,12},{8,0},{12,4},{1,9},{5,13},{9,1},{13,5},{2,10},{6,14},... | collective-permute-start | bytes 196616 | tf_op jit(solution)/shard_map/ppermute | solution.py:369
  6.9 14.9 %collective-permute-start.1 = (bf16[512,256]{1,0:T(8,128)(2,1)}, bf16[512,256]{1,0:T(8,128)(2,1)}, u32[]{:S(2)}, u32[]{:S(2)}) collective-permute-start(bf16[512,256]{1,0:T(8,128)(2,1)} %get-tuple-element.44.kv_ref.refs_0_), channel_id=1, source_target_pairs={{0,8},{1,9},{2,10},{3,11},{16,24},{17,25},{18,26},{19,27}} | collective-permute-start | bytes 786440 | tf_op jit(solution)/shard_map/ppermute | solution.py:396
  13.1 12.9 %collective-permute-start = (bf16[512,256]{1,0:T(8,128)(2,1)S(1)}, bf16[512,256]{1,0:T(8,128)(2,1)S(1)}, u32[]{:S(2)}, u32[]{:S(2)}) collective-permute-start(bf16[512,256]{1,0:T(8,128)(2,1)S(1)} %get-tuple-element.59.refs_1_.kv_ref), channel_id=1, source_target_pairs={{0,8},{1,9},{2,10},{3,11},{16,24},{17,25},{18,26},{19,27}} | collective-permute-start | bytes 786440 | tf_op jit(solution)/shard_map/ppermute | solution.py:398
  16.8 20.5 %collective-permute-start.9 = (bf16[64,2176]{1,0:T(8,128)(2,1)S(1)}, bf16[64,2176]{1,0:T(8,128)(2,1)S(1)}, u32[]{:S(2)}, u32[]{:S(2)}) collective-permute-start(bf16[64,2176]{1,0:T(8,128)(2,1)S(1)} %get-tuple-element.77), channel_id=1, source_target_pairs={{0,4},{4,0},{8,12},{12,8},{1,5},{5,1},{9,13},{13,9},{2,6},{6,2},{1... | collective-permute-start | bytes 835592 | tf_op jit(solution)/shard_map/ppermute | solution.py:369
  21.8 6.2 %collective-permute-start.8 = (bf16[512,256]{1,0:T(8,128)(2,1)}, bf16[512,256]{1,0:T(8,128)(2,1)S(1)}, u32[]{:S(2)}, u32[]{:S(2)}) collective-permute-start(bf16[512,256]{1,0:T(8,128)(2,1)} %collective-permute-done.1.refs_1_), channel_id=1, source_target_pairs={{8,12},{9,13},{10,14},{11,15},{24,28},{25,29},{26,30},{27,31}} | collective-permute-start | bytes 786440 | tf_op jit(solution)/shard_map/ppermute | solution.py:401
  22.5 9.6 %collective-permute-start.7 = (bf16[512,256]{1,0:T(8,128)(2,1)}, bf16[512,256]{1,0:T(8,128)(2,1)S(1)}, u32[]{:S(2)}, u32[]{:S(2)}) collective-permute-start(bf16[512,256]{1,0:T(8,128)(2,1)} %collective-permute-done.1.refs_1_), channel_id=1, source_target_pairs={{8,4},{9,5},{10,6},{11,7},{24,20},{25,21},{26,22},{27,23}} | collective-permute-start | bytes 786440 | tf_op jit(solution)/shard_map/ppermute | solution.py:401
  26.1 13.1 %collective-permute-start.6 = (bf16[512,256]{1,0:T(8,128)(2,1)S(1)}, bf16[512,256]{1,0:T(8,128)(2,1)S(1)}, u32[]{:S(2)}, u32[]{:S(2)}) collective-permute-start(bf16[512,256]{1,0:T(8,128)(2,1)S(1)} %collective-permute-done.refs_1_), channel_id=1, source_target_pairs={{8,12},{9,13},{10,14},{11,15},{24,28},{25,29},{26,30},{27,31}} | collective-permute-start | bytes 786440 | tf_op jit(solution)/shard_map/ppermute | solution.py:401
  26.8 12.4 %collective-permute-start.5 = (bf16[512,256]{1,0:T(8,128)(2,1)S(1)}, bf16[512,256]{1,0:T(8,128)(2,1)S(1)}, u32[]{:S(2)}, u32[]{:S(2)}) collective-permute-start(bf16[512,256]{1,0:T(8,128)(2,1)S(1)} %collective-permute-done.refs_1_), channel_id=1, source_target_pairs={{8,4},{9,5},{10,6},{11,7},{24,20},{25,21},{26,22},{27,23}} | collective-permute-start | bytes 786440 | tf_op jit(solution)/shard_map/ppermute | solution.py:401
  37.9 6.0 %collective-permute-start.10 = (bf16[32,2176]{1,0:T(8,128)(2,1)S(1)}, bf16[32,2176]{1,0:T(8,128)(2,1)S(1)}, u32[]{:S(2)}, u32[]{:S(2)}) collective-permute-start(bf16[32,2176]{1,0:T(8,128)(2,1)S(1)} %get-tuple-element.80), channel_id=1, source_target_pairs={{0,8},{4,12},{8,0},{12,4},{1,9},{5,13},{9,1},{13,5},{2,10},{6,14},... | collective-permute-start | bytes 417800 | tf_op jit(solution)/shard_map/ppermute | solution.py:369

commit v8 on v7

--- a/solution.py
+++ b/solution.py
@@ -22,7 +22,7 @@
 SMEM = pl.BlockSpec(memory_space=pltpu.SMEM)
 HBM = pl.BlockSpec(memory_space=pltpu.HBM)
 ANY = pl.BlockSpec(memory_space=pl.ANY)
-LONG = pl.CostEstimate(flops=10**11, bytes_accessed=1, transcendentals=0)
+LONG = pl.CostEstimate(flops=10**9, bytes_accessed=1, transcendentals=0)
 BRIEF = pl.CostEstimate(flops=1, bytes_accessed=1, transcendentals=0)
 
 
@@ -385,6 +385,7 @@
 
     blk_arr, ctx_key = hold((blk_arr, ctx_key))
     kvs = parts(ctx_key, ctx_value)
+    kvs, opt_query = hold((kvs, opt_query))
     queries = [opt_query] + [swap(opt_query, n, mask) for mask in range(1, n)]
     state, (ctx_query, *smalls, queries[0]) = local_attention(
         kvs[0], 0, ctx_query, [row(opt_owner), row(opt_slot), row(opt_length), opt_query]

time: 45.2 us -> 52.2 us (1.15)
  waiting for transfers between devices: 4.47 us -> 14.1 us
  Pallas kernels: 22.9 us -> 19.4 us
  starting transfers between devices: 16.7 us -> 17.7 us
    ppermute x5, waiting for transfers between devices: 0.44 us -> 7.32 us  [swap(): return lax.ppermute(x, 'blk', [(i, i ^ mask) for i in range(n)])]
    ppermute x2, waiting for transfers between devices: 4.02 us -> 6.77 us  [body(): lax.ppermute(got, 'blk', [(2, 1)])]
    ppermute x5, starting transfers between devices: 10.7 us -> 12.4 us  [swap(): return lax.ppermute(x, 'blk', [(i, i ^ mask) for i in range(n)])]
    pallas_call x1, Pallas kernels: 2.98 us -> 2.02 us  [option_partials(): pl.pallas_call(functools.partial(option_kernel, n, heads), out_shape=[jax...]
    pallas_call x2, Pallas kernels: 9.46 us -> 8.51 us  [anchor_attention(): pl.pallas_call(functools.partial(anchor_kernel, g, len(cands), len(alias)...]
    pallas_call x2, Pallas kernels: 7.12 us -> 6.19 us  [local_attention(): pl.pallas_call(functools.partial(local_kernel, g, count), out_shape=[pltp...]
    pallas_call x1, Pallas kernels: 1.83 us -> 1.13 us  [parts(): pl.pallas_call(functools.partial(parts_kernel, heads), out_shape=[pltpu.V...]
    ppermute x1, starting transfers between devices: 1.36 us -> 0.68 us  [body(): first = [lax.ppermute(kvs[0], 'blk', [(0, 2)])]]
  transfers between devices with their start and end apart: 11 -> 11, of which waited for: 2 -> 3; matrix products, arithmetic and copies ran while one was open for 0% -> 0% of each run, Pallas kernels for 49% -> 33%
where the time goes in v8:
time: 52.2 us; the launch traced here: 52 us
  Pallas kernels  19.4 us (37%)
  starting transfers between devices  17.7 us (34%)
  waiting for transfers between devices  14.1 us (27%)
  between operations  0.78 us (1%)
    ppermute x5, starting transfers between devices, swap(): return lax.ppermute(x, 'blk', [(i, i ^ mask) for i in range(n)])  12.4 us
    pallas_call x2, Pallas kernels, anchor_attention(): pl.pallas_call(functools.partial(anchor_kernel, g, len(cands), len(alias)...  8.51 us
    ppermute x5, waiting for transfers between devices, swap(): return lax.ppermute(x, 'blk', [(i, i ^ mask) for i in range(n)])  7.32 us
    ppermute x2, waiting for transfers between devices, body(): lax.ppermute(got, 'blk', [(2, 1)])  6.77 us
    pallas_call x2, Pallas kernels, local_attention(): pl.pallas_call(functools.partial(local_kernel, g, count), out_shape=[pltp...  6.19 us
    ppermute x2, starting transfers between devices, body(): lax.ppermute(got, 'blk', [(2, 1)])  2.58 us
    pallas_call x1, Pallas kernels, option_partials(): pl.pallas_call(functools.partial(option_kernel, n, heads), out_shape=[jax...  2.02 us
    pallas_call x2, Pallas kernels, merge(): pl.pallas_call(functools.partial(merge_kernel, heads), out_shape=shapes,...  1.55 us
  transfers between devices with their start and end apart: 11, of which 3 were waited for; matrix products, arithmetic and copies ran while one was open for 0% of the time, Pallas kernels for 33%

profile of v8, /device:TPU:12, one launch (start us, length us, event | category | flops | bytes accessed | tf_op | source)
XLA Modules:
  0.0 52.0 jit_solution(13099587181671410380)
XLA Ops:
  0.6 1.1 %parts.1 = (bf16[512,256]{1,0:T(8,128)(2,1)S(1)}, bf16[512,256]{1,0:T(8,128)(2,1)S(1)}) custom-call(bf16[512,256]{1,0:T(8,128)(2,1)} %k_ref, bf16[512,256]{1,0:T(8,128)(2,1)} %v_ref.1), custom_call_target="tpu_custom_call" | custom-call | flops 1 | bytes 1 | tf_op jit(solution)/shard_map/parts/pallas_call | solution.py:68
  1.8 0.7 %collective-permute-start.1 = (bf16[512,256]{1,0:T(8,128)(2,1)S(1)}, bf16[512,256]{1,0:T(8,128)(2,1)S(1)}, u32[]{:S(2)}, u32[]{:S(2)}) collective-permute-start(bf16[512,256]{1,0:T(8,128)(2,1)S(1)} %get-tuple-element.49.kv_ref.refs_0_), channel_id=1, source_target_pairs={{0,8},{1,9},{2,10},{3,11},{16,24},{17,25},{18,26},{19,27}} | collective-permute-start | bytes 786440 | tf_op jit(solution)/shard_map/ppermute | solution.py:397
  2.5 2.3 %collective-permute-start.4 = (bf16[16,2048]{1,0:T(8,128)(2,1)}, bf16[16,2048]{1,0:T(8,128)(2,1)S(1)}, u32[]{:S(2)}, u32[]{:S(2)}) collective-permute-start(bf16[16,2048]{1,0:T(8,128)(2,1)} %refs_4_), channel_id=1, source_target_pairs={{0,12},{4,8},{8,4},{12,0},{1,13},{5,9},{9,5},{13,1},{2,14},{6,10},... | collective-permute-start | bytes 196616 | tf_op jit(solution)/shard_map/ppermute | solution.py:369
  4.7 4.5 %collective-permute-start.3 = (bf16[16,2048]{1,0:T(8,128)(2,1)}, bf16[16,2048]{1,0:T(8,128)(2,1)S(1)}, u32[]{:S(2)}, u32[]{:S(2)}) collective-permute-start(bf16[16,2048]{1,0:T(8,128)(2,1)} %refs_4_), channel_id=1, source_target_pairs={{0,8},{4,12},{8,0},{12,4},{1,9},{5,13},{9,1},{13,5},{2,10},{6,14},... | collective-permute-start | bytes 196616 | tf_op jit(solution)/shard_map/ppermute | solution.py:369
  9.2 0.0 collective-permute-start.2
  9.2 3.9 %local_attention.2 = (f32[512,1024]{1,0:T(8,128)S(1)}, f32[512,1024]{1,0:T(8,128)S(1)}, f32[512,1024]{1,0:T(8,128)S(1)}, bf16[512,2048]{1,0:T(8,128)(2,1)S(1)}, ...) custom-call(bf16[512,256]{1,0:T(8,128)(2,1)S(1)} %get-tuple-element.49.kv_ref.ref, ...), custom_call_target="tpu_custom_call" | custom-call | flops 1000000000 | bytes 1 | tf_op jit(solution)/shard_map/local_attention/pallas_call | solution.py:148
  13.1 0.7 %collective-permute-start = (bf16[512,256]{1,0:T(8,128)(2,1)S(1)}, bf16[512,256]{1,0:T(8,128)(2,1)S(1)}, u32[]{:S(2)}, u32[]{:S(2)}) collective-permute-start(bf16[512,256]{1,0:T(8,128)(2,1)S(1)} %get-tuple-element.65.refs_1_.kv_ref), channel_id=1, source_target_pairs={{0,8},{1,9},{2,10},{3,11},{16,24},{17,25},{18,26},{19,27}} | collective-permute-start | bytes 786440 | tf_op jit(solution)/shard_map/ppermute | solution.py:399
  13.8 1.9 %collective-permute-done.4.refs_5_ = bf16[16,2048]{1,0:T(8,128)(2,1)S(1)} collective-permute-done((bf16[16,2048]{1,0:T(8,128)(2,1)}, bf16[16,2048]{1,0:T(8,128)(2,1)S(1)}, u32[]{:S(2)}, u32[]{:S(2)}) %collective-permute-start.4) | collective-permute-done | bytes 65568 | tf_op jit(solution)/shard_map/ppermute | solution.py:369
  15.6 5.5 %collective-permute-done.3.refs_4_ = bf16[16,2048]{1,0:T(8,128)(2,1)S(1)} collective-permute-done((bf16[16,2048]{1,0:T(8,128)(2,1)}, bf16[16,2048]{1,0:T(8,128)(2,1)S(1)}, u32[]{:S(2)}, u32[]{:S(2)}) %collective-permute-start.3) | collective-permute-done | bytes 65568 | tf_op jit(solution)/shard_map/ppermute | solution.py:369
  21.1 2.0 %option_partials.1 = (bf16[64,2176]{1,0:T(8,128)(2,1)S(1)}, bf16[64,2176]{1,0:T(8,128)(2,1)S(1)}) custom-call(s32[1]{0:T(128)} %bitcast.blk_ref, s32[1,64]{1,0:T(1,128)S(1)} %get-tuple-element.60.owner_ref, s32[1,64]{1,0:T(1,128)S(1)} %get-tuple-element.61.slot_ref, s32[1,64]{1,0:T(1,128)S(1)} %get-tuple-element.62.length_ref, ...), custom_call_target="tpu_custom_call" | custom-call | flops 1000000000 | bytes 1 | tf_op jit(solution)/shard_map/option_partials/pallas_call | solution.py:309
  23.1 0.1 collective-permute-start.9
  23.2 0.0 collective-permute-done.1.refs_1_
  23.2 0.7 %collective-permute-start.8 = (bf16[512,256]{1,0:T(8,128)(2,1)S(1)}, bf16[512,256]{1,0:T(8,128)(2,1)S(1)}, u32[]{:S(2)}, u32[]{:S(2)}) collective-permute-start(bf16[512,256]{1,0:T(8,128)(2,1)S(1)} %collective-permute-done.1.refs_1_), channel_id=1, source_target_pairs={{8,12},{9,13},{10,14},{11,15},{24,28},{25,29},{26,30},{27,31}} | collective-permute-start | bytes 786440 | tf_op jit(solution)/shard_map/ppermute | solution.py:402
  23.9 1.3 %collective-permute-start.7 = (bf16[512,256]{1,0:T(8,128)(2,1)S(1)}, bf16[512,256]{1,0:T(8,128)(2,1)S(1)}, u32[]{:S(2)}, u32[]{:S(2)}) collective-permute-start(bf16[512,256]{1,0:T(8,128)(2,1)S(1)} %collective-permute-done.1.refs_1_), channel_id=1, source_target_pairs={{8,4},{9,5},{10,6},{11,7},{24,20},{25,21},{26,22},{27,23}} | collective-permute-start | bytes 786440 | tf_op jit(solution)/shard_map/ppermute | solution.py:402
  25.2 2.3 %local_attention.3 = (f32[512,1024]{1,0:T(8,128)S(1)}, f32[512,1024]{1,0:T(8,128)S(1)}, f32[512,1024]{1,0:T(8,128)S(1)}) custom-call(bf16[512,256]{1,0:T(8,128)(2,1)S(1)} %get-tuple-element.65.refs_1_.kv_ref, bf16[512,2048]{1,0:T(8,128)(2,1)S(1)} %get-tuple-element.51.refs_0_.q_ref), custom_call_target="tpu_custom_call" | custom-call | flops 1 | bytes 1 | tf_op jit(solution)/shard_map/local_attention/pallas_call | solution.py:148
  27.5 0.7 %collective-permute-start.6 = (bf16[512,256]{1,0:T(8,128)(2,1)S(1)}, bf16[512,256]{1,0:T(8,128)(2,1)S(1)}, u32[]{:S(2)}, u32[]{:S(2)}) collective-permute-start(bf16[512,256]{1,0:T(8,128)(2,1)S(1)} %collective-permute-done.refs_1_), channel_id=1, source_target_pairs={{8,12},{9,13},{10,14},{11,15},{24,28},{25,29},{26,30},{27,31}} | collective-permute-start | bytes 786440 | tf_op jit(solution)/shard_map/ppermute | solution.py:402
  28.2 1.3 %collective-permute-start.5 = (bf16[512,256]{1,0:T(8,128)(2,1)S(1)}, bf16[512,256]{1,0:T(8,128)(2,1)S(1)}, u32[]{:S(2)}, u32[]{:S(2)}) collective-permute-start(bf16[512,256]{1,0:T(8,128)(2,1)S(1)} %collective-permute-done.refs_1_), channel_id=1, source_target_pairs={{8,4},{9,5},{10,6},{11,7},{24,20},{25,21},{26,22},{27,23}} | collective-permute-start | bytes 786440 | tf_op jit(solution)/shard_map/ppermute | solution.py:402
  29.5 0.0 collective-permute-done.8.refs_2_
  29.5 6.8 %collective-permute-done.7.refs_0_ = bf16[512,256]{1,0:T(8,128)(2,1)S(1)} collective-permute-done((bf16[512,256]{1,0:T(8,128)(2,1)S(1)}, bf16[512,256]{1,0:T(8,128)(2,1)S(1)}, u32[]{:S(2)}, u32[]{:S(2)}) %collective-permute-start.7) | collective-permute-done | bytes 262176 | tf_op jit(solution)/shard_map/ppermute | solution.py:402
  36.2 4.3 %anchor_attention.2 = (bf16[512,2048]{1,0:T(8,128)(2,1)}, f32[8,128]{1,0:T(8,128)S(1)}) custom-call(s32[1]{0:T(128)} %bitcast.blk_ref, bf16[512,2048]{1,0:T(8,128)(2,1)S(1)} %get-tuple-element.51.refs_0_.q_ref, f32[512,1024]{1,0:T(8,128)S(1)} %get-tuple-element.73.acc_ref, f32[512,1024]{1,0:T(8,128)S(1)} %get-tuple-element.74.refs_6_.top_ref, ...), custom_call_target="tpu_custom_call" | custom-call | flops 1 | bytes 1 | tf_op jit(solution)/shard_map/anchor_attention/pallas_call | solution.py:226
  40.5 0.6 %merge.2 = (bf16[32,2176]{1,0:T(8,128)(2,1)S(1)}, bf16[32,2176]{1,0:T(8,128)(2,1)S(1)}) custom-call(bf16[64,2176]{1,0:T(8,128)(2,1)S(1)} %get-tuple-element.82.a, bf16[64,2176]{1,0:T(8,128)(2,1)S(1)} %collective-permute-done.9.b, f32[8,128]{1,0:T(8,128)S(1)} %get-tuple-element.84.after), custom_call_target="tpu_custom_call" | custom-call | flops 1 | bytes 1 | tf_op jit(solution)/shard_map/merge/pallas_call | solution.py:357
  41.1 5.6 %collective-permute-start.10 = (bf16[32,2176]{1,0:T(8,128)(2,1)S(1)}, bf16[32,2176]{1,0:T(8,128)(2,1)S(1)}, u32[]{:S(2)}, u32[]{:S(2)}) collective-permute-start(bf16[32,2176]{1,0:T(8,128)(2,1)S(1)} %get-tuple-element.86), channel_id=1, source_target_pairs={{0,8},{4,12},{8,0},{12,4},{1,9},{5,13},{9,1},{13,5},{2,10},{6,14},... | collective-permute-start | bytes 417800 | tf_op jit(solution)/shard_map/ppermute | solution.py:369
  46.7 4.3 %anchor_attention.3 = (bf16[512,2048]{1,0:T(8,128)(2,1)}, f32[8,128]{1,0:T(8,128)S(1)}) custom-call(s32[1]{0:T(128)} %bitcast.blk_ref, bf16[512,2048]{1,0:T(8,128)(2,1)S(1)} %get-tuple-element.51.refs_0_.q_ref, f32[512,1024]{1,0:T(8,128)S(1)} %get-tuple-element.69.acc_ref, ...), custom_call_target="tpu_custom_call", output_to_operand_aliasing={{0}: (8, {})} | custom-call | flops 1 | bytes 1 | tf_op jit(solution)/shard_map/anchor_attention/pallas_call | solution.py:226
  51.0 1.0 %merge.3 = bf16[32,2048]{1,0:T(8,128)(2,1)} custom-call(bf16[32,2176]{1,0:T(8,128)(2,1)S(1)} %get-tuple-element.85.a, bf16[32,2176]{1,0:T(8,128)(2,1)S(1)} %collective-permute-done.10.b, f32[8,128]{1,0:T(8,128)S(1)} %get-tuple-element.87.after), custom_call_target="tpu_custom_call" | custom-call | flops 1 | bytes 1 | tf_op jit(solution)/shard_map/merge/pallas_call | solution.py:357
  (6 shorter events, 0.0 us)
Async XLA Ops:
  1.8 21.4 %collective-permute-start.1 = (bf16[512,256]{1,0:T(8,128)(2,1)S(1)}, bf16[512,256]{1,0:T(8,128)(2,1)S(1)}, u32[]{:S(2)}, u32[]{:S(2)}) collective-permute-start(bf16[512,256]{1,0:T(8,128)(2,1)S(1)} %get-tuple-element.49.kv_ref.refs_0_), channel_id=1, source_target_pairs={{0,8},{1,9},{2,10},{3,11},{16,24},{17,25},{18,26},{19,27}} | collective-permute-start | bytes 786440 | tf_op jit(solution)/shard_map/ppermute | solution.py:397
  2.5 13.2 %collective-permute-start.4 = (bf16[16,2048]{1,0:T(8,128)(2,1)}, bf16[16,2048]{1,0:T(8,128)(2,1)S(1)}, u32[]{:S(2)}, u32[]{:S(2)}) collective-permute-start(bf16[16,2048]{1,0:T(8,128)(2,1)} %refs_4_), channel_id=1, source_target_pairs={{0,12},{4,8},{8,4},{12,0},{1,13},{5,9},{9,5},{13,1},{2,14},{6,10},... | collective-permute-start | bytes 196616 | tf_op jit(solution)/shard_map/ppermute | solution.py:369
  4.7 16.4 %collective-permute-start.3 = (bf16[16,2048]{1,0:T(8,128)(2,1)}, bf16[16,2048]{1,0:T(8,128)(2,1)S(1)}, u32[]{:S(2)}, u32[]{:S(2)}) collective-permute-start(bf16[16,2048]{1,0:T(8,128)(2,1)} %refs_4_), channel_id=1, source_target_pairs={{0,8},{4,12},{8,0},{12,4},{1,9},{5,13},{9,1},{13,5},{2,10},{6,14},... | collective-permute-start | bytes 196616 | tf_op jit(solution)/shard_map/ppermute | solution.py:369
  9.2 11.9 %collective-permute-start.2 = (bf16[16,2048]{1,0:T(8,128)(2,1)}, bf16[16,2048]{1,0:T(8,128)(2,1)S(1)}, u32[]{:S(2)}, u32[]{:S(2)}) collective-permute-start(bf16[16,2048]{1,0:T(8,128)(2,1)} %refs_4_), channel_id=1, source_target_pairs={{0,4},{4,0},{8,12},{12,8},{1,5},{5,1},{9,13},{13,9},{2,6},{6,2},{1... | collective-permute-start | bytes 196616 | tf_op jit(solution)/shard_map/ppermute | solution.py:369
  13.1 14.4 %collective-permute-start = (bf16[512,256]{1,0:T(8,128)(2,1)S(1)}, bf16[512,256]{1,0:T(8,128)(2,1)S(1)}, u32[]{:S(2)}, u32[]{:S(2)}) collective-permute-start(bf16[512,256]{1,0:T(8,128)(2,1)S(1)} %get-tuple-element.65.refs_1_.kv_ref), channel_id=1, source_target_pairs={{0,8},{1,9},{2,10},{3,11},{16,24},{17,25},{18,26},{19,27}} | collective-permute-start | bytes 786440 | tf_op jit(solution)/shard_map/ppermute | solution.py:399
  23.1 17.4 %collective-permute-start.9 = (bf16[64,2176]{1,0:T(8,128)(2,1)S(1)}, bf16[64,2176]{1,0:T(8,128)(2,1)S(1)}, u32[]{:S(2)}, u32[]{:S(2)}) collective-permute-start(bf16[64,2176]{1,0:T(8,128)(2,1)S(1)} %get-tuple-element.83), channel_id=1, source_target_pairs={{0,4},{4,0},{8,12},{12,8},{1,5},{5,1},{9,13},{13,9},{2,6},{6,2},{1... | collective-permute-start | bytes 835592 | tf_op jit(solution)/shard_map/ppermute | solution.py:369
  23.2 6.3 %collective-permute-start.8 = (bf16[512,256]{1,0:T(8,128)(2,1)S(1)}, bf16[512,256]{1,0:T(8,128)(2,1)S(1)}, u32[]{:S(2)}, u32[]{:S(2)}) collective-permute-start(bf16[512,256]{1,0:T(8,128)(2,1)S(1)} %collective-permute-done.1.refs_1_), channel_id=1, source_target_pairs={{8,12},{9,13},{10,14},{11,15},{24,28},{25,29},{26,30},{27,31}} | collective-permute-start | bytes 786440 | tf_op jit(solution)/shard_map/ppermute | solution.py:402
  23.9 12.4 %collective-permute-start.7 = (bf16[512,256]{1,0:T(8,128)(2,1)S(1)}, bf16[512,256]{1,0:T(8,128)(2,1)S(1)}, u32[]{:S(2)}, u32[]{:S(2)}) collective-permute-start(bf16[512,256]{1,0:T(8,128)(2,1)S(1)} %collective-permute-done.1.refs_1_), channel_id=1, source_target_pairs={{8,4},{9,5},{10,6},{11,7},{24,20},{25,21},{26,22},{27,23}} | collective-permute-start | bytes 786440 | tf_op jit(solution)/shard_map/ppermute | solution.py:402
  27.5 19.2 %collective-permute-start.6 = (bf16[512,256]{1,0:T(8,128)(2,1)S(1)}, bf16[512,256]{1,0:T(8,128)(2,1)S(1)}, u32[]{:S(2)}, u32[]{:S(2)}) collective-permute-start(bf16[512,256]{1,0:T(8,128)(2,1)S(1)} %collective-permute-done.refs_1_), channel_id=1, source_target_pairs={{8,12},{9,13},{10,14},{11,15},{24,28},{25,29},{26,30},{27,31}} | collective-permute-start | bytes 786440 | tf_op jit(solution)/shard_map/ppermute | solution.py:402
  28.2 18.5 %collective-permute-start.5 = (bf16[512,256]{1,0:T(8,128)(2,1)S(1)}, bf16[512,256]{1,0:T(8,128)(2,1)S(1)}, u32[]{:S(2)}, u32[]{:S(2)}) collective-permute-start(bf16[512,256]{1,0:T(8,128)(2,1)S(1)} %collective-permute-done.refs_1_), channel_id=1, source_target_pairs={{8,4},{9,5},{10,6},{11,7},{24,20},{25,21},{26,22},{27,23}} | collective-permute-start | bytes 786440 | tf_op jit(solution)/shard_map/ppermute | solution.py:402
  41.1 9.9 %collective-permute-start.10 = (bf16[32,2176]{1,0:T(8,128)(2,1)S(1)}, bf16[32,2176]{1,0:T(8,128)(2,1)S(1)}, u32[]{:S(2)}, u32[]{:S(2)}) collective-permute-start(bf16[32,2176]{1,0:T(8,128)(2,1)S(1)} %get-tuple-element.86), channel_id=1, source_target_pairs={{0,8},{4,12},{8,0},{12,4},{1,9},{5,13},{9,1},{13,5},{2,10},{6,14},... | collective-permute-start | bytes 417800 | tf_op jit(solution)/shard_map/ppermute | solution.py:369

commit v9 on v8

--- a/solution.py
+++ b/solution.py
@@ -91,21 +91,8 @@
     return slice(h * HD, (h + 1) * HD)
 
 
-def local_kernel(g, loads, kv_ref, *refs):
-    ins = max(loads, 1)
-    sources, (acc_ref, top_ref, sum_ref) = refs[:ins], refs[ins : ins + 3]
-    held, ve = refs[ins + 3 : ins + 3 + loads] or sources, refs[ins + 3 + loads]
-    q_ref, rows = held[0], kv_ref.shape[0]
-    queries, others = {}, []
-    if loads:
-        sem = refs[-1]
-        order = list(range(g * GROUP, g * GROUP + GROUP)) + [h for h in range(q_ref.shape[1] // HD) if h // GROUP != g]
-        spots = [slice(h * HD, (h + PAIR) * HD) for h in order[::PAIR]]
-        copies = [(sources[0].at[:, spot], q_ref.at[:, spot]) for spot in spots]
-        copies += list(zip(sources[1:], held[1:]))
-        copies = start_all(copies, sem)
-        queries = dict(zip(order[:GROUP:PAIR], copies))
-        others = copies[GROUP // PAIR :]
+def local_pass(g, q_ref, kv_ref, ve, arrived, emit):
+    rows = kv_ref.shape[0]
     ve[:, :HD] = kv_ref[:, HD:]
     ve[:, HD:] = jnp.ones((rows, HD), jnp.bfloat16)
     row = lax.broadcasted_iota(jnp.int32, (PAIR * TILE, TILE), 0)
@@ -113,8 +100,8 @@
 
     def scores(task):
         first, at = task
-        if at == 0 and loads:
-            queries[g * GROUP + first].wait()
+        if at == 0:
+            arrived(first)
         q = jnp.concatenate([q_ref[at : at + TILE, head_columns(g * GROUP + first + j)] for j in range(PAIR)], axis=0)
         parts = [nt(q, kv_ref[:at, :HD])] if at else []
         parts.append(jnp.where(seen, nt(q, kv_ref[at : at + TILE, :HD]), NEG))
@@ -128,38 +115,76 @@
             p = jnp.exp2((s - top) * C2).astype(jnp.bfloat16)
             part = nn(p, ve[start : start + s.shape[1], :])
             total = part if total is None else total + part
-        top = jnp.broadcast_to(top * C2, (PAIR * TILE, HD))
         for j in range(PAIR):
-            here, at_j = (slice(at, at + TILE), head_columns(first + j)), slice(j * TILE, (j + 1) * TILE)
-            acc_ref[here] = total[at_j, :HD]
-            sum_ref[here] = total[at_j, HD:]
-            top_ref[here] = top[at_j]
+            mine = slice(j * TILE, (j + 1) * TILE)
+            emit(slice(at, at + TILE), first + j, total[mine, :HD], total[mine, HD:], top[mine] * C2)
 
     pipelined([(h, at) for h in range(0, GROUP, PAIR) for at in range(0, rows, TILE)], scores, finish)
+
+
+def local_kernel(g, loads, joined, blk_ref, kv_ref, *refs):
+    ins = max(loads + joined, 1)
+    sources, (acc_ref, top_ref, sum_ref) = refs[:ins], refs[ins : ins + 3]
+    held = refs[ins + 3 : ins + 3 + loads + (joined > 0)] or sources
+    ve = refs[ins + 3 + loads + (joined > 0)]
+    q_ref, queries, others = held[0], {}, []
+    if loads:
+        order = list(range(g * GROUP, g * GROUP + GROUP)) + [h for h in range(q_ref.shape[1] // HD) if h // GROUP != g]
+        spots = [slice(h * HD, (h + PAIR) * HD) for h in order[::PAIR]]
+        copies = [(sources[0].at[:, spot], q_ref.at[:, spot]) for spot in spots]
+        copies += list(zip(sources[1:loads], held[1:loads]))
+        each = sources[loads].shape[0]
+        copies += [(x, held[loads].at[i * each : (i + 1) * each]) for i, x in enumerate(sources[loads:])]
+        copies = start_all(copies, refs[-1])
+        queries = dict(zip(range(0, GROUP, PAIR), copies))
+        others = copies[GROUP // PAIR :]
+
+    def arrived(first):
+        if loads:
+            queries[first].wait()
+
+    def emit(rows, h, total, z, top):
+        here = (rows, head_columns(h))
+        acc_ref[here], sum_ref[here], top_ref[here] = total, z, jnp.broadcast_to(top, total.shape)
+
+    @pl.when(blk_ref[0] > 0)
+    def _():
+        local_pass(g, q_ref, kv_ref, ve, arrived, emit)
+
+    @pl.when(blk_ref[0] == 0)
+    def _():
+        for copy in queries.values():
+            copy.wait()
+
     for copy in others:
         copy.wait()
 
 
-def local_attention(kv, g, query, loads=()):
+def local_attention(blk, kv, g, query, loads=(), joined=()):
     rows = kv.shape[0]
-    sources = [in_hbm(x) for x in (query, *loads)] if loads else [query]
-    held = [pltpu.VMEM(x.shape, x.dtype) for x in sources] if loads else []
-    count = len(held)
+    sources, held = [query], []
+    if loads:
+        sources = [in_hbm(x) for x in (query, *loads)]
+        height, width = joined[0].shape
+        held = [pltpu.VMEM(x.shape, x.dtype) for x in sources]
+        held.append(pltpu.VMEM((len(joined) * height, width), joined[0].dtype))
+        sources += [in_hbm(joined[0]), *joined[1:]]
+    semaphores = query.shape[1] // HD // PAIR + len(loads) + len(joined)
     outs = pl.pallas_call(
-        functools.partial(local_kernel, g, count),
+        functools.partial(local_kernel, g, len(loads) + 1 if loads else 0, len(joined)),
         out_shape=[pltpu.VMEM((rows, GROUP * HD), jnp.float32)] * 3 + held,
-        in_specs=[VMEM] + [HBM if loads else VMEM] * len(sources),
-        out_specs=[VMEM] * (3 + count),
+        in_specs=[SMEM, VMEM] + ([HBM] * (len(loads) + 1) + [ANY] * len(joined) if loads else [VMEM]),
+        out_specs=[VMEM] * (3 + len(held)),
         scratch_shapes=[pltpu.VMEM((rows, 2 * HD), jnp.bfloat16)]
-        + ([pltpu.SemaphoreType.DMA((query.shape[1] // HD // PAIR + len(loads),))] if loads else []),
+        + ([pltpu.SemaphoreType.DMA((semaphores,))] if loads else []),
         compiler_params=params(6),
-        cost_estimate=LONG if loads else BRIEF,
+        cost_estimate=LONG,
         name="local_attention",
-    )(kv, *sources)
+    )(blk, kv, *sources)
     return list(outs[:3]), list(outs[3:])
 
 
-def anchor_kernel(g, count, prior, blk_ref, q_ref, acc_ref, top_ref, sum_ref, *refs):
+def anchor_kernel(g, count, prior, blk_ref, q_ref, kv_ref, acc_ref, top_ref, sum_ref, *refs):
     cand, (o_ref, token, ka, vae, out, sem) = refs[:count], refs[count + prior :]
     rows = q_ref.shape[0]
     blk = blk_ref[0]
@@ -171,13 +196,6 @@
     def take(ref):
         ka[...] = ref[:, :HD]
         vae[:, :HD] = ref[:, HD:]
-
-    if count == 1:
-        take(cand[0])
-    else:
-        pl.when(blk == 1)(lambda: take(cand[0]))
-        pl.when(blk == 2)(lambda: take(cand[1]))
-        pl.when(blk == 3)(lambda: take(cand[2]))
 
     def scores(h):
         return nt(q_ref[:, head_columns(g * GROUP + h)], ka[...])
@@ -195,15 +213,22 @@
 
     @pl.when(blk > 0)
     def _():
+        if count == 1:
+            take(cand[0])
+        else:
+            for i, ref in enumerate(cand):
+                pl.when(blk == i + 1)(functools.partial(take, ref))
         vae[:, HD:] = jnp.ones((rows, HD), jnp.bfloat16)
         pipelined(list(range(GROUP)), scores, finish)
 
+    def emit(here, h, total, z, top):
+        out[h, here, :] = (total * inverse(z)).astype(jnp.bfloat16)
+        if here.stop == rows:
+            leave(h).start()
+
     @pl.when(blk == 0)
     def _():
-        for h in range(GROUP):
-            held = (slice(None), head_columns(h))
-            out[h] = (acc_ref[held] * inverse(sum_ref[held])).astype(jnp.bfloat16)
-            leave(h).start()
+        local_pass(g, q_ref, kv_ref, vae, lambda first: None, emit)
 
     for h in range(GROUP):
         leave(h).wait()
@@ -214,10 +239,10 @@
     return guess * (2.0 - x * guess)
 
 
-def anchor_attention(blk, query, state, cands, g, prior):
+def anchor_attention(blk, query, kv, state, cands, g, prior):
     rows = query.shape[0]
-    args = [blk, query, *state, *cands]
-    specs = [SMEM] + [VMEM] * (4 + len(cands))
+    args = [blk, query, kv, *state, *cands]
+    specs = [SMEM] + [VMEM] * (5 + len(cands))
     alias = {}
     if prior is not None:
         alias = {len(args): 0}
@@ -236,7 +261,7 @@
         ],
         input_output_aliases=alias,
         compiler_params=params(6),
-        cost_estimate=BRIEF,
+        cost_estimate=LONG,
         name="anchor_attention",
     )(*args)
 
@@ -246,17 +271,19 @@
     return sorted(range(n), key=lambda x: int(format(x, "0%db" % bits)[::-1], 2))
 
 
-def option_kernel(n, heads, blk_ref, owner_ref, slot_ref, length_ref, *refs):
+def option_kernel(masks, heads, blk_ref, owner_ref, slot_ref, length_ref, *refs):
+    n = len(masks)
     kv_heads = heads // GROUP
-    kv, queries = refs[:kv_heads], refs[kv_heads : kv_heads + n]
-    keep, send, q_all, part = refs[kv_heads + n + 1 :]
+    kv, queries = refs[:kv_heads], refs[kv_heads : kv_heads + 2]
+    keep, send, q_all, part = refs[kv_heads + 3 :]
     blk = blk_ref[0]
     rows = kv[0].shape[0]
-    each = queries[0].shape[0]
-    options = n * each
-    for mask, query in enumerate(queries):
+    half = queries[0].shape[0]
+    options, each = 2 * half, 2 * half // n
+    for i, mask in enumerate(masks):
         at = jnp.bitwise_xor(blk, mask) * each
-        q_all[pl.ds(pl.multiple_of(at, each), each), :] = query[...]
+        here = queries[i * each // half].at[i * each % half : i * each % half + each]
+        q_all[pl.ds(pl.multiple_of(at, each), each), :] = here[...]
     eye = lax.broadcasted_iota(jnp.int32, (options, options), 0) == lax.broadcasted_iota(jnp.int32, (options, options), 1)
     length = jnp.sum(jnp.where(eye, length_ref[...].astype(jnp.float32), 0.0), axis=1, keepdims=True)
     seen = length - (blk * rows).astype(jnp.float32)
@@ -301,22 +328,22 @@
     return jnp.where(lane < heads, high, jnp.where(lane < 2 * heads, mid, low)).astype(jnp.bfloat16)
 
 
-def option_partials(blk, owner, slot, length, kvs, queries, after):
-    n, heads = len(queries), queries[0].shape[1] // HD
-    options = n * queries[0].shape[0]
+def option_partials(blk, owner, slot, length, kvs, masks, queries, after):
+    n, heads = len(masks), queries[0].shape[1] // HD
+    options = 2 * queries[0].shape[0]
     width = (heads + 1) * HD
     rows = kvs[0].shape[0]
     return pl.pallas_call(
-        functools.partial(option_kernel, n, heads),
+        functools.partial(option_kernel, masks, heads),
         out_shape=[jax.ShapeDtypeStruct((n // 2 * CAP, width), jnp.bfloat16)] * 2,
-        in_specs=[SMEM] + [VMEM] * (3 + len(kvs) + n) + [ANY],
+        in_specs=[SMEM] + [VMEM] * (5 + len(kvs)) + [ANY],
         out_specs=[VMEM] * 2,
         scratch_shapes=[
             pltpu.VMEM((options, heads * HD), jnp.bfloat16),
             pltpu.VMEM((options, width), jnp.bfloat16),
         ],
         compiler_params=params(4 + options // 32),
-        cost_estimate=LONG,
+        cost_estimate=BRIEF,
         name="option_partials",
     )(blk, owner, slot, length, *kvs, *queries, after)
 
@@ -384,32 +411,34 @@
     row = lambda x: x.reshape(1, options)
 
     blk_arr, ctx_key = hold((blk_arr, ctx_key))
+    masks, shards = [0], [opt_query]
+    for bit in reversed(range(1, rounds)):
+        mine = shards[0] if len(shards) == 1 else jnp.concatenate(shards, axis=0)
+        shards = [mine, swap(mine, n, 1 << bit)]
+        masks = masks + [mask | 1 << bit for mask in masks]
+    masks = masks + [mask | 1 for mask in masks]
     kvs = parts(ctx_key, ctx_value)
-    kvs, opt_query = hold((kvs, opt_query))
-    queries = [opt_query] + [swap(opt_query, n, mask) for mask in range(1, n)]
-    state, (ctx_query, *smalls, queries[0]) = local_attention(
-        kvs[0], 0, ctx_query, [row(opt_owner), row(opt_slot), row(opt_length), opt_query]
-    )
-    states = [state]
-    keep, send = option_partials(blk_arr, *smalls, kvs, queries, state[1])
     if n == 4:
-        anchors = []
         first = [lax.ppermute(kvs[0], "blk", [(0, 2)])]
-        kvs, states = hold((kvs, states))
+    small = [row(opt_owner), row(opt_slot), row(opt_length)]
+    state, (ctx_query, *small, mine) = local_attention(blk_arr, kvs[0], 0, ctx_query, small, shards)
+    queries = [mine, swap(mine, n, 1)]
+    kvs, states = hold((kvs, [state]))
+    if n == 4:
         first += [lax.ppermute(kv, "blk", [(0, 2)]) for kv in kvs[1:]]
-        first[0], keep, kvs = hold((first[0], keep, kvs))
-        for g, got in enumerate(first):
-            anchors.append([lax.ppermute(got, "blk", [(2, 1)]), got, lax.ppermute(got, "blk", [(2, 3)])])
-            if g + 1 < len(kvs):
-                states.append(local_attention(kvs[g + 1], g + 1, ctx_query)[0])
-                first[g + 1], states = hold((first[g + 1], states))
+    states += [local_attention(blk_arr, kv, g, ctx_query)[0] for g, kv in enumerate(kvs) if g]
+    if n == 4:
+        first[0], queries, states = hold((first[0], queries, states))
+    keep, send = option_partials(blk_arr, *small, kvs, masks, queries, states[-1][1])
+    if n == 4:
+        first[1:], keep = hold((first[1:], keep))
+        anchors = [[lax.ppermute(x, "blk", [(2, 1)]), x, lax.ppermute(x, "blk", [(2, 3)])] for x in first]
         anchors[0], first = hold((anchors[0], first))
     else:
-        states += [local_attention(kv, g, ctx_query)[0] for g, kv in enumerate(kvs) if g]
         anchors = [[from_root(kv, blk)] for kv in kvs]
     ctx_out, tokens = None, []
     for g, state in enumerate(states):
-        ctx_out, token = anchor_attention(blk_arr, ctx_query, state, anchors[g], g, ctx_out)
+        ctx_out, token = anchor_attention(blk_arr, ctx_query, kvs[g], state, anchors[g], g, ctx_out)
         tokens.append(token)
     for bit in range(rounds):
         got = swap(send, n, 1 << bit)

time: 52.2 us -> 43.7 us (0.84)
  the two profiles are of different devices: /device:TPU:12 before, /device:TPU:0 now
where the time goes in v9:
time: 43.7 us; the launch traced here: 43.5 us
  starting transfers between devices  24.7 us (57%)
  Pallas kernels  12.6 us (29%)
  waiting for transfers between devices  5.5 us (13%)
  between operations  0.77 us (2%)
    ppermute x4, starting transfers between devices, swap(): return lax.ppermute(x, 'blk', [(i, i ^ mask) for i in range(n)])  14.8 us
    pallas_call x2, Pallas kernels, anchor_attention(): pl.pallas_call(functools.partial(anchor_kernel, g, len(cands), len(alias)...  6.2 us
    ppermute x1, starting transfers between devices, body(): first += [lax.ppermute(kv, 'blk', [(0, 2)]) for kv in kvs[1:]]  5.18 us
    ppermute x4, waiting for transfers between devices, swap(): return lax.ppermute(x, 'blk', [(i, i ^ mask) for i in range(n)])  3.14 us
    ppermute x1, waiting for transfers between devices, body(): first += [lax.ppermute(kv, 'blk', [(0, 2)]) for kv in kvs[1:]]  2.35 us
    pallas_call x1, Pallas kernels, option_partials(): pl.pallas_call(functools.partial(option_kernel, masks, heads), out_shape=...  2.03 us
    ppermute x1, starting transfers between devices, body(): first = [lax.ppermute(kvs[0], 'blk', [(0, 2)])]  1.94 us
    pallas_call x2, Pallas kernels, local_attention(): pl.pallas_call(functools.partial(local_kernel, g, len(loads) + 1 if loads...  1.66 us
  transfers between devices with their start and end apart: 10, of which 3 were waited for; matrix products, arithmetic and copies ran while one was open for 0% of the time, Pallas kernels for 27%

profile of v9, /device:TPU:0, one launch (start us, length us, event | category | flops | bytes accessed | tf_op | source)
XLA Modules:
  0.0 43.5 jit_solution(16997554299634271519)
XLA Ops:
  0.6 4.1 %collective-permute-start = (bf16[16,2048]{1,0:T(8,128)(2,1)}, bf16[16,2048]{1,0:T(8,128)(2,1)S(1)}, u32[]{:S(2)}, u32[]{:S(2)}) collective-permute-start(bf16[16,2048]{1,0:T(8,128)(2,1)} %refs_4_.1), channel_id=1, source_target_pairs={{0,8},{4,12},{8,0},{12,4},{1,9},{5,13},{9,1},{13,5},{2,10},{6,14},... | collective-permute-start | bytes 196616 | tf_op jit(solution)/shard_map/ppermute | solution.py:396
  4.7 1.1 %parts.1 = (bf16[512,256]{1,0:T(8,128)(2,1)S(1)}, bf16[512,256]{1,0:T(8,128)(2,1)S(1)}) custom-call(bf16[512,256]{1,0:T(8,128)(2,1)} %k_ref, bf16[512,256]{1,0:T(8,128)(2,1)} %v_ref.1), custom_call_target="tpu_custom_call" | custom-call | flops 1 | bytes 1 | tf_op jit(solution)/shard_map/parts/pallas_call | solution.py:68
  5.9 1.9 %collective-permute-start.1 = (bf16[512,256]{1,0:T(8,128)(2,1)S(1)}, bf16[512,256]{1,0:T(8,128)(2,1)S(1)}, u32[]{:S(2)}, u32[]{:S(2)}) collective-permute-start(bf16[512,256]{1,0:T(8,128)(2,1)S(1)} %get-tuple-element.66.kv_ref.refs_0_), channel_id=1, source_target_pairs={{0,8},{1,9},{2,10},{3,11},{16,24},{17,25},{18,26},{19,27}} | collective-permute-start | bytes 786440 | tf_op jit(solution)/shard_map/ppermute | solution.py:422
  7.8 0.8 %collective-permute-done.refs_5_ = bf16[16,2048]{1,0:T(8,128)(2,1)S(1)} collective-permute-done((bf16[16,2048]{1,0:T(8,128)(2,1)}, bf16[16,2048]{1,0:T(8,128)(2,1)S(1)}, u32[]{:S(2)}, u32[]{:S(2)}) %collective-permute-start) | collective-permute-done | bytes 65568 | tf_op jit(solution)/shard_map/ppermute | solution.py:396
  8.6 1.7 %local_attention.2 = (f32[512,1024]{1,0:T(8,128)S(1)}, f32[512,1024]{1,0:T(8,128)S(1)}, f32[512,1024]{1,0:T(8,128)S(1)}, bf16[512,2048]{1,0:T(8,128)(2,1)S(1)}, ...) custom-call(s32[1]{0:T(128)} %bitcast.blk_ref, ...), custom_call_target="tpu_custom_call" | custom-call | flops 1000000000 | bytes 1 | tf_op jit(solution)/shard_map/local_attention/pallas_call | solution.py:173
  10.3 3.0 %collective-permute-start.2 = (bf16[32,2048]{1,0:T(8,128)(2,1)S(1)}, bf16[32,2048]{1,0:T(8,128)(2,1)S(1)}, u32[]{:S(2)}, u32[]{:S(2)}) collective-permute-start(bf16[32,2048]{1,0:T(8,128)(2,1)S(1)} %get-tuple-element.67.refs_2_), channel_id=1, source_target_pairs={{0,4},{4,0},{8,12},{12,8},{1,5},{5,1},{9,13},{13,9},{2,6},{6,2},{1... | collective-permute-start | bytes 393224 | tf_op jit(solution)/shard_map/ppermute | solution.py:396
  13.2 5.2 %collective-permute-start.3 = (bf16[512,256]{1,0:T(8,128)(2,1)S(1)}, bf16[512,256]{1,0:T(8,128)(2,1)S(1)}, u32[]{:S(2)}, u32[]{:S(2)}) collective-permute-start(bf16[512,256]{1,0:T(8,128)(2,1)S(1)} %get-tuple-element.52.kv_ref.refs_1_), channel_id=1, source_target_pairs={{0,8},{1,9},{2,10},{3,11},{16,24},{17,25},{18,26},{19,27}} | collective-permute-start | bytes 786440 | tf_op jit(solution)/shard_map/ppermute | solution.py:428
  18.5 0.0 collective-permute-done.2.refs_3_
  18.5 0.0 collective-permute-done.1.refs_1_
  18.5 0.7 %collective-permute-start.7 = (bf16[512,256]{1,0:T(8,128)(2,1)S(1)}, bf16[512,256]{1,0:T(8,128)(2,1)S(1)}, u32[]{:S(2)}, u32[]{:S(2)}) collective-permute-start(bf16[512,256]{1,0:T(8,128)(2,1)S(1)} %collective-permute-done.1.refs_1_), channel_id=1, source_target_pairs={{8,12},{9,13},{10,14},{11,15},{24,28},{25,29},{26,30},{27,31}} | collective-permute-start | bytes 786440 | tf_op jit(solution)/shard_map/ppermute | solution.py:435
  19.2 0.7 %collective-permute-start.6 = (bf16[512,256]{1,0:T(8,128)(2,1)S(1)}, bf16[512,256]{1,0:T(8,128)(2,1)S(1)}, u32[]{:S(2)}, u32[]{:S(2)}) collective-permute-start(bf16[512,256]{1,0:T(8,128)(2,1)S(1)} %collective-permute-done.1.refs_1_), channel_id=1, source_target_pairs={{8,4},{9,5},{10,6},{11,7},{24,20},{25,21},{26,22},{27,23}} | collective-permute-start | bytes 786440 | tf_op jit(solution)/shard_map/ppermute | solution.py:435
  19.8 2.0 %option_partials.1 = (bf16[64,2176]{1,0:T(8,128)(2,1)S(1)}, bf16[64,2176]{1,0:T(8,128)(2,1)S(1)}) custom-call(s32[1]{0:T(128)} %bitcast.blk_ref, s32[1,64]{1,0:T(1,128)S(1)} %get-tuple-element.63.owner_ref, s32[1,64]{1,0:T(1,128)S(1)} %get-tuple-element.64.slot_ref, s32[1,64]{1,0:T(1,128)S(1)} %get-tuple-element.65.length_ref, ...), custom_call_target="tpu_custom_call" | custom-call | flops 1 | bytes 1 | tf_op jit(solution)/shard_map/option_partials/pallas_call | solution.py:336
  21.9 0.8 %collective-permute-start.8 = (bf16[64,2176]{1,0:T(8,128)(2,1)S(1)}, bf16[64,2176]{1,0:T(8,128)(2,1)S(1)}, u32[]{:S(2)}, u32[]{:S(2)}) collective-permute-start(bf16[64,2176]{1,0:T(8,128)(2,1)S(1)} %get-tuple-element.81), channel_id=1, source_target_pairs={{0,4},{4,0},{8,12},{12,8},{1,5},{5,1},{9,13},{13,9},{2,6},{6,2},{1... | collective-permute-start | bytes 835592 | tf_op jit(solution)/shard_map/ppermute | solution.py:396
  22.7 2.3 %collective-permute-done.3.refs_1_ = bf16[512,256]{1,0:T(8,128)(2,1)S(1)} collective-permute-done((bf16[512,256]{1,0:T(8,128)(2,1)S(1)}, bf16[512,256]{1,0:T(8,128)(2,1)S(1)}, u32[]{:S(2)}, u32[]{:S(2)}) %collective-permute-start.3) | collective-permute-done | bytes 262176 | tf_op jit(solution)/shard_map/ppermute | solution.py:428
  25.1 0.7 %collective-permute-start.5 = (bf16[512,256]{1,0:T(8,128)(2,1)S(1)}, bf16[512,256]{1,0:T(8,128)(2,1)S(1)}, u32[]{:S(2)}, u32[]{:S(2)}) collective-permute-start(bf16[512,256]{1,0:T(8,128)(2,1)S(1)} %collective-permute-done.3.refs_1_), channel_id=1, source_target_pairs={{8,12},{9,13},{10,14},{11,15},{24,28},{25,29},{26,30},{27,31}} | collective-permute-start | bytes 786440 | tf_op jit(solution)/shard_map/ppermute | solution.py:435
  25.7 0.7 %collective-permute-start.4 = (bf16[512,256]{1,0:T(8,128)(2,1)S(1)}, bf16[512,256]{1,0:T(8,128)(2,1)S(1)}, u32[]{:S(2)}, u32[]{:S(2)}) collective-permute-start(bf16[512,256]{1,0:T(8,128)(2,1)S(1)} %collective-permute-done.3.refs_1_), channel_id=1, source_target_pairs={{8,4},{9,5},{10,6},{11,7},{24,20},{25,21},{26,22},{27,23}} | collective-permute-start | bytes 786440 | tf_op jit(solution)/shard_map/ppermute | solution.py:435
  26.4 0.0 collective-permute-done.7.refs_2_
  26.4 0.0 collective-permute-done.6.refs_0_
  26.4 3.2 %anchor_attention.2 = (bf16[512,2048]{1,0:T(8,128)(2,1)}, f32[8,128]{1,0:T(8,128)S(1)}) custom-call(s32[1]{0:T(128)} %bitcast.blk_ref, bf16[512,2048]{1,0:T(8,128)(2,1)S(1)} %get-tuple-element.47.refs_0_.q_ref, bf16[512,256]{1,0:T(8,128)(2,1)S(1)} %get-tuple-element.66.kv_ref.refs_0_, f32[512,1024]{1,0:T(8,128)S(1)} %get-tuple-element.71.acc_ref, ...), custom_call_target="tpu_custom_call" | custom-call | flops 1000000000 | bytes 1 | tf_op jit(solution)/shard_map/anchor_attention/pallas_call | solution.py:251
  29.7 0.6 %merge.2 = (bf16[32,2176]{1,0:T(8,128)(2,1)S(1)}, bf16[32,2176]{1,0:T(8,128)(2,1)S(1)}) custom-call(bf16[64,2176]{1,0:T(8,128)(2,1)S(1)} %get-tuple-element.80.a, bf16[64,2176]{1,0:T(8,128)(2,1)S(1)} %collective-permute-done.8.b, f32[8,128]{1,0:T(8,128)S(1)} %get-tuple-element.82.after), custom_call_target="tpu_custom_call" | custom-call | flops 1 | bytes 1 | tf_op jit(solution)/shard_map/merge/pallas_call | solution.py:384
  30.2 6.9 %collective-permute-start.9 = (bf16[32,2176]{1,0:T(8,128)(2,1)S(1)}, bf16[32,2176]{1,0:T(8,128)(2,1)S(1)}, u32[]{:S(2)}, u32[]{:S(2)}) collective-permute-start(bf16[32,2176]{1,0:T(8,128)(2,1)S(1)} %get-tuple-element.84), channel_id=1, source_target_pairs={{0,8},{4,12},{8,0},{12,4},{1,9},{5,13},{9,1},{13,5},{2,10},{6,14},... | collective-permute-start | bytes 417800 | tf_op jit(solution)/shard_map/ppermute | solution.py:396
  37.1 3.0 %anchor_attention.3 = (bf16[512,2048]{1,0:T(8,128)(2,1)}, f32[8,128]{1,0:T(8,128)S(1)}) custom-call(s32[1]{0:T(128)} %bitcast.blk_ref, bf16[512,2048]{1,0:T(8,128)(2,1)S(1)} %get-tuple-element.47.refs_0_.q_ref, bf16[512,256]{1,0:T(8,128)(2,1)S(1)} %get-tuple-element.52.kv_ref.refs_1_, ...), custom_call_target="tpu_custom_call", output_to_operand_aliasing={{0}: (9, {})} | custom-call | flops 1000000000 | bytes 1 | tf_op jit(solution)/shard_map/anchor_attention/pallas_call | solution.py:251
  40.1 2.4 %collective-permute-done.9.b = bf16[32,2176]{1,0:T(8,128)(2,1)S(1)} collective-permute-done((bf16[32,2176]{1,0:T(8,128)(2,1)S(1)}, bf16[32,2176]{1,0:T(8,128)(2,1)S(1)}, u32[]{:S(2)}, u32[]{:S(2)}) %collective-permute-start.9) | collective-permute-done | bytes 139296 | tf_op jit(solution)/shard_map/ppermute | solution.py:396
  42.5 1.0 %merge.3 = bf16[32,2048]{1,0:T(8,128)(2,1)} custom-call(bf16[32,2176]{1,0:T(8,128)(2,1)S(1)} %get-tuple-element.83.a, bf16[32,2176]{1,0:T(8,128)(2,1)S(1)} %collective-permute-done.9.b, f32[8,128]{1,0:T(8,128)S(1)} %get-tuple-element.85.after), custom_call_target="tpu_custom_call" | custom-call | flops 1 | bytes 1 | tf_op jit(solution)/shard_map/merge/pallas_call | solution.py:384
  (4 shorter events, 0.0 us)
Async XLA Ops:
  0.6 8.0 %collective-permute-start = (bf16[16,2048]{1,0:T(8,128)(2,1)}, bf16[16,2048]{1,0:T(8,128)(2,1)S(1)}, u32[]{:S(2)}, u32[]{:S(2)}) collective-permute-start(bf16[16,2048]{1,0:T(8,128)(2,1)} %refs_4_.1), channel_id=1, source_target_pairs={{0,8},{4,12},{8,0},{12,4},{1,9},{5,13},{9,1},{13,5},{2,10},{6,14},... | collective-permute-start | bytes 196616 | tf_op jit(solution)/shard_map/ppermute | solution.py:396
  5.9 12.6 %collective-permute-start.1 = (bf16[512,256]{1,0:T(8,128)(2,1)S(1)}, bf16[512,256]{1,0:T(8,128)(2,1)S(1)}, u32[]{:S(2)}, u32[]{:S(2)}) collective-permute-start(bf16[512,256]{1,0:T(8,128)(2,1)S(1)} %get-tuple-element.66.kv_ref.refs_0_), channel_id=1, source_target_pairs={{0,8},{1,9},{2,10},{3,11},{16,24},{17,25},{18,26},{19,27}} | collective-permute-start | bytes 786440 | tf_op jit(solution)/shard_map/ppermute | solution.py:422
  10.3 8.2 %collective-permute-start.2 = (bf16[32,2048]{1,0:T(8,128)(2,1)S(1)}, bf16[32,2048]{1,0:T(8,128)(2,1)S(1)}, u32[]{:S(2)}, u32[]{:S(2)}) collective-permute-start(bf16[32,2048]{1,0:T(8,128)(2,1)S(1)} %get-tuple-element.67.refs_2_), channel_id=1, source_target_pairs={{0,4},{4,0},{8,12},{12,8},{1,5},{5,1},{9,13},{13,9},{2,6},{6,2},{1... | collective-permute-start | bytes 393224 | tf_op jit(solution)/shard_map/ppermute | solution.py:396
  13.2 11.8 %collective-permute-start.3 = (bf16[512,256]{1,0:T(8,128)(2,1)S(1)}, bf16[512,256]{1,0:T(8,128)(2,1)S(1)}, u32[]{:S(2)}, u32[]{:S(2)}) collective-permute-start(bf16[512,256]{1,0:T(8,128)(2,1)S(1)} %get-tuple-element.52.kv_ref.refs_1_), channel_id=1, source_target_pairs={{0,8},{1,9},{2,10},{3,11},{16,24},{17,25},{18,26},{19,27}} | collective-permute-start | bytes 786440 | tf_op jit(solution)/shard_map/ppermute | solution.py:428
  18.5 8.0 %collective-permute-start.7 = (bf16[512,256]{1,0:T(8,128)(2,1)S(1)}, bf16[512,256]{1,0:T(8,128)(2,1)S(1)}, u32[]{:S(2)}, u32[]{:S(2)}) collective-permute-start(bf16[512,256]{1,0:T(8,128)(2,1)S(1)} %collective-permute-done.1.refs_1_), channel_id=1, source_target_pairs={{8,12},{9,13},{10,14},{11,15},{24,28},{25,29},{26,30},{27,31}} | collective-permute-start | bytes 786440 | tf_op jit(solution)/shard_map/ppermute | solution.py:435
  19.2 7.3 %collective-permute-start.6 = (bf16[512,256]{1,0:T(8,128)(2,1)S(1)}, bf16[512,256]{1,0:T(8,128)(2,1)S(1)}, u32[]{:S(2)}, u32[]{:S(2)}) collective-permute-start(bf16[512,256]{1,0:T(8,128)(2,1)S(1)} %collective-permute-done.1.refs_1_), channel_id=1, source_target_pairs={{8,4},{9,5},{10,6},{11,7},{24,20},{25,21},{26,22},{27,23}} | collective-permute-start | bytes 786440 | tf_op jit(solution)/shard_map/ppermute | solution.py:435
  21.9 7.8 %collective-permute-start.8 = (bf16[64,2176]{1,0:T(8,128)(2,1)S(1)}, bf16[64,2176]{1,0:T(8,128)(2,1)S(1)}, u32[]{:S(2)}, u32[]{:S(2)}) collective-permute-start(bf16[64,2176]{1,0:T(8,128)(2,1)S(1)} %get-tuple-element.81), channel_id=1, source_target_pairs={{0,4},{4,0},{8,12},{12,8},{1,5},{5,1},{9,13},{13,9},{2,6},{6,2},{1... | collective-permute-start | bytes 835592 | tf_op jit(solution)/shard_map/ppermute | solution.py:396
  25.1 12.1 %collective-permute-start.5 = (bf16[512,256]{1,0:T(8,128)(2,1)S(1)}, bf16[512,256]{1,0:T(8,128)(2,1)S(1)}, u32[]{:S(2)}, u32[]{:S(2)}) collective-permute-start(bf16[512,256]{1,0:T(8,128)(2,1)S(1)} %collective-permute-done.3.refs_1_), channel_id=1, source_target_pairs={{8,12},{9,13},{10,14},{11,15},{24,28},{25,29},{26,30},{27,31}} | collective-permute-start | bytes 786440 | tf_op jit(solution)/shard_map/ppermute | solution.py:435
  25.7 11.4 %collective-permute-start.4 = (bf16[512,256]{1,0:T(8,128)(2,1)S(1)}, bf16[512,256]{1,0:T(8,128)(2,1)S(1)}, u32[]{:S(2)}, u32[]{:S(2)}) collective-permute-start(bf16[512,256]{1,0:T(8,128)(2,1)S(1)} %collective-permute-done.3.refs_1_), channel_id=1, source_target_pairs={{8,4},{9,5},{10,6},{11,7},{24,20},{25,21},{26,22},{27,23}} | collective-permute-start | bytes 786440 | tf_op jit(solution)/shard_map/ppermute | solution.py:435
  30.2 12.3 %collective-permute-start.9 = (bf16[32,2176]{1,0:T(8,128)(2,1)S(1)}, bf16[32,2176]{1,0:T(8,128)(2,1)S(1)}, u32[]{:S(2)}, u32[]{:S(2)}) collective-permute-start(bf16[32,2176]{1,0:T(8,128)(2,1)S(1)} %get-tuple-element.84), channel_id=1, source_target_pairs={{0,8},{4,12},{8,0},{12,4},{1,9},{5,13},{9,1},{13,5},{2,10},{6,14},... | collective-permute-start | bytes 417800 | tf_op jit(solution)/shard_map/ppermute | solution.py:396

commit v10 on v9

--- a/solution.py
+++ b/solution.py
@@ -22,8 +22,13 @@
 SMEM = pl.BlockSpec(memory_space=pltpu.SMEM)
 HBM = pl.BlockSpec(memory_space=pltpu.HBM)
 ANY = pl.BlockSpec(memory_space=pl.ANY)
-LONG = pl.CostEstimate(flops=10**9, bytes_accessed=1, transcendentals=0)
-BRIEF = pl.CostEstimate(flops=1, bytes_accessed=1, transcendentals=0)
+
+
+def cost(flops):
+    return pl.CostEstimate(flops=flops, bytes_accessed=1, transcendentals=0)
+
+
+BRIEF = cost(1)
 
 
 def nt(a, b):
@@ -178,7 +183,7 @@
         scratch_shapes=[pltpu.VMEM((rows, 2 * HD), jnp.bfloat16)]
         + ([pltpu.SemaphoreType.DMA((semaphores,))] if loads else []),
         compiler_params=params(6),
-        cost_estimate=LONG,
+        cost_estimate=cost(1000000000 if loads else 1000000000),
         name="local_attention",
     )(blk, kv, *sources)
     return list(outs[:3]), list(outs[3:])
@@ -261,7 +266,7 @@
         ],
         input_output_aliases=alias,
         compiler_params=params(6),
-        cost_estimate=LONG,
+        cost_estimate=cost(1000000000),
         name="anchor_attention",
     )(*args)
 
@@ -343,7 +348,7 @@
             pltpu.VMEM((options, width), jnp.bfloat16),
         ],
         compiler_params=params(4 + options // 32),
-        cost_estimate=BRIEF,
+        cost_estimate=cost(1000000000),
         name="option_partials",
     )(blk, owner, slot, length, *kvs, *queries, after)
 
@@ -426,12 +431,12 @@
     kvs, states = hold((kvs, [state]))
     if n == 4:
         first += [lax.ppermute(kv, "blk", [(0, 2)]) for kv in kvs[1:]]
+        first[0], kvs = hold((first[0], kvs))
+    keep, send = option_partials(blk_arr, *small, kvs, masks, queries, state[1])
+    keep, kvs = hold((keep, kvs))
     states += [local_attention(blk_arr, kv, g, ctx_query)[0] for g, kv in enumerate(kvs) if g]
     if n == 4:
-        first[0], queries, states = hold((first[0], queries, states))
-    keep, send = option_partials(blk_arr, *small, kvs, masks, queries, states[-1][1])
-    if n == 4:
-        first[1:], keep = hold((first[1:], keep))
+        first[1:], states = hold((first[1:], states))
         anchors = [[lax.ppermute(x, "blk", [(2, 1)]), x, lax.ppermute(x, "blk", [(2, 3)])] for x in first]
         anchors[0], first = hold((anchors[0], first))
     else:

time: 43.7 us -> 42.7 us (0.977)
  the two profiles are of different devices: /device:TPU:0 before, /device:TPU:12 now
where the time goes in v10:
time: 42.7 us; the launch traced here: 41.9 us
  Pallas kernels  19.4 us (45%)
  starting transfers between devices  13.1 us (31%)
  waiting for transfers between devices  8.57 us (20%)
  between operations  0.78 us (2%)
    pallas_call x2, Pallas kernels, anchor_attention(): pl.pallas_call(functools.partial(anchor_kernel, g, len(cands), len(alias)...  8.51 us
    ppermute x4, starting transfers between devices, swap(): return lax.ppermute(x, 'blk', [(i, i ^ mask) for i in range(n)])  7.82 us
    pallas_call x2, Pallas kernels, local_attention(): pl.pallas_call(functools.partial(local_kernel, g, len(loads) + 1 if loads...  6.21 us
    ppermute x2, waiting for transfers between devices, body(): lax.ppermute(x, 'blk', [(2, 1)])  4.69 us
    ppermute x4, waiting for transfers between devices, swap(): return lax.ppermute(x, 'blk', [(i, i ^ mask) for i in range(n)])  3.86 us
    ppermute x2, starting transfers between devices, body(): lax.ppermute(x, 'blk', [(2, 1)])  2.58 us
    pallas_call x1, Pallas kernels, option_partials(): pl.pallas_call(functools.partial(option_kernel, masks, heads), out_shape=...  2.02 us
    pallas_call x2, Pallas kernels, merge(): pl.pallas_call(functools.partial(merge_kernel, heads), out_shape=shapes,...  1.55 us
  transfers between devices with their start and end apart: 10, of which 3 were waited for; matrix products, arithmetic and copies ran while one was open for 0% of the time, Pallas kernels for 44%

profile of v10, /device:TPU:12, one launch (start us, length us, event | category | flops | bytes accessed | tf_op | source)
XLA Modules:
  0.0 41.9 jit_solution(11710963590928205313)
XLA Ops:
  0.6 2.7 %collective-permute-start = (bf16[16,2048]{1,0:T(8,128)(2,1)}, bf16[16,2048]{1,0:T(8,128)(2,1)S(1)}, u32[]{:S(2)}, u32[]{:S(2)}) collective-permute-start(bf16[16,2048]{1,0:T(8,128)(2,1)} %refs_4_.1), channel_id=1, source_target_pairs={{0,8},{4,12},{8,0},{12,4},{1,9},{5,13},{9,1},{13,5},{2,10},{6,14},... | collective-permute-start | bytes 196616 | tf_op jit(solution)/shard_map/ppermute | solution.py:401
  3.3 1.1 %parts.1 = (bf16[512,256]{1,0:T(8,128)(2,1)S(1)}, bf16[512,256]{1,0:T(8,128)(2,1)S(1)}) custom-call(bf16[512,256]{1,0:T(8,128)(2,1)} %k_ref, bf16[512,256]{1,0:T(8,128)(2,1)} %v_ref.1), custom_call_target="tpu_custom_call" | custom-call | flops 1 | bytes 1 | tf_op jit(solution)/shard_map/parts/pallas_call | solution.py:73
  4.4 0.7 %collective-permute-start.1 = (bf16[512,256]{1,0:T(8,128)(2,1)S(1)}, bf16[512,256]{1,0:T(8,128)(2,1)S(1)}, u32[]{:S(2)}, u32[]{:S(2)}) collective-permute-start(bf16[512,256]{1,0:T(8,128)(2,1)S(1)} %get-tuple-element.74.kv_ref.refs_0_), channel_id=1, source_target_pairs={{0,8},{1,9},{2,10},{3,11},{16,24},{17,25},{18,26},{19,27}} | collective-permute-start | bytes 786440 | tf_op jit(solution)/shard_map/ppermute | solution.py:427
  5.1 1.1 %collective-permute-done.refs_5_ = bf16[16,2048]{1,0:T(8,128)(2,1)S(1)} collective-permute-done((bf16[16,2048]{1,0:T(8,128)(2,1)}, bf16[16,2048]{1,0:T(8,128)(2,1)S(1)}, u32[]{:S(2)}, u32[]{:S(2)}) %collective-permute-start) | collective-permute-done | bytes 65568 | tf_op jit(solution)/shard_map/ppermute | solution.py:401
  6.2 3.9 %local_attention.2 = (f32[512,1024]{1,0:T(8,128)S(1)}, f32[512,1024]{1,0:T(8,128)S(1)}, f32[512,1024]{1,0:T(8,128)S(1)}, bf16[512,2048]{1,0:T(8,128)(2,1)S(1)}, ...) custom-call(s32[1]{0:T(128)} %bitcast.blk_ref, ...), custom_call_target="tpu_custom_call" | custom-call | flops 1000000000 | bytes 1 | tf_op jit(solution)/shard_map/local_attention/pallas_call | solution.py:178
  10.2 0.1 collective-permute-start.2
  10.2 0.7 %collective-permute-start.3 = (bf16[512,256]{1,0:T(8,128)(2,1)S(1)}, bf16[512,256]{1,0:T(8,128)(2,1)S(1)}, u32[]{:S(2)}, u32[]{:S(2)}) collective-permute-start(bf16[512,256]{1,0:T(8,128)(2,1)S(1)} %get-tuple-element.63.refs_1_.kv_ref), channel_id=1, source_target_pairs={{0,8},{1,9},{2,10},{3,11},{16,24},{17,25},{18,26},{19,27}} | collective-permute-start | bytes 786440 | tf_op jit(solution)/shard_map/ppermute | solution.py:433
  10.9 0.7 %collective-permute-start.7 = (bf16[512,256]{1,0:T(8,128)(2,1)S(1)}, bf16[512,256]{1,0:T(8,128)(2,1)S(1)}, u32[]{:S(2)}, u32[]{:S(2)}) collective-permute-start(bf16[512,256]{1,0:T(8,128)(2,1)S(1)} %collective-permute-done.1.refs_1_), channel_id=1, source_target_pairs={{8,12},{9,13},{10,14},{11,15},{24,28},{25,29},{26,30},{27,31}} | collective-permute-start | bytes 786440 | tf_op jit(solution)/shard_map/ppermute | solution.py:440
  11.6 1.3 %collective-permute-start.6 = (bf16[512,256]{1,0:T(8,128)(2,1)S(1)}, bf16[512,256]{1,0:T(8,128)(2,1)S(1)}, u32[]{:S(2)}, u32[]{:S(2)}) collective-permute-start(bf16[512,256]{1,0:T(8,128)(2,1)S(1)} %collective-permute-done.1.refs_1_), channel_id=1, source_target_pairs={{8,4},{9,5},{10,6},{11,7},{24,20},{25,21},{26,22},{27,23}} | collective-permute-start | bytes 786440 | tf_op jit(solution)/shard_map/ppermute | solution.py:440
  12.9 2.7 %collective-permute-done.2.refs_3_ = bf16[32,2048]{1,0:T(8,128)(2,1)S(1)} collective-permute-done((bf16[32,2048]{1,0:T(8,128)(2,1)S(1)}, bf16[32,2048]{1,0:T(8,128)(2,1)S(1)}, u32[]{:S(2)}, u32[]{:S(2)}) %collective-permute-start.2) | collective-permute-done | bytes 131104 | tf_op jit(solution)/shard_map/ppermute | solution.py:401
  15.6 2.0 %option_partials.1 = (bf16[64,2176]{1,0:T(8,128)(2,1)S(1)}, bf16[64,2176]{1,0:T(8,128)(2,1)S(1)}) custom-call(s32[1]{0:T(128)} %bitcast.blk_ref, s32[1,64]{1,0:T(1,128)S(1)} %get-tuple-element.50.owner_ref, s32[1,64]{1,0:T(1,128)S(1)} %get-tuple-element.51.slot_ref, s32[1,64]{1,0:T(1,128)S(1)} %get-tuple-element.52.length_ref, ...), custom_call_target="tpu_custom_call" | custom-call | flops 1000000000 | bytes 1 | tf_op jit(solution)/shard_map/option_partials/pallas_call | solution.py:341
  17.7 3.3 %collective-permute-start.8 = (bf16[64,2176]{1,0:T(8,128)(2,1)S(1)}, bf16[64,2176]{1,0:T(8,128)(2,1)S(1)}, u32[]{:S(2)}, u32[]{:S(2)}) collective-permute-start(bf16[64,2176]{1,0:T(8,128)(2,1)S(1)} %get-tuple-element.85), channel_id=1, source_target_pairs={{0,4},{4,0},{8,12},{12,8},{1,5},{5,1},{9,13},{13,9},{2,6},{6,2},{1... | collective-permute-start | bytes 835592 | tf_op jit(solution)/shard_map/ppermute | solution.py:401
  20.9 2.3 %local_attention.3 = (f32[512,1024]{1,0:T(8,128)S(1)}, f32[512,1024]{1,0:T(8,128)S(1)}, f32[512,1024]{1,0:T(8,128)S(1)}) custom-call(s32[1]{0:T(128)} %bitcast.blk_ref, bf16[512,256]{1,0:T(8,128)(2,1)S(1)} %get-tuple-element.63.refs_1_.kv_ref, bf16[512,2048]{1,0:T(8,128)(2,1)S(1)} %get-tuple-element.49.refs_0_.q_ref), custom_call_target="tpu_custom_call" | custom-call | flops 1000000000 | bytes 1 | tf_op jit(solution)/shard_map/local_attention/pallas_call | solution.py:178
  23.2 0.0 collective-permute-done.3.refs_1_
  23.3 0.7 %collective-permute-start.5 = (bf16[512,256]{1,0:T(8,128)(2,1)S(1)}, bf16[512,256]{1,0:T(8,128)(2,1)S(1)}, u32[]{:S(2)}, u32[]{:S(2)}) collective-permute-start(bf16[512,256]{1,0:T(8,128)(2,1)S(1)} %collective-permute-done.3.refs_1_), channel_id=1, source_target_pairs={{8,12},{9,13},{10,14},{11,15},{24,28},{25,29},{26,30},{27,31}} | collective-permute-start | bytes 786440 | tf_op jit(solution)/shard_map/ppermute | solution.py:440
  23.9 1.3 %collective-permute-start.4 = (bf16[512,256]{1,0:T(8,128)(2,1)S(1)}, bf16[512,256]{1,0:T(8,128)(2,1)S(1)}, u32[]{:S(2)}, u32[]{:S(2)}) collective-permute-start(bf16[512,256]{1,0:T(8,128)(2,1)S(1)} %collective-permute-done.3.refs_1_), channel_id=1, source_target_pairs={{8,4},{9,5},{10,6},{11,7},{24,20},{25,21},{26,22},{27,23}} | collective-permute-start | bytes 786440 | tf_op jit(solution)/shard_map/ppermute | solution.py:440
  25.2 0.0 collective-permute-done.7.refs_2_
  25.3 0.0 collective-permute-done.6.refs_0_
  25.3 4.3 %anchor_attention.2 = (bf16[512,2048]{1,0:T(8,128)(2,1)}, f32[8,128]{1,0:T(8,128)S(1)}) custom-call(s32[1]{0:T(128)} %bitcast.blk_ref, bf16[512,2048]{1,0:T(8,128)(2,1)S(1)} %get-tuple-element.49.refs_0_.q_ref, bf16[512,256]{1,0:T(8,128)(2,1)S(1)} %get-tuple-element.74.kv_ref.refs_0_, f32[512,1024]{1,0:T(8,128)S(1)} %get-tuple-element.75.acc_ref, ...), custom_call_target="tpu_custom_call" | custom-call | flops 1000000000 | bytes 1 | tf_op jit(solution)/shard_map/anchor_attention/pallas_call | solution.py:256
  29.5 0.6 %merge.2 = (bf16[32,2176]{1,0:T(8,128)(2,1)S(1)}, bf16[32,2176]{1,0:T(8,128)(2,1)S(1)}) custom-call(bf16[64,2176]{1,0:T(8,128)(2,1)S(1)} %get-tuple-element.84.a, bf16[64,2176]{1,0:T(8,128)(2,1)S(1)} %collective-permute-done.8.b, f32[8,128]{1,0:T(8,128)S(1)} %get-tuple-element.86.after), custom_call_target="tpu_custom_call" | custom-call | flops 1 | bytes 1 | tf_op jit(solution)/shard_map/merge/pallas_call | solution.py:389
  30.1 1.8 %collective-permute-start.9 = (bf16[32,2176]{1,0:T(8,128)(2,1)S(1)}, bf16[32,2176]{1,0:T(8,128)(2,1)S(1)}, u32[]{:S(2)}, u32[]{:S(2)}) collective-permute-start(bf16[32,2176]{1,0:T(8,128)(2,1)S(1)} %get-tuple-element.88), channel_id=1, source_target_pairs={{0,8},{4,12},{8,0},{12,4},{1,9},{5,13},{9,1},{13,5},{2,10},{6,14},... | collective-permute-start | bytes 417800 | tf_op jit(solution)/shard_map/ppermute | solution.py:401
  31.9 4.7 %collective-permute-done.4.refs_0_ = bf16[512,256]{1,0:T(8,128)(2,1)S(1)} collective-permute-done((bf16[512,256]{1,0:T(8,128)(2,1)S(1)}, bf16[512,256]{1,0:T(8,128)(2,1)S(1)}, u32[]{:S(2)}, u32[]{:S(2)}) %collective-permute-start.4) | collective-permute-done | bytes 262176 | tf_op jit(solution)/shard_map/ppermute | solution.py:440
  36.6 4.2 %anchor_attention.3 = (bf16[512,2048]{1,0:T(8,128)(2,1)}, f32[8,128]{1,0:T(8,128)S(1)}) custom-call(s32[1]{0:T(128)} %bitcast.blk_ref, bf16[512,2048]{1,0:T(8,128)(2,1)S(1)} %get-tuple-element.49.refs_0_.q_ref, bf16[512,256]{1,0:T(8,128)(2,1)S(1)} %get-tuple-element.63.refs_1_.kv_ref, ...), custom_call_target="tpu_custom_call", output_to_operand_aliasing={{0}: (9, {})} | custom-call | flops 1000000000 | bytes 1 | tf_op jit(solution)/shard_map/anchor_attention/pallas_call | solution.py:256
  40.9 1.0 %merge.3 = bf16[32,2048]{1,0:T(8,128)(2,1)} custom-call(bf16[32,2176]{1,0:T(8,128)(2,1)S(1)} %get-tuple-element.87.a, bf16[32,2176]{1,0:T(8,128)(2,1)S(1)} %collective-permute-done.9.b, f32[8,128]{1,0:T(8,128)S(1)} %get-tuple-element.89.after), custom_call_target="tpu_custom_call" | custom-call | flops 1 | bytes 1 | tf_op jit(solution)/shard_map/merge/pallas_call | solution.py:389
  (4 shorter events, 0.0 us)
Async XLA Ops:
  0.6 5.6 %collective-permute-start = (bf16[16,2048]{1,0:T(8,128)(2,1)}, bf16[16,2048]{1,0:T(8,128)(2,1)S(1)}, u32[]{:S(2)}, u32[]{:S(2)}) collective-permute-start(bf16[16,2048]{1,0:T(8,128)(2,1)} %refs_4_.1), channel_id=1, source_target_pairs={{0,8},{4,12},{8,0},{12,4},{1,9},{5,13},{9,1},{13,5},{2,10},{6,14},... | collective-permute-start | bytes 196616 | tf_op jit(solution)/shard_map/ppermute | solution.py:401
  4.4 6.5 %collective-permute-start.1 = (bf16[512,256]{1,0:T(8,128)(2,1)S(1)}, bf16[512,256]{1,0:T(8,128)(2,1)S(1)}, u32[]{:S(2)}, u32[]{:S(2)}) collective-permute-start(bf16[512,256]{1,0:T(8,128)(2,1)S(1)} %get-tuple-element.74.kv_ref.refs_0_), channel_id=1, source_target_pairs={{0,8},{1,9},{2,10},{3,11},{16,24},{17,25},{18,26},{19,27}} | collective-permute-start | bytes 786440 | tf_op jit(solution)/shard_map/ppermute | solution.py:427
  10.2 5.5 %collective-permute-start.2 = (bf16[32,2048]{1,0:T(8,128)(2,1)S(1)}, bf16[32,2048]{1,0:T(8,128)(2,1)S(1)}, u32[]{:S(2)}, u32[]{:S(2)}) collective-permute-start(bf16[32,2048]{1,0:T(8,128)(2,1)S(1)} %get-tuple-element.61.refs_2_), channel_id=1, source_target_pairs={{0,4},{4,0},{8,12},{12,8},{1,5},{5,1},{9,13},{13,9},{2,6},{6,2},{1... | collective-permute-start | bytes 393224 | tf_op jit(solution)/shard_map/ppermute | solution.py:401
  10.2 13.0 %collective-permute-start.3 = (bf16[512,256]{1,0:T(8,128)(2,1)S(1)}, bf16[512,256]{1,0:T(8,128)(2,1)S(1)}, u32[]{:S(2)}, u32[]{:S(2)}) collective-permute-start(bf16[512,256]{1,0:T(8,128)(2,1)S(1)} %get-tuple-element.63.refs_1_.kv_ref), channel_id=1, source_target_pairs={{0,8},{1,9},{2,10},{3,11},{16,24},{17,25},{18,26},{19,27}} | collective-permute-start | bytes 786440 | tf_op jit(solution)/shard_map/ppermute | solution.py:433
  10.9 14.3 %collective-permute-start.7 = (bf16[512,256]{1,0:T(8,128)(2,1)S(1)}, bf16[512,256]{1,0:T(8,128)(2,1)S(1)}, u32[]{:S(2)}, u32[]{:S(2)}) collective-permute-start(bf16[512,256]{1,0:T(8,128)(2,1)S(1)} %collective-permute-done.1.refs_1_), channel_id=1, source_target_pairs={{8,12},{9,13},{10,14},{11,15},{24,28},{25,29},{26,30},{27,31}} | collective-permute-start | bytes 786440 | tf_op jit(solution)/shard_map/ppermute | solution.py:440
  11.6 13.6 %collective-permute-start.6 = (bf16[512,256]{1,0:T(8,128)(2,1)S(1)}, bf16[512,256]{1,0:T(8,128)(2,1)S(1)}, u32[]{:S(2)}, u32[]{:S(2)}) collective-permute-start(bf16[512,256]{1,0:T(8,128)(2,1)S(1)} %collective-permute-done.1.refs_1_), channel_id=1, source_target_pairs={{8,4},{9,5},{10,6},{11,7},{24,20},{25,21},{26,22},{27,23}} | collective-permute-start | bytes 786440 | tf_op jit(solution)/shard_map/ppermute | solution.py:440
  17.7 11.9 %collective-permute-start.8 = (bf16[64,2176]{1,0:T(8,128)(2,1)S(1)}, bf16[64,2176]{1,0:T(8,128)(2,1)S(1)}, u32[]{:S(2)}, u32[]{:S(2)}) collective-permute-start(bf16[64,2176]{1,0:T(8,128)(2,1)S(1)} %get-tuple-element.85), channel_id=1, source_target_pairs={{0,4},{4,0},{8,12},{12,8},{1,5},{5,1},{9,13},{13,9},{2,6},{6,2},{1... | collective-permute-start | bytes 835592 | tf_op jit(solution)/shard_map/ppermute | solution.py:401
  23.3 8.7 %collective-permute-start.5 = (bf16[512,256]{1,0:T(8,128)(2,1)S(1)}, bf16[512,256]{1,0:T(8,128)(2,1)S(1)}, u32[]{:S(2)}, u32[]{:S(2)}) collective-permute-start(bf16[512,256]{1,0:T(8,128)(2,1)S(1)} %collective-permute-done.3.refs_1_), channel_id=1, source_target_pairs={{8,12},{9,13},{10,14},{11,15},{24,28},{25,29},{26,30},{27,31}} | collective-permute-start | bytes 786440 | tf_op jit(solution)/shard_map/ppermute | solution.py:440
  23.9 12.7 %collective-permute-start.4 = (bf16[512,256]{1,0:T(8,128)(2,1)S(1)}, bf16[512,256]{1,0:T(8,128)(2,1)S(1)}, u32[]{:S(2)}, u32[]{:S(2)}) collective-permute-start(bf16[512,256]{1,0:T(8,128)(2,1)S(1)} %collective-permute-done.3.refs_1_), channel_id=1, source_target_pairs={{8,4},{9,5},{10,6},{11,7},{24,20},{25,21},{26,22},{27,23}} | collective-permute-start | bytes 786440 | tf_op jit(solution)/shard_map/ppermute | solution.py:440
  30.1 10.8 %collective-permute-start.9 = (bf16[32,2176]{1,0:T(8,128)(2,1)S(1)}, bf16[32,2176]{1,0:T(8,128)(2,1)S(1)}, u32[]{:S(2)}, u32[]{:S(2)}) collective-permute-start(bf16[32,2176]{1,0:T(8,128)(2,1)S(1)} %get-tuple-element.88), channel_id=1, source_target_pairs={{0,8},{4,12},{8,0},{12,4},{1,9},{5,13},{9,1},{13,5},{2,10},{6,14},... | collective-permute-start | bytes 417800 | tf_op jit(solution)/shard_map/ppermute | solution.py:401

commit v11 on v10

--- a/solution.py
+++ b/solution.py
@@ -127,19 +127,16 @@
     pipelined([(h, at) for h in range(0, GROUP, PAIR) for at in range(0, rows, TILE)], scores, finish)
 
 
-def local_kernel(g, loads, joined, blk_ref, kv_ref, *refs):
-    ins = max(loads + joined, 1)
+def local_kernel(g, loads, blk_ref, kv_ref, *refs):
+    ins = max(loads, 1)
     sources, (acc_ref, top_ref, sum_ref) = refs[:ins], refs[ins : ins + 3]
-    held = refs[ins + 3 : ins + 3 + loads + (joined > 0)] or sources
-    ve = refs[ins + 3 + loads + (joined > 0)]
+    held, ve = refs[ins + 3 : ins + 3 + loads] or sources, refs[ins + 3 + loads]
     q_ref, queries, others = held[0], {}, []
     if loads:
         order = list(range(g * GROUP, g * GROUP + GROUP)) + [h for h in range(q_ref.shape[1] // HD) if h // GROUP != g]
         spots = [slice(h * HD, (h + PAIR) * HD) for h in order[::PAIR]]
         copies = [(sources[0].at[:, spot], q_ref.at[:, spot]) for spot in spots]
-        copies += list(zip(sources[1:loads], held[1:loads]))
-        each = sources[loads].shape[0]
-        copies += [(x, held[loads].at[i * each : (i + 1) * each]) for i, x in enumerate(sources[loads:])]
+        copies += list(zip(sources[1:], held[1:]))
         copies = start_all(copies, refs[-1])
         queries = dict(zip(range(0, GROUP, PAIR), copies))
         others = copies[GROUP // PAIR :]
@@ -165,25 +162,22 @@
         copy.wait()
 
 
-def local_attention(blk, kv, g, query, loads=(), joined=()):
+def local_attention(blk, kv, g, query, loads=()):
     rows = kv.shape[0]
     sources, held = [query], []
     if loads:
         sources = [in_hbm(x) for x in (query, *loads)]
-        height, width = joined[0].shape
         held = [pltpu.VMEM(x.shape, x.dtype) for x in sources]
-        held.append(pltpu.VMEM((len(joined) * height, width), joined[0].dtype))
-        sources += [in_hbm(joined[0]), *joined[1:]]
-    semaphores = query.shape[1] // HD // PAIR + len(loads) + len(joined)
+    semaphores = query.shape[1] // HD // PAIR + len(loads)
     outs = pl.pallas_call(
-        functools.partial(local_kernel, g, len(loads) + 1 if loads else 0, len(joined)),
+        functools.partial(local_kernel, g, len(held)),
         out_shape=[pltpu.VMEM((rows, GROUP * HD), jnp.float32)] * 3 + held,
-        in_specs=[SMEM, VMEM] + ([HBM] * (len(loads) + 1) + [ANY] * len(joined) if loads else [VMEM]),
+        in_specs=[SMEM, VMEM] + [HBM if loads else VMEM] * len(sources),
         out_specs=[VMEM] * (3 + len(held)),
         scratch_shapes=[pltpu.VMEM((rows, 2 * HD), jnp.bfloat16)]
         + ([pltpu.SemaphoreType.DMA((semaphores,))] if loads else []),
         compiler_params=params(6),
-        cost_estimate=cost(1000000000 if loads else 1000000000),
+        cost_estimate=cost(2 * 10**9 if loads else 10**9),
         name="local_attention",
     )(blk, kv, *sources)
     return list(outs[:3]), list(outs[3:])
@@ -274,6 +268,26 @@
 def fold_order(n):
     bits = n.bit_length() - 1
     return sorted(range(n), key=lambda x: int(format(x, "0%db" % bits)[::-1], 2))
+
+
+def join_kernel(*refs):
+    at = 0
+    for ref in refs[:-1]:
+        refs[-1][at : at + ref.shape[0], :] = ref[...]
+        at += ref.shape[0]
+
+
+def join(arrays):
+    height, width = sum(x.shape[0] for x in arrays), arrays[0].shape[1]
+    return pl.pallas_call(
+        join_kernel,
+        out_shape=pltpu.VMEM((height, width), arrays[0].dtype),
+        in_specs=[VMEM] * len(arrays),
+        out_specs=VMEM,
+        compiler_params=params(2),
+        cost_estimate=BRIEF,
+        name="join",
+    )(*arrays)
 
 
 def option_kernel(masks, heads, blk_ref, owner_ref, slot_ref, length_ref, *refs):
@@ -426,9 +440,10 @@
     if n == 4:
         first = [lax.ppermute(kvs[0], "blk", [(0, 2)])]
     small = [row(opt_owner), row(opt_slot), row(opt_length)]
-    state, (ctx_query, *small, mine) = local_attention(blk_arr, kvs[0], 0, ctx_query, small, shards)
+    state, (ctx_query, *small, own) = local_attention(blk_arr, kvs[0], 0, ctx_query, small + shards[:1])
+    kvs, states, shards = hold((kvs, [state], shards))
+    mine = join([own, *shards[1:]])
     queries = [mine, swap(mine, n, 1)]
-    kvs, states = hold((kvs, [state]))
     if n == 4:
         first += [lax.ppermute(kv, "blk", [(0, 2)]) for kv in kvs[1:]]
         first[0], kvs = hold((first[0], kvs))

time: 42.7 us -> 42.4 us (level); the launches traced: 41.9 us -> 42.1 us
  waiting for transfers between devices: 8.57 us -> 9.96 us
  starting transfers between devices: 13.1 us -> 11.9 us
    ppermute x4, waiting for transfers between devices: 3.86 us -> 5.3 us  [swap(): return lax.ppermute(x, 'blk', [(i, i ^ mask) for i in range(n)])]
    ppermute x4, starting transfers between devices: 7.82 us -> 6.61 us  [swap(): return lax.ppermute(x, 'blk', [(i, i ^ mask) for i in range(n)])]
    pallas_call x2 -> x3, Pallas kernels: 6.21 us -> 6.23 us  [the longest x2 6.21 us: local_attention(): pl.pallas_call(functools.partial(local_kernel, g, len(held)), out_shape=[...]
  transfers between devices with their start and end apart: 10 -> 10, of which waited for: 3 -> 2; matrix products, arithmetic and copies ran while one was open for 0% -> 0% of each run, Pallas kernels for 44% -> 44%
where the time goes in v11:
time: 42.4 us; the launch traced here: 42.1 us
  Pallas kernels  19.4 us (46%)
  starting transfers between devices  11.9 us (28%)
  waiting for transfers between devices  9.96 us (23%)
  between operations  0.81 us (2%)
    pallas_call x2, Pallas kernels, anchor_attention(): pl.pallas_call(functools.partial(anchor_kernel, g, len(cands), len(alias)...  8.5 us
    ppermute x4, starting transfers between devices, swap(): return lax.ppermute(x, 'blk', [(i, i ^ mask) for i in range(n)])  6.61 us
    pallas_call x2, Pallas kernels, local_attention(): pl.pallas_call(functools.partial(local_kernel, g, len(held)), out_shape=[...  6.21 us
    ppermute x4, waiting for transfers between devices, swap(): return lax.ppermute(x, 'blk', [(i, i ^ mask) for i in range(n)])  5.3 us
    ppermute x2, waiting for transfers between devices, body(): lax.ppermute(x, 'blk', [(2, 1)])  4.65 us
    ppermute x2, starting transfers between devices, body(): lax.ppermute(x, 'blk', [(2, 1)])  2.58 us
    pallas_call x1, Pallas kernels, option_partials(): pl.pallas_call(functools.partial(option_kernel, masks, heads), out_shape=...  2.03 us
    pallas_call x2, Pallas kernels, merge(): pl.pallas_call(functools.partial(merge_kernel, heads), out_shape=shapes,...  1.55 us
  transfers between devices with their start and end apart: 10, of which 2 were waited for; matrix products, arithmetic and copies ran while one was open for 0% of the time, Pallas kernels for 44%

profile of v11, /device:TPU:12, one launch (start us, length us, event | category | flops | bytes accessed | tf_op | source)
XLA Modules:
  0.0 42.1 jit_solution(14989591210841364362)
XLA Ops:
  0.6 2.7 %collective-permute-start.1 = (bf16[16,2048]{1,0:T(8,128)(2,1)}, bf16[16,2048]{1,0:T(8,128)(2,1)S(1)}, u32[]{:S(2)}, u32[]{:S(2)}) collective-permute-start(bf16[16,2048]{1,0:T(8,128)(2,1)} %refs_4_.1), channel_id=1, source_target_pairs={{0,8},{4,12},{8,0},{12,4},{1,9},{5,13},{9,1},{13,5},{2,10},{6,14},... | collective-permute-start | bytes 196616 | tf_op jit(solution)/shard_map/ppermute | solution.py:415
  3.3 1.1 %parts.1 = (bf16[512,256]{1,0:T(8,128)(2,1)S(1)}, bf16[512,256]{1,0:T(8,128)(2,1)S(1)}) custom-call(bf16[512,256]{1,0:T(8,128)(2,1)} %k_ref, bf16[512,256]{1,0:T(8,128)(2,1)} %v_ref.1), custom_call_target="tpu_custom_call" | custom-call | flops 1 | bytes 1 | tf_op jit(solution)/shard_map/parts/pallas_call | solution.py:73
  4.4 0.7 %collective-permute-start = (bf16[512,256]{1,0:T(8,128)(2,1)S(1)}, bf16[512,256]{1,0:T(8,128)(2,1)S(1)}, u32[]{:S(2)}, u32[]{:S(2)}) collective-permute-start(bf16[512,256]{1,0:T(8,128)(2,1)S(1)} %get-tuple-element.76.kv_ref.refs_0_), channel_id=1, source_target_pairs={{0,8},{1,9},{2,10},{3,11},{16,24},{17,25},{18,26},{19,27}} | collective-permute-start | bytes 786440 | tf_op jit(solution)/shard_map/ppermute | solution.py:441
  5.1 3.9 %local_attention.2 = (f32[512,1024]{1,0:T(8,128)S(1)}, f32[512,1024]{1,0:T(8,128)S(1)}, f32[512,1024]{1,0:T(8,128)S(1)}, bf16[512,2048]{1,0:T(8,128)(2,1)S(1)}, ...) custom-call(s32[1]{0:T(128)} %bitcast.blk_ref, ...), custom_call_target="tpu_custom_call" | custom-call | flops 2000000000 | bytes 1 | tf_op jit(solution)/shard_map/local_attention/pallas_call | solution.py:172
  9.0 0.0 collective-permute-done.1.refs_1_
  9.1 0.1 collective-permute-start.2
  9.1 0.7 %collective-permute-start.3 = (bf16[512,256]{1,0:T(8,128)(2,1)S(1)}, bf16[512,256]{1,0:T(8,128)(2,1)S(1)}, u32[]{:S(2)}, u32[]{:S(2)}) collective-permute-start(bf16[512,256]{1,0:T(8,128)(2,1)S(1)} %get-tuple-element.65.refs_1_.kv_ref), channel_id=1, source_target_pairs={{0,8},{1,9},{2,10},{3,11},{16,24},{17,25},{18,26},{19,27}} | collective-permute-start | bytes 786440 | tf_op jit(solution)/shard_map/ppermute | solution.py:448
  9.8 0.0 collective-permute-done.refs_1_
  9.8 0.7 %collective-permute-start.7 = (bf16[512,256]{1,0:T(8,128)(2,1)S(1)}, bf16[512,256]{1,0:T(8,128)(2,1)S(1)}, u32[]{:S(2)}, u32[]{:S(2)}) collective-permute-start(bf16[512,256]{1,0:T(8,128)(2,1)S(1)} %collective-permute-done.refs_1_), channel_id=1, source_target_pairs={{8,12},{9,13},{10,14},{11,15},{24,28},{25,29},{26,30},{27,31}} | collective-permute-start | bytes 786440 | tf_op jit(solution)/shard_map/ppermute | solution.py:455
  10.5 1.3 %collective-permute-start.6 = (bf16[512,256]{1,0:T(8,128)(2,1)S(1)}, bf16[512,256]{1,0:T(8,128)(2,1)S(1)}, u32[]{:S(2)}, u32[]{:S(2)}) collective-permute-start(bf16[512,256]{1,0:T(8,128)(2,1)S(1)} %collective-permute-done.refs_1_), channel_id=1, source_target_pairs={{8,4},{9,5},{10,6},{11,7},{24,20},{25,21},{26,22},{27,23}} | collective-permute-start | bytes 786440 | tf_op jit(solution)/shard_map/ppermute | solution.py:455
  11.8 5.3 %collective-permute-done.2.refs_3_ = bf16[32,2048]{1,0:T(8,128)(2,1)S(1)} collective-permute-done((bf16[32,2048]{1,0:T(8,128)(2,1)S(1)}, bf16[32,2048]{1,0:T(8,128)(2,1)S(1)}, u32[]{:S(2)}, u32[]{:S(2)}) %collective-permute-start.2) | collective-permute-done | bytes 131104 | tf_op jit(solution)/shard_map/ppermute | solution.py:415
  17.1 2.0 %option_partials.1 = (bf16[64,2176]{1,0:T(8,128)(2,1)S(1)}, bf16[64,2176]{1,0:T(8,128)(2,1)S(1)}) custom-call(s32[1]{0:T(128)} %bitcast.blk_ref, s32[1,64]{1,0:T(1,128)S(1)} %get-tuple-element.51.owner_ref, s32[1,64]{1,0:T(1,128)S(1)} %get-tuple-element.52.slot_ref, s32[1,64]{1,0:T(1,128)S(1)} %get-tuple-element.53.length_ref, ...), custom_call_target="tpu_custom_call" | custom-call | flops 1000000000 | bytes 1 | tf_op jit(solution)/shard_map/option_partials/pallas_call | solution.py:355
  19.1 0.1 collective-permute-start.8
  19.2 2.3 %local_attention.3 = (f32[512,1024]{1,0:T(8,128)S(1)}, f32[512,1024]{1,0:T(8,128)S(1)}, f32[512,1024]{1,0:T(8,128)S(1)}) custom-call(s32[1]{0:T(128)} %bitcast.blk_ref, bf16[512,256]{1,0:T(8,128)(2,1)S(1)} %get-tuple-element.65.refs_1_.kv_ref, bf16[512,2048]{1,0:T(8,128)(2,1)S(1)} %get-tuple-element.50.refs_0_.q_ref), custom_call_target="tpu_custom_call" | custom-call | flops 1000000000 | bytes 1 | tf_op jit(solution)/shard_map/local_attention/pallas_call | solution.py:172
  21.5 0.0 collective-permute-done.3.refs_1_
  21.5 0.7 %collective-permute-start.5 = (bf16[512,256]{1,0:T(8,128)(2,1)S(1)}, bf16[512,256]{1,0:T(8,128)(2,1)S(1)}, u32[]{:S(2)}, u32[]{:S(2)}) collective-permute-start(bf16[512,256]{1,0:T(8,128)(2,1)S(1)} %collective-permute-done.3.refs_1_), channel_id=1, source_target_pairs={{8,12},{9,13},{10,14},{11,15},{24,28},{25,29},{26,30},{27,31}} | collective-permute-start | bytes 786440 | tf_op jit(solution)/shard_map/ppermute | solution.py:455
  22.2 1.3 %collective-permute-start.4 = (bf16[512,256]{1,0:T(8,128)(2,1)S(1)}, bf16[512,256]{1,0:T(8,128)(2,1)S(1)}, u32[]{:S(2)}, u32[]{:S(2)}) collective-permute-start(bf16[512,256]{1,0:T(8,128)(2,1)S(1)} %collective-permute-done.3.refs_1_), channel_id=1, source_target_pairs={{8,4},{9,5},{10,6},{11,7},{24,20},{25,21},{26,22},{27,23}} | collective-permute-start | bytes 786440 | tf_op jit(solution)/shard_map/ppermute | solution.py:455
  23.5 0.0 collective-permute-done.6.refs_0_
  23.5 4.3 %anchor_attention.2 = (bf16[512,2048]{1,0:T(8,128)(2,1)}, f32[8,128]{1,0:T(8,128)S(1)}) custom-call(s32[1]{0:T(128)} %bitcast.blk_ref, bf16[512,2048]{1,0:T(8,128)(2,1)S(1)} %get-tuple-element.50.refs_0_.q_ref, bf16[512,256]{1,0:T(8,128)(2,1)S(1)} %get-tuple-element.76.kv_ref.refs_0_, f32[512,1024]{1,0:T(8,128)S(1)} %get-tuple-element.77.acc_ref, ...), custom_call_target="tpu_custom_call" | custom-call | flops 1000000000 | bytes 1 | tf_op jit(solution)/shard_map/anchor_attention/pallas_call | solution.py:250
  27.8 0.6 %merge.2 = (bf16[32,2176]{1,0:T(8,128)(2,1)S(1)}, bf16[32,2176]{1,0:T(8,128)(2,1)S(1)}) custom-call(bf16[64,2176]{1,0:T(8,128)(2,1)S(1)} %get-tuple-element.86.a, bf16[64,2176]{1,0:T(8,128)(2,1)S(1)} %collective-permute-done.8.b, f32[8,128]{1,0:T(8,128)S(1)} %get-tuple-element.88.after), custom_call_target="tpu_custom_call" | custom-call | flops 1 | bytes 1 | tf_op jit(solution)/shard_map/merge/pallas_call | solution.py:403
  28.4 3.8 %collective-permute-start.9 = (bf16[32,2176]{1,0:T(8,128)(2,1)S(1)}, bf16[32,2176]{1,0:T(8,128)(2,1)S(1)}, u32[]{:S(2)}, u32[]{:S(2)}) collective-permute-start(bf16[32,2176]{1,0:T(8,128)(2,1)S(1)} %get-tuple-element.90), channel_id=1, source_target_pairs={{0,8},{4,12},{8,0},{12,4},{1,9},{5,13},{9,1},{13,5},{2,10},{6,14},... | collective-permute-start | bytes 417800 | tf_op jit(solution)/shard_map/ppermute | solution.py:415
  32.2 4.6 %collective-permute-done.4.refs_0_ = bf16[512,256]{1,0:T(8,128)(2,1)S(1)} collective-permute-done((bf16[512,256]{1,0:T(8,128)(2,1)S(1)}, bf16[512,256]{1,0:T(8,128)(2,1)S(1)}, u32[]{:S(2)}, u32[]{:S(2)}) %collective-permute-start.4) | collective-permute-done | bytes 262176 | tf_op jit(solution)/shard_map/ppermute | solution.py:455
  36.9 4.2 %anchor_attention.3 = (bf16[512,2048]{1,0:T(8,128)(2,1)}, f32[8,128]{1,0:T(8,128)S(1)}) custom-call(s32[1]{0:T(128)} %bitcast.blk_ref, bf16[512,2048]{1,0:T(8,128)(2,1)S(1)} %get-tuple-element.50.refs_0_.q_ref, bf16[512,256]{1,0:T(8,128)(2,1)S(1)} %get-tuple-element.65.refs_1_.kv_ref, ...), custom_call_target="tpu_custom_call", output_to_operand_aliasing={{0}: (9, {})} | custom-call | flops 1000000000 | bytes 1 | tf_op jit(solution)/shard_map/anchor_attention/pallas_call | solution.py:250
  41.1 1.0 %merge.3 = bf16[32,2048]{1,0:T(8,128)(2,1)} custom-call(bf16[32,2176]{1,0:T(8,128)(2,1)S(1)} %get-tuple-element.89.a, bf16[32,2176]{1,0:T(8,128)(2,1)S(1)} %collective-permute-done.9.b, f32[8,128]{1,0:T(8,128)S(1)} %get-tuple-element.91.after), custom_call_target="tpu_custom_call" | custom-call | flops 1 | bytes 1 | tf_op jit(solution)/shard_map/merge/pallas_call | solution.py:403
  (5 shorter events, 0.0 us)
Async XLA Ops:
  0.6 8.4 %collective-permute-start.1 = (bf16[16,2048]{1,0:T(8,128)(2,1)}, bf16[16,2048]{1,0:T(8,128)(2,1)S(1)}, u32[]{:S(2)}, u32[]{:S(2)}) collective-permute-start(bf16[16,2048]{1,0:T(8,128)(2,1)} %refs_4_.1), channel_id=1, source_target_pairs={{0,8},{4,12},{8,0},{12,4},{1,9},{5,13},{9,1},{13,5},{2,10},{6,14},... | collective-permute-start | bytes 196616 | tf_op jit(solution)/shard_map/ppermute | solution.py:415
  4.4 5.4 %collective-permute-start = (bf16[512,256]{1,0:T(8,128)(2,1)S(1)}, bf16[512,256]{1,0:T(8,128)(2,1)S(1)}, u32[]{:S(2)}, u32[]{:S(2)}) collective-permute-start(bf16[512,256]{1,0:T(8,128)(2,1)S(1)} %get-tuple-element.76.kv_ref.refs_0_), channel_id=1, source_target_pairs={{0,8},{1,9},{2,10},{3,11},{16,24},{17,25},{18,26},{19,27}} | collective-permute-start | bytes 786440 | tf_op jit(solution)/shard_map/ppermute | solution.py:441
  9.1 8.1 %collective-permute-start.2 = (bf16[32,2048]{1,0:T(8,128)(2,1)S(1)}, bf16[32,2048]{1,0:T(8,128)(2,1)S(1)}, u32[]{:S(2)}, u32[]{:S(2)}) collective-permute-start(bf16[32,2048]{1,0:T(8,128)(2,1)S(1)} %join.1.refs_2_), channel_id=1, source_target_pairs={{0,4},{4,0},{8,12},{12,8},{1,5},{5,1},{9,13},{13,9},{2,6},{6,2},{1... | collective-permute-start | bytes 393224 | tf_op jit(solution)/shard_map/ppermute | solution.py:415
  9.1 12.4 %collective-permute-start.3 = (bf16[512,256]{1,0:T(8,128)(2,1)S(1)}, bf16[512,256]{1,0:T(8,128)(2,1)S(1)}, u32[]{:S(2)}, u32[]{:S(2)}) collective-permute-start(bf16[512,256]{1,0:T(8,128)(2,1)S(1)} %get-tuple-element.65.refs_1_.kv_ref), channel_id=1, source_target_pairs={{0,8},{1,9},{2,10},{3,11},{16,24},{17,25},{18,26},{19,27}} | collective-permute-start | bytes 786440 | tf_op jit(solution)/shard_map/ppermute | solution.py:448
  9.8 13.7 %collective-permute-start.7 = (bf16[512,256]{1,0:T(8,128)(2,1)S(1)}, bf16[512,256]{1,0:T(8,128)(2,1)S(1)}, u32[]{:S(2)}, u32[]{:S(2)}) collective-permute-start(bf16[512,256]{1,0:T(8,128)(2,1)S(1)} %collective-permute-done.refs_1_), channel_id=1, source_target_pairs={{8,12},{9,13},{10,14},{11,15},{24,28},{25,29},{26,30},{27,31}} | collective-permute-start | bytes 786440 | tf_op jit(solution)/shard_map/ppermute | solution.py:455
  10.5 13.0 %collective-permute-start.6 = (bf16[512,256]{1,0:T(8,128)(2,1)S(1)}, bf16[512,256]{1,0:T(8,128)(2,1)S(1)}, u32[]{:S(2)}, u32[]{:S(2)}) collective-permute-start(bf16[512,256]{1,0:T(8,128)(2,1)S(1)} %collective-permute-done.refs_1_), channel_id=1, source_target_pairs={{8,4},{9,5},{10,6},{11,7},{24,20},{25,21},{26,22},{27,23}} | collective-permute-start | bytes 786440 | tf_op jit(solution)/shard_map/ppermute | solution.py:455
  19.1 8.7 %collective-permute-start.8 = (bf16[64,2176]{1,0:T(8,128)(2,1)S(1)}, bf16[64,2176]{1,0:T(8,128)(2,1)S(1)}, u32[]{:S(2)}, u32[]{:S(2)}) collective-permute-start(bf16[64,2176]{1,0:T(8,128)(2,1)S(1)} %get-tuple-element.87), channel_id=1, source_target_pairs={{0,4},{4,0},{8,12},{12,8},{1,5},{5,1},{9,13},{13,9},{2,6},{6,2},{1... | collective-permute-start | bytes 835592 | tf_op jit(solution)/shard_map/ppermute | solution.py:415
  21.5 10.7 %collective-permute-start.5 = (bf16[512,256]{1,0:T(8,128)(2,1)S(1)}, bf16[512,256]{1,0:T(8,128)(2,1)S(1)}, u32[]{:S(2)}, u32[]{:S(2)}) collective-permute-start(bf16[512,256]{1,0:T(8,128)(2,1)S(1)} %collective-permute-done.3.refs_1_), channel_id=1, source_target_pairs={{8,12},{9,13},{10,14},{11,15},{24,28},{25,29},{26,30},{27,31}} | collective-permute-start | bytes 786440 | tf_op jit(solution)/shard_map/ppermute | solution.py:455
  22.2 14.6 %collective-permute-start.4 = (bf16[512,256]{1,0:T(8,128)(2,1)S(1)}, bf16[512,256]{1,0:T(8,128)(2,1)S(1)}, u32[]{:S(2)}, u32[]{:S(2)}) collective-permute-start(bf16[512,256]{1,0:T(8,128)(2,1)S(1)} %collective-permute-done.3.refs_1_), channel_id=1, source_target_pairs={{8,4},{9,5},{10,6},{11,7},{24,20},{25,21},{26,22},{27,23}} | collective-permute-start | bytes 786440 | tf_op jit(solution)/shard_map/ppermute | solution.py:455
  28.4 12.7 %collective-permute-start.9 = (bf16[32,2176]{1,0:T(8,128)(2,1)S(1)}, bf16[32,2176]{1,0:T(8,128)(2,1)S(1)}, u32[]{:S(2)}, u32[]{:S(2)}) collective-permute-start(bf16[32,2176]{1,0:T(8,128)(2,1)S(1)} %get-tuple-element.90), channel_id=1, source_target_pairs={{0,8},{4,12},{8,0},{12,4},{1,9},{5,13},{9,1},{13,5},{2,10},{6,14},... | collective-permute-start | bytes 417800 | tf_op jit(solution)/shard_map/ppermute | solution.py:415

commit v12 on v11

--- a/solution.py
+++ b/solution.py
@@ -451,8 +451,11 @@
     keep, kvs = hold((keep, kvs))
     states += [local_attention(blk_arr, kv, g, ctx_query)[0] for g, kv in enumerate(kvs) if g]
     if n == 4:
+        kvs, states = hold((kvs, states))
+        near = [lax.ppermute(first[0], "blk", [(2, 1)])]
+        near += [lax.ppermute(kv, "blk", [(0, 1)]) for kv in kvs[1:]]
         first[1:], states = hold((first[1:], states))
-        anchors = [[lax.ppermute(x, "blk", [(2, 1)]), x, lax.ppermute(x, "blk", [(2, 3)])] for x in first]
+        anchors = [[x, y, lax.ppermute(y, "blk", [(2, 3)])] for x, y in zip(near, first)]
         anchors[0], first = hold((anchors[0], first))
     else:
         anchors = [[from_root(kv, blk)] for kv in kvs]

time: 42.4 us -> 40.2 us (0.948)
  starting transfers between devices: 11.9 us -> 10.5 us
  waiting for transfers between devices: 9.96 us -> 8.87 us
    ppermute x4, waiting for transfers between devices: 4.65 us -> 2.57 us  [the longest x1 2.57 us: body(): near += [lax.ppermute(kv, 'blk', [(0, 1)]) for kv in kvs[1:]]]
    ppermute x4, starting transfers between devices: 6.61 us -> 5.19 us  [swap(): return lax.ppermute(x, 'blk', [(i, i ^ mask) for i in range(n)])]
    ppermute x4, waiting for transfers between devices: 5.3 us -> 6.29 us  [swap(): return lax.ppermute(x, 'blk', [(i, i ^ mask) for i in range(n)])]
  transfers between devices with their start and end apart: 10 -> 10, of which waited for: 2 -> 3; matrix products, arithmetic and copies ran while one was open for 0% -> 0% of each run, Pallas kernels for 44% -> 47%
where the time goes in v12:
time: 40.2 us; the launch traced here: 39.6 us
  Pallas kernels  19.4 us (48%)
  starting transfers between devices  10.5 us (26%)
  waiting for transfers between devices  8.87 us (22%)
  between operations  0.8 us (2%)
    pallas_call x2, Pallas kernels, anchor_attention(): pl.pallas_call(functools.partial(anchor_kernel, g, len(cands), len(alias)...  8.51 us
    ppermute x4, waiting for transfers between devices, swap(): return lax.ppermute(x, 'blk', [(i, i ^ mask) for i in range(n)])  6.29 us
    pallas_call x2, Pallas kernels, local_attention(): pl.pallas_call(functools.partial(local_kernel, g, len(held)), out_shape=[...  6.21 us
    ppermute x4, starting transfers between devices, swap(): return lax.ppermute(x, 'blk', [(i, i ^ mask) for i in range(n)])  5.19 us
    ppermute x1, waiting for transfers between devices, body(): near += [lax.ppermute(kv, 'blk', [(0, 1)]) for kv in kvs[1:]]  2.57 us
    pallas_call x1, Pallas kernels, option_partials(): pl.pallas_call(functools.partial(option_kernel, masks, heads), out_shape=...  2.03 us
    pallas_call x2, Pallas kernels, merge(): pl.pallas_call(functools.partial(merge_kernel, heads), out_shape=shapes,...  1.55 us
    ppermute x2, starting transfers between devices, body(): lax.ppermute(y, 'blk', [(2, 3)])  1.35 us
  transfers between devices with their start and end apart: 10, of which 3 were waited for; matrix products, arithmetic and copies ran while one was open for 0% of the time, Pallas kernels for 47%

profile of v12, /device:TPU:12, one launch (start us, length us, event | category | flops | bytes accessed | tf_op | source)
XLA Modules:
  0.0 39.6 jit_solution(11944726796768766677)
XLA Ops:
  0.6 2.7 %collective-permute-start.1 = (bf16[16,2048]{1,0:T(8,128)(2,1)}, bf16[16,2048]{1,0:T(8,128)(2,1)S(1)}, u32[]{:S(2)}, u32[]{:S(2)}) collective-permute-start(bf16[16,2048]{1,0:T(8,128)(2,1)} %refs_4_.1), channel_id=1, source_target_pairs={{0,8},{4,12},{8,0},{12,4},{1,9},{5,13},{9,1},{13,5},{2,10},{6,14},... | collective-permute-start | bytes 196616 | tf_op jit(solution)/shard_map/ppermute | solution.py:415
  3.3 1.1 %parts.1 = (bf16[512,256]{1,0:T(8,128)(2,1)S(1)}, bf16[512,256]{1,0:T(8,128)(2,1)S(1)}) custom-call(bf16[512,256]{1,0:T(8,128)(2,1)} %k_ref, bf16[512,256]{1,0:T(8,128)(2,1)} %v_ref.1), custom_call_target="tpu_custom_call" | custom-call | flops 1 | bytes 1 | tf_op jit(solution)/shard_map/parts/pallas_call | solution.py:73
  4.4 0.7 %collective-permute-start = (bf16[512,256]{1,0:T(8,128)(2,1)S(1)}, bf16[512,256]{1,0:T(8,128)(2,1)S(1)}, u32[]{:S(2)}, u32[]{:S(2)}) collective-permute-start(bf16[512,256]{1,0:T(8,128)(2,1)S(1)} %get-tuple-element.92.kv_ref.refs_0_), channel_id=1, source_target_pairs={{0,8},{1,9},{2,10},{3,11},{16,24},{17,25},{18,26},{19,27}} | collective-permute-start | bytes 786440 | tf_op jit(solution)/shard_map/ppermute | solution.py:441
  5.1 3.9 %local_attention.2 = (f32[512,1024]{1,0:T(8,128)S(1)}, f32[512,1024]{1,0:T(8,128)S(1)}, f32[512,1024]{1,0:T(8,128)S(1)}, bf16[512,2048]{1,0:T(8,128)(2,1)S(1)}, ...) custom-call(s32[1]{0:T(128)} %bitcast.blk_ref, ...), custom_call_target="tpu_custom_call" | custom-call | flops 2000000000 | bytes 1 | tf_op jit(solution)/shard_map/local_attention/pallas_call | solution.py:172
  9.0 0.0 collective-permute-done.1.refs_1_
  9.1 0.1 collective-permute-start.2
  9.1 0.7 %collective-permute-start.3 = (bf16[512,256]{1,0:T(8,128)(2,1)S(1)}, bf16[512,256]{1,0:T(8,128)(2,1)S(1)}, u32[]{:S(2)}, u32[]{:S(2)}) collective-permute-start(bf16[512,256]{1,0:T(8,128)(2,1)S(1)} %get-tuple-element.81.refs_1_.kv_ref), channel_id=1, source_target_pairs={{0,8},{1,9},{2,10},{3,11},{16,24},{17,25},{18,26},{19,27}} | collective-permute-start | bytes 786440 | tf_op jit(solution)/shard_map/ppermute | solution.py:448
  9.8 0.0 collective-permute-done.refs_1_
  9.8 0.7 %collective-permute-start.7 = (bf16[512,256]{1,0:T(8,128)(2,1)S(1)}, bf16[512,256]{1,0:T(8,128)(2,1)S(1)}, u32[]{:S(2)}, u32[]{:S(2)}) collective-permute-start(bf16[512,256]{1,0:T(8,128)(2,1)S(1)} %collective-permute-done.refs_1_), channel_id=1, source_target_pairs={{8,12},{9,13},{10,14},{11,15},{24,28},{25,29},{26,30},{27,31}} | collective-permute-start | bytes 786440 | tf_op jit(solution)/shard_map/ppermute | solution.py:458
  10.5 1.3 %collective-permute-start.6 = (bf16[512,256]{1,0:T(8,128)(2,1)S(1)}, bf16[512,256]{1,0:T(8,128)(2,1)S(1)}, u32[]{:S(2)}, u32[]{:S(2)}) collective-permute-start(bf16[512,256]{1,0:T(8,128)(2,1)S(1)} %collective-permute-done.refs_1_), channel_id=1, source_target_pairs={{8,4},{9,5},{10,6},{11,7},{24,20},{25,21},{26,22},{27,23}} | collective-permute-start | bytes 786440 | tf_op jit(solution)/shard_map/ppermute | solution.py:455
  11.8 5.3 %collective-permute-done.2.refs_3_ = bf16[32,2048]{1,0:T(8,128)(2,1)S(1)} collective-permute-done((bf16[32,2048]{1,0:T(8,128)(2,1)S(1)}, bf16[32,2048]{1,0:T(8,128)(2,1)S(1)}, u32[]{:S(2)}, u32[]{:S(2)}) %collective-permute-start.2) | collective-permute-done | bytes 131104 | tf_op jit(solution)/shard_map/ppermute | solution.py:415
  17.1 2.0 %option_partials.1 = (bf16[64,2176]{1,0:T(8,128)(2,1)S(1)}, bf16[64,2176]{1,0:T(8,128)(2,1)S(1)}) custom-call(s32[1]{0:T(128)} %bitcast.blk_ref, s32[1,64]{1,0:T(1,128)S(1)} %get-tuple-element.59.owner_ref, s32[1,64]{1,0:T(1,128)S(1)} %get-tuple-element.60.slot_ref, s32[1,64]{1,0:T(1,128)S(1)} %get-tuple-element.61.length_ref, ...), custom_call_target="tpu_custom_call" | custom-call | flops 1000000000 | bytes 1 | tf_op jit(solution)/shard_map/option_partials/pallas_call | solution.py:355
  19.1 0.1 collective-permute-start.8
  19.2 2.3 %local_attention.3 = (f32[512,1024]{1,0:T(8,128)S(1)}, f32[512,1024]{1,0:T(8,128)S(1)}, f32[512,1024]{1,0:T(8,128)S(1)}) custom-call(s32[1]{0:T(128)} %bitcast.blk_ref, bf16[512,256]{1,0:T(8,128)(2,1)S(1)} %get-tuple-element.81.refs_1_.kv_ref, bf16[512,2048]{1,0:T(8,128)(2,1)S(1)} %get-tuple-element.58.refs_0_.q_ref), custom_call_target="tpu_custom_call" | custom-call | flops 1000000000 | bytes 1 | tf_op jit(solution)/shard_map/local_attention/pallas_call | solution.py:172
  21.5 1.3 %collective-permute-start.4 = (bf16[512,256]{1,0:T(8,128)(2,1)S(1)}, bf16[512,256]{1,0:T(8,128)(2,1)S(1)}, u32[]{:S(2)}, u32[]{:S(2)}) collective-permute-start(bf16[512,256]{1,0:T(8,128)(2,1)S(1)} %get-tuple-element.81.refs_1_.kv_ref), channel_id=1, source_target_pairs={{0,4},{1,5},{2,6},{3,7},{16,20},{17,21},{18,22},{19,23}} | collective-permute-start | bytes 786440 | tf_op jit(solution)/shard_map/ppermute | solution.py:456
  22.8 0.0 collective-permute-done.3.refs_1_
  22.8 0.7 %collective-permute-start.5 = (bf16[512,256]{1,0:T(8,128)(2,1)S(1)}, bf16[512,256]{1,0:T(8,128)(2,1)S(1)}, u32[]{:S(2)}, u32[]{:S(2)}) collective-permute-start(bf16[512,256]{1,0:T(8,128)(2,1)S(1)} %collective-permute-done.3.refs_1_), channel_id=1, source_target_pairs={{8,12},{9,13},{10,14},{11,15},{24,28},{25,29},{26,30},{27,31}} | collective-permute-start | bytes 786440 | tf_op jit(solution)/shard_map/ppermute | solution.py:458
  23.5 4.3 %anchor_attention.2 = (bf16[512,2048]{1,0:T(8,128)(2,1)}, f32[8,128]{1,0:T(8,128)S(1)}) custom-call(s32[1]{0:T(128)} %bitcast.blk_ref, bf16[512,2048]{1,0:T(8,128)(2,1)S(1)} %get-tuple-element.58.refs_0_.q_ref, bf16[512,256]{1,0:T(8,128)(2,1)S(1)} %get-tuple-element.92.kv_ref.refs_0_, f32[512,1024]{1,0:T(8,128)S(1)} %get-tuple-element.93.acc_ref, ...), custom_call_target="tpu_custom_call" | custom-call | flops 1000000000 | bytes 1 | tf_op jit(solution)/shard_map/anchor_attention/pallas_call | solution.py:250
  27.8 1.0 %collective-permute-done.8.b = bf16[64,2176]{1,0:T(8,128)(2,1)S(1)} collective-permute-done((bf16[64,2176]{1,0:T(8,128)(2,1)S(1)}, bf16[64,2176]{1,0:T(8,128)(2,1)S(1)}, u32[]{:S(2)}, u32[]{:S(2)}) %collective-permute-start.8) | collective-permute-done | bytes 278560 | tf_op jit(solution)/shard_map/ppermute | solution.py:415
  28.8 0.6 %merge.2 = (bf16[32,2176]{1,0:T(8,128)(2,1)S(1)}, bf16[32,2176]{1,0:T(8,128)(2,1)S(1)}) custom-call(bf16[64,2176]{1,0:T(8,128)(2,1)S(1)} %get-tuple-element.102.a, bf16[64,2176]{1,0:T(8,128)(2,1)S(1)} %collective-permute-done.8.b, f32[8,128]{1,0:T(8,128)S(1)} %get-tuple-element.104.after), custom_call_target="tpu_custom_call" | custom-call | flops 1 | bytes 1 | tf_op jit(solution)/shard_map/merge/pallas_call | solution.py:403
  29.4 2.4 %collective-permute-start.9 = (bf16[32,2176]{1,0:T(8,128)(2,1)S(1)}, bf16[32,2176]{1,0:T(8,128)(2,1)S(1)}, u32[]{:S(2)}, u32[]{:S(2)}) collective-permute-start(bf16[32,2176]{1,0:T(8,128)(2,1)S(1)} %get-tuple-element.106), channel_id=1, source_target_pairs={{0,8},{4,12},{8,0},{12,4},{1,9},{5,13},{9,1},{13,5},{2,10},{6,14},... | collective-permute-start | bytes 417800 | tf_op jit(solution)/shard_map/ppermute | solution.py:415
  31.8 2.6 %collective-permute-done.4.refs_0_ = bf16[512,256]{1,0:T(8,128)(2,1)S(1)} collective-permute-done((bf16[512,256]{1,0:T(8,128)(2,1)S(1)}, bf16[512,256]{1,0:T(8,128)(2,1)S(1)}, u32[]{:S(2)}, u32[]{:S(2)}) %collective-permute-start.4) | collective-permute-done | bytes 262176 | tf_op jit(solution)/shard_map/ppermute | solution.py:456
  34.3 4.3 %anchor_attention.3 = (bf16[512,2048]{1,0:T(8,128)(2,1)}, f32[8,128]{1,0:T(8,128)S(1)}) custom-call(s32[1]{0:T(128)} %bitcast.blk_ref, bf16[512,2048]{1,0:T(8,128)(2,1)S(1)} %get-tuple-element.58.refs_0_.q_ref, bf16[512,256]{1,0:T(8,128)(2,1)S(1)} %get-tuple-element.81.refs_1_.kv_ref, ...), custom_call_target="tpu_custom_call", output_to_operand_aliasing={{0}: (9, {})} | custom-call | flops 1000000000 | bytes 1 | tf_op jit(solution)/shard_map/anchor_attention/pallas_call | solution.py:250
  38.6 1.0 %merge.3 = bf16[32,2048]{1,0:T(8,128)(2,1)} custom-call(bf16[32,2176]{1,0:T(8,128)(2,1)S(1)} %get-tuple-element.105.a, bf16[32,2176]{1,0:T(8,128)(2,1)S(1)} %collective-permute-done.9.b, f32[8,128]{1,0:T(8,128)S(1)} %get-tuple-element.107.after), custom_call_target="tpu_custom_call" | custom-call | flops 1 | bytes 1 | tf_op jit(solution)/shard_map/merge/pallas_call | solution.py:403
  (5 shorter events, 0.0 us)
Async XLA Ops:
  0.6 8.4 %collective-permute-start.1 = (bf16[16,2048]{1,0:T(8,128)(2,1)}, bf16[16,2048]{1,0:T(8,128)(2,1)S(1)}, u32[]{:S(2)}, u32[]{:S(2)}) collective-permute-start(bf16[16,2048]{1,0:T(8,128)(2,1)} %refs_4_.1), channel_id=1, source_target_pairs={{0,8},{4,12},{8,0},{12,4},{1,9},{5,13},{9,1},{13,5},{2,10},{6,14},... | collective-permute-start | bytes 196616 | tf_op jit(solution)/shard_map/ppermute | solution.py:415
  4.4 5.4 %collective-permute-start = (bf16[512,256]{1,0:T(8,128)(2,1)S(1)}, bf16[512,256]{1,0:T(8,128)(2,1)S(1)}, u32[]{:S(2)}, u32[]{:S(2)}) collective-permute-start(bf16[512,256]{1,0:T(8,128)(2,1)S(1)} %get-tuple-element.92.kv_ref.refs_0_), channel_id=1, source_target_pairs={{0,8},{1,9},{2,10},{3,11},{16,24},{17,25},{18,26},{19,27}} | collective-permute-start | bytes 786440 | tf_op jit(solution)/shard_map/ppermute | solution.py:441
  9.1 8.1 %collective-permute-start.2 = (bf16[32,2048]{1,0:T(8,128)(2,1)S(1)}, bf16[32,2048]{1,0:T(8,128)(2,1)S(1)}, u32[]{:S(2)}, u32[]{:S(2)}) collective-permute-start(bf16[32,2048]{1,0:T(8,128)(2,1)S(1)} %join.1.refs_2_), channel_id=1, source_target_pairs={{0,4},{4,0},{8,12},{12,8},{1,5},{5,1},{9,13},{13,9},{2,6},{6,2},{1... | collective-permute-start | bytes 393224 | tf_op jit(solution)/shard_map/ppermute | solution.py:415
  9.1 13.7 %collective-permute-start.3 = (bf16[512,256]{1,0:T(8,128)(2,1)S(1)}, bf16[512,256]{1,0:T(8,128)(2,1)S(1)}, u32[]{:S(2)}, u32[]{:S(2)}) collective-permute-start(bf16[512,256]{1,0:T(8,128)(2,1)S(1)} %get-tuple-element.81.refs_1_.kv_ref), channel_id=1, source_target_pairs={{0,8},{1,9},{2,10},{3,11},{16,24},{17,25},{18,26},{19,27}} | collective-permute-start | bytes 786440 | tf_op jit(solution)/shard_map/ppermute | solution.py:448
  9.8 13.7 %collective-permute-start.7 = (bf16[512,256]{1,0:T(8,128)(2,1)S(1)}, bf16[512,256]{1,0:T(8,128)(2,1)S(1)}, u32[]{:S(2)}, u32[]{:S(2)}) collective-permute-start(bf16[512,256]{1,0:T(8,128)(2,1)S(1)} %collective-permute-done.refs_1_), channel_id=1, source_target_pairs={{8,12},{9,13},{10,14},{11,15},{24,28},{25,29},{26,30},{27,31}} | collective-permute-start | bytes 786440 | tf_op jit(solution)/shard_map/ppermute | solution.py:458
  10.5 13.0 %collective-permute-start.6 = (bf16[512,256]{1,0:T(8,128)(2,1)S(1)}, bf16[512,256]{1,0:T(8,128)(2,1)S(1)}, u32[]{:S(2)}, u32[]{:S(2)}) collective-permute-start(bf16[512,256]{1,0:T(8,128)(2,1)S(1)} %collective-permute-done.refs_1_), channel_id=1, source_target_pairs={{8,4},{9,5},{10,6},{11,7},{24,20},{25,21},{26,22},{27,23}} | collective-permute-start | bytes 786440 | tf_op jit(solution)/shard_map/ppermute | solution.py:455
  19.1 9.7 %collective-permute-start.8 = (bf16[64,2176]{1,0:T(8,128)(2,1)S(1)}, bf16[64,2176]{1,0:T(8,128)(2,1)S(1)}, u32[]{:S(2)}, u32[]{:S(2)}) collective-permute-start(bf16[64,2176]{1,0:T(8,128)(2,1)S(1)} %get-tuple-element.103), channel_id=1, source_target_pairs={{0,4},{4,0},{8,12},{12,8},{1,5},{5,1},{9,13},{13,9},{2,6},{6,2},{1... | collective-permute-start | bytes 835592 | tf_op jit(solution)/shard_map/ppermute | solution.py:415
  21.5 12.8 %collective-permute-start.4 = (bf16[512,256]{1,0:T(8,128)(2,1)S(1)}, bf16[512,256]{1,0:T(8,128)(2,1)S(1)}, u32[]{:S(2)}, u32[]{:S(2)}) collective-permute-start(bf16[512,256]{1,0:T(8,128)(2,1)S(1)} %get-tuple-element.81.refs_1_.kv_ref), channel_id=1, source_target_pairs={{0,4},{1,5},{2,6},{3,7},{16,20},{17,21},{18,22},{19,23}} | collective-permute-start | bytes 786440 | tf_op jit(solution)/shard_map/ppermute | solution.py:456
  22.8 11.5 %collective-permute-start.5 = (bf16[512,256]{1,0:T(8,128)(2,1)S(1)}, bf16[512,256]{1,0:T(8,128)(2,1)S(1)}, u32[]{:S(2)}, u32[]{:S(2)}) collective-permute-start(bf16[512,256]{1,0:T(8,128)(2,1)S(1)} %collective-permute-done.3.refs_1_), channel_id=1, source_target_pairs={{8,12},{9,13},{10,14},{11,15},{24,28},{25,29},{26,30},{27,31}} | collective-permute-start | bytes 786440 | tf_op jit(solution)/shard_map/ppermute | solution.py:458
  29.4 9.2 %collective-permute-start.9 = (bf16[32,2176]{1,0:T(8,128)(2,1)S(1)}, bf16[32,2176]{1,0:T(8,128)(2,1)S(1)}, u32[]{:S(2)}, u32[]{:S(2)}) collective-permute-start(bf16[32,2176]{1,0:T(8,128)(2,1)S(1)} %get-tuple-element.106), channel_id=1, source_target_pairs={{0,8},{4,12},{8,0},{12,4},{1,9},{5,13},{9,1},{13,5},{2,10},{6,14},... | collective-permute-start | bytes 417800 | tf_op jit(solution)/shard_map/ppermute | solution.py:415

commit v13 on v12

--- a/solution.py
+++ b/solution.py
@@ -58,28 +58,35 @@
     return pltpu.with_memory_space_constraint(x, pltpu.HBM)
 
 
-def parts_kernel(heads, k_ref, v_ref, *refs):
-    kv, sem = refs[:heads], refs[heads]
+def beside(heads, k_ref, v_ref, kv):
     copies = []
     for g in range(heads):
         for ref, at in ((k_ref, 0), (v_ref, HD)):
             copies.append((ref.at[:, g * HD : (g + 1) * HD], kv[g].at[:, at : at + HD]))
-    for copy in start_all(copies, sem):
-        copy.wait()
-
-
-def parts(key, value):
+    return copies
+
+
+def parts_kernel(heads, blk_ref, k_ref, v_ref, *refs):
+    kv, sem = refs[:heads], refs[heads]
+
+    @pl.when(blk_ref[0] == 0)
+    def _():
+        for copy in start_all(beside(heads, k_ref, v_ref, kv), sem):
+            copy.wait()
+
+
+def parts(blk, key, value):
     rows, heads = key.shape[0], key.shape[1] // HD
     outs = pl.pallas_call(
         functools.partial(parts_kernel, heads),
         out_shape=[pltpu.VMEM((rows, 2 * HD), key.dtype)] * heads,
-        in_specs=[HBM] * 2,
+        in_specs=[SMEM] + [HBM] * 2,
         out_specs=[VMEM] * heads,
         scratch_shapes=[pltpu.SemaphoreType.DMA((2 * heads,))],
         compiler_params=params(2),
         cost_estimate=BRIEF,
         name="parts",
-    )(in_hbm(key), in_hbm(value))
+    )(blk, in_hbm(key), in_hbm(value))
     return list(outs)
 
 
@@ -127,60 +134,83 @@
     pipelined([(h, at) for h in range(0, GROUP, PAIR) for at in range(0, rows, TILE)], scores, finish)
 
 
-def local_kernel(g, loads, blk_ref, kv_ref, *refs):
-    ins = max(loads, 1)
-    sources, (acc_ref, top_ref, sum_ref) = refs[:ins], refs[ins : ins + 3]
-    held, ve = refs[ins + 3 : ins + 3 + loads] or sources, refs[ins + 3 + loads]
-    q_ref, queries, others = held[0], {}, []
-    if loads:
-        order = list(range(g * GROUP, g * GROUP + GROUP)) + [h for h in range(q_ref.shape[1] // HD) if h // GROUP != g]
-        spots = [slice(h * HD, (h + PAIR) * HD) for h in order[::PAIR]]
-        copies = [(sources[0].at[:, spot], q_ref.at[:, spot]) for spot in spots]
-        copies += list(zip(sources[1:], held[1:]))
-        copies = start_all(copies, refs[-1])
-        queries = dict(zip(range(0, GROUP, PAIR), copies))
-        others = copies[GROUP // PAIR :]
-
-    def arrived(first):
-        if loads:
-            queries[first].wait()
+def first_kernel(heads, blk_ref, k_ref, v_ref, *refs):
+    count = (len(refs) - heads - 5) // 2
+    sources, state, kv = refs[:count], refs[count : count + 3], refs[count + 3 : count + 3 + heads]
+    held, (ve, sem) = refs[count + 3 + heads : -2], refs[-2:]
+    q_ref = held[0]
+    spots = [slice(h * HD, (h + PAIR) * HD) for h in range(0, q_ref.shape[1] // HD, PAIR)]
+    copies = beside(heads, k_ref, v_ref, kv)[:2] + [(sources[0].at[:, x], q_ref.at[:, x]) for x in spots]
+    copies += beside(heads, k_ref, v_ref, kv)[2:] + list(zip(sources[1:], held[1:]))
+    copies = start_all(copies, sem)
+    ahead = 2 + GROUP // PAIR
+
+    @pl.when(blk_ref[0] > 0)
+    def _():
+        for copy in copies[:2]:
+            copy.wait()
+        local_pass(0, q_ref, kv[0], ve, lambda h: copies[2 + h // PAIR].wait(), keep_in(state))
+
+    @pl.when(blk_ref[0] == 0)
+    def _():
+        for copy in copies[:ahead]:
+            copy.wait()
+
+    for copy in copies[ahead:]:
+        copy.wait()
+
+
+def first_attention(blk, key, value, query, others):
+    rows, heads = key.shape[0], key.shape[1] // HD
+    sources = [query, *others]
+    outs = pl.pallas_call(
+        functools.partial(first_kernel, heads),
+        out_shape=[pltpu.VMEM((rows, GROUP * HD), jnp.float32)] * 3
+        + [pltpu.VMEM((rows, 2 * HD), key.dtype)] * heads
+        + [pltpu.VMEM(x.shape, x.dtype) for x in sources],
+        in_specs=[SMEM] + [HBM] * (2 + len(sources)),
+        out_specs=[VMEM] * (3 + heads + len(sources)),
+        scratch_shapes=[
+            pltpu.VMEM((rows, 2 * HD), jnp.bfloat16),
+            pltpu.SemaphoreType.DMA((2 * heads + query.shape[1] // HD // PAIR + len(others),)),
+        ],
+        compiler_params=params(6),
+        cost_estimate=cost(2 * 10**9),
+        name="local_attention",
+    )(blk, *[in_hbm(x) for x in (key, value, *sources)])
+    return list(outs[:3]), list(outs[3 : 3 + heads]), list(outs[3 + heads :])
+
+
+def keep_in(state):
+    acc_ref, top_ref, sum_ref = state
 
     def emit(rows, h, total, z, top):
         here = (rows, head_columns(h))
         acc_ref[here], sum_ref[here], top_ref[here] = total, z, jnp.broadcast_to(top, total.shape)
 
+    return emit
+
+
+def local_kernel(g, blk_ref, kv_ref, q_ref, *refs):
     @pl.when(blk_ref[0] > 0)
     def _():
-        local_pass(g, q_ref, kv_ref, ve, arrived, emit)
-
-    @pl.when(blk_ref[0] == 0)
-    def _():
-        for copy in queries.values():
-            copy.wait()
-
-    for copy in others:
-        copy.wait()
-
-
-def local_attention(blk, kv, g, query, loads=()):
+        local_pass(g, q_ref, kv_ref, refs[3], lambda h: None, keep_in(refs[:3]))
+
+
+def local_attention(blk, kv, g, query):
     rows = kv.shape[0]
-    sources, held = [query], []
-    if loads:
-        sources = [in_hbm(x) for x in (query, *loads)]
-        held = [pltpu.VMEM(x.shape, x.dtype) for x in sources]
-    semaphores = query.shape[1] // HD // PAIR + len(loads)
-    outs = pl.pallas_call(
-        functools.partial(local_kernel, g, len(held)),
-        out_shape=[pltpu.VMEM((rows, GROUP * HD), jnp.float32)] * 3 + held,
-        in_specs=[SMEM, VMEM] + [HBM if loads else VMEM] * len(sources),
-        out_specs=[VMEM] * (3 + len(held)),
-        scratch_shapes=[pltpu.VMEM((rows, 2 * HD), jnp.bfloat16)]
-        + ([pltpu.SemaphoreType.DMA((semaphores,))] if loads else []),
-        compiler_params=params(6),
-        cost_estimate=cost(2 * 10**9 if loads else 10**9),
-        name="local_attention",
-    )(blk, kv, *sources)
-    return list(outs[:3]), list(outs[3:])
+    return list(
+        pl.pallas_call(
+            functools.partial(local_kernel, g),
+            out_shape=[pltpu.VMEM((rows, GROUP * HD), jnp.float32)] * 3,
+            in_specs=[SMEM, VMEM, VMEM],
+            out_specs=[VMEM] * 3,
+            scratch_shapes=[pltpu.VMEM((rows, 2 * HD), jnp.bfloat16)],
+            compiler_params=params(6),
+            cost_estimate=cost(10**9),
+            name="local_attention",
+        )(blk, kv, query)
+    )
 
 
 def anchor_kernel(g, count, prior, blk_ref, q_ref, kv_ref, acc_ref, top_ref, sum_ref, *refs):
@@ -430,35 +460,38 @@
     row = lambda x: x.reshape(1, options)
 
     blk_arr, ctx_key = hold((blk_arr, ctx_key))
-    masks, shards = [0], [opt_query]
+    sent = parts(blk_arr, ctx_key, ctx_value)
+    sent, opt_query = hold((sent, opt_query))
+    shards = [opt_query]
+    masks = [0]
     for bit in reversed(range(1, rounds)):
         mine = shards[0] if len(shards) == 1 else jnp.concatenate(shards, axis=0)
         shards = [mine, swap(mine, n, 1 << bit)]
         masks = masks + [mask | 1 << bit for mask in masks]
     masks = masks + [mask | 1 for mask in masks]
-    kvs = parts(ctx_key, ctx_value)
     if n == 4:
-        first = [lax.ppermute(kvs[0], "blk", [(0, 2)])]
-    small = [row(opt_owner), row(opt_slot), row(opt_length)]
-    state, (ctx_query, *small, own) = local_attention(blk_arr, kvs[0], 0, ctx_query, small + shards[:1])
-    kvs, states, shards = hold((kvs, [state], shards))
+        first = [lax.ppermute(sent[0], "blk", [(0, 2)])]
+    small = [row(opt_owner), row(opt_slot), row(opt_length), shards[0]]
+    state, kvs, (ctx_query, *small, own) = first_attention(blk_arr, ctx_key, ctx_value, ctx_query, small)
+    kvs, state, sent, shards = hold((kvs, state, sent, shards))
     mine = join([own, *shards[1:]])
     queries = [mine, swap(mine, n, 1)]
+    states = [state]
     if n == 4:
-        first += [lax.ppermute(kv, "blk", [(0, 2)]) for kv in kvs[1:]]
-        first[0], kvs = hold((first[0], kvs))
-    keep, send = option_partials(blk_arr, *small, kvs, masks, queries, state[1])
-    keep, kvs = hold((keep, kvs))
-    states += [local_attention(blk_arr, kv, g, ctx_query)[0] for g, kv in enumerate(kvs) if g]
+        first += [lax.ppermute(x, "blk", [(0, 2)]) for x in sent[1:]]
+    states += [local_attention(blk_arr, kv, g, ctx_query) for g, kv in enumerate(kvs) if g]
     if n == 4:
-        kvs, states = hold((kvs, states))
+        first[0], states = hold((first[0], states))
+    keep, send = option_partials(blk_arr, *small, kvs, masks, queries, states[-1][1])
+    if n == 4:
         near = [lax.ppermute(first[0], "blk", [(2, 1)])]
-        near += [lax.ppermute(kv, "blk", [(0, 1)]) for kv in kvs[1:]]
-        first[1:], states = hold((first[1:], states))
+        sent, keep = hold((sent, keep))
+        near += [lax.ppermute(x, "blk", [(0, 1)]) for x in sent[1:]]
+        first[1:], keep = hold((first[1:], keep))
         anchors = [[x, y, lax.ppermute(y, "blk", [(2, 3)])] for x, y in zip(near, first)]
         anchors[0], first = hold((anchors[0], first))
     else:
-        anchors = [[from_root(kv, blk)] for kv in kvs]
+        anchors = [[from_root(x, blk)] for x in sent]
     ctx_out, tokens = None, []
     for g, state in enumerate(states):
         ctx_out, token = anchor_attention(blk_arr, ctx_query, kvs[g], state, anchors[g], g, ctx_out)

time: 40.2 us -> 44.1 us (1.097)
  the two profiles are of different devices: /device:TPU:12 before, /device:TPU:24 now
where the time goes in v13:
time: 44.1 us; the launch traced here: 43.9 us
  Pallas kernels  18.5 us (42%)
  waiting for transfers between devices  15.5 us (35%)
  starting transfers between devices  9.1 us (21%)
  between operations  0.78 us (2%)
    ppermute x4, waiting for transfers between devices, swap(): return lax.ppermute(x, 'blk', [(i, i ^ mask) for i in range(n)])  8.53 us
    pallas_call x2, Pallas kernels, anchor_attention(): pl.pallas_call(functools.partial(anchor_kernel, g, len(cands), len(alias)...  8.49 us
    ppermute x2, waiting for transfers between devices, body(): lax.ppermute(y, 'blk', [(2, 3)])  6.91 us
    pallas_call x1, Pallas kernels, first_attention(): pl.pallas_call(functools.partial(first_kernel, heads), out_shape=[pltpu.V...  4.09 us
    ppermute x4, starting transfers between devices, swap(): return lax.ppermute(x, 'blk', [(i, i ^ mask) for i in range(n)])  3.83 us
    ppermute x2, starting transfers between devices, body(): lax.ppermute(y, 'blk', [(2, 3)])  2.58 us
    pallas_call x1, Pallas kernels, local_attention(): pl.pallas_call(functools.partial(local_kernel, g), out_shape=[pltpu.VMEM(...  2.29 us
    pallas_call x1, Pallas kernels, option_partials(): pl.pallas_call(functools.partial(option_kernel, masks, heads), out_shape=...  2.03 us
  transfers between devices with their start and end apart: 10, of which 5 were waited for; matrix products, arithmetic and copies ran while one was open for 0% of the time, Pallas kernels for 40%

profile of v13, /device:TPU:24, one launch (start us, length us, event | category | flops | bytes accessed | tf_op | source)
XLA Modules:
  0.0 43.9 jit_solution(8951438949855194352)
XLA Ops:
  0.7 0.4 collective-permute-start
  1.1 0.7 %collective-permute-start.1 = (bf16[512,256]{1,0:T(8,128)(2,1)S(1)}, bf16[512,256]{1,0:T(8,128)(2,1)S(1)}, u32[]{:S(2)}, u32[]{:S(2)}) collective-permute-start(bf16[512,256]{1,0:T(8,128)(2,1)S(1)} %get-tuple-element.62), channel_id=1, source_target_pairs={{0,8},{1,9},{2,10},{3,11},{16,24},{17,25},{18,26},{19,27}} | collective-permute-start | bytes 786440 | tf_op jit(solution)/shard_map/ppermute | solution.py:473
  1.8 4.1 %local_attention.2 = (f32[512,1024]{1,0:T(8,128)S(1)}, f32[512,1024]{1,0:T(8,128)S(1)}, f32[512,1024]{1,0:T(8,128)S(1)}, bf16[512,256]{1,0:T(8,128)(2,1)S(1)}, b...) custom-call(s32[1]{0:T(128)} %bitcast.blk_ref, ...), custom_call_target="tpu_custom_call" | custom-call | flops 2000000000 | bytes 1 | tf_op jit(solution)/shard_map/local_attention/pallas_call | solution.py:166
  5.9 6.7 %collective-permute-done.refs_1_ = bf16[16,2048]{1,0:T(8,128)(2,1)S(1)} collective-permute-done((bf16[16,2048]{1,0:T(8,128)(2,1)}, bf16[16,2048]{1,0:T(8,128)(2,1)S(1)}, u32[]{:S(2)}, u32[]{:S(2)}) %collective-permute-start) | collective-permute-done | bytes 65568 | tf_op jit(solution)/shard_map/ppermute | solution.py:445
  12.6 0.1 collective-permute-start.2
  12.7 0.7 %collective-permute-start.4 = (bf16[512,256]{1,0:T(8,128)(2,1)S(1)}, bf16[512,256]{1,0:T(8,128)(2,1)S(1)}, u32[]{:S(2)}, u32[]{:S(2)}) collective-permute-start(bf16[512,256]{1,0:T(8,128)(2,1)S(1)} %get-tuple-element.82), channel_id=1, source_target_pairs={{0,8},{1,9},{2,10},{3,11},{16,24},{17,25},{18,26},{19,27}} | collective-permute-start | bytes 786440 | tf_op jit(solution)/shard_map/ppermute | solution.py:481
  13.4 2.3 %local_attention.3 = (f32[512,1024]{1,0:T(8,128)S(1)}, f32[512,1024]{1,0:T(8,128)S(1)}, f32[512,1024]{1,0:T(8,128)S(1)}) custom-call(s32[1]{0:T(128)} %bitcast.blk_ref, bf16[512,256]{1,0:T(8,128)(2,1)S(1)} %get-tuple-element.64.kv_ref.refs_1_, bf16[512,2048]{1,0:T(8,128)(2,1)S(1)} %get-tuple-element.56.q_ref), custom_call_target="tpu_custom_call" | custom-call | flops 1000000000 | bytes 1 | tf_op jit(solution)/shard_map/local_attention/pallas_call | solution.py:203
  15.7 0.0 collective-permute-done.1.refs_1_
  15.7 1.3 %collective-permute-start.7 = (bf16[512,256]{1,0:T(8,128)(2,1)S(1)}, bf16[512,256]{1,0:T(8,128)(2,1)S(1)}, u32[]{:S(2)}, u32[]{:S(2)}) collective-permute-start(bf16[512,256]{1,0:T(8,128)(2,1)S(1)} %collective-permute-done.1.refs_1_), channel_id=1, source_target_pairs={{8,12},{9,13},{10,14},{11,15},{24,28},{25,29},{26,30},{27,31}} | collective-permute-start | bytes 786440 | tf_op jit(solution)/shard_map/ppermute | solution.py:491
  17.0 0.7 %collective-permute-start.6 = (bf16[512,256]{1,0:T(8,128)(2,1)S(1)}, bf16[512,256]{1,0:T(8,128)(2,1)S(1)}, u32[]{:S(2)}, u32[]{:S(2)}) collective-permute-start(bf16[512,256]{1,0:T(8,128)(2,1)S(1)} %collective-permute-done.1.refs_1_), channel_id=1, source_target_pairs={{8,4},{9,5},{10,6},{11,7},{24,20},{25,21},{26,22},{27,23}} | collective-permute-start | bytes 786440 | tf_op jit(solution)/shard_map/ppermute | solution.py:487
  17.7 0.1 collective-permute-done.2.refs_3_
  17.8 2.0 %option_partials.1 = (bf16[64,2176]{1,0:T(8,128)(2,1)S(1)}, bf16[64,2176]{1,0:T(8,128)(2,1)S(1)}) custom-call(s32[1]{0:T(128)} %bitcast.blk_ref, s32[1,64]{1,0:T(1,128)S(1)} %get-tuple-element.75.owner_ref, s32[1,64]{1,0:T(1,128)S(1)} %get-tuple-element.76.slot_ref, s32[1,64]{1,0:T(1,128)S(1)} %get-tuple-element.77.length_ref, ...), custom_call_target="tpu_custom_call" | custom-call | flops 1000000000 | bytes 1 | tf_op jit(solution)/shard_map/option_partials/pallas_call | solution.py:385
  19.8 3.3 %collective-permute-start.8 = (bf16[64,2176]{1,0:T(8,128)(2,1)S(1)}, bf16[64,2176]{1,0:T(8,128)(2,1)S(1)}, u32[]{:S(2)}, u32[]{:S(2)}) collective-permute-start(bf16[64,2176]{1,0:T(8,128)(2,1)S(1)} %get-tuple-element.95), channel_id=1, source_target_pairs={{0,4},{4,0},{8,12},{12,8},{1,5},{5,1},{9,13},{13,9},{2,6},{6,2},{1... | collective-permute-start | bytes 835592 | tf_op jit(solution)/shard_map/ppermute | solution.py:445
  23.1 0.7 %collective-permute-start.3 = (bf16[512,256]{1,0:T(8,128)(2,1)S(1)}, bf16[512,256]{1,0:T(8,128)(2,1)S(1)}, u32[]{:S(2)}, u32[]{:S(2)}) collective-permute-start(bf16[512,256]{1,0:T(8,128)(2,1)S(1)} %get-tuple-element.82), channel_id=1, source_target_pairs={{0,4},{1,5},{2,6},{3,7},{16,20},{17,21},{18,22},{19,23}} | collective-permute-start | bytes 786440 | tf_op jit(solution)/shard_map/ppermute | solution.py:489
  23.7 0.0 collective-permute-done.4.refs_1_
  23.8 1.3 %collective-permute-start.5 = (bf16[512,256]{1,0:T(8,128)(2,1)S(1)}, bf16[512,256]{1,0:T(8,128)(2,1)S(1)}, u32[]{:S(2)}, u32[]{:S(2)}) collective-permute-start(bf16[512,256]{1,0:T(8,128)(2,1)S(1)} %collective-permute-done.4.refs_1_), channel_id=1, source_target_pairs={{8,12},{9,13},{10,14},{11,15},{24,28},{25,29},{26,30},{27,31}} | collective-permute-start | bytes 786440 | tf_op jit(solution)/shard_map/ppermute | solution.py:491
  25.1 1.7 %collective-permute-done.7.refs_2_ = bf16[512,256]{1,0:T(8,128)(2,1)S(1)} collective-permute-done((bf16[512,256]{1,0:T(8,128)(2,1)S(1)}, bf16[512,256]{1,0:T(8,128)(2,1)S(1)}, u32[]{:S(2)}, u32[]{:S(2)}) %collective-permute-start.7) | collective-permute-done | bytes 262176 | tf_op jit(solution)/shard_map/ppermute | solution.py:491
  26.8 4.2 %anchor_attention.2 = (bf16[512,2048]{1,0:T(8,128)(2,1)}, f32[8,128]{1,0:T(8,128)S(1)}) custom-call(s32[1]{0:T(128)} %bitcast.blk_ref, bf16[512,2048]{1,0:T(8,128)(2,1)S(1)} %get-tuple-element.56.q_ref, bf16[512,256]{1,0:T(8,128)(2,1)S(1)} %get-tuple-element.78.refs_0_.kv_ref, f32[512,1024]{1,0:T(8,128)S(1)} %get-tuple-element.85.acc_ref, ...), custom_call_target="tpu_custom_call" | custom-call | flops 1000000000 | bytes 1 | tf_op jit(solution)/shard_map/anchor_attention/pallas_call | solution.py:280
  31.1 1.7 %collective-permute-done.8.b = bf16[64,2176]{1,0:T(8,128)(2,1)S(1)} collective-permute-done((bf16[64,2176]{1,0:T(8,128)(2,1)S(1)}, bf16[64,2176]{1,0:T(8,128)(2,1)S(1)}, u32[]{:S(2)}, u32[]{:S(2)}) %collective-permute-start.8) | collective-permute-done | bytes 278560 | tf_op jit(solution)/shard_map/ppermute | solution.py:445
  32.8 0.6 %merge.2 = (bf16[32,2176]{1,0:T(8,128)(2,1)S(1)}, bf16[32,2176]{1,0:T(8,128)(2,1)S(1)}) custom-call(bf16[64,2176]{1,0:T(8,128)(2,1)S(1)} %get-tuple-element.94.a, bf16[64,2176]{1,0:T(8,128)(2,1)S(1)} %collective-permute-done.8.b, f32[8,128]{1,0:T(8,128)S(1)} %get-tuple-element.96.after), custom_call_target="tpu_custom_call" | custom-call | flops 1 | bytes 1 | tf_op jit(solution)/shard_map/merge/pallas_call | solution.py:433
  33.3 0.1 collective-permute-start.9
  33.4 5.2 %collective-permute-done.5.refs_2_ = bf16[512,256]{1,0:T(8,128)(2,1)S(1)} collective-permute-done((bf16[512,256]{1,0:T(8,128)(2,1)S(1)}, bf16[512,256]{1,0:T(8,128)(2,1)S(1)}, u32[]{:S(2)}, u32[]{:S(2)}) %collective-permute-start.5) | collective-permute-done | bytes 262176 | tf_op jit(solution)/shard_map/ppermute | solution.py:491
  38.6 4.2 %anchor_attention.3 = (bf16[512,2048]{1,0:T(8,128)(2,1)}, f32[8,128]{1,0:T(8,128)S(1)}) custom-call(s32[1]{0:T(128)} %bitcast.blk_ref, bf16[512,2048]{1,0:T(8,128)(2,1)S(1)} %get-tuple-element.56.q_ref, bf16[512,256]{1,0:T(8,128)(2,1)S(1)} %get-tuple-element.64.kv_ref.refs_1_, ...), custom_call_target="tpu_custom_call", output_to_operand_aliasing={{0}: (9, {})} | custom-call | flops 1000000000 | bytes 1 | tf_op jit(solution)/shard_map/anchor_attention/pallas_call | solution.py:280
  42.9 1.0 %merge.3 = bf16[32,2048]{1,0:T(8,128)(2,1)} custom-call(bf16[32,2176]{1,0:T(8,128)(2,1)S(1)} %get-tuple-element.97.a, bf16[32,2176]{1,0:T(8,128)(2,1)S(1)} %collective-permute-done.9.b, f32[8,128]{1,0:T(8,128)S(1)} %get-tuple-element.99.after), custom_call_target="tpu_custom_call" | custom-call | flops 1 | bytes 1 | tf_op jit(solution)/shard_map/merge/pallas_call | solution.py:433
  (5 shorter events, 0.1 us)
Async XLA Ops:
  0.7 11.9 %collective-permute-start = (bf16[16,2048]{1,0:T(8,128)(2,1)}, bf16[16,2048]{1,0:T(8,128)(2,1)S(1)}, u32[]{:S(2)}, u32[]{:S(2)}) collective-permute-start(bf16[16,2048]{1,0:T(8,128)(2,1)} %refs_4_), channel_id=1, source_target_pairs={{0,8},{4,12},{8,0},{12,4},{1,9},{5,13},{9,1},{13,5},{2,10},{6,14},... | collective-permute-start | bytes 196616 | tf_op jit(solution)/shard_map/ppermute | solution.py:445
  1.1 14.6 %collective-permute-start.1 = (bf16[512,256]{1,0:T(8,128)(2,1)S(1)}, bf16[512,256]{1,0:T(8,128)(2,1)S(1)}, u32[]{:S(2)}, u32[]{:S(2)}) collective-permute-start(bf16[512,256]{1,0:T(8,128)(2,1)S(1)} %get-tuple-element.62), channel_id=1, source_target_pairs={{0,8},{1,9},{2,10},{3,11},{16,24},{17,25},{18,26},{19,27}} | collective-permute-start | bytes 786440 | tf_op jit(solution)/shard_map/ppermute | solution.py:473
  12.6 5.1 %collective-permute-start.2 = (bf16[32,2048]{1,0:T(8,128)(2,1)S(1)}, bf16[32,2048]{1,0:T(8,128)(2,1)S(1)}, u32[]{:S(2)}, u32[]{:S(2)}) collective-permute-start(bf16[32,2048]{1,0:T(8,128)(2,1)S(1)} %join.1.refs_2_), channel_id=1, source_target_pairs={{0,4},{4,0},{8,12},{12,8},{1,5},{5,1},{9,13},{13,9},{2,6},{6,2},{1... | collective-permute-start | bytes 393224 | tf_op jit(solution)/shard_map/ppermute | solution.py:445
  12.7 11.1 %collective-permute-start.4 = (bf16[512,256]{1,0:T(8,128)(2,1)S(1)}, bf16[512,256]{1,0:T(8,128)(2,1)S(1)}, u32[]{:S(2)}, u32[]{:S(2)}) collective-permute-start(bf16[512,256]{1,0:T(8,128)(2,1)S(1)} %get-tuple-element.82), channel_id=1, source_target_pairs={{0,8},{1,9},{2,10},{3,11},{16,24},{17,25},{18,26},{19,27}} | collective-permute-start | bytes 786440 | tf_op jit(solution)/shard_map/ppermute | solution.py:481
  15.7 11.1 %collective-permute-start.7 = (bf16[512,256]{1,0:T(8,128)(2,1)S(1)}, bf16[512,256]{1,0:T(8,128)(2,1)S(1)}, u32[]{:S(2)}, u32[]{:S(2)}) collective-permute-start(bf16[512,256]{1,0:T(8,128)(2,1)S(1)} %collective-permute-done.1.refs_1_), channel_id=1, source_target_pairs={{8,12},{9,13},{10,14},{11,15},{24,28},{25,29},{26,30},{27,31}} | collective-permute-start | bytes 786440 | tf_op jit(solution)/shard_map/ppermute | solution.py:491
  17.0 9.8 %collective-permute-start.6 = (bf16[512,256]{1,0:T(8,128)(2,1)S(1)}, bf16[512,256]{1,0:T(8,128)(2,1)S(1)}, u32[]{:S(2)}, u32[]{:S(2)}) collective-permute-start(bf16[512,256]{1,0:T(8,128)(2,1)S(1)} %collective-permute-done.1.refs_1_), channel_id=1, source_target_pairs={{8,4},{9,5},{10,6},{11,7},{24,20},{25,21},{26,22},{27,23}} | collective-permute-start | bytes 786440 | tf_op jit(solution)/shard_map/ppermute | solution.py:487
  19.8 13.0 %collective-permute-start.8 = (bf16[64,2176]{1,0:T(8,128)(2,1)S(1)}, bf16[64,2176]{1,0:T(8,128)(2,1)S(1)}, u32[]{:S(2)}, u32[]{:S(2)}) collective-permute-start(bf16[64,2176]{1,0:T(8,128)(2,1)S(1)} %get-tuple-element.95), channel_id=1, source_target_pairs={{0,4},{4,0},{8,12},{12,8},{1,5},{5,1},{9,13},{13,9},{2,6},{6,2},{1... | collective-permute-start | bytes 835592 | tf_op jit(solution)/shard_map/ppermute | solution.py:445
  23.1 10.4 %collective-permute-start.3 = (bf16[512,256]{1,0:T(8,128)(2,1)S(1)}, bf16[512,256]{1,0:T(8,128)(2,1)S(1)}, u32[]{:S(2)}, u32[]{:S(2)}) collective-permute-start(bf16[512,256]{1,0:T(8,128)(2,1)S(1)} %get-tuple-element.82), channel_id=1, source_target_pairs={{0,4},{1,5},{2,6},{3,7},{16,20},{17,21},{18,22},{19,23}} | collective-permute-start | bytes 786440 | tf_op jit(solution)/shard_map/ppermute | solution.py:489
  23.8 14.8 %collective-permute-start.5 = (bf16[512,256]{1,0:T(8,128)(2,1)S(1)}, bf16[512,256]{1,0:T(8,128)(2,1)S(1)}, u32[]{:S(2)}, u32[]{:S(2)}) collective-permute-start(bf16[512,256]{1,0:T(8,128)(2,1)S(1)} %collective-permute-done.4.refs_1_), channel_id=1, source_target_pairs={{8,12},{9,13},{10,14},{11,15},{24,28},{25,29},{26,30},{27,31}} | collective-permute-start | bytes 786440 | tf_op jit(solution)/shard_map/ppermute | solution.py:491
  33.3 9.5 %collective-permute-start.9 = (bf16[32,2176]{1,0:T(8,128)(2,1)S(1)}, bf16[32,2176]{1,0:T(8,128)(2,1)S(1)}, u32[]{:S(2)}, u32[]{:S(2)}) collective-permute-start(bf16[32,2176]{1,0:T(8,128)(2,1)S(1)} %get-tuple-element.98), channel_id=1, source_target_pairs={{0,8},{4,12},{8,0},{12,4},{1,9},{5,13},{9,1},{13,5},{2,10},{6,14},... | collective-permute-start | bytes 417800 | tf_op jit(solution)/shard_map/ppermute | solution.py:445

commit v14 on v13

--- a/solution.py
+++ b/solution.py
@@ -66,27 +66,24 @@
     return copies
 
 
-def parts_kernel(heads, blk_ref, k_ref, v_ref, *refs):
+def parts_kernel(heads, k_ref, v_ref, *refs):
     kv, sem = refs[:heads], refs[heads]
-
-    @pl.when(blk_ref[0] == 0)
-    def _():
-        for copy in start_all(beside(heads, k_ref, v_ref, kv), sem):
-            copy.wait()
-
-
-def parts(blk, key, value):
+    for copy in start_all(beside(heads, k_ref, v_ref, kv), sem):
+        copy.wait()
+
+
+def parts(key, value):
     rows, heads = key.shape[0], key.shape[1] // HD
     outs = pl.pallas_call(
         functools.partial(parts_kernel, heads),
         out_shape=[pltpu.VMEM((rows, 2 * HD), key.dtype)] * heads,
-        in_specs=[SMEM] + [HBM] * 2,
+        in_specs=[HBM] * 2,
         out_specs=[VMEM] * heads,
         scratch_shapes=[pltpu.SemaphoreType.DMA((2 * heads,))],
         compiler_params=params(2),
         cost_estimate=BRIEF,
         name="parts",
-    )(blk, in_hbm(key), in_hbm(value))
+    )(in_hbm(key), in_hbm(value))
     return list(outs)
 
 
@@ -134,22 +131,18 @@
     pipelined([(h, at) for h in range(0, GROUP, PAIR) for at in range(0, rows, TILE)], scores, finish)
 
 
-def first_kernel(heads, blk_ref, k_ref, v_ref, *refs):
-    count = (len(refs) - heads - 5) // 2
-    sources, state, kv = refs[:count], refs[count : count + 3], refs[count + 3 : count + 3 + heads]
-    held, (ve, sem) = refs[count + 3 + heads : -2], refs[-2:]
+def first_kernel(blk_ref, kv_ref, *refs):
+    count = (len(refs) - 5) // 2
+    sources, state, held, (ve, sem) = refs[:count], refs[count : count + 3], refs[count + 3 : -2], refs[-2:]
     q_ref = held[0]
     spots = [slice(h * HD, (h + PAIR) * HD) for h in range(0, q_ref.shape[1] // HD, PAIR)]
-    copies = beside(heads, k_ref, v_ref, kv)[:2] + [(sources[0].at[:, x], q_ref.at[:, x]) for x in spots]
-    copies += beside(heads, k_ref, v_ref, kv)[2:] + list(zip(sources[1:], held[1:]))
+    copies = [(sources[0].at[:, x], q_ref.at[:, x]) for x in spots] + list(zip(sources[1:], held[1:]))
     copies = start_all(copies, sem)
-    ahead = 2 + GROUP // PAIR
+    ahead = GROUP // PAIR
 
     @pl.when(blk_ref[0] > 0)
     def _():
-        for copy in copies[:2]:
-            copy.wait()
-        local_pass(0, q_ref, kv[0], ve, lambda h: copies[2 + h // PAIR].wait(), keep_in(state))
+        local_pass(0, q_ref, kv_ref, ve, lambda h: copies[h // PAIR].wait(), keep_in(state))
 
     @pl.when(blk_ref[0] == 0)
     def _():
@@ -160,25 +153,23 @@
         copy.wait()
 
 
-def first_attention(blk, key, value, query, others):
-    rows, heads = key.shape[0], key.shape[1] // HD
+def first_attention(blk, kv, query, others):
+    rows = kv.shape[0]
     sources = [query, *others]
     outs = pl.pallas_call(
-        functools.partial(first_kernel, heads),
-        out_shape=[pltpu.VMEM((rows, GROUP * HD), jnp.float32)] * 3
-        + [pltpu.VMEM((rows, 2 * HD), key.dtype)] * heads
-        + [pltpu.VMEM(x.shape, x.dtype) for x in sources],
-        in_specs=[SMEM] + [HBM] * (2 + len(sources)),
-        out_specs=[VMEM] * (3 + heads + len(sources)),
+        first_kernel,
+        out_shape=[pltpu.VMEM((rows, GROUP * HD), jnp.float32)] * 3 + [pltpu.VMEM(x.shape, x.dtype) for x in sources],
+        in_specs=[SMEM, VMEM] + [HBM] * len(sources),
+        out_specs=[VMEM] * (3 + len(sources)),
         scratch_shapes=[
             pltpu.VMEM((rows, 2 * HD), jnp.bfloat16),
-            pltpu.SemaphoreType.DMA((2 * heads + query.shape[1] // HD // PAIR + len(others),)),
+            pltpu.SemaphoreType.DMA((query.shape[1] // HD // PAIR + len(others),)),
         ],
         compiler_params=params(6),
         cost_estimate=cost(2 * 10**9),
         name="local_attention",
-    )(blk, *[in_hbm(x) for x in (key, value, *sources)])
-    return list(outs[:3]), list(outs[3 : 3 + heads]), list(outs[3 + heads :])
+    )(blk, kv, *[in_hbm(x) for x in sources])
+    return list(outs[:3]), list(outs[3:])
 
 
 def keep_in(state):
@@ -460,8 +451,7 @@
     row = lambda x: x.reshape(1, options)
 
     blk_arr, ctx_key = hold((blk_arr, ctx_key))
-    sent = parts(blk_arr, ctx_key, ctx_value)
-    sent, opt_query = hold((sent, opt_query))
+    kvs = parts(ctx_key, ctx_value)
     shards = [opt_query]
     masks = [0]
     for bit in reversed(range(1, rounds)):
@@ -470,28 +460,28 @@
         masks = masks + [mask | 1 << bit for mask in masks]
     masks = masks + [mask | 1 for mask in masks]
     if n == 4:
-        first = [lax.ppermute(sent[0], "blk", [(0, 2)])]
+        first = [lax.ppermute(kvs[0], "blk", [(0, 2)])]
     small = [row(opt_owner), row(opt_slot), row(opt_length), shards[0]]
-    state, kvs, (ctx_query, *small, own) = first_attention(blk_arr, ctx_key, ctx_value, ctx_query, small)
-    kvs, state, sent, shards = hold((kvs, state, sent, shards))
+    state, (ctx_query, *small, own) = first_attention(blk_arr, kvs[0], ctx_query, small)
+    kvs, state, shards = hold((kvs, state, shards))
     mine = join([own, *shards[1:]])
     queries = [mine, swap(mine, n, 1)]
     states = [state]
     if n == 4:
-        first += [lax.ppermute(x, "blk", [(0, 2)]) for x in sent[1:]]
+        first += [lax.ppermute(x, "blk", [(0, 2)]) for x in kvs[1:]]
     states += [local_attention(blk_arr, kv, g, ctx_query) for g, kv in enumerate(kvs) if g]
     if n == 4:
         first[0], states = hold((first[0], states))
     keep, send = option_partials(blk_arr, *small, kvs, masks, queries, states[-1][1])
     if n == 4:
         near = [lax.ppermute(first[0], "blk", [(2, 1)])]
-        sent, keep = hold((sent, keep))
-        near += [lax.ppermute(x, "blk", [(0, 1)]) for x in sent[1:]]
+        kvs, keep = hold((kvs, keep))
+        near += [lax.ppermute(x, "blk", [(0, 1)]) for x in kvs[1:]]
         first[1:], keep = hold((first[1:], keep))
         anchors = [[x, y, lax.ppermute(y, "blk", [(2, 3)])] for x, y in zip(near, first)]
         anchors[0], first = hold((anchors[0], first))
     else:
-        anchors = [[from_root(x, blk)] for x in sent]
+        anchors = [[from_root(x, blk)] for x in kvs]
     ctx_out, tokens = None, []
     for g, state in enumerate(states):
         ctx_out, token = anchor_attention(blk_arr, ctx_query, kvs[g], state, anchors[g], g, ctx_out)

time: 44.1 us -> 39.8 us (0.902)
  the two profiles are of different devices: /device:TPU:24 before, /device:TPU:12 now
where the time goes in v14:
time: 39.8 us; the launch traced here: 39.5 us
  Pallas kernels  19.3 us (48%)
  starting transfers between devices  11.9 us (30%)
  waiting for transfers between devices  7.53 us (19%)
  between operations  0.79 us (2%)
    pallas_call x2, Pallas kernels, anchor_attention(): pl.pallas_call(functools.partial(anchor_kernel, g, len(cands), len(alias)...  8.43 us
    ppermute x4, starting transfers between devices, swap(): return lax.ppermute(x, 'blk', [(i, i ^ mask) for i in range(n)])  6.57 us
    ppermute x4, waiting for transfers between devices, swap(): return lax.ppermute(x, 'blk', [(i, i ^ mask) for i in range(n)])  4.84 us
    pallas_call x1, Pallas kernels, first_attention(): pl.pallas_call(first_kernel, out_shape=[pltpu.VMEM((rows, GROUP * HD), jn...  3.91 us
    pallas_call x1, Pallas kernels, local_attention(): pl.pallas_call(functools.partial(local_kernel, g), out_shape=[pltpu.VMEM(...  2.29 us
    pallas_call x1, Pallas kernels, option_partials(): pl.pallas_call(functools.partial(option_kernel, masks, heads), out_shape=...  2.03 us
    pallas_call x2, Pallas kernels, merge(): pl.pallas_call(functools.partial(merge_kernel, heads), out_shape=shapes,...  1.55 us
    ppermute x1, waiting for transfers between devices, body(): near = [lax.ppermute(first[0], 'blk', [(2, 1)])]  1.49 us
  transfers between devices with their start and end apart: 10, of which 4 were waited for; matrix products, arithmetic and copies ran while one was open for 0% of the time, Pallas kernels for 46%

profile of v14, /device:TPU:12, one launch (start us, length us, event | category | flops | bytes accessed | tf_op | source)
XLA Modules:
  0.0 39.5 jit_solution(9341760867573373128)
XLA Ops:
  0.6 2.7 %collective-permute-start = (bf16[16,2048]{1,0:T(8,128)(2,1)}, bf16[16,2048]{1,0:T(8,128)(2,1)S(1)}, u32[]{:S(2)}, u32[]{:S(2)}) collective-permute-start(bf16[16,2048]{1,0:T(8,128)(2,1)} %refs_4_.1), channel_id=1, source_target_pairs={{0,8},{4,12},{8,0},{12,4},{1,9},{5,13},{9,1},{13,5},{2,10},{6,14},... | collective-permute-start | bytes 196616 | tf_op jit(solution)/shard_map/ppermute | solution.py:436
  3.3 1.1 %parts.1 = (bf16[512,256]{1,0:T(8,128)(2,1)S(1)}, bf16[512,256]{1,0:T(8,128)(2,1)S(1)}) custom-call(bf16[512,256]{1,0:T(8,128)(2,1)} %k_ref, bf16[512,256]{1,0:T(8,128)(2,1)} %v_ref.1), custom_call_target="tpu_custom_call" | custom-call | flops 1 | bytes 1 | tf_op jit(solution)/shard_map/parts/pallas_call | solution.py:77
  4.4 0.7 %collective-permute-start.2 = (bf16[512,256]{1,0:T(8,128)(2,1)S(1)}, bf16[512,256]{1,0:T(8,128)(2,1)S(1)}, u32[]{:S(2)}, u32[]{:S(2)}) collective-permute-start(bf16[512,256]{1,0:T(8,128)(2,1)S(1)} %get-tuple-element.74.kv_ref.refs_0_), channel_id=1, source_target_pairs={{0,8},{1,9},{2,10},{3,11},{16,24},{17,25},{18,26},{19,27}} | collective-permute-start | bytes 786440 | tf_op jit(solution)/shard_map/ppermute | solution.py:463
  5.1 3.9 %local_attention.2 = (f32[512,1024]{1,0:T(8,128)S(1)}, f32[512,1024]{1,0:T(8,128)S(1)}, f32[512,1024]{1,0:T(8,128)S(1)}, bf16[512,2048]{1,0:T(8,128)(2,1)S(1)}, ...) custom-call(s32[1]{0:T(128)} %bitcast.blk_ref, ...), custom_call_target="tpu_custom_call" | custom-call | flops 2000000000 | bytes 1 | tf_op jit(solution)/shard_map/local_attention/pallas_call | solution.py:159
  9.0 0.0 collective-permute-done.refs_1_
  9.0 0.1 collective-permute-start.1
  9.1 0.7 %collective-permute-start.4 = (bf16[512,256]{1,0:T(8,128)(2,1)S(1)}, bf16[512,256]{1,0:T(8,128)(2,1)S(1)}, u32[]{:S(2)}, u32[]{:S(2)}) collective-permute-start(bf16[512,256]{1,0:T(8,128)(2,1)S(1)} %get-tuple-element.69.kv_ref.refs_1_), channel_id=1, source_target_pairs={{0,8},{1,9},{2,10},{3,11},{16,24},{17,25},{18,26},{19,27}} | collective-permute-start | bytes 786440 | tf_op jit(solution)/shard_map/ppermute | solution.py:471
  9.8 2.3 %local_attention.3 = (f32[512,1024]{1,0:T(8,128)S(1)}, f32[512,1024]{1,0:T(8,128)S(1)}, f32[512,1024]{1,0:T(8,128)S(1)}) custom-call(s32[1]{0:T(128)} %bitcast.blk_ref, bf16[512,256]{1,0:T(8,128)(2,1)S(1)} %get-tuple-element.69.kv_ref.refs_1_, bf16[512,2048]{1,0:T(8,128)(2,1)S(1)} %get-tuple-element.49.q_ref), custom_call_target="tpu_custom_call" | custom-call | flops 1000000000 | bytes 1 | tf_op jit(solution)/shard_map/local_attention/pallas_call | solution.py:194
  12.1 0.7 %collective-permute-start.7 = (bf16[512,256]{1,0:T(8,128)(2,1)S(1)}, bf16[512,256]{1,0:T(8,128)(2,1)S(1)}, u32[]{:S(2)}, u32[]{:S(2)}) collective-permute-start(bf16[512,256]{1,0:T(8,128)(2,1)S(1)} %collective-permute-done.2.refs_1_), channel_id=1, source_target_pairs={{8,12},{9,13},{10,14},{11,15},{24,28},{25,29},{26,30},{27,31}} | collective-permute-start | bytes 786440 | tf_op jit(solution)/shard_map/ppermute | solution.py:481
  12.8 1.3 %collective-permute-start.6 = (bf16[512,256]{1,0:T(8,128)(2,1)S(1)}, bf16[512,256]{1,0:T(8,128)(2,1)S(1)}, u32[]{:S(2)}, u32[]{:S(2)}) collective-permute-start(bf16[512,256]{1,0:T(8,128)(2,1)S(1)} %collective-permute-done.2.refs_1_), channel_id=1, source_target_pairs={{8,4},{9,5},{10,6},{11,7},{24,20},{25,21},{26,22},{27,23}} | collective-permute-start | bytes 786440 | tf_op jit(solution)/shard_map/ppermute | solution.py:477
  14.1 3.0 %collective-permute-done.1.refs_3_ = bf16[32,2048]{1,0:T(8,128)(2,1)S(1)} collective-permute-done((bf16[32,2048]{1,0:T(8,128)(2,1)S(1)}, bf16[32,2048]{1,0:T(8,128)(2,1)S(1)}, u32[]{:S(2)}, u32[]{:S(2)}) %collective-permute-start.1) | collective-permute-done | bytes 131104 | tf_op jit(solution)/shard_map/ppermute | solution.py:436
  17.1 2.0 %option_partials.1 = (bf16[64,2176]{1,0:T(8,128)(2,1)S(1)}, bf16[64,2176]{1,0:T(8,128)(2,1)S(1)}) custom-call(s32[1]{0:T(128)} %bitcast.blk_ref, s32[1,64]{1,0:T(1,128)S(1)} %get-tuple-element.56.owner_ref, s32[1,64]{1,0:T(1,128)S(1)} %get-tuple-element.57.slot_ref, s32[1,64]{1,0:T(1,128)S(1)} %get-tuple-element.58.length_ref, ...), custom_call_target="tpu_custom_call" | custom-call | flops 1000000000 | bytes 1 | tf_op jit(solution)/shard_map/option_partials/pallas_call | solution.py:376
  19.1 0.1 collective-permute-start.8
  19.2 1.3 %collective-permute-start.3 = (bf16[512,256]{1,0:T(8,128)(2,1)S(1)}, bf16[512,256]{1,0:T(8,128)(2,1)S(1)}, u32[]{:S(2)}, u32[]{:S(2)}) collective-permute-start(bf16[512,256]{1,0:T(8,128)(2,1)S(1)} %get-tuple-element.69.kv_ref.refs_1_), channel_id=1, source_target_pairs={{0,4},{1,5},{2,6},{3,7},{16,20},{17,21},{18,22},{19,23}} | collective-permute-start | bytes 786440 | tf_op jit(solution)/shard_map/ppermute | solution.py:479
  20.5 0.7 %collective-permute-start.5 = (bf16[512,256]{1,0:T(8,128)(2,1)S(1)}, bf16[512,256]{1,0:T(8,128)(2,1)S(1)}, u32[]{:S(2)}, u32[]{:S(2)}) collective-permute-start(bf16[512,256]{1,0:T(8,128)(2,1)S(1)} %collective-permute-done.4.refs_1_), channel_id=1, source_target_pairs={{8,12},{9,13},{10,14},{11,15},{24,28},{25,29},{26,30},{27,31}} | collective-permute-start | bytes 786440 | tf_op jit(solution)/shard_map/ppermute | solution.py:481
  21.2 0.0 collective-permute-done.7.refs_2_
  21.2 1.5 %collective-permute-done.6.refs_0_ = bf16[512,256]{1,0:T(8,128)(2,1)S(1)} collective-permute-done((bf16[512,256]{1,0:T(8,128)(2,1)S(1)}, bf16[512,256]{1,0:T(8,128)(2,1)S(1)}, u32[]{:S(2)}, u32[]{:S(2)}) %collective-permute-start.6) | collective-permute-done | bytes 262176 | tf_op jit(solution)/shard_map/ppermute | solution.py:477
  22.7 4.3 %anchor_attention.2 = (bf16[512,2048]{1,0:T(8,128)(2,1)}, f32[8,128]{1,0:T(8,128)S(1)}) custom-call(s32[1]{0:T(128)} %bitcast.blk_ref, bf16[512,2048]{1,0:T(8,128)(2,1)S(1)} %get-tuple-element.49.q_ref, bf16[512,256]{1,0:T(8,128)(2,1)S(1)} %get-tuple-element.74.kv_ref.refs_0_, f32[512,1024]{1,0:T(8,128)S(1)} %get-tuple-element.75.acc_ref, ...), custom_call_target="tpu_custom_call" | custom-call | flops 1000000000 | bytes 1 | tf_op jit(solution)/shard_map/anchor_attention/pallas_call | solution.py:271
  27.0 1.8 %collective-permute-done.8.b = bf16[64,2176]{1,0:T(8,128)(2,1)S(1)} collective-permute-done((bf16[64,2176]{1,0:T(8,128)(2,1)S(1)}, bf16[64,2176]{1,0:T(8,128)(2,1)S(1)}, u32[]{:S(2)}, u32[]{:S(2)}) %collective-permute-start.8) | collective-permute-done | bytes 278560 | tf_op jit(solution)/shard_map/ppermute | solution.py:436
  28.8 0.6 %merge.2 = (bf16[32,2176]{1,0:T(8,128)(2,1)S(1)}, bf16[32,2176]{1,0:T(8,128)(2,1)S(1)}) custom-call(bf16[64,2176]{1,0:T(8,128)(2,1)S(1)} %get-tuple-element.84.a, bf16[64,2176]{1,0:T(8,128)(2,1)S(1)} %collective-permute-done.8.b, f32[8,128]{1,0:T(8,128)S(1)} %get-tuple-element.86.after), custom_call_target="tpu_custom_call" | custom-call | flops 1 | bytes 1 | tf_op jit(solution)/shard_map/merge/pallas_call | solution.py:424
  29.4 3.8 %collective-permute-start.9 = (bf16[32,2176]{1,0:T(8,128)(2,1)S(1)}, bf16[32,2176]{1,0:T(8,128)(2,1)S(1)}, u32[]{:S(2)}, u32[]{:S(2)}) collective-permute-start(bf16[32,2176]{1,0:T(8,128)(2,1)S(1)} %get-tuple-element.88), channel_id=1, source_target_pairs={{0,8},{4,12},{8,0},{12,4},{1,9},{5,13},{9,1},{13,5},{2,10},{6,14},... | collective-permute-start | bytes 417800 | tf_op jit(solution)/shard_map/ppermute | solution.py:436
  33.2 1.2 %collective-permute-done.3.refs_0_ = bf16[512,256]{1,0:T(8,128)(2,1)S(1)} collective-permute-done((bf16[512,256]{1,0:T(8,128)(2,1)S(1)}, bf16[512,256]{1,0:T(8,128)(2,1)S(1)}, u32[]{:S(2)}, u32[]{:S(2)}) %collective-permute-start.3) | collective-permute-done | bytes 262176 | tf_op jit(solution)/shard_map/ppermute | solution.py:479
  34.3 4.2 %anchor_attention.3 = (bf16[512,2048]{1,0:T(8,128)(2,1)}, f32[8,128]{1,0:T(8,128)S(1)}) custom-call(s32[1]{0:T(128)} %bitcast.blk_ref, bf16[512,2048]{1,0:T(8,128)(2,1)S(1)} %get-tuple-element.49.q_ref, bf16[512,256]{1,0:T(8,128)(2,1)S(1)} %get-tuple-element.69.kv_ref.refs_1_, ...), custom_call_target="tpu_custom_call", output_to_operand_aliasing={{0}: (9, {})} | custom-call | flops 1000000000 | bytes 1 | tf_op jit(solution)/shard_map/anchor_attention/pallas_call | solution.py:271
  38.5 1.0 %merge.3 = bf16[32,2048]{1,0:T(8,128)(2,1)} custom-call(bf16[32,2176]{1,0:T(8,128)(2,1)S(1)} %get-tuple-element.87.a, bf16[32,2176]{1,0:T(8,128)(2,1)S(1)} %collective-permute-done.9.b, f32[8,128]{1,0:T(8,128)S(1)} %get-tuple-element.89.after), custom_call_target="tpu_custom_call" | custom-call | flops 1 | bytes 1 | tf_op jit(solution)/shard_map/merge/pallas_call | solution.py:424
  (5 shorter events, 0.0 us)
Async XLA Ops:
  0.6 8.4 %collective-permute-start = (bf16[16,2048]{1,0:T(8,128)(2,1)}, bf16[16,2048]{1,0:T(8,128)(2,1)S(1)}, u32[]{:S(2)}, u32[]{:S(2)}) collective-permute-start(bf16[16,2048]{1,0:T(8,128)(2,1)} %refs_4_.1), channel_id=1, source_target_pairs={{0,8},{4,12},{8,0},{12,4},{1,9},{5,13},{9,1},{13,5},{2,10},{6,14},... | collective-permute-start | bytes 196616 | tf_op jit(solution)/shard_map/ppermute | solution.py:436
  4.4 7.7 %collective-permute-start.2 = (bf16[512,256]{1,0:T(8,128)(2,1)S(1)}, bf16[512,256]{1,0:T(8,128)(2,1)S(1)}, u32[]{:S(2)}, u32[]{:S(2)}) collective-permute-start(bf16[512,256]{1,0:T(8,128)(2,1)S(1)} %get-tuple-element.74.kv_ref.refs_0_), channel_id=1, source_target_pairs={{0,8},{1,9},{2,10},{3,11},{16,24},{17,25},{18,26},{19,27}} | collective-permute-start | bytes 786440 | tf_op jit(solution)/shard_map/ppermute | solution.py:463
  9.0 8.1 %collective-permute-start.1 = (bf16[32,2048]{1,0:T(8,128)(2,1)S(1)}, bf16[32,2048]{1,0:T(8,128)(2,1)S(1)}, u32[]{:S(2)}, u32[]{:S(2)}) collective-permute-start(bf16[32,2048]{1,0:T(8,128)(2,1)S(1)} %join.1.refs_2_), channel_id=1, source_target_pairs={{0,4},{4,0},{8,12},{12,8},{1,5},{5,1},{9,13},{13,9},{2,6},{6,2},{1... | collective-permute-start | bytes 393224 | tf_op jit(solution)/shard_map/ppermute | solution.py:436
  9.1 11.4 %collective-permute-start.4 = (bf16[512,256]{1,0:T(8,128)(2,1)S(1)}, bf16[512,256]{1,0:T(8,128)(2,1)S(1)}, u32[]{:S(2)}, u32[]{:S(2)}) collective-permute-start(bf16[512,256]{1,0:T(8,128)(2,1)S(1)} %get-tuple-element.69.kv_ref.refs_1_), channel_id=1, source_target_pairs={{0,8},{1,9},{2,10},{3,11},{16,24},{17,25},{18,26},{19,27}} | collective-permute-start | bytes 786440 | tf_op jit(solution)/shard_map/ppermute | solution.py:471
  12.1 9.1 %collective-permute-start.7 = (bf16[512,256]{1,0:T(8,128)(2,1)S(1)}, bf16[512,256]{1,0:T(8,128)(2,1)S(1)}, u32[]{:S(2)}, u32[]{:S(2)}) collective-permute-start(bf16[512,256]{1,0:T(8,128)(2,1)S(1)} %collective-permute-done.2.refs_1_), channel_id=1, source_target_pairs={{8,12},{9,13},{10,14},{11,15},{24,28},{25,29},{26,30},{27,31}} | collective-permute-start | bytes 786440 | tf_op jit(solution)/shard_map/ppermute | solution.py:481
  12.8 9.9 %collective-permute-start.6 = (bf16[512,256]{1,0:T(8,128)(2,1)S(1)}, bf16[512,256]{1,0:T(8,128)(2,1)S(1)}, u32[]{:S(2)}, u32[]{:S(2)}) collective-permute-start(bf16[512,256]{1,0:T(8,128)(2,1)S(1)} %collective-permute-done.2.refs_1_), channel_id=1, source_target_pairs={{8,4},{9,5},{10,6},{11,7},{24,20},{25,21},{26,22},{27,23}} | collective-permute-start | bytes 786440 | tf_op jit(solution)/shard_map/ppermute | solution.py:477
  19.1 9.7 %collective-permute-start.8 = (bf16[64,2176]{1,0:T(8,128)(2,1)S(1)}, bf16[64,2176]{1,0:T(8,128)(2,1)S(1)}, u32[]{:S(2)}, u32[]{:S(2)}) collective-permute-start(bf16[64,2176]{1,0:T(8,128)(2,1)S(1)} %get-tuple-element.85), channel_id=1, source_target_pairs={{0,4},{4,0},{8,12},{12,8},{1,5},{5,1},{9,13},{13,9},{2,6},{6,2},{1... | collective-permute-start | bytes 835592 | tf_op jit(solution)/shard_map/ppermute | solution.py:436
  19.2 15.1 %collective-permute-start.3 = (bf16[512,256]{1,0:T(8,128)(2,1)S(1)}, bf16[512,256]{1,0:T(8,128)(2,1)S(1)}, u32[]{:S(2)}, u32[]{:S(2)}) collective-permute-start(bf16[512,256]{1,0:T(8,128)(2,1)S(1)} %get-tuple-element.69.kv_ref.refs_1_), channel_id=1, source_target_pairs={{0,4},{1,5},{2,6},{3,7},{16,20},{17,21},{18,22},{19,23}} | collective-permute-start | bytes 786440 | tf_op jit(solution)/shard_map/ppermute | solution.py:479
  20.5 13.8 %collective-permute-start.5 = (bf16[512,256]{1,0:T(8,128)(2,1)S(1)}, bf16[512,256]{1,0:T(8,128)(2,1)S(1)}, u32[]{:S(2)}, u32[]{:S(2)}) collective-permute-start(bf16[512,256]{1,0:T(8,128)(2,1)S(1)} %collective-permute-done.4.refs_1_), channel_id=1, source_target_pairs={{8,12},{9,13},{10,14},{11,15},{24,28},{25,29},{26,30},{27,31}} | collective-permute-start | bytes 786440 | tf_op jit(solution)/shard_map/ppermute | solution.py:481
  29.4 9.1 %collective-permute-start.9 = (bf16[32,2176]{1,0:T(8,128)(2,1)S(1)}, bf16[32,2176]{1,0:T(8,128)(2,1)S(1)}, u32[]{:S(2)}, u32[]{:S(2)}) collective-permute-start(bf16[32,2176]{1,0:T(8,128)(2,1)S(1)} %get-tuple-element.88), channel_id=1, source_target_pairs={{0,8},{4,12},{8,0},{12,4},{1,9},{5,13},{9,1},{13,5},{2,10},{6,14},... | collective-permute-start | bytes 417800 | tf_op jit(solution)/shard_map/ppermute | solution.py:436

commit v15 on v14

--- a/solution.py
+++ b/solution.py
@@ -18,6 +18,7 @@
 NEG = -1e30
 TILE = 256
 PAIR = 2
+SLAB = 64
 VMEM = pl.BlockSpec(memory_space=pltpu.VMEM)
 SMEM = pl.BlockSpec(memory_space=pltpu.SMEM)
 HBM = pl.BlockSpec(memory_space=pltpu.HBM)
@@ -204,8 +205,9 @@
     )
 
 
-def anchor_kernel(g, count, prior, blk_ref, q_ref, kv_ref, acc_ref, top_ref, sum_ref, *refs):
-    cand, (o_ref, token, ka, vae, out, sem) = refs[:count], refs[count + prior :]
+def anchor_kernel(g, groups, prior, blk_ref, q_ref, kv_ref, acc_ref, top_ref, sum_ref, *refs):
+    count = sum(groups)
+    cand, (o_ref, token, ka, vae, s_buf, p_buf, w_buf, out, sem) = refs[:count], refs[count + prior :]
     rows = q_ref.shape[0]
     blk = blk_ref[0]
     token[...] = jnp.zeros(token.shape, jnp.float32)
@@ -213,31 +215,44 @@
     def leave(h):
         return pltpu.make_async_copy(out.at[h], o_ref.at[:, head_columns(g * GROUP + h)], sem.at[h])
 
-    def take(ref):
-        ka[...] = ref[:, :HD]
-        vae[:, :HD] = ref[:, HD:]
+    def take(refs):
+        at = 0
+        for ref in refs:
+            here = slice(at, at + ref.shape[0])
+            ka[here, :] = ref[:, :HD]
+            vae[here, :HD] = ref[:, HD:]
+            at = here.stop
 
     def scores(h):
-        return nt(q_ref[:, head_columns(g * GROUP + h)], ka[...])
-
-    def finish(h, s):
-        held = (slice(None), head_columns(h))
-        before = top_ref[held]
-        top = jnp.maximum(jnp.max(s, axis=1, keepdims=True) * C2, before)
-        p = [jnp.exp2(s[:, at : at + HD] * C2 - top).astype(jnp.bfloat16) for at in range(0, rows, HD)]
-        total = nn(jnp.concatenate(p, axis=1), vae[...])
-        w = jnp.exp2(before - top)
-        o = (total[:, :HD] + w * acc_ref[held]) * inverse(total[:, HD:] + w * sum_ref[held])
-        out[h] = o.astype(jnp.bfloat16)
+        s_buf[h % 2] = nt(q_ref[:, head_columns(g * GROUP + h)], ka[...])
+
+    def finish(h, _):
+        mine = head_columns(h)
+        for at in range(0, rows, SLAB):
+            here = slice(at, at + SLAB)
+            s = s_buf[h % 2, here, :]
+            before = top_ref[here, mine]
+            top = jnp.maximum(jnp.max(s, axis=1, keepdims=True) * C2, before)
+            for x in range(0, rows, HD):
+                p_buf[h % 2, here, x : x + HD] = jnp.exp2(s[:, x : x + HD] * C2 - top).astype(jnp.bfloat16)
+            w_buf[h % 2, here, :] = jnp.exp2(before - top)
+        total = nn(p_buf[h % 2], vae[...])
+        for at in range(0, rows, SLAB):
+            here = slice(at, at + SLAB)
+            w = w_buf[h % 2, here, :]
+            o = (total[here, :HD] + w * acc_ref[here, mine]) * inverse(total[here, HD:] + w * sum_ref[here, mine])
+            out[h, here, :] = o.astype(jnp.bfloat16)
         leave(h).start()
 
     @pl.when(blk > 0)
     def _():
-        if count == 1:
-            take(cand[0])
+        if len(groups) == 1:
+            take(cand)
         else:
-            for i, ref in enumerate(cand):
-                pl.when(blk == i + 1)(functools.partial(take, ref))
+            at = 0
+            for i, size in enumerate(groups):
+                pl.when(blk == i + 1)(functools.partial(take, cand[at : at + size]))
+                at += size
         vae[:, HD:] = jnp.ones((rows, HD), jnp.bfloat16)
         pipelined(list(range(GROUP)), scores, finish)
 
@@ -261,26 +276,30 @@
 
 def anchor_attention(blk, query, kv, state, cands, g, prior):
     rows = query.shape[0]
-    args = [blk, query, kv, *state, *cands]
-    specs = [SMEM] + [VMEM] * (5 + len(cands))
+    flat = [x for group in cands for x in group]
+    args = [blk, query, kv, *state, *flat]
+    specs = [SMEM] + [VMEM] * (5 + len(flat))
     alias = {}
     if prior is not None:
         alias = {len(args): 0}
         args.append(prior)
         specs.append(ANY)
     return pl.pallas_call(
-        functools.partial(anchor_kernel, g, len(cands), len(alias)),
+        functools.partial(anchor_kernel, g, [len(group) for group in cands], len(alias)),
         out_shape=[jax.ShapeDtypeStruct(query.shape, query.dtype), jax.ShapeDtypeStruct((8, HD), jnp.float32)],
         in_specs=specs,
         out_specs=[ANY, VMEM],
         scratch_shapes=[
             pltpu.VMEM((rows, HD), jnp.bfloat16),
             pltpu.VMEM((rows, 2 * HD), jnp.bfloat16),
+            pltpu.VMEM((2, rows, rows), jnp.float32),
+            pltpu.VMEM((2, rows, rows), jnp.bfloat16),
+            pltpu.VMEM((2, rows, HD), jnp.float32),
             pltpu.VMEM((GROUP, rows, HD), jnp.bfloat16),
             pltpu.SemaphoreType.DMA((GROUP,)),
         ],
         input_output_aliases=alias,
-        compiler_params=params(6),
+        compiler_params=params(10),
         cost_estimate=cost(1000000000),
         name="anchor_attention",
     )(*args)
@@ -309,6 +328,23 @@
         cost_estimate=BRIEF,
         name="join",
     )(*arrays)
+
+
+def half_kernel(which, x_ref, o_ref):
+    rows = o_ref.shape[0]
+    o_ref[...] = x_ref[which * rows : (which + 1) * rows, :]
+
+
+def half_rows(x, which):
+    return pl.pallas_call(
+        functools.partial(half_kernel, which),
+        out_shape=pltpu.VMEM((x.shape[0] // 2, x.shape[1]), x.dtype),
+        in_specs=[VMEM],
+        out_specs=VMEM,
+        compiler_params=params(2),
+        cost_estimate=BRIEF,
+        name="half_rows",
+    )(x)
 
 
 def option_kernel(masks, heads, blk_ref, owner_ref, slot_ref, length_ref, *refs):
@@ -474,14 +510,17 @@
         first[0], states = hold((first[0], states))
     keep, send = option_partials(blk_arr, *small, kvs, masks, queries, states[-1][1])
     if n == 4:
-        near = [lax.ppermute(first[0], "blk", [(2, 1)])]
+        near = [[lax.ppermute(first[0], "blk", [(2, 1)])]]
         kvs, keep = hold((kvs, keep))
-        near += [lax.ppermute(x, "blk", [(0, 1)]) for x in kvs[1:]]
-        first[1:], keep = hold((first[1:], keep))
-        anchors = [[x, y, lax.ppermute(y, "blk", [(2, 3)])] for x, y in zip(near, first)]
+        tops = [half_rows(x, 0) for x in kvs[1:]]
+        near += [[lax.ppermute(x, "blk", [(0, 1)])] for x in tops]
+        first[1:], keep, tops = hold((first[1:], keep, tops))
+        for x, y in zip(near[1:], first[1:]):
+            x.append(lax.ppermute(half_rows(y, 1), "blk", [(2, 1)]))
+        anchors = [[x, [y], [lax.ppermute(y, "blk", [(2, 3)])]] for x, y in zip(near, first)]
         anchors[0], first = hold((anchors[0], first))
     else:
-        anchors = [[from_root(x, blk)] for x in kvs]
+        anchors = [[[from_root(x, blk)]] for x in kvs]
     ctx_out, tokens = None, []
     for g, state in enumerate(states):
         ctx_out, token = anchor_attention(blk_arr, ctx_query, kvs[g], state, anchors[g], g, ctx_out)

time: 39.8 us -> 40.2 us (1.010)
  the two profiles are of different devices: /device:TPU:12 before, /device:TPU:0 now
where the time goes in v15:
time: 40.2 us; the launch traced here: 40 us
  starting transfers between devices  22.7 us (56%)
  Pallas kernels  12.6 us (31%)
  waiting for transfers between devices  3.91 us (10%)
  between operations  0.8 us (2%)
    ppermute x4, starting transfers between devices, swap(): return lax.ppermute(x, 'blk', [(i, i ^ mask) for i in range(n)])  14.4 us
    pallas_call x2, Pallas kernels, anchor_attention(): pl.pallas_call(functools.partial(anchor_kernel, g, [len(group) for group...  6.21 us
    ppermute x4, waiting for transfers between devices, swap(): return lax.ppermute(x, 'blk', [(i, i ^ mask) for i in range(n)])  2.88 us
    ppermute x1, starting transfers between devices, body(): first += [lax.ppermute(x, 'blk', [(0, 2)]) for x in kvs[1:]]  2.39 us
    pallas_call x1, Pallas kernels, option_partials(): pl.pallas_call(functools.partial(option_kernel, masks, heads), out_shape=...  2.01 us
    ppermute x1, starting transfers between devices, body(): first = [lax.ppermute(kvs[0], 'blk', [(0, 2)])]  1.94 us
    pallas_call x1, Pallas kernels, first_attention(): pl.pallas_call(first_kernel, out_shape=[pltpu.VMEM((rows, GROUP * HD), jn...  1.65 us
    pallas_call x2, Pallas kernels, merge(): pl.pallas_call(functools.partial(merge_kernel, heads), out_shape=shapes,...  1.55 us
  transfers between devices with their start and end apart: 11, of which 4 were waited for; matrix products, arithmetic and copies ran while one was open for 0% of the time, Pallas kernels for 29%

profile of v15, /device:TPU:0, one launch (start us, length us, event | category | flops | bytes accessed | tf_op | source)
XLA Modules:
  0.0 40.0 jit_solution(2413209471179542106)
XLA Ops:
  0.6 4.1 %collective-permute-start = (bf16[16,2048]{1,0:T(8,128)(2,1)}, bf16[16,2048]{1,0:T(8,128)(2,1)S(1)}, u32[]{:S(2)}, u32[]{:S(2)}) collective-permute-start(bf16[16,2048]{1,0:T(8,128)(2,1)} %refs_4_.1), channel_id=1, source_target_pairs={{0,8},{4,12},{8,0},{12,4},{1,9},{5,13},{9,1},{13,5},{2,10},{6,14},... | collective-permute-start | bytes 196616 | tf_op jit(solution)/shard_map/ppermute | solution.py:472
  4.7 1.1 %parts.1 = (bf16[512,256]{1,0:T(8,128)(2,1)S(1)}, bf16[512,256]{1,0:T(8,128)(2,1)S(1)}) custom-call(bf16[512,256]{1,0:T(8,128)(2,1)} %k_ref, bf16[512,256]{1,0:T(8,128)(2,1)} %v_ref.1), custom_call_target="tpu_custom_call" | custom-call | flops 1 | bytes 1 | tf_op jit(solution)/shard_map/parts/pallas_call | solution.py:78
  5.9 1.9 %collective-permute-start.2 = (bf16[512,256]{1,0:T(8,128)(2,1)S(1)}, bf16[512,256]{1,0:T(8,128)(2,1)S(1)}, u32[]{:S(2)}, u32[]{:S(2)}) collective-permute-start(bf16[512,256]{1,0:T(8,128)(2,1)S(1)} %get-tuple-element.74.kv_ref.refs_0_), channel_id=1, source_target_pairs={{0,8},{1,9},{2,10},{3,11},{16,24},{17,25},{18,26},{19,27}} | collective-permute-start | bytes 786440 | tf_op jit(solution)/shard_map/ppermute | solution.py:499
  7.8 1.7 %local_attention.2 = (f32[512,1024]{1,0:T(8,128)S(1)}, f32[512,1024]{1,0:T(8,128)S(1)}, f32[512,1024]{1,0:T(8,128)S(1)}, bf16[512,2048]{1,0:T(8,128)(2,1)S(1)}, ...) custom-call(s32[1]{0:T(128)} %bitcast.blk_ref, ...), custom_call_target="tpu_custom_call" | custom-call | flops 2000000000 | bytes 1 | tf_op jit(solution)/shard_map/local_attention/pallas_call | solution.py:160
  9.5 2.6 %collective-permute-start.1 = (bf16[32,2048]{1,0:T(8,128)(2,1)S(1)}, bf16[32,2048]{1,0:T(8,128)(2,1)S(1)}, u32[]{:S(2)}, u32[]{:S(2)}) collective-permute-start(bf16[32,2048]{1,0:T(8,128)(2,1)S(1)} %join.1.refs_2_), channel_id=1, source_target_pairs={{0,4},{4,0},{8,12},{12,8},{1,5},{5,1},{9,13},{13,9},{2,6},{6,2},{1... | collective-permute-start | bytes 393224 | tf_op jit(solution)/shard_map/ppermute | solution.py:472
  12.1 2.4 %collective-permute-start.4 = (bf16[512,256]{1,0:T(8,128)(2,1)S(1)}, bf16[512,256]{1,0:T(8,128)(2,1)S(1)}, u32[]{:S(2)}, u32[]{:S(2)}) collective-permute-start(bf16[512,256]{1,0:T(8,128)(2,1)S(1)} %get-tuple-element.69.kv_ref.refs_1_.x_ref), channel_id=1, source_target_pairs={{0,8},{1,9},{2,10},{3,11},{16,24},{17,25},{18,26},{19,27}} | collective-permute-start | bytes 786440 | tf_op jit(solution)/shard_map/ppermute | solution.py:507
  14.6 0.0 collective-permute-done.2.refs_1_
  14.6 0.7 %collective-permute-start.8 = (bf16[512,256]{1,0:T(8,128)(2,1)S(1)}, bf16[512,256]{1,0:T(8,128)(2,1)S(1)}, u32[]{:S(2)}, u32[]{:S(2)}) collective-permute-start(bf16[512,256]{1,0:T(8,128)(2,1)S(1)} %collective-permute-done.2.refs_1_), channel_id=1, source_target_pairs={{8,12},{9,13},{10,14},{11,15},{24,28},{25,29},{26,30},{27,31}} | collective-permute-start | bytes 786440 | tf_op jit(solution)/shard_map/ppermute | solution.py:520
  15.2 0.7 %collective-permute-start.7 = (bf16[512,256]{1,0:T(8,128)(2,1)S(1)}, bf16[512,256]{1,0:T(8,128)(2,1)S(1)}, u32[]{:S(2)}, u32[]{:S(2)}) collective-permute-start(bf16[512,256]{1,0:T(8,128)(2,1)S(1)} %collective-permute-done.2.refs_1_), channel_id=1, source_target_pairs={{8,4},{9,5},{10,6},{11,7},{24,20},{25,21},{26,22},{27,23}} | collective-permute-start | bytes 786440 | tf_op jit(solution)/shard_map/ppermute | solution.py:513
  15.9 1.4 %collective-permute-done.1.refs_3_ = bf16[32,2048]{1,0:T(8,128)(2,1)S(1)} collective-permute-done((bf16[32,2048]{1,0:T(8,128)(2,1)S(1)}, bf16[32,2048]{1,0:T(8,128)(2,1)S(1)}, u32[]{:S(2)}, u32[]{:S(2)}) %collective-permute-start.1) | collective-permute-done | bytes 131104 | tf_op jit(solution)/shard_map/ppermute | solution.py:472
  17.3 2.0 %option_partials.1 = (bf16[64,2176]{1,0:T(8,128)(2,1)S(1)}, bf16[64,2176]{1,0:T(8,128)(2,1)S(1)}) custom-call(s32[1]{0:T(128)} %bitcast.blk_ref, s32[1,64]{1,0:T(1,128)S(1)} %get-tuple-element.56.owner_ref, s32[1,64]{1,0:T(1,128)S(1)} %get-tuple-element.57.slot_ref, s32[1,64]{1,0:T(1,128)S(1)} %get-tuple-element.58.length_ref, ...), custom_call_target="tpu_custom_call" | custom-call | flops 1000000000 | bytes 1 | tf_op jit(solution)/shard_map/option_partials/pallas_call | solution.py:412
  19.3 2.6 %collective-permute-start.9 = (bf16[64,2176]{1,0:T(8,128)(2,1)S(1)}, bf16[64,2176]{1,0:T(8,128)(2,1)S(1)}, u32[]{:S(2)}, u32[]{:S(2)}) collective-permute-start(bf16[64,2176]{1,0:T(8,128)(2,1)S(1)} %get-tuple-element.85), channel_id=1, source_target_pairs={{0,4},{4,0},{8,12},{12,8},{1,5},{5,1},{9,13},{13,9},{2,6},{6,2},{1... | collective-permute-start | bytes 835592 | tf_op jit(solution)/shard_map/ppermute | solution.py:472
  21.9 1.0 %collective-permute-done.4.x_ref.refs_2_ = bf16[512,256]{1,0:T(8,128)(2,1)S(1)} collective-permute-done((bf16[512,256]{1,0:T(8,128)(2,1)S(1)}, bf16[512,256]{1,0:T(8,128)(2,1)S(1)}, u32[]{:S(2)}, u32[]{:S(2)}) %collective-permute-start.4) | collective-permute-done | bytes 262176 | tf_op jit(solution)/shard_map/ppermute | solution.py:507
  22.9 0.7 %collective-permute-start.6 = (bf16[512,256]{1,0:T(8,128)(2,1)S(1)}, bf16[512,256]{1,0:T(8,128)(2,1)S(1)}, u32[]{:S(2)}, u32[]{:S(2)}) collective-permute-start(bf16[512,256]{1,0:T(8,128)(2,1)S(1)} %collective-permute-done.4.x_ref.refs_2_), channel_id=1, source_target_pairs={{8,12},{9,13},{10,14},{11,15},{24,28},{25,29},{26,30},{27,31}} | collective-permute-start | bytes 786440 | tf_op jit(solution)/shard_map/ppermute | solution.py:520
  23.6 1.3 %collective-permute-start.3 = (bf16[256,256]{1,0:T(8,128)(2,1)S(1)}, bf16[256,256]{1,0:T(8,128)(2,1)S(1)}, u32[]{:S(2)}, u32[]{:S(2)}) collective-permute-start(bf16[256,256]{1,0:T(8,128)(2,1)S(1)} %half_rows.2), channel_id=1, source_target_pairs={{0,4},{1,5},{2,6},{3,7},{16,20},{17,21},{18,22},{19,23}} | collective-permute-start | bytes 393224 | tf_op jit(solution)/shard_map/ppermute | solution.py:516
  24.9 0.7 %collective-permute-start.5 = (bf16[256,256]{1,0:T(8,128)(2,1)S(1)}, bf16[256,256]{1,0:T(8,128)(2,1)S(1)}, u32[]{:S(2)}, u32[]{:S(2)}) collective-permute-start(bf16[256,256]{1,0:T(8,128)(2,1)S(1)} %half_rows.3), channel_id=1, source_target_pairs={{8,4},{9,5},{10,6},{11,7},{24,20},{25,21},{26,22},{27,23}} | collective-permute-start | bytes 393224 | tf_op jit(solution)/shard_map/ppermute | solution.py:519
  25.6 0.0 collective-permute-done.7.refs_0_
  25.6 3.2 %anchor_attention.2 = (bf16[512,2048]{1,0:T(8,128)(2,1)}, f32[8,128]{1,0:T(8,128)S(1)}) custom-call(s32[1]{0:T(128)} %bitcast.blk_ref, bf16[512,2048]{1,0:T(8,128)(2,1)S(1)} %get-tuple-element.49.q_ref, bf16[512,256]{1,0:T(8,128)(2,1)S(1)} %get-tuple-element.74.kv_ref.refs_0_, f32[512,1024]{1,0:T(8,128)S(1)} %get-tuple-element.75.acc_ref, ...), custom_call_target="tpu_custom_call" | custom-call | flops 1000000000 | bytes 1 | tf_op jit(solution)/shard_map/anchor_attention/pallas_call | solution.py:287
  28.8 0.2 collective-permute-done.9.b
  29.0 0.6 %merge.2 = (bf16[32,2176]{1,0:T(8,128)(2,1)S(1)}, bf16[32,2176]{1,0:T(8,128)(2,1)S(1)}) custom-call(bf16[64,2176]{1,0:T(8,128)(2,1)S(1)} %get-tuple-element.84.a, bf16[64,2176]{1,0:T(8,128)(2,1)S(1)} %collective-permute-done.9.b, f32[8,128]{1,0:T(8,128)S(1)} %get-tuple-element.86.after), custom_call_target="tpu_custom_call" | custom-call | flops 1 | bytes 1 | tf_op jit(solution)/shard_map/merge/pallas_call | solution.py:460
  29.6 5.1 %collective-permute-start.10 = (bf16[32,2176]{1,0:T(8,128)(2,1)S(1)}, bf16[32,2176]{1,0:T(8,128)(2,1)S(1)}, u32[]{:S(2)}, u32[]{:S(2)}) collective-permute-start(bf16[32,2176]{1,0:T(8,128)(2,1)S(1)} %get-tuple-element.88), channel_id=1, source_target_pairs={{0,8},{4,12},{8,0},{12,4},{1,9},{5,13},{9,1},{13,5},{2,10},{6,14},... | collective-permute-start | bytes 417800 | tf_op jit(solution)/shard_map/ppermute | solution.py:472
  34.7 3.0 %anchor_attention.3 = (bf16[512,2048]{1,0:T(8,128)(2,1)}, f32[8,128]{1,0:T(8,128)S(1)}) custom-call(s32[1]{0:T(128)} %bitcast.blk_ref, bf16[512,2048]{1,0:T(8,128)(2,1)S(1)} %get-tuple-element.49.q_ref, bf16[512,256]{1,0:T(8,128)(2,1)S(1)} %get-tuple-element.69.kv_ref.refs_1_.x_ref, ...), custom_call_target="tpu_custom_call", output_to_operand_aliasing={{0}: (10, {})} | custom-call | flops 1000000000 | bytes 1 | tf_op jit(solution)/shard_map/anchor_attention/pallas_call | solution.py:287
  37.7 1.3 %collective-permute-done.10.b = bf16[32,2176]{1,0:T(8,128)(2,1)S(1)} collective-permute-done((bf16[32,2176]{1,0:T(8,128)(2,1)S(1)}, bf16[32,2176]{1,0:T(8,128)(2,1)S(1)}, u32[]{:S(2)}, u32[]{:S(2)}) %collective-permute-start.10) | collective-permute-done | bytes 139296 | tf_op jit(solution)/shard_map/ppermute | solution.py:472
  39.0 1.0 %merge.3 = bf16[32,2048]{1,0:T(8,128)(2,1)} custom-call(bf16[32,2176]{1,0:T(8,128)(2,1)S(1)} %get-tuple-element.87.a, bf16[32,2176]{1,0:T(8,128)(2,1)S(1)} %collective-permute-done.10.b, f32[8,128]{1,0:T(8,128)S(1)} %get-tuple-element.89.after), custom_call_target="tpu_custom_call" | custom-call | flops 1 | bytes 1 | tf_op jit(solution)/shard_map/merge/pallas_call | solution.py:460
  (9 shorter events, 0.1 us)
Async XLA Ops:
  0.6 8.8 %collective-permute-start = (bf16[16,2048]{1,0:T(8,128)(2,1)}, bf16[16,2048]{1,0:T(8,128)(2,1)S(1)}, u32[]{:S(2)}, u32[]{:S(2)}) collective-permute-start(bf16[16,2048]{1,0:T(8,128)(2,1)} %refs_4_.1), channel_id=1, source_target_pairs={{0,8},{4,12},{8,0},{12,4},{1,9},{5,13},{9,1},{13,5},{2,10},{6,14},... | collective-permute-start | bytes 196616 | tf_op jit(solution)/shard_map/ppermute | solution.py:472
  5.9 8.7 %collective-permute-start.2 = (bf16[512,256]{1,0:T(8,128)(2,1)S(1)}, bf16[512,256]{1,0:T(8,128)(2,1)S(1)}, u32[]{:S(2)}, u32[]{:S(2)}) collective-permute-start(bf16[512,256]{1,0:T(8,128)(2,1)S(1)} %get-tuple-element.74.kv_ref.refs_0_), channel_id=1, source_target_pairs={{0,8},{1,9},{2,10},{3,11},{16,24},{17,25},{18,26},{19,27}} | collective-permute-start | bytes 786440 | tf_op jit(solution)/shard_map/ppermute | solution.py:499
  9.5 7.8 %collective-permute-start.1 = (bf16[32,2048]{1,0:T(8,128)(2,1)S(1)}, bf16[32,2048]{1,0:T(8,128)(2,1)S(1)}, u32[]{:S(2)}, u32[]{:S(2)}) collective-permute-start(bf16[32,2048]{1,0:T(8,128)(2,1)S(1)} %join.1.refs_2_), channel_id=1, source_target_pairs={{0,4},{4,0},{8,12},{12,8},{1,5},{5,1},{9,13},{13,9},{2,6},{6,2},{1... | collective-permute-start | bytes 393224 | tf_op jit(solution)/shard_map/ppermute | solution.py:472
  12.1 10.8 %collective-permute-start.4 = (bf16[512,256]{1,0:T(8,128)(2,1)S(1)}, bf16[512,256]{1,0:T(8,128)(2,1)S(1)}, u32[]{:S(2)}, u32[]{:S(2)}) collective-permute-start(bf16[512,256]{1,0:T(8,128)(2,1)S(1)} %get-tuple-element.69.kv_ref.refs_1_.x_ref), channel_id=1, source_target_pairs={{0,8},{1,9},{2,10},{3,11},{16,24},{17,25},{18,26},{19,27}} | collective-permute-start | bytes 786440 | tf_op jit(solution)/shard_map/ppermute | solution.py:507
  14.6 10.4 %collective-permute-start.8 = (bf16[512,256]{1,0:T(8,128)(2,1)S(1)}, bf16[512,256]{1,0:T(8,128)(2,1)S(1)}, u32[]{:S(2)}, u32[]{:S(2)}) collective-permute-start(bf16[512,256]{1,0:T(8,128)(2,1)S(1)} %collective-permute-done.2.refs_1_), channel_id=1, source_target_pairs={{8,12},{9,13},{10,14},{11,15},{24,28},{25,29},{26,30},{27,31}} | collective-permute-start | bytes 786440 | tf_op jit(solution)/shard_map/ppermute | solution.py:520
  15.2 10.4 %collective-permute-start.7 = (bf16[512,256]{1,0:T(8,128)(2,1)S(1)}, bf16[512,256]{1,0:T(8,128)(2,1)S(1)}, u32[]{:S(2)}, u32[]{:S(2)}) collective-permute-start(bf16[512,256]{1,0:T(8,128)(2,1)S(1)} %collective-permute-done.2.refs_1_), channel_id=1, source_target_pairs={{8,4},{9,5},{10,6},{11,7},{24,20},{25,21},{26,22},{27,23}} | collective-permute-start | bytes 786440 | tf_op jit(solution)/shard_map/ppermute | solution.py:513
  19.3 9.7 %collective-permute-start.9 = (bf16[64,2176]{1,0:T(8,128)(2,1)S(1)}, bf16[64,2176]{1,0:T(8,128)(2,1)S(1)}, u32[]{:S(2)}, u32[]{:S(2)}) collective-permute-start(bf16[64,2176]{1,0:T(8,128)(2,1)S(1)} %get-tuple-element.85), channel_id=1, source_target_pairs={{0,4},{4,0},{8,12},{12,8},{1,5},{5,1},{9,13},{13,9},{2,6},{6,2},{1... | collective-permute-start | bytes 835592 | tf_op jit(solution)/shard_map/ppermute | solution.py:472
  22.9 11.7 %collective-permute-start.6 = (bf16[512,256]{1,0:T(8,128)(2,1)S(1)}, bf16[512,256]{1,0:T(8,128)(2,1)S(1)}, u32[]{:S(2)}, u32[]{:S(2)}) collective-permute-start(bf16[512,256]{1,0:T(8,128)(2,1)S(1)} %collective-permute-done.4.x_ref.refs_2_), channel_id=1, source_target_pairs={{8,12},{9,13},{10,14},{11,15},{24,28},{25,29},{26,30},{27,31}} | collective-permute-start | bytes 786440 | tf_op jit(solution)/shard_map/ppermute | solution.py:520
  23.6 11.1 %collective-permute-start.3 = (bf16[256,256]{1,0:T(8,128)(2,1)S(1)}, bf16[256,256]{1,0:T(8,128)(2,1)S(1)}, u32[]{:S(2)}, u32[]{:S(2)}) collective-permute-start(bf16[256,256]{1,0:T(8,128)(2,1)S(1)} %half_rows.2), channel_id=1, source_target_pairs={{0,4},{1,5},{2,6},{3,7},{16,20},{17,21},{18,22},{19,23}} | collective-permute-start | bytes 393224 | tf_op jit(solution)/shard_map/ppermute | solution.py:516
  24.9 9.7 %collective-permute-start.5 = (bf16[256,256]{1,0:T(8,128)(2,1)S(1)}, bf16[256,256]{1,0:T(8,128)(2,1)S(1)}, u32[]{:S(2)}, u32[]{:S(2)}) collective-permute-start(bf16[256,256]{1,0:T(8,128)(2,1)S(1)} %half_rows.3), channel_id=1, source_target_pairs={{8,4},{9,5},{10,6},{11,7},{24,20},{25,21},{26,22},{27,23}} | collective-permute-start | bytes 393224 | tf_op jit(solution)/shard_map/ppermute | solution.py:519
  29.6 9.4 %collective-permute-start.10 = (bf16[32,2176]{1,0:T(8,128)(2,1)S(1)}, bf16[32,2176]{1,0:T(8,128)(2,1)S(1)}, u32[]{:S(2)}, u32[]{:S(2)}) collective-permute-start(bf16[32,2176]{1,0:T(8,128)(2,1)S(1)} %get-tuple-element.88), channel_id=1, source_target_pairs={{0,8},{4,12},{8,0},{12,4},{1,9},{5,13},{9,1},{13,5},{2,10},{6,14},... | collective-permute-start | bytes 417800 | tf_op jit(solution)/shard_map/ppermute | solution.py:472

commit v16 on v14

--- a/solution.py
+++ b/solution.py
@@ -314,16 +314,25 @@
 def option_kernel(masks, heads, blk_ref, owner_ref, slot_ref, length_ref, *refs):
     n = len(masks)
     kv_heads = heads // GROUP
-    kv, queries = refs[:kv_heads], refs[kv_heads : kv_heads + 2]
-    keep, send, q_all, part = refs[kv_heads + 3 :]
+    count = len(refs) - kv_heads - 5
+    kv, queries = refs[:kv_heads], refs[kv_heads : kv_heads + count]
+    keep, send, q_all, part = refs[kv_heads + count + 1 :]
     blk = blk_ref[0]
     rows = kv[0].shape[0]
     half = queries[0].shape[0]
     options, each = 2 * half, 2 * half // n
-    for i, mask in enumerate(masks):
-        at = jnp.bitwise_xor(blk, mask) * each
-        here = queries[i * each // half].at[i * each % half : i * each % half + each]
-        q_all[pl.ds(pl.multiple_of(at, each), each), :] = here[...]
+
+    def place(ref, masks, flip):
+        for i, mask in enumerate(masks):
+            at = jnp.bitwise_xor(blk, jnp.bitwise_xor(mask, flip)) * each
+            q_all[pl.ds(pl.multiple_of(at, each), each), :] = ref[i * each : (i + 1) * each, :]
+
+    place(queries[0], masks[: n // 2], 0)
+    if count == 2:
+        place(queries[1], masks[n // 2 :], 0)
+    else:
+        pl.when(blk < 3)(lambda: place(queries[1], masks[n // 2 :], jnp.where(blk == 1, 2, 0)))
+        pl.when(blk == 3)(lambda: place(queries[2], masks[n // 2 :], 0))
     eye = lax.broadcasted_iota(jnp.int32, (options, options), 0) == lax.broadcasted_iota(jnp.int32, (options, options), 1)
     length = jnp.sum(jnp.where(eye, length_ref[...].astype(jnp.float32), 0.0), axis=1, keepdims=True)
     seen = length - (blk * rows).astype(jnp.float32)
@@ -376,7 +385,7 @@
     return pl.pallas_call(
         functools.partial(option_kernel, masks, heads),
         out_shape=[jax.ShapeDtypeStruct((n // 2 * CAP, width), jnp.bfloat16)] * 2,
-        in_specs=[SMEM] + [VMEM] * (5 + len(kvs)) + [ANY],
+        in_specs=[SMEM] + [VMEM] * (3 + len(kvs) + len(queries)) + [ANY],
         out_specs=[VMEM] * 2,
         scratch_shapes=[
             pltpu.VMEM((options, heads * HD), jnp.bfloat16),
@@ -465,7 +474,11 @@
     state, (ctx_query, *small, own) = first_attention(blk_arr, kvs[0], ctx_query, small)
     kvs, state, shards = hold((kvs, state, shards))
     mine = join([own, *shards[1:]])
-    queries = [mine, swap(mine, n, 1)]
+    queries = [mine]
+    if n == 4:
+        queries += [lax.ppermute(mine, "blk", pairs) for pairs in ([(2, 1), (1, 0), (3, 2)], [(2, 3)])]
+    else:
+        queries.append(swap(mine, n, 1))
     states = [state]
     if n == 4:
         first += [lax.ppermute(x, "blk", [(0, 2)]) for x in kvs[1:]]

time: 39.8 us -> 43.9 us (1.10)
  the two profiles are of different devices: /device:TPU:12 before, /device:TPU:30 now
where the time goes in v16:
time: 43.9 us; the launch traced here: 43.6 us
  Pallas kernels  19.3 us (44%)
  starting transfers between devices  13.3 us (30%)
  waiting for transfers between devices  10.2 us (23%)
  between operations  0.8 us (2%)
    pallas_call x2, Pallas kernels, anchor_attention(): pl.pallas_call(functools.partial(anchor_kernel, g, len(cands), len(alias)...  8.41 us
    ppermute x2, waiting for transfers between devices, body(): lax.ppermute(y, 'blk', [(2, 3)])  7.74 us
    ppermute x2, starting transfers between devices, body(): lax.ppermute(mine, 'blk', pairs)  4.12 us
    pallas_call x1, Pallas kernels, first_attention(): pl.pallas_call(first_kernel, out_shape=[pltpu.VMEM((rows, GROUP * HD), jn...  3.91 us
    ppermute x3, starting transfers between devices, swap(): return lax.ppermute(x, 'blk', [(i, i ^ mask) for i in range(n)])  3.89 us
    ppermute x2, starting transfers between devices, body(): lax.ppermute(y, 'blk', [(2, 3)])  2.58 us
    pallas_call x1, Pallas kernels, local_attention(): pl.pallas_call(functools.partial(local_kernel, g), out_shape=[pltpu.VMEM(...  2.29 us
    pallas_call x1, Pallas kernels, option_partials(): pl.pallas_call(functools.partial(option_kernel, masks, heads), out_shape=...  2.05 us
  transfers between devices with their start and end apart: 11, of which 5 were waited for; matrix products, arithmetic and copies ran while one was open for 0% of the time, Pallas kernels for 42%

profile of v16, /device:TPU:30, one launch (start us, length us, event | category | flops | bytes accessed | tf_op | source)
XLA Modules:
  0.0 43.6 jit_solution(3538600513758683941)
XLA Ops:
  0.6 0.4 collective-permute-start
  1.0 1.1 %parts.1 = (bf16[512,256]{1,0:T(8,128)(2,1)S(1)}, bf16[512,256]{1,0:T(8,128)(2,1)S(1)}) custom-call(bf16[512,256]{1,0:T(8,128)(2,1)} %k_ref, bf16[512,256]{1,0:T(8,128)(2,1)} %v_ref.1), custom_call_target="tpu_custom_call" | custom-call | flops 1 | bytes 1 | tf_op jit(solution)/shard_map/parts/pallas_call | solution.py:77
  2.2 0.7 %collective-permute-start.3 = (bf16[512,256]{1,0:T(8,128)(2,1)S(1)}, bf16[512,256]{1,0:T(8,128)(2,1)S(1)}, u32[]{:S(2)}, u32[]{:S(2)}) collective-permute-start(bf16[512,256]{1,0:T(8,128)(2,1)S(1)} %get-tuple-element.74.kv_ref.refs_0_), channel_id=1, source_target_pairs={{0,8},{1,9},{2,10},{3,11},{16,24},{17,25},{18,26},{19,27}} | collective-permute-start | bytes 786440 | tf_op jit(solution)/shard_map/ppermute | solution.py:472
  2.9 3.9 %local_attention.2 = (f32[512,1024]{1,0:T(8,128)S(1)}, f32[512,1024]{1,0:T(8,128)S(1)}, f32[512,1024]{1,0:T(8,128)S(1)}, bf16[512,2048]{1,0:T(8,128)(2,1)S(1)}, ...) custom-call(s32[1]{0:T(128)} %bitcast.blk_ref, ...), custom_call_target="tpu_custom_call" | custom-call | flops 2000000000 | bytes 1 | tf_op jit(solution)/shard_map/local_attention/pallas_call | solution.py:159
  6.8 0.2 collective-permute-done.refs_1_
  6.9 2.8 %collective-permute-start.1 = (bf16[32,2048]{1,0:T(8,128)(2,1)S(1)}, bf16[32,2048]{1,0:T(8,128)(2,1)S(1)}, u32[]{:S(2)}, u32[]{:S(2)}) collective-permute-start(bf16[32,2048]{1,0:T(8,128)(2,1)S(1)} %join.1.refs_2_), channel_id=1, source_target_pairs={{8,4},{4,0},{12,8},{9,5},{5,1},{13,9},{10,6},{6,2},{14,10},{11,7},... | collective-permute-start | bytes 393224 | tf_op jit(solution)/shard_map/ppermute | solution.py:479
  9.8 1.3 %collective-permute-start.2 = (bf16[32,2048]{1,0:T(8,128)(2,1)S(1)}, bf16[32,2048]{1,0:T(8,128)(2,1)S(1)}, u32[]{:S(2)}, u32[]{:S(2)}) collective-permute-start(bf16[32,2048]{1,0:T(8,128)(2,1)S(1)} %join.1.refs_2_), channel_id=1, source_target_pairs={{8,12},{9,13},{10,14},{11,15},{24,28},{25,29},{26,30},{27,31}} | collective-permute-start | bytes 393224 | tf_op jit(solution)/shard_map/ppermute | solution.py:479
  11.1 0.7 %collective-permute-start.5 = (bf16[512,256]{1,0:T(8,128)(2,1)S(1)}, bf16[512,256]{1,0:T(8,128)(2,1)S(1)}, u32[]{:S(2)}, u32[]{:S(2)}) collective-permute-start(bf16[512,256]{1,0:T(8,128)(2,1)S(1)} %get-tuple-element.69.kv_ref.refs_1_), channel_id=1, source_target_pairs={{0,8},{1,9},{2,10},{3,11},{16,24},{17,25},{18,26},{19,27}} | collective-permute-start | bytes 786440 | tf_op jit(solution)/shard_map/ppermute | solution.py:484
  11.8 2.3 %local_attention.3 = (f32[512,1024]{1,0:T(8,128)S(1)}, f32[512,1024]{1,0:T(8,128)S(1)}, f32[512,1024]{1,0:T(8,128)S(1)}) custom-call(s32[1]{0:T(128)} %bitcast.blk_ref, bf16[512,256]{1,0:T(8,128)(2,1)S(1)} %get-tuple-element.69.kv_ref.refs_1_, bf16[512,2048]{1,0:T(8,128)(2,1)S(1)} %get-tuple-element.49.q_ref), custom_call_target="tpu_custom_call" | custom-call | flops 1000000000 | bytes 1 | tf_op jit(solution)/shard_map/local_attention/pallas_call | solution.py:194
  14.1 0.7 %collective-permute-start.7 = (bf16[512,256]{1,0:T(8,128)(2,1)S(1)}, bf16[512,256]{1,0:T(8,128)(2,1)S(1)}, u32[]{:S(2)}, u32[]{:S(2)}) collective-permute-start(bf16[512,256]{1,0:T(8,128)(2,1)S(1)} %collective-permute-done.3.refs_1_), channel_id=1, source_target_pairs={{8,4},{9,5},{10,6},{11,7},{24,20},{25,21},{26,22},{27,23}} | collective-permute-start | bytes 786440 | tf_op jit(solution)/shard_map/ppermute | solution.py:490
  14.8 1.3 %collective-permute-start.8 = (bf16[512,256]{1,0:T(8,128)(2,1)S(1)}, bf16[512,256]{1,0:T(8,128)(2,1)S(1)}, u32[]{:S(2)}, u32[]{:S(2)}) collective-permute-start(bf16[512,256]{1,0:T(8,128)(2,1)S(1)} %collective-permute-done.3.refs_1_), channel_id=1, source_target_pairs={{8,12},{9,13},{10,14},{11,15},{24,28},{25,29},{26,30},{27,31}} | collective-permute-start | bytes 786440 | tf_op jit(solution)/shard_map/ppermute | solution.py:494
  16.1 0.6 %collective-permute-done.2.refs_4_ = bf16[32,2048]{1,0:T(8,128)(2,1)S(1)} collective-permute-done((bf16[32,2048]{1,0:T(8,128)(2,1)S(1)}, bf16[32,2048]{1,0:T(8,128)(2,1)S(1)}, u32[]{:S(2)}, u32[]{:S(2)}) %collective-permute-start.2) | collective-permute-done | bytes 131104 | tf_op jit(solution)/shard_map/ppermute | solution.py:479
  16.6 2.0 %option_partials.1 = (bf16[64,2176]{1,0:T(8,128)(2,1)S(1)}, bf16[64,2176]{1,0:T(8,128)(2,1)S(1)}) custom-call(s32[1]{0:T(128)} %bitcast.blk_ref, s32[1,64]{1,0:T(1,128)S(1)} %get-tuple-element.56.owner_ref, s32[1,64]{1,0:T(1,128)S(1)} %get-tuple-element.57.slot_ref, s32[1,64]{1,0:T(1,128)S(1)} %get-tuple-element.58.length_ref, ...), custom_call_target="tpu_custom_call" | custom-call | flops 1000000000 | bytes 1 | tf_op jit(solution)/shard_map/option_partials/pallas_call | solution.py:385
  18.7 3.4 %collective-permute-start.9 = (bf16[64,2176]{1,0:T(8,128)(2,1)S(1)}, bf16[64,2176]{1,0:T(8,128)(2,1)S(1)}, u32[]{:S(2)}, u32[]{:S(2)}) collective-permute-start(bf16[64,2176]{1,0:T(8,128)(2,1)S(1)} %get-tuple-element.85), channel_id=1, source_target_pairs={{0,4},{4,0},{8,12},{12,8},{1,5},{5,1},{9,13},{13,9},{2,6},{6,2},{1... | collective-permute-start | bytes 835592 | tf_op jit(solution)/shard_map/ppermute | solution.py:445
  22.1 0.7 %collective-permute-start.4 = (bf16[512,256]{1,0:T(8,128)(2,1)S(1)}, bf16[512,256]{1,0:T(8,128)(2,1)S(1)}, u32[]{:S(2)}, u32[]{:S(2)}) collective-permute-start(bf16[512,256]{1,0:T(8,128)(2,1)S(1)} %get-tuple-element.69.kv_ref.refs_1_), channel_id=1, source_target_pairs={{0,4},{1,5},{2,6},{3,7},{16,20},{17,21},{18,22},{19,23}} | collective-permute-start | bytes 786440 | tf_op jit(solution)/shard_map/ppermute | solution.py:492
  22.8 1.3 %collective-permute-start.6 = (bf16[512,256]{1,0:T(8,128)(2,1)S(1)}, bf16[512,256]{1,0:T(8,128)(2,1)S(1)}, u32[]{:S(2)}, u32[]{:S(2)}) collective-permute-start(bf16[512,256]{1,0:T(8,128)(2,1)S(1)} %collective-permute-done.5.refs_1_), channel_id=1, source_target_pairs={{8,12},{9,13},{10,14},{11,15},{24,28},{25,29},{26,30},{27,31}} | collective-permute-start | bytes 786440 | tf_op jit(solution)/shard_map/ppermute | solution.py:494
  24.1 3.0 %collective-permute-done.8.refs_2_ = bf16[512,256]{1,0:T(8,128)(2,1)S(1)} collective-permute-done((bf16[512,256]{1,0:T(8,128)(2,1)S(1)}, bf16[512,256]{1,0:T(8,128)(2,1)S(1)}, u32[]{:S(2)}, u32[]{:S(2)}) %collective-permute-start.8) | collective-permute-done | bytes 262176 | tf_op jit(solution)/shard_map/ppermute | solution.py:494
  27.1 4.2 %anchor_attention.2 = (bf16[512,2048]{1,0:T(8,128)(2,1)}, f32[8,128]{1,0:T(8,128)S(1)}) custom-call(s32[1]{0:T(128)} %bitcast.blk_ref, bf16[512,2048]{1,0:T(8,128)(2,1)S(1)} %get-tuple-element.49.q_ref, bf16[512,256]{1,0:T(8,128)(2,1)S(1)} %get-tuple-element.74.kv_ref.refs_0_, f32[512,1024]{1,0:T(8,128)S(1)} %get-tuple-element.75.acc_ref, ...), custom_call_target="tpu_custom_call" | custom-call | flops 1000000000 | bytes 1 | tf_op jit(solution)/shard_map/anchor_attention/pallas_call | solution.py:271
  31.4 1.7 %collective-permute-done.9.b = bf16[64,2176]{1,0:T(8,128)(2,1)S(1)} collective-permute-done((bf16[64,2176]{1,0:T(8,128)(2,1)S(1)}, bf16[64,2176]{1,0:T(8,128)(2,1)S(1)}, u32[]{:S(2)}, u32[]{:S(2)}) %collective-permute-start.9) | collective-permute-done | bytes 278560 | tf_op jit(solution)/shard_map/ppermute | solution.py:445
  33.1 0.6 %merge.2 = (bf16[32,2176]{1,0:T(8,128)(2,1)S(1)}, bf16[32,2176]{1,0:T(8,128)(2,1)S(1)}) custom-call(bf16[64,2176]{1,0:T(8,128)(2,1)S(1)} %get-tuple-element.84.a, bf16[64,2176]{1,0:T(8,128)(2,1)S(1)} %collective-permute-done.9.b, f32[8,128]{1,0:T(8,128)S(1)} %get-tuple-element.86.after), custom_call_target="tpu_custom_call" | custom-call | flops 1 | bytes 1 | tf_op jit(solution)/shard_map/merge/pallas_call | solution.py:433
  33.7 0.1 collective-permute-start.10
  33.8 4.7 %collective-permute-done.6.refs_2_ = bf16[512,256]{1,0:T(8,128)(2,1)S(1)} collective-permute-done((bf16[512,256]{1,0:T(8,128)(2,1)S(1)}, bf16[512,256]{1,0:T(8,128)(2,1)S(1)}, u32[]{:S(2)}, u32[]{:S(2)}) %collective-permute-start.6) | collective-permute-done | bytes 262176 | tf_op jit(solution)/shard_map/ppermute | solution.py:494
  38.5 4.2 %anchor_attention.3 = (bf16[512,2048]{1,0:T(8,128)(2,1)}, f32[8,128]{1,0:T(8,128)S(1)}) custom-call(s32[1]{0:T(128)} %bitcast.blk_ref, bf16[512,2048]{1,0:T(8,128)(2,1)S(1)} %get-tuple-element.49.q_ref, bf16[512,256]{1,0:T(8,128)(2,1)S(1)} %get-tuple-element.69.kv_ref.refs_1_, ...), custom_call_target="tpu_custom_call", output_to_operand_aliasing={{0}: (9, {})} | custom-call | flops 1000000000 | bytes 1 | tf_op jit(solution)/shard_map/anchor_attention/pallas_call | solution.py:271
  42.7 1.0 %merge.3 = bf16[32,2048]{1,0:T(8,128)(2,1)} custom-call(bf16[32,2176]{1,0:T(8,128)(2,1)S(1)} %get-tuple-element.87.a, bf16[32,2176]{1,0:T(8,128)(2,1)S(1)} %collective-permute-done.10.b, f32[8,128]{1,0:T(8,128)S(1)} %get-tuple-element.89.after), custom_call_target="tpu_custom_call" | custom-call | flops 1 | bytes 1 | tf_op jit(solution)/shard_map/merge/pallas_call | solution.py:433
  (7 shorter events, 0.0 us)
Async XLA Ops:
  0.6 6.3 %collective-permute-start = (bf16[16,2048]{1,0:T(8,128)(2,1)}, bf16[16,2048]{1,0:T(8,128)(2,1)S(1)}, u32[]{:S(2)}, u32[]{:S(2)}) collective-permute-start(bf16[16,2048]{1,0:T(8,128)(2,1)} %refs_4_.1), channel_id=1, source_target_pairs={{0,8},{4,12},{8,0},{12,4},{1,9},{5,13},{9,1},{13,5},{2,10},{6,14},... | collective-permute-start | bytes 196616 | tf_op jit(solution)/shard_map/ppermute | solution.py:445
  2.2 11.9 %collective-permute-start.3 = (bf16[512,256]{1,0:T(8,128)(2,1)S(1)}, bf16[512,256]{1,0:T(8,128)(2,1)S(1)}, u32[]{:S(2)}, u32[]{:S(2)}) collective-permute-start(bf16[512,256]{1,0:T(8,128)(2,1)S(1)} %get-tuple-element.74.kv_ref.refs_0_), channel_id=1, source_target_pairs={{0,8},{1,9},{2,10},{3,11},{16,24},{17,25},{18,26},{19,27}} | collective-permute-start | bytes 786440 | tf_op jit(solution)/shard_map/ppermute | solution.py:472
  6.9 9.1 %collective-permute-start.1 = (bf16[32,2048]{1,0:T(8,128)(2,1)S(1)}, bf16[32,2048]{1,0:T(8,128)(2,1)S(1)}, u32[]{:S(2)}, u32[]{:S(2)}) collective-permute-start(bf16[32,2048]{1,0:T(8,128)(2,1)S(1)} %join.1.refs_2_), channel_id=1, source_target_pairs={{8,4},{4,0},{12,8},{9,5},{5,1},{13,9},{10,6},{6,2},{14,10},{11,7},... | collective-permute-start | bytes 393224 | tf_op jit(solution)/shard_map/ppermute | solution.py:479
  9.8 6.9 %collective-permute-start.2 = (bf16[32,2048]{1,0:T(8,128)(2,1)S(1)}, bf16[32,2048]{1,0:T(8,128)(2,1)S(1)}, u32[]{:S(2)}, u32[]{:S(2)}) collective-permute-start(bf16[32,2048]{1,0:T(8,128)(2,1)S(1)} %join.1.refs_2_), channel_id=1, source_target_pairs={{8,12},{9,13},{10,14},{11,15},{24,28},{25,29},{26,30},{27,31}} | collective-permute-start | bytes 393224 | tf_op jit(solution)/shard_map/ppermute | solution.py:479
  11.1 11.7 %collective-permute-start.5 = (bf16[512,256]{1,0:T(8,128)(2,1)S(1)}, bf16[512,256]{1,0:T(8,128)(2,1)S(1)}, u32[]{:S(2)}, u32[]{:S(2)}) collective-permute-start(bf16[512,256]{1,0:T(8,128)(2,1)S(1)} %get-tuple-element.69.kv_ref.refs_1_), channel_id=1, source_target_pairs={{0,8},{1,9},{2,10},{3,11},{16,24},{17,25},{18,26},{19,27}} | collective-permute-start | bytes 786440 | tf_op jit(solution)/shard_map/ppermute | solution.py:484
  14.1 10.0 %collective-permute-start.7 = (bf16[512,256]{1,0:T(8,128)(2,1)S(1)}, bf16[512,256]{1,0:T(8,128)(2,1)S(1)}, u32[]{:S(2)}, u32[]{:S(2)}) collective-permute-start(bf16[512,256]{1,0:T(8,128)(2,1)S(1)} %collective-permute-done.3.refs_1_), channel_id=1, source_target_pairs={{8,4},{9,5},{10,6},{11,7},{24,20},{25,21},{26,22},{27,23}} | collective-permute-start | bytes 786440 | tf_op jit(solution)/shard_map/ppermute | solution.py:490
  14.8 12.4 %collective-permute-start.8 = (bf16[512,256]{1,0:T(8,128)(2,1)S(1)}, bf16[512,256]{1,0:T(8,128)(2,1)S(1)}, u32[]{:S(2)}, u32[]{:S(2)}) collective-permute-start(bf16[512,256]{1,0:T(8,128)(2,1)S(1)} %collective-permute-done.3.refs_1_), channel_id=1, source_target_pairs={{8,12},{9,13},{10,14},{11,15},{24,28},{25,29},{26,30},{27,31}} | collective-permute-start | bytes 786440 | tf_op jit(solution)/shard_map/ppermute | solution.py:494
  18.7 14.4 %collective-permute-start.9 = (bf16[64,2176]{1,0:T(8,128)(2,1)S(1)}, bf16[64,2176]{1,0:T(8,128)(2,1)S(1)}, u32[]{:S(2)}, u32[]{:S(2)}) collective-permute-start(bf16[64,2176]{1,0:T(8,128)(2,1)S(1)} %get-tuple-element.85), channel_id=1, source_target_pairs={{0,4},{4,0},{8,12},{12,8},{1,5},{5,1},{9,13},{13,9},{2,6},{6,2},{1... | collective-permute-start | bytes 835592 | tf_op jit(solution)/shard_map/ppermute | solution.py:445
  22.1 11.7 %collective-permute-start.4 = (bf16[512,256]{1,0:T(8,128)(2,1)S(1)}, bf16[512,256]{1,0:T(8,128)(2,1)S(1)}, u32[]{:S(2)}, u32[]{:S(2)}) collective-permute-start(bf16[512,256]{1,0:T(8,128)(2,1)S(1)} %get-tuple-element.69.kv_ref.refs_1_), channel_id=1, source_target_pairs={{0,4},{1,5},{2,6},{3,7},{16,20},{17,21},{18,22},{19,23}} | collective-permute-start | bytes 786440 | tf_op jit(solution)/shard_map/ppermute | solution.py:492
  22.8 15.7 %collective-permute-start.6 = (bf16[512,256]{1,0:T(8,128)(2,1)S(1)}, bf16[512,256]{1,0:T(8,128)(2,1)S(1)}, u32[]{:S(2)}, u32[]{:S(2)}) collective-permute-start(bf16[512,256]{1,0:T(8,128)(2,1)S(1)} %collective-permute-done.5.refs_1_), channel_id=1, source_target_pairs={{8,12},{9,13},{10,14},{11,15},{24,28},{25,29},{26,30},{27,31}} | collective-permute-start | bytes 786440 | tf_op jit(solution)/shard_map/ppermute | solution.py:494
  33.7 9.0 %collective-permute-start.10 = (bf16[32,2176]{1,0:T(8,128)(2,1)S(1)}, bf16[32,2176]{1,0:T(8,128)(2,1)S(1)}, u32[]{:S(2)}, u32[]{:S(2)}) collective-permute-start(bf16[32,2176]{1,0:T(8,128)(2,1)S(1)} %get-tuple-element.88), channel_id=1, source_target_pairs={{0,8},{4,12},{8,0},{12,4},{1,9},{5,13},{9,1},{13,5},{2,10},{6,14},... | collective-permute-start | bytes 417800 | tf_op jit(solution)/shard_map/ppermute | solution.py:445

commit v17 on v16

--- a/solution.py
+++ b/solution.py
@@ -198,7 +198,7 @@
             out_specs=[VMEM] * 3,
             scratch_shapes=[pltpu.VMEM((rows, 2 * HD), jnp.bfloat16)],
             compiler_params=params(6),
-            cost_estimate=cost(10**9),
+            cost_estimate=cost(1000000000),
             name="local_attention",
         )(blk, kv, query)
     )
@@ -392,7 +392,7 @@
             pltpu.VMEM((options, width), jnp.bfloat16),
         ],
         compiler_params=params(4 + options // 32),
-        cost_estimate=cost(1000000000),
+        cost_estimate=cost(1),
         name="option_partials",
     )(blk, owner, slot, length, *kvs, *queries, after)
 
@@ -474,15 +474,16 @@
     state, (ctx_query, *small, own) = first_attention(blk_arr, kvs[0], ctx_query, small)
     kvs, state, shards = hold((kvs, state, shards))
     mine = join([own, *shards[1:]])
+    states = [state]
+    if n == 4:
+        first += [lax.ppermute(x, "blk", [(0, 2)]) for x in kvs[1:]]
+    states += [local_attention(blk_arr, kv, g, ctx_query) for g, kv in enumerate(kvs) if g]
+    mine, states = hold((mine, states))
     queries = [mine]
     if n == 4:
         queries += [lax.ppermute(mine, "blk", pairs) for pairs in ([(2, 1), (1, 0), (3, 2)], [(2, 3)])]
     else:
         queries.append(swap(mine, n, 1))
-    states = [state]
-    if n == 4:
-        first += [lax.ppermute(x, "blk", [(0, 2)]) for x in kvs[1:]]
-    states += [local_attention(blk_arr, kv, g, ctx_query) for g, kv in enumerate(kvs) if g]
     if n == 4:
         first[0], states = hold((first[0], states))
     keep, send = option_partials(blk_arr, *small, kvs, masks, queries, states[-1][1])

time: 43.9 us -> 45.9 us (1.046)
  the two profiles are of different devices: /device:TPU:30 before, /device:TPU:28 now
where the time goes in v17:
time: 45.9 us; the launch traced here: 45.6 us
  Pallas kernels  19.4 us (42%)
  waiting for transfers between devices  14.9 us (32%)
  starting transfers between devices  10.6 us (23%)
  between operations  0.82 us (2%)
    ppermute x2, waiting for transfers between devices, body(): lax.ppermute(y, 'blk', [(2, 3)])  8.94 us
    pallas_call x2, Pallas kernels, anchor_attention(): pl.pallas_call(functools.partial(anchor_kernel, g, len(cands), len(alias)...  8.5 us
    ppermute x2, starting transfers between devices, body(): lax.ppermute(mine, 'blk', pairs)  4.74 us
    ppermute x2, waiting for transfers between devices, body(): lax.ppermute(mine, 'blk', pairs)  4.04 us
    pallas_call x1, Pallas kernels, first_attention(): pl.pallas_call(first_kernel, out_shape=[pltpu.VMEM((rows, GROUP * HD), jn...  3.9 us
    ppermute x2, starting transfers between devices, body(): lax.ppermute(y, 'blk', [(2, 3)])  2.58 us
    pallas_call x1, Pallas kernels, local_attention(): pl.pallas_call(functools.partial(local_kernel, g), out_shape=[pltpu.VMEM(...  2.27 us
    pallas_call x1, Pallas kernels, option_partials(): pl.pallas_call(functools.partial(option_kernel, masks, heads), out_shape=...  2.04 us
  transfers between devices with their start and end apart: 11, of which 5 were waited for; matrix products, arithmetic and copies ran while one was open for 0% of the time, Pallas kernels for 40%

profile of v17, /device:TPU:28, one launch (start us, length us, event | category | flops | bytes accessed | tf_op | source)
XLA Modules:
  0.0 45.6 jit_solution(13006581798844058106)
XLA Ops:
  0.6 0.4 collective-permute-start
  1.0 1.1 %parts.1 = (bf16[512,256]{1,0:T(8,128)(2,1)S(1)}, bf16[512,256]{1,0:T(8,128)(2,1)S(1)}) custom-call(bf16[512,256]{1,0:T(8,128)(2,1)} %k_ref, bf16[512,256]{1,0:T(8,128)(2,1)} %v_ref.1), custom_call_target="tpu_custom_call" | custom-call | flops 1 | bytes 1 | tf_op jit(solution)/shard_map/parts/pallas_call | solution.py:77
  2.2 0.7 %collective-permute-start.3 = (bf16[512,256]{1,0:T(8,128)(2,1)S(1)}, bf16[512,256]{1,0:T(8,128)(2,1)S(1)}, u32[]{:S(2)}, u32[]{:S(2)}) collective-permute-start(bf16[512,256]{1,0:T(8,128)(2,1)S(1)} %get-tuple-element.88.kv_ref.refs_0_), channel_id=1, source_target_pairs={{0,8},{1,9},{2,10},{3,11},{16,24},{17,25},{18,26},{19,27}} | collective-permute-start | bytes 786440 | tf_op jit(solution)/shard_map/ppermute | solution.py:472
  2.9 3.9 %local_attention.2 = (f32[512,1024]{1,0:T(8,128)S(1)}, f32[512,1024]{1,0:T(8,128)S(1)}, f32[512,1024]{1,0:T(8,128)S(1)}, bf16[512,2048]{1,0:T(8,128)(2,1)S(1)}, ...) custom-call(s32[1]{0:T(128)} %bitcast.blk_ref, ...), custom_call_target="tpu_custom_call" | custom-call | flops 2000000000 | bytes 1 | tf_op jit(solution)/shard_map/local_attention/pallas_call | solution.py:159
  6.8 0.2 collective-permute-done.refs_1_
  6.9 0.7 %collective-permute-start.5 = (bf16[512,256]{1,0:T(8,128)(2,1)S(1)}, bf16[512,256]{1,0:T(8,128)(2,1)S(1)}, u32[]{:S(2)}, u32[]{:S(2)}) collective-permute-start(bf16[512,256]{1,0:T(8,128)(2,1)S(1)} %get-tuple-element.83.kv_ref.refs_1_), channel_id=1, source_target_pairs={{0,8},{1,9},{2,10},{3,11},{16,24},{17,25},{18,26},{19,27}} | collective-permute-start | bytes 786440 | tf_op jit(solution)/shard_map/ppermute | solution.py:479
  7.6 2.3 %local_attention.3 = (f32[512,1024]{1,0:T(8,128)S(1)}, f32[512,1024]{1,0:T(8,128)S(1)}, f32[512,1024]{1,0:T(8,128)S(1)}) custom-call(s32[1]{0:T(128)} %bitcast.blk_ref, bf16[512,256]{1,0:T(8,128)(2,1)S(1)} %get-tuple-element.83.kv_ref.refs_1_, bf16[512,2048]{1,0:T(8,128)(2,1)S(1)} %get-tuple-element.56.q_ref), custom_call_target="tpu_custom_call" | custom-call | flops 1000000000 | bytes 1 | tf_op jit(solution)/shard_map/local_attention/pallas_call | solution.py:194
  9.9 3.4 %collective-permute-start.1 = (bf16[32,2048]{1,0:T(8,128)(2,1)S(1)}, bf16[32,2048]{1,0:T(8,128)(2,1)S(1)}, u32[]{:S(2)}, u32[]{:S(2)}) collective-permute-start(bf16[32,2048]{1,0:T(8,128)(2,1)S(1)} %join.1.refs_2_), channel_id=1, source_target_pairs={{8,4},{4,0},{12,8},{9,5},{5,1},{13,9},{10,6},{6,2},{14,10},{11,7},... | collective-permute-start | bytes 393224 | tf_op jit(solution)/shard_map/ppermute | solution.py:484
  13.3 1.3 %collective-permute-start.2 = (bf16[32,2048]{1,0:T(8,128)(2,1)S(1)}, bf16[32,2048]{1,0:T(8,128)(2,1)S(1)}, u32[]{:S(2)}, u32[]{:S(2)}) collective-permute-start(bf16[32,2048]{1,0:T(8,128)(2,1)S(1)} %join.1.refs_2_), channel_id=1, source_target_pairs={{8,12},{9,13},{10,14},{11,15},{24,28},{25,29},{26,30},{27,31}} | collective-permute-start | bytes 393224 | tf_op jit(solution)/shard_map/ppermute | solution.py:484
  14.7 0.7 %collective-permute-start.7 = (bf16[512,256]{1,0:T(8,128)(2,1)S(1)}, bf16[512,256]{1,0:T(8,128)(2,1)S(1)}, u32[]{:S(2)}, u32[]{:S(2)}) collective-permute-start(bf16[512,256]{1,0:T(8,128)(2,1)S(1)} %collective-permute-done.3.refs_1_), channel_id=1, source_target_pairs={{8,4},{9,5},{10,6},{11,7},{24,20},{25,21},{26,22},{27,23}} | collective-permute-start | bytes 786440 | tf_op jit(solution)/shard_map/ppermute | solution.py:491
  15.3 1.3 %collective-permute-start.8 = (bf16[512,256]{1,0:T(8,128)(2,1)S(1)}, bf16[512,256]{1,0:T(8,128)(2,1)S(1)}, u32[]{:S(2)}, u32[]{:S(2)}) collective-permute-start(bf16[512,256]{1,0:T(8,128)(2,1)S(1)} %collective-permute-done.3.refs_1_), channel_id=1, source_target_pairs={{8,12},{9,13},{10,14},{11,15},{24,28},{25,29},{26,30},{27,31}} | collective-permute-start | bytes 786440 | tf_op jit(solution)/shard_map/ppermute | solution.py:495
  16.7 4.0 %collective-permute-done.2.refs_4_ = bf16[32,2048]{1,0:T(8,128)(2,1)S(1)} collective-permute-done((bf16[32,2048]{1,0:T(8,128)(2,1)S(1)}, bf16[32,2048]{1,0:T(8,128)(2,1)S(1)}, u32[]{:S(2)}, u32[]{:S(2)}) %collective-permute-start.2) | collective-permute-done | bytes 131104 | tf_op jit(solution)/shard_map/ppermute | solution.py:484
  20.7 2.0 %option_partials.1 = (bf16[64,2176]{1,0:T(8,128)(2,1)S(1)}, bf16[64,2176]{1,0:T(8,128)(2,1)S(1)}) custom-call(s32[1]{0:T(128)} %bitcast.blk_ref, s32[1,64]{1,0:T(1,128)S(1)} %get-tuple-element.63.owner_ref, s32[1,64]{1,0:T(1,128)S(1)} %get-tuple-element.64.slot_ref, s32[1,64]{1,0:T(1,128)S(1)} %get-tuple-element.65.length_ref, ...), custom_call_target="tpu_custom_call" | custom-call | flops 1 | bytes 1 | tf_op jit(solution)/shard_map/option_partials/pallas_call | solution.py:385
  22.7 0.1 collective-permute-start.9
  22.8 0.7 %collective-permute-start.4 = (bf16[512,256]{1,0:T(8,128)(2,1)S(1)}, bf16[512,256]{1,0:T(8,128)(2,1)S(1)}, u32[]{:S(2)}, u32[]{:S(2)}) collective-permute-start(bf16[512,256]{1,0:T(8,128)(2,1)S(1)} %get-tuple-element.83.kv_ref.refs_1_), channel_id=1, source_target_pairs={{0,4},{1,5},{2,6},{3,7},{16,20},{17,21},{18,22},{19,23}} | collective-permute-start | bytes 786440 | tf_op jit(solution)/shard_map/ppermute | solution.py:493
  23.5 1.3 %collective-permute-start.6 = (bf16[512,256]{1,0:T(8,128)(2,1)S(1)}, bf16[512,256]{1,0:T(8,128)(2,1)S(1)}, u32[]{:S(2)}, u32[]{:S(2)}) collective-permute-start(bf16[512,256]{1,0:T(8,128)(2,1)S(1)} %collective-permute-done.5.refs_1_), channel_id=1, source_target_pairs={{8,12},{9,13},{10,14},{11,15},{24,28},{25,29},{26,30},{27,31}} | collective-permute-start | bytes 786440 | tf_op jit(solution)/shard_map/ppermute | solution.py:495
  24.8 2.3 %collective-permute-done.8.refs_2_ = bf16[512,256]{1,0:T(8,128)(2,1)S(1)} collective-permute-done((bf16[512,256]{1,0:T(8,128)(2,1)S(1)}, bf16[512,256]{1,0:T(8,128)(2,1)S(1)}, u32[]{:S(2)}, u32[]{:S(2)}) %collective-permute-start.8) | collective-permute-done | bytes 262176 | tf_op jit(solution)/shard_map/ppermute | solution.py:495
  27.1 4.3 %anchor_attention.2 = (bf16[512,2048]{1,0:T(8,128)(2,1)}, f32[8,128]{1,0:T(8,128)S(1)}) custom-call(s32[1]{0:T(128)} %bitcast.blk_ref, bf16[512,2048]{1,0:T(8,128)(2,1)S(1)} %get-tuple-element.56.q_ref, bf16[512,256]{1,0:T(8,128)(2,1)S(1)} %get-tuple-element.88.kv_ref.refs_0_, f32[512,1024]{1,0:T(8,128)S(1)} %get-tuple-element.89.acc_ref, ...), custom_call_target="tpu_custom_call" | custom-call | flops 1000000000 | bytes 1 | tf_op jit(solution)/shard_map/anchor_attention/pallas_call | solution.py:271
  31.4 1.7 %collective-permute-done.9.b = bf16[64,2176]{1,0:T(8,128)(2,1)S(1)} collective-permute-done((bf16[64,2176]{1,0:T(8,128)(2,1)S(1)}, bf16[64,2176]{1,0:T(8,128)(2,1)S(1)}, u32[]{:S(2)}, u32[]{:S(2)}) %collective-permute-start.9) | collective-permute-done | bytes 278560 | tf_op jit(solution)/shard_map/ppermute | solution.py:445
  33.1 0.6 %merge.2 = (bf16[32,2176]{1,0:T(8,128)(2,1)S(1)}, bf16[32,2176]{1,0:T(8,128)(2,1)S(1)}) custom-call(bf16[64,2176]{1,0:T(8,128)(2,1)S(1)} %get-tuple-element.98.a, bf16[64,2176]{1,0:T(8,128)(2,1)S(1)} %collective-permute-done.9.b, f32[8,128]{1,0:T(8,128)S(1)} %get-tuple-element.100.after), custom_call_target="tpu_custom_call" | custom-call | flops 1 | bytes 1 | tf_op jit(solution)/shard_map/merge/pallas_call | solution.py:433
  33.7 0.1 collective-permute-start.10
  33.7 6.6 %collective-permute-done.6.refs_2_ = bf16[512,256]{1,0:T(8,128)(2,1)S(1)} collective-permute-done((bf16[512,256]{1,0:T(8,128)(2,1)S(1)}, bf16[512,256]{1,0:T(8,128)(2,1)S(1)}, u32[]{:S(2)}, u32[]{:S(2)}) %collective-permute-start.6) | collective-permute-done | bytes 262176 | tf_op jit(solution)/shard_map/ppermute | solution.py:495
  40.4 4.2 %anchor_attention.3 = (bf16[512,2048]{1,0:T(8,128)(2,1)}, f32[8,128]{1,0:T(8,128)S(1)}) custom-call(s32[1]{0:T(128)} %bitcast.blk_ref, bf16[512,2048]{1,0:T(8,128)(2,1)S(1)} %get-tuple-element.56.q_ref, bf16[512,256]{1,0:T(8,128)(2,1)S(1)} %get-tuple-element.83.kv_ref.refs_1_, ...), custom_call_target="tpu_custom_call", output_to_operand_aliasing={{0}: (9, {})} | custom-call | flops 1000000000 | bytes 1 | tf_op jit(solution)/shard_map/anchor_attention/pallas_call | solution.py:271
  44.7 1.0 %merge.3 = bf16[32,2048]{1,0:T(8,128)(2,1)} custom-call(bf16[32,2176]{1,0:T(8,128)(2,1)S(1)} %get-tuple-element.101.a, bf16[32,2176]{1,0:T(8,128)(2,1)S(1)} %collective-permute-done.10.b, f32[8,128]{1,0:T(8,128)S(1)} %get-tuple-element.103.after), custom_call_target="tpu_custom_call" | custom-call | flops 1 | bytes 1 | tf_op jit(solution)/shard_map/merge/pallas_call | solution.py:433
  (7 shorter events, 0.0 us)
Async XLA Ops:
  0.6 6.3 %collective-permute-start = (bf16[16,2048]{1,0:T(8,128)(2,1)}, bf16[16,2048]{1,0:T(8,128)(2,1)S(1)}, u32[]{:S(2)}, u32[]{:S(2)}) collective-permute-start(bf16[16,2048]{1,0:T(8,128)(2,1)} %refs_4_.1), channel_id=1, source_target_pairs={{0,8},{4,12},{8,0},{12,4},{1,9},{5,13},{9,1},{13,5},{2,10},{6,14},... | collective-permute-start | bytes 196616 | tf_op jit(solution)/shard_map/ppermute | solution.py:445
  2.2 12.5 %collective-permute-start.3 = (bf16[512,256]{1,0:T(8,128)(2,1)S(1)}, bf16[512,256]{1,0:T(8,128)(2,1)S(1)}, u32[]{:S(2)}, u32[]{:S(2)}) collective-permute-start(bf16[512,256]{1,0:T(8,128)(2,1)S(1)} %get-tuple-element.88.kv_ref.refs_0_), channel_id=1, source_target_pairs={{0,8},{1,9},{2,10},{3,11},{16,24},{17,25},{18,26},{19,27}} | collective-permute-start | bytes 786440 | tf_op jit(solution)/shard_map/ppermute | solution.py:472
  6.9 16.6 %collective-permute-start.5 = (bf16[512,256]{1,0:T(8,128)(2,1)S(1)}, bf16[512,256]{1,0:T(8,128)(2,1)S(1)}, u32[]{:S(2)}, u32[]{:S(2)}) collective-permute-start(bf16[512,256]{1,0:T(8,128)(2,1)S(1)} %get-tuple-element.83.kv_ref.refs_1_), channel_id=1, source_target_pairs={{0,8},{1,9},{2,10},{3,11},{16,24},{17,25},{18,26},{19,27}} | collective-permute-start | bytes 786440 | tf_op jit(solution)/shard_map/ppermute | solution.py:479
  9.9 6.8 %collective-permute-start.1 = (bf16[32,2048]{1,0:T(8,128)(2,1)S(1)}, bf16[32,2048]{1,0:T(8,128)(2,1)S(1)}, u32[]{:S(2)}, u32[]{:S(2)}) collective-permute-start(bf16[32,2048]{1,0:T(8,128)(2,1)S(1)} %join.1.refs_2_), channel_id=1, source_target_pairs={{8,4},{4,0},{12,8},{9,5},{5,1},{13,9},{10,6},{6,2},{14,10},{11,7},... | collective-permute-start | bytes 393224 | tf_op jit(solution)/shard_map/ppermute | solution.py:484
  13.3 7.3 %collective-permute-start.2 = (bf16[32,2048]{1,0:T(8,128)(2,1)S(1)}, bf16[32,2048]{1,0:T(8,128)(2,1)S(1)}, u32[]{:S(2)}, u32[]{:S(2)}) collective-permute-start(bf16[32,2048]{1,0:T(8,128)(2,1)S(1)} %join.1.refs_2_), channel_id=1, source_target_pairs={{8,12},{9,13},{10,14},{11,15},{24,28},{25,29},{26,30},{27,31}} | collective-permute-start | bytes 393224 | tf_op jit(solution)/shard_map/ppermute | solution.py:484
  14.7 10.2 %collective-permute-start.7 = (bf16[512,256]{1,0:T(8,128)(2,1)S(1)}, bf16[512,256]{1,0:T(8,128)(2,1)S(1)}, u32[]{:S(2)}, u32[]{:S(2)}) collective-permute-start(bf16[512,256]{1,0:T(8,128)(2,1)S(1)} %collective-permute-done.3.refs_1_), channel_id=1, source_target_pairs={{8,4},{9,5},{10,6},{11,7},{24,20},{25,21},{26,22},{27,23}} | collective-permute-start | bytes 786440 | tf_op jit(solution)/shard_map/ppermute | solution.py:491
  15.3 11.8 %collective-permute-start.8 = (bf16[512,256]{1,0:T(8,128)(2,1)S(1)}, bf16[512,256]{1,0:T(8,128)(2,1)S(1)}, u32[]{:S(2)}, u32[]{:S(2)}) collective-permute-start(bf16[512,256]{1,0:T(8,128)(2,1)S(1)} %collective-permute-done.3.refs_1_), channel_id=1, source_target_pairs={{8,12},{9,13},{10,14},{11,15},{24,28},{25,29},{26,30},{27,31}} | collective-permute-start | bytes 786440 | tf_op jit(solution)/shard_map/ppermute | solution.py:495
  22.7 10.3 %collective-permute-start.9 = (bf16[64,2176]{1,0:T(8,128)(2,1)S(1)}, bf16[64,2176]{1,0:T(8,128)(2,1)S(1)}, u32[]{:S(2)}, u32[]{:S(2)}) collective-permute-start(bf16[64,2176]{1,0:T(8,128)(2,1)S(1)} %get-tuple-element.99), channel_id=1, source_target_pairs={{0,4},{4,0},{8,12},{12,8},{1,5},{5,1},{9,13},{13,9},{2,6},{6,2},{1... | collective-permute-start | bytes 835592 | tf_op jit(solution)/shard_map/ppermute | solution.py:445
  22.8 10.9 %collective-permute-start.4 = (bf16[512,256]{1,0:T(8,128)(2,1)S(1)}, bf16[512,256]{1,0:T(8,128)(2,1)S(1)}, u32[]{:S(2)}, u32[]{:S(2)}) collective-permute-start(bf16[512,256]{1,0:T(8,128)(2,1)S(1)} %get-tuple-element.83.kv_ref.refs_1_), channel_id=1, source_target_pairs={{0,4},{1,5},{2,6},{3,7},{16,20},{17,21},{18,22},{19,23}} | collective-permute-start | bytes 786440 | tf_op jit(solution)/shard_map/ppermute | solution.py:493
  23.5 16.9 %collective-permute-start.6 = (bf16[512,256]{1,0:T(8,128)(2,1)S(1)}, bf16[512,256]{1,0:T(8,128)(2,1)S(1)}, u32[]{:S(2)}, u32[]{:S(2)}) collective-permute-start(bf16[512,256]{1,0:T(8,128)(2,1)S(1)} %collective-permute-done.5.refs_1_), channel_id=1, source_target_pairs={{8,12},{9,13},{10,14},{11,15},{24,28},{25,29},{26,30},{27,31}} | collective-permute-start | bytes 786440 | tf_op jit(solution)/shard_map/ppermute | solution.py:495
  33.7 11.0 %collective-permute-start.10 = (bf16[32,2176]{1,0:T(8,128)(2,1)S(1)}, bf16[32,2176]{1,0:T(8,128)(2,1)S(1)}, u32[]{:S(2)}, u32[]{:S(2)}) collective-permute-start(bf16[32,2176]{1,0:T(8,128)(2,1)S(1)} %get-tuple-element.102), channel_id=1, source_target_pairs={{0,8},{4,12},{8,0},{12,4},{1,9},{5,13},{9,1},{13,5},{2,10},{6,14},... | collective-permute-start | bytes 417800 | tf_op jit(solution)/shard_map/ppermute | solution.py:445

commit v18 on v14

--- a/solution.py
+++ b/solution.py
@@ -105,7 +105,7 @@
     ve[:, :HD] = kv_ref[:, HD:]
     ve[:, HD:] = jnp.ones((rows, HD), jnp.bfloat16)
     row = lax.broadcasted_iota(jnp.int32, (PAIR * TILE, TILE), 0)
-    seen = lax.rem(row, TILE) >= lax.broadcasted_iota(jnp.int32, (PAIR * TILE, TILE), 1)
+    seen = (row & (TILE - 1)) >= lax.broadcasted_iota(jnp.int32, (PAIR * TILE, TILE), 1)
 
     def scores(task):
         first, at = task
@@ -220,13 +220,14 @@
     def scores(h):
         return nt(q_ref[:, head_columns(g * GROUP + h)], ka[...])
 
-    def finish(h, s):
-        held = (slice(None), head_columns(h))
-        before = top_ref[held]
+    def weigh(h, s):
+        before = top_ref[:, head_columns(h)]
         top = jnp.maximum(jnp.max(s, axis=1, keepdims=True) * C2, before)
         p = [jnp.exp2(s[:, at : at + HD] * C2 - top).astype(jnp.bfloat16) for at in range(0, rows, HD)]
-        total = nn(jnp.concatenate(p, axis=1), vae[...])
-        w = jnp.exp2(before - top)
+        return jnp.concatenate(p, axis=1), jnp.exp2(before - top)
+
+    def finish(h, total, w):
+        held = (slice(None), head_columns(h))
         o = (total[:, :HD] + w * acc_ref[held]) * inverse(total[:, HD:] + w * sum_ref[held])
         out[h] = o.astype(jnp.bfloat16)
         leave(h).start()
@@ -239,7 +240,17 @@
             for i, ref in enumerate(cand):
                 pl.when(blk == i + 1)(functools.partial(take, ref))
         vae[:, HD:] = jnp.ones((rows, HD), jnp.bfloat16)
-        pipelined(list(range(GROUP)), scores, finish)
+        ahead, weighed = scores(0), None
+        for h in range(GROUP + 1):
+            s = ahead
+            if h + 1 < GROUP:
+                ahead = scores(h + 1)
+            if weighed is not None:
+                total, w = nn(weighed[0], vae[...]), weighed[1]
+            if h < GROUP:
+                weighed = weigh(h, s)
+            if h:
+                finish(h - 1, total, w)
 
     def emit(here, h, total, z, top):
         out[h, here, :] = (total * inverse(z)).astype(jnp.bfloat16)
@@ -329,6 +340,7 @@
     seen = length - (blk * rows).astype(jnp.float32)
     lane = lax.broadcasted_iota(jnp.int32, (options, HD), 1)
     logs = jnp.zeros((options, HD), jnp.float32)
+    home = head_of(lane, heads)
     stack = max(1, min(GROUP, 512 // options))
     spots = lax.broadcasted_iota(jnp.int32, (options * stack, rows), 1).astype(jnp.float32)
     seen_all = jnp.concatenate([seen] * stack, axis=0)
@@ -347,7 +359,7 @@
         for j in range(stack):
             h = first + j
             part[:, h * HD : (h + 1) * HD] = o[j * options : (j + 1) * options]
-            logs = jnp.where(lax.rem(lane, heads) == h, log[j * options : (j + 1) * options], logs)
+            logs = jnp.where(home == h, log[j * options : (j + 1) * options], logs)
     part[:, heads * HD :] = summands(logs, heads)
     slot = lax.broadcasted_iota(jnp.int32, (CAP, options), 0)
     order = fold_order(n)
@@ -388,11 +400,15 @@
     )(blk, owner, slot, length, *kvs, *queries, after)
 
 
+def head_of(lane, heads):
+    return lane & (heads - 1) if heads & (heads - 1) == 0 else lax.rem(lane, heads)
+
+
 def merge_kernel(heads, a, b, after, *outs):
     width = heads * HD
-    lane = lax.broadcasted_iota(jnp.int32, (HD, width), 0)
-    head = lax.broadcasted_iota(jnp.int32, (HD, width), 1) // HD
-    pick = jnp.where((lax.rem(lane, heads) == head) & (lane < 3 * heads), 1.0, 0.0).astype(jnp.bfloat16)
+    home = head_of(lax.broadcasted_iota(jnp.int32, (HD, HD), 0), heads)
+    home = jnp.where(lax.broadcasted_iota(jnp.int32, (HD, HD), 0) < 3 * heads, home, heads)
+    pick = jnp.concatenate([jnp.where(home == h, 1.0, 0.0).astype(jnp.bfloat16) for h in range(heads)], axis=1)
     logs = [nn(x[:, width:], pick) for x in (a, b)]
     top = jnp.maximum(*logs)
     weights = [jnp.exp(log - top) for log in logs]
@@ -405,8 +421,9 @@
     log = top + jnp.log(total)
     lane = lax.broadcasted_iota(jnp.int32, (a.shape[0], HD), 1)
     packed = jnp.zeros((a.shape[0], HD), jnp.float32)
+    home = head_of(lane, heads)
     for h in range(heads):
-        packed = jnp.where(lax.rem(lane, heads) == h, log[:, h * HD : (h + 1) * HD], packed)
+        packed = jnp.where(home == h, log[:, h * HD : (h + 1) * HD], packed)
     packed = summands(packed, heads)
     half = a.shape[0] // 2
     for i, out in enumerate(outs):

time: 39.8 us -> 39.9 us (level)
  transfers between devices with their start and end apart: 10 -> 10, of which waited for: 4 -> 4; matrix products, arithmetic and copies ran while one was open for 0% -> 0% of each run, Pallas kernels for 46% -> 47%
where the time goes in v18:
time: 39.9 us; the launch traced here: 39.6 us
  Pallas kernels  19.5 us (49%)
  starting transfers between devices  11.9 us (30%)
  waiting for transfers between devices  7.46 us (19%)
  between operations  0.79 us (2%)
    pallas_call x2, Pallas kernels, anchor_attention(): pl.pallas_call(functools.partial(anchor_kernel, g, len(cands), len(alias)...  8.59 us
    ppermute x4, starting transfers between devices, swap(): return lax.ppermute(x, 'blk', [(i, i ^ mask) for i in range(n)])  6.57 us
    ppermute x4, waiting for transfers between devices, swap(): return lax.ppermute(x, 'blk', [(i, i ^ mask) for i in range(n)])  4.77 us
    pallas_call x1, Pallas kernels, first_attention(): pl.pallas_call(first_kernel, out_shape=[pltpu.VMEM((rows, GROUP * HD), jn...  3.91 us
    pallas_call x1, Pallas kernels, local_attention(): pl.pallas_call(functools.partial(local_kernel, g), out_shape=[pltpu.VMEM(...  2.29 us
    pallas_call x1, Pallas kernels, option_partials(): pl.pallas_call(functools.partial(option_kernel, masks, heads), out_shape=...  2.03 us
    pallas_call x2, Pallas kernels, merge(): pl.pallas_call(functools.partial(merge_kernel, heads), out_shape=shapes,...  1.54 us
    ppermute x1, waiting for transfers between devices, body(): near = [lax.ppermute(first[0], 'blk', [(2, 1)])]  1.49 us
  transfers between devices with their start and end apart: 10, of which 4 were waited for; matrix products, arithmetic and copies ran while one was open for 0% of the time, Pallas kernels for 47%

profile of v18, /device:TPU:12, one launch (start us, length us, event | category | flops | bytes accessed | tf_op | source)
XLA Modules:
  0.0 39.6 jit_solution(9005008651614572991)
XLA Ops:
  0.6 2.7 %collective-permute-start = (bf16[16,2048]{1,0:T(8,128)(2,1)}, bf16[16,2048]{1,0:T(8,128)(2,1)S(1)}, u32[]{:S(2)}, u32[]{:S(2)}) collective-permute-start(bf16[16,2048]{1,0:T(8,128)(2,1)} %refs_4_.1), channel_id=1, source_target_pairs={{0,8},{4,12},{8,0},{12,4},{1,9},{5,13},{9,1},{13,5},{2,10},{6,14},... | collective-permute-start | bytes 196616 | tf_op jit(solution)/shard_map/ppermute | solution.py:453
  3.3 1.1 %parts.1 = (bf16[512,256]{1,0:T(8,128)(2,1)S(1)}, bf16[512,256]{1,0:T(8,128)(2,1)S(1)}) custom-call(bf16[512,256]{1,0:T(8,128)(2,1)} %k_ref, bf16[512,256]{1,0:T(8,128)(2,1)} %v_ref.1), custom_call_target="tpu_custom_call" | custom-call | flops 1 | bytes 1 | tf_op jit(solution)/shard_map/parts/pallas_call | solution.py:77
  4.4 0.7 %collective-permute-start.2 = (bf16[512,256]{1,0:T(8,128)(2,1)S(1)}, bf16[512,256]{1,0:T(8,128)(2,1)S(1)}, u32[]{:S(2)}, u32[]{:S(2)}) collective-permute-start(bf16[512,256]{1,0:T(8,128)(2,1)S(1)} %get-tuple-element.74.kv_ref.refs_0_), channel_id=1, source_target_pairs={{0,8},{1,9},{2,10},{3,11},{16,24},{17,25},{18,26},{19,27}} | collective-permute-start | bytes 786440 | tf_op jit(solution)/shard_map/ppermute | solution.py:480
  5.1 3.9 %local_attention.2 = (f32[512,1024]{1,0:T(8,128)S(1)}, f32[512,1024]{1,0:T(8,128)S(1)}, f32[512,1024]{1,0:T(8,128)S(1)}, bf16[512,2048]{1,0:T(8,128)(2,1)S(1)}, ...) custom-call(s32[1]{0:T(128)} %bitcast.blk_ref, ...), custom_call_target="tpu_custom_call" | custom-call | flops 2000000000 | bytes 1 | tf_op jit(solution)/shard_map/local_attention/pallas_call | solution.py:159
  9.0 0.1 collective-permute-start.1
  9.1 0.7 %collective-permute-start.4 = (bf16[512,256]{1,0:T(8,128)(2,1)S(1)}, bf16[512,256]{1,0:T(8,128)(2,1)S(1)}, u32[]{:S(2)}, u32[]{:S(2)}) collective-permute-start(bf16[512,256]{1,0:T(8,128)(2,1)S(1)} %get-tuple-element.69.kv_ref.refs_1_), channel_id=1, source_target_pairs={{0,8},{1,9},{2,10},{3,11},{16,24},{17,25},{18,26},{19,27}} | collective-permute-start | bytes 786440 | tf_op jit(solution)/shard_map/ppermute | solution.py:488
  9.8 2.3 %local_attention.3 = (f32[512,1024]{1,0:T(8,128)S(1)}, f32[512,1024]{1,0:T(8,128)S(1)}, f32[512,1024]{1,0:T(8,128)S(1)}) custom-call(s32[1]{0:T(128)} %bitcast.blk_ref, bf16[512,256]{1,0:T(8,128)(2,1)S(1)} %get-tuple-element.69.kv_ref.refs_1_, bf16[512,2048]{1,0:T(8,128)(2,1)S(1)} %get-tuple-element.49.q_ref), custom_call_target="tpu_custom_call" | custom-call | flops 1000000000 | bytes 1 | tf_op jit(solution)/shard_map/local_attention/pallas_call | solution.py:194
  12.1 0.0 collective-permute-done.2.refs_1_
  12.1 0.7 %collective-permute-start.7 = (bf16[512,256]{1,0:T(8,128)(2,1)S(1)}, bf16[512,256]{1,0:T(8,128)(2,1)S(1)}, u32[]{:S(2)}, u32[]{:S(2)}) collective-permute-start(bf16[512,256]{1,0:T(8,128)(2,1)S(1)} %collective-permute-done.2.refs_1_), channel_id=1, source_target_pairs={{8,12},{9,13},{10,14},{11,15},{24,28},{25,29},{26,30},{27,31}} | collective-permute-start | bytes 786440 | tf_op jit(solution)/shard_map/ppermute | solution.py:498
  12.8 1.3 %collective-permute-start.6 = (bf16[512,256]{1,0:T(8,128)(2,1)S(1)}, bf16[512,256]{1,0:T(8,128)(2,1)S(1)}, u32[]{:S(2)}, u32[]{:S(2)}) collective-permute-start(bf16[512,256]{1,0:T(8,128)(2,1)S(1)} %collective-permute-done.2.refs_1_), channel_id=1, source_target_pairs={{8,4},{9,5},{10,6},{11,7},{24,20},{25,21},{26,22},{27,23}} | collective-permute-start | bytes 786440 | tf_op jit(solution)/shard_map/ppermute | solution.py:494
  14.1 3.0 %collective-permute-done.1.refs_3_ = bf16[32,2048]{1,0:T(8,128)(2,1)S(1)} collective-permute-done((bf16[32,2048]{1,0:T(8,128)(2,1)S(1)}, bf16[32,2048]{1,0:T(8,128)(2,1)S(1)}, u32[]{:S(2)}, u32[]{:S(2)}) %collective-permute-start.1) | collective-permute-done | bytes 131104 | tf_op jit(solution)/shard_map/ppermute | solution.py:453
  17.1 2.0 %option_partials.1 = (bf16[64,2176]{1,0:T(8,128)(2,1)S(1)}, bf16[64,2176]{1,0:T(8,128)(2,1)S(1)}) custom-call(s32[1]{0:T(128)} %bitcast.blk_ref, s32[1,64]{1,0:T(1,128)S(1)} %get-tuple-element.56.owner_ref, s32[1,64]{1,0:T(1,128)S(1)} %get-tuple-element.57.slot_ref, s32[1,64]{1,0:T(1,128)S(1)} %get-tuple-element.58.length_ref, ...), custom_call_target="tpu_custom_call" | custom-call | flops 1000000000 | bytes 1 | tf_op jit(solution)/shard_map/option_partials/pallas_call | solution.py:388
  19.1 0.1 collective-permute-start.8
  19.2 1.3 %collective-permute-start.3 = (bf16[512,256]{1,0:T(8,128)(2,1)S(1)}, bf16[512,256]{1,0:T(8,128)(2,1)S(1)}, u32[]{:S(2)}, u32[]{:S(2)}) collective-permute-start(bf16[512,256]{1,0:T(8,128)(2,1)S(1)} %get-tuple-element.69.kv_ref.refs_1_), channel_id=1, source_target_pairs={{0,4},{1,5},{2,6},{3,7},{16,20},{17,21},{18,22},{19,23}} | collective-permute-start | bytes 786440 | tf_op jit(solution)/shard_map/ppermute | solution.py:496
  20.5 0.7 %collective-permute-start.5 = (bf16[512,256]{1,0:T(8,128)(2,1)S(1)}, bf16[512,256]{1,0:T(8,128)(2,1)S(1)}, u32[]{:S(2)}, u32[]{:S(2)}) collective-permute-start(bf16[512,256]{1,0:T(8,128)(2,1)S(1)} %collective-permute-done.4.refs_1_), channel_id=1, source_target_pairs={{8,12},{9,13},{10,14},{11,15},{24,28},{25,29},{26,30},{27,31}} | collective-permute-start | bytes 786440 | tf_op jit(solution)/shard_map/ppermute | solution.py:498
  21.2 0.0 collective-permute-done.7.refs_2_
  21.2 1.5 %collective-permute-done.6.refs_0_ = bf16[512,256]{1,0:T(8,128)(2,1)S(1)} collective-permute-done((bf16[512,256]{1,0:T(8,128)(2,1)S(1)}, bf16[512,256]{1,0:T(8,128)(2,1)S(1)}, u32[]{:S(2)}, u32[]{:S(2)}) %collective-permute-start.6) | collective-permute-done | bytes 262176 | tf_op jit(solution)/shard_map/ppermute | solution.py:494
  22.7 4.3 %anchor_attention.2 = (bf16[512,2048]{1,0:T(8,128)(2,1)}, f32[8,128]{1,0:T(8,128)S(1)}) custom-call(s32[1]{0:T(128)} %bitcast.blk_ref, bf16[512,2048]{1,0:T(8,128)(2,1)S(1)} %get-tuple-element.49.q_ref, bf16[512,256]{1,0:T(8,128)(2,1)S(1)} %get-tuple-element.74.kv_ref.refs_0_, f32[512,1024]{1,0:T(8,128)S(1)} %get-tuple-element.75.acc_ref, ...), custom_call_target="tpu_custom_call" | custom-call | flops 1000000000 | bytes 1 | tf_op jit(solution)/shard_map/anchor_attention/pallas_call | solution.py:282
  27.1 1.8 %collective-permute-done.8.b = bf16[64,2176]{1,0:T(8,128)(2,1)S(1)} collective-permute-done((bf16[64,2176]{1,0:T(8,128)(2,1)S(1)}, bf16[64,2176]{1,0:T(8,128)(2,1)S(1)}, u32[]{:S(2)}, u32[]{:S(2)}) %collective-permute-start.8) | collective-permute-done | bytes 278560 | tf_op jit(solution)/shard_map/ppermute | solution.py:453
  28.8 0.6 %merge.2 = (bf16[32,2176]{1,0:T(8,128)(2,1)S(1)}, bf16[32,2176]{1,0:T(8,128)(2,1)S(1)}) custom-call(bf16[64,2176]{1,0:T(8,128)(2,1)S(1)} %get-tuple-element.84.a, bf16[64,2176]{1,0:T(8,128)(2,1)S(1)} %collective-permute-done.8.b, f32[8,128]{1,0:T(8,128)S(1)} %get-tuple-element.86.after), custom_call_target="tpu_custom_call" | custom-call | flops 1 | bytes 1 | tf_op jit(solution)/shard_map/merge/pallas_call | solution.py:441
  29.4 3.8 %collective-permute-start.9 = (bf16[32,2176]{1,0:T(8,128)(2,1)S(1)}, bf16[32,2176]{1,0:T(8,128)(2,1)S(1)}, u32[]{:S(2)}, u32[]{:S(2)}) collective-permute-start(bf16[32,2176]{1,0:T(8,128)(2,1)S(1)} %get-tuple-element.88), channel_id=1, source_target_pairs={{0,8},{4,12},{8,0},{12,4},{1,9},{5,13},{9,1},{13,5},{2,10},{6,14},... | collective-permute-start | bytes 417800 | tf_op jit(solution)/shard_map/ppermute | solution.py:453
  33.1 1.2 %collective-permute-done.3.refs_0_ = bf16[512,256]{1,0:T(8,128)(2,1)S(1)} collective-permute-done((bf16[512,256]{1,0:T(8,128)(2,1)S(1)}, bf16[512,256]{1,0:T(8,128)(2,1)S(1)}, u32[]{:S(2)}, u32[]{:S(2)}) %collective-permute-start.3) | collective-permute-done | bytes 262176 | tf_op jit(solution)/shard_map/ppermute | solution.py:496
  34.3 4.3 %anchor_attention.3 = (bf16[512,2048]{1,0:T(8,128)(2,1)}, f32[8,128]{1,0:T(8,128)S(1)}) custom-call(s32[1]{0:T(128)} %bitcast.blk_ref, bf16[512,2048]{1,0:T(8,128)(2,1)S(1)} %get-tuple-element.49.q_ref, bf16[512,256]{1,0:T(8,128)(2,1)S(1)} %get-tuple-element.69.kv_ref.refs_1_, ...), custom_call_target="tpu_custom_call", output_to_operand_aliasing={{0}: (9, {})} | custom-call | flops 1000000000 | bytes 1 | tf_op jit(solution)/shard_map/anchor_attention/pallas_call | solution.py:282
  38.6 1.0 %merge.3 = bf16[32,2048]{1,0:T(8,128)(2,1)} custom-call(bf16[32,2176]{1,0:T(8,128)(2,1)S(1)} %get-tuple-element.87.a, bf16[32,2176]{1,0:T(8,128)(2,1)S(1)} %collective-permute-done.9.b, f32[8,128]{1,0:T(8,128)S(1)} %get-tuple-element.89.after), custom_call_target="tpu_custom_call" | custom-call | flops 1 | bytes 1 | tf_op jit(solution)/shard_map/merge/pallas_call | solution.py:441
  (5 shorter events, 0.0 us)
Async XLA Ops:
  0.6 8.4 %collective-permute-start = (bf16[16,2048]{1,0:T(8,128)(2,1)}, bf16[16,2048]{1,0:T(8,128)(2,1)S(1)}, u32[]{:S(2)}, u32[]{:S(2)}) collective-permute-start(bf16[16,2048]{1,0:T(8,128)(2,1)} %refs_4_.1), channel_id=1, source_target_pairs={{0,8},{4,12},{8,0},{12,4},{1,9},{5,13},{9,1},{13,5},{2,10},{6,14},... | collective-permute-start | bytes 196616 | tf_op jit(solution)/shard_map/ppermute | solution.py:453
  4.4 7.7 %collective-permute-start.2 = (bf16[512,256]{1,0:T(8,128)(2,1)S(1)}, bf16[512,256]{1,0:T(8,128)(2,1)S(1)}, u32[]{:S(2)}, u32[]{:S(2)}) collective-permute-start(bf16[512,256]{1,0:T(8,128)(2,1)S(1)} %get-tuple-element.74.kv_ref.refs_0_), channel_id=1, source_target_pairs={{0,8},{1,9},{2,10},{3,11},{16,24},{17,25},{18,26},{19,27}} | collective-permute-start | bytes 786440 | tf_op jit(solution)/shard_map/ppermute | solution.py:480
  9.0 8.1 %collective-permute-start.1 = (bf16[32,2048]{1,0:T(8,128)(2,1)S(1)}, bf16[32,2048]{1,0:T(8,128)(2,1)S(1)}, u32[]{:S(2)}, u32[]{:S(2)}) collective-permute-start(bf16[32,2048]{1,0:T(8,128)(2,1)S(1)} %join.1.refs_2_), channel_id=1, source_target_pairs={{0,4},{4,0},{8,12},{12,8},{1,5},{5,1},{9,13},{13,9},{2,6},{6,2},{1... | collective-permute-start | bytes 393224 | tf_op jit(solution)/shard_map/ppermute | solution.py:453
  9.1 11.4 %collective-permute-start.4 = (bf16[512,256]{1,0:T(8,128)(2,1)S(1)}, bf16[512,256]{1,0:T(8,128)(2,1)S(1)}, u32[]{:S(2)}, u32[]{:S(2)}) collective-permute-start(bf16[512,256]{1,0:T(8,128)(2,1)S(1)} %get-tuple-element.69.kv_ref.refs_1_), channel_id=1, source_target_pairs={{0,8},{1,9},{2,10},{3,11},{16,24},{17,25},{18,26},{19,27}} | collective-permute-start | bytes 786440 | tf_op jit(solution)/shard_map/ppermute | solution.py:488
  12.1 9.1 %collective-permute-start.7 = (bf16[512,256]{1,0:T(8,128)(2,1)S(1)}, bf16[512,256]{1,0:T(8,128)(2,1)S(1)}, u32[]{:S(2)}, u32[]{:S(2)}) collective-permute-start(bf16[512,256]{1,0:T(8,128)(2,1)S(1)} %collective-permute-done.2.refs_1_), channel_id=1, source_target_pairs={{8,12},{9,13},{10,14},{11,15},{24,28},{25,29},{26,30},{27,31}} | collective-permute-start | bytes 786440 | tf_op jit(solution)/shard_map/ppermute | solution.py:498
  12.8 9.9 %collective-permute-start.6 = (bf16[512,256]{1,0:T(8,128)(2,1)S(1)}, bf16[512,256]{1,0:T(8,128)(2,1)S(1)}, u32[]{:S(2)}, u32[]{:S(2)}) collective-permute-start(bf16[512,256]{1,0:T(8,128)(2,1)S(1)} %collective-permute-done.2.refs_1_), channel_id=1, source_target_pairs={{8,4},{9,5},{10,6},{11,7},{24,20},{25,21},{26,22},{27,23}} | collective-permute-start | bytes 786440 | tf_op jit(solution)/shard_map/ppermute | solution.py:494
  19.1 9.7 %collective-permute-start.8 = (bf16[64,2176]{1,0:T(8,128)(2,1)S(1)}, bf16[64,2176]{1,0:T(8,128)(2,1)S(1)}, u32[]{:S(2)}, u32[]{:S(2)}) collective-permute-start(bf16[64,2176]{1,0:T(8,128)(2,1)S(1)} %get-tuple-element.85), channel_id=1, source_target_pairs={{0,4},{4,0},{8,12},{12,8},{1,5},{5,1},{9,13},{13,9},{2,6},{6,2},{1... | collective-permute-start | bytes 835592 | tf_op jit(solution)/shard_map/ppermute | solution.py:453
  19.2 15.1 %collective-permute-start.3 = (bf16[512,256]{1,0:T(8,128)(2,1)S(1)}, bf16[512,256]{1,0:T(8,128)(2,1)S(1)}, u32[]{:S(2)}, u32[]{:S(2)}) collective-permute-start(bf16[512,256]{1,0:T(8,128)(2,1)S(1)} %get-tuple-element.69.kv_ref.refs_1_), channel_id=1, source_target_pairs={{0,4},{1,5},{2,6},{3,7},{16,20},{17,21},{18,22},{19,23}} | collective-permute-start | bytes 786440 | tf_op jit(solution)/shard_map/ppermute | solution.py:496
  20.5 13.8 %collective-permute-start.5 = (bf16[512,256]{1,0:T(8,128)(2,1)S(1)}, bf16[512,256]{1,0:T(8,128)(2,1)S(1)}, u32[]{:S(2)}, u32[]{:S(2)}) collective-permute-start(bf16[512,256]{1,0:T(8,128)(2,1)S(1)} %collective-permute-done.4.refs_1_), channel_id=1, source_target_pairs={{8,12},{9,13},{10,14},{11,15},{24,28},{25,29},{26,30},{27,31}} | collective-permute-start | bytes 786440 | tf_op jit(solution)/shard_map/ppermute | solution.py:498
  29.4 9.2 %collective-permute-start.9 = (bf16[32,2176]{1,0:T(8,128)(2,1)S(1)}, bf16[32,2176]{1,0:T(8,128)(2,1)S(1)}, u32[]{:S(2)}, u32[]{:S(2)}) collective-permute-start(bf16[32,2176]{1,0:T(8,128)(2,1)S(1)} %get-tuple-element.88), channel_id=1, source_target_pairs={{0,8},{4,12},{8,0},{12,4},{1,9},{5,13},{9,1},{13,5},{2,10},{6,14},... | collective-permute-start | bytes 417800 | tf_op jit(solution)/shard_map/ppermute | solution.py:453

commit v19 on v18

--- a/solution.py
+++ b/solution.py
@@ -198,13 +198,14 @@
             out_specs=[VMEM] * 3,
             scratch_shapes=[pltpu.VMEM((rows, 2 * HD), jnp.bfloat16)],
             compiler_params=params(6),
-            cost_estimate=cost(10**9),
+            cost_estimate=cost(1000000000),
             name="local_attention",
         )(blk, kv, query)
     )
 
 
-def anchor_kernel(g, count, prior, blk_ref, q_ref, kv_ref, acc_ref, top_ref, sum_ref, *refs):
+def anchor_kernel(g, groups, prior, blk_ref, q_ref, kv_ref, acc_ref, top_ref, sum_ref, *refs):
+    count = sum(groups)
     cand, (o_ref, token, ka, vae, out, sem) = refs[:count], refs[count + prior :]
     rows = q_ref.shape[0]
     blk = blk_ref[0]
@@ -213,9 +214,13 @@
     def leave(h):
         return pltpu.make_async_copy(out.at[h], o_ref.at[:, head_columns(g * GROUP + h)], sem.at[h])
 
-    def take(ref):
-        ka[...] = ref[:, :HD]
-        vae[:, :HD] = ref[:, HD:]
+    def take(refs):
+        at = 0
+        for ref in refs:
+            here = slice(at, at + ref.shape[0])
+            ka[here, :] = ref[:, :HD]
+            vae[here, :HD] = ref[:, HD:]
+            at = here.stop
 
     def scores(h):
         return nt(q_ref[:, head_columns(g * GROUP + h)], ka[...])
@@ -234,11 +239,13 @@
 
     @pl.when(blk > 0)
     def _():
-        if count == 1:
-            take(cand[0])
+        if len(groups) == 1:
+            take(cand)
         else:
-            for i, ref in enumerate(cand):
-                pl.when(blk == i + 1)(functools.partial(take, ref))
+            at = 0
+            for i, size in enumerate(groups):
+                pl.when(blk == i + 1)(functools.partial(take, cand[at : at + size]))
+                at += size
         vae[:, HD:] = jnp.ones((rows, HD), jnp.bfloat16)
         ahead, weighed = scores(0), None
         for h in range(GROUP + 1):
@@ -272,15 +279,16 @@
 
 def anchor_attention(blk, query, kv, state, cands, g, prior):
     rows = query.shape[0]
-    args = [blk, query, kv, *state, *cands]
-    specs = [SMEM] + [VMEM] * (5 + len(cands))
+    flat = [x for group in cands for x in group]
+    args = [blk, query, kv, *state, *flat]
+    specs = [SMEM] + [VMEM] * (5 + len(flat))
     alias = {}
     if prior is not None:
         alias = {len(args): 0}
         args.append(prior)
         specs.append(ANY)
     return pl.pallas_call(
-        functools.partial(anchor_kernel, g, len(cands), len(alias)),
+        functools.partial(anchor_kernel, g, [len(group) for group in cands], len(alias)),
         out_shape=[jax.ShapeDtypeStruct(query.shape, query.dtype), jax.ShapeDtypeStruct((8, HD), jnp.float32)],
         in_specs=specs,
         out_specs=[ANY, VMEM],
@@ -320,6 +328,23 @@
         cost_estimate=BRIEF,
         name="join",
     )(*arrays)
+
+
+def half_kernel(which, x_ref, o_ref):
+    rows = o_ref.shape[0]
+    o_ref[...] = x_ref[which * rows : (which + 1) * rows, :]
+
+
+def half_rows(x, which):
+    return pl.pallas_call(
+        functools.partial(half_kernel, which),
+        out_shape=pltpu.VMEM((x.shape[0] // 2, x.shape[1]), x.dtype),
+        in_specs=[VMEM],
+        out_specs=VMEM,
+        compiler_params=params(2),
+        cost_estimate=BRIEF,
+        name="half_rows",
+    )(x)
 
 
 def option_kernel(masks, heads, blk_ref, owner_ref, slot_ref, length_ref, *refs):
@@ -395,7 +420,7 @@
             pltpu.VMEM((options, width), jnp.bfloat16),
         ],
         compiler_params=params(4 + options // 32),
-        cost_estimate=cost(1000000000),
+        cost_estimate=cost(1),
         name="option_partials",
     )(blk, owner, slot, length, *kvs, *queries, after)
 
@@ -491,14 +516,17 @@
         first[0], states = hold((first[0], states))
     keep, send = option_partials(blk_arr, *small, kvs, masks, queries, states[-1][1])
     if n == 4:
-        near = [lax.ppermute(first[0], "blk", [(2, 1)])]
+        near = [[lax.ppermute(first[0], "blk", [(2, 1)])]]
         kvs, keep = hold((kvs, keep))
-        near += [lax.ppermute(x, "blk", [(0, 1)]) for x in kvs[1:]]
-        first[1:], keep = hold((first[1:], keep))
-        anchors = [[x, y, lax.ppermute(y, "blk", [(2, 3)])] for x, y in zip(near, first)]
+        tops = [half_rows(x, 0) for x in kvs[1:]]
+        near += [[lax.ppermute(x, "blk", [(0, 1)])] for x in tops]
+        first[1:], keep, tops = hold((first[1:], keep, tops))
+        for x, y in zip(near[1:], first[1:]):
+            x.append(lax.ppermute(half_rows(y, 1), "blk", [(2, 1)]))
+        anchors = [[x, [y], [lax.ppermute(y, "blk", [(2, 3)])]] for x, y in zip(near, first)]
         anchors[0], first = hold((anchors[0], first))
     else:
-        anchors = [[from_root(x, blk)] for x in kvs]
+        anchors = [[[from_root(x, blk)]] for x in kvs]
     ctx_out, tokens = None, []
     for g, state in enumerate(states):
         ctx_out, token = anchor_attention(blk_arr, ctx_query, kvs[g], state, anchors[g], g, ctx_out)

time: 39.9 us -> 44 us (1.10)
  the two profiles are of different devices: /device:TPU:12 before, /device:TPU:0 now
where the time goes in v19:
time: 44 us; the launch traced here: 43.7 us
  starting transfers between devices  19.9 us (45%)
  Pallas kernels  12.6 us (29%)
  waiting for transfers between devices  10.4 us (24%)
  between operations  0.8 us (2%)
    ppermute x4, waiting for transfers between devices, swap(): return lax.ppermute(x, 'blk', [(i, i ^ mask) for i in range(n)])  9.84 us
    ppermute x4, starting transfers between devices, swap(): return lax.ppermute(x, 'blk', [(i, i ^ mask) for i in range(n)])  9.77 us
    pallas_call x2, Pallas kernels, anchor_attention(): pl.pallas_call(functools.partial(anchor_kernel, g, [len(group) for group...  6.24 us
    ppermute x1, starting transfers between devices, body(): first += [lax.ppermute(x, 'blk', [(0, 2)]) for x in kvs[1:]]  3.54 us
    pallas_call x1, Pallas kernels, option_partials(): pl.pallas_call(functools.partial(option_kernel, masks, heads), out_shape=...  2.02 us
    ppermute x1, starting transfers between devices, body(): first = [lax.ppermute(kvs[0], 'blk', [(0, 2)])]  1.94 us
    ppermute x1, starting transfers between devices, body(): near += [[lax.ppermute(x, 'blk', [(0, 1)])] for x in tops]  1.93 us
    pallas_call x1, Pallas kernels, first_attention(): pl.pallas_call(first_kernel, out_shape=[pltpu.VMEM((rows, GROUP * HD), jn...  1.65 us
  transfers between devices with their start and end apart: 11, of which 4 were waited for; matrix products, arithmetic and copies ran while one was open for 0% of the time, Pallas kernels for 27%

profile of v19, /device:TPU:0, one launch (start us, length us, event | category | flops | bytes accessed | tf_op | source)
XLA Modules:
  0.0 43.7 jit_solution(15834576425962364980)
XLA Ops:
  0.6 4.1 %collective-permute-start = (bf16[16,2048]{1,0:T(8,128)(2,1)}, bf16[16,2048]{1,0:T(8,128)(2,1)S(1)}, u32[]{:S(2)}, u32[]{:S(2)}) collective-permute-start(bf16[16,2048]{1,0:T(8,128)(2,1)} %refs_4_.1), channel_id=1, source_target_pairs={{0,8},{4,12},{8,0},{12,4},{1,9},{5,13},{9,1},{13,5},{2,10},{6,14},... | collective-permute-start | bytes 196616 | tf_op jit(solution)/shard_map/ppermute | solution.py:478
  4.7 1.1 %parts.1 = (bf16[512,256]{1,0:T(8,128)(2,1)S(1)}, bf16[512,256]{1,0:T(8,128)(2,1)S(1)}) custom-call(bf16[512,256]{1,0:T(8,128)(2,1)} %k_ref, bf16[512,256]{1,0:T(8,128)(2,1)} %v_ref.1), custom_call_target="tpu_custom_call" | custom-call | flops 1 | bytes 1 | tf_op jit(solution)/shard_map/parts/pallas_call | solution.py:77
  5.9 1.9 %collective-permute-start.2 = (bf16[512,256]{1,0:T(8,128)(2,1)S(1)}, bf16[512,256]{1,0:T(8,128)(2,1)S(1)}, u32[]{:S(2)}, u32[]{:S(2)}) collective-permute-start(bf16[512,256]{1,0:T(8,128)(2,1)S(1)} %get-tuple-element.74.kv_ref.refs_0_), channel_id=1, source_target_pairs={{0,8},{1,9},{2,10},{3,11},{16,24},{17,25},{18,26},{19,27}} | collective-permute-start | bytes 786440 | tf_op jit(solution)/shard_map/ppermute | solution.py:505
  7.8 1.7 %local_attention.2 = (f32[512,1024]{1,0:T(8,128)S(1)}, f32[512,1024]{1,0:T(8,128)S(1)}, f32[512,1024]{1,0:T(8,128)S(1)}, bf16[512,2048]{1,0:T(8,128)(2,1)S(1)}, ...) custom-call(s32[1]{0:T(128)} %bitcast.blk_ref, ...), custom_call_target="tpu_custom_call" | custom-call | flops 2000000000 | bytes 1 | tf_op jit(solution)/shard_map/local_attention/pallas_call | solution.py:159
  9.5 0.0 collective-permute-done.refs_1_
  9.5 3.5 %collective-permute-start.4 = (bf16[512,256]{1,0:T(8,128)(2,1)S(1)}, bf16[512,256]{1,0:T(8,128)(2,1)S(1)}, u32[]{:S(2)}, u32[]{:S(2)}) collective-permute-start(bf16[512,256]{1,0:T(8,128)(2,1)S(1)} %get-tuple-element.69.kv_ref.refs_1_.x_ref), channel_id=1, source_target_pairs={{0,8},{1,9},{2,10},{3,11},{16,24},{17,25},{18,26},{19,27}} | collective-permute-start | bytes 786440 | tf_op jit(solution)/shard_map/ppermute | solution.py:513
  13.1 0.1 collective-permute-start.1
  13.2 0.5 %collective-permute-done.2.refs_1_ = bf16[512,256]{1,0:T(8,128)(2,1)S(1)} collective-permute-done((bf16[512,256]{1,0:T(8,128)(2,1)S(1)}, bf16[512,256]{1,0:T(8,128)(2,1)S(1)}, u32[]{:S(2)}, u32[]{:S(2)}) %collective-permute-start.2) | collective-permute-done | bytes 262176 | tf_op jit(solution)/shard_map/ppermute | solution.py:505
  13.7 0.7 %collective-permute-start.8 = (bf16[512,256]{1,0:T(8,128)(2,1)S(1)}, bf16[512,256]{1,0:T(8,128)(2,1)S(1)}, u32[]{:S(2)}, u32[]{:S(2)}) collective-permute-start(bf16[512,256]{1,0:T(8,128)(2,1)S(1)} %collective-permute-done.2.refs_1_), channel_id=1, source_target_pairs={{8,12},{9,13},{10,14},{11,15},{24,28},{25,29},{26,30},{27,31}} | collective-permute-start | bytes 786440 | tf_op jit(solution)/shard_map/ppermute | solution.py:526
  14.4 0.7 %collective-permute-start.7 = (bf16[512,256]{1,0:T(8,128)(2,1)S(1)}, bf16[512,256]{1,0:T(8,128)(2,1)S(1)}, u32[]{:S(2)}, u32[]{:S(2)}) collective-permute-start(bf16[512,256]{1,0:T(8,128)(2,1)S(1)} %collective-permute-done.2.refs_1_), channel_id=1, source_target_pairs={{8,4},{9,5},{10,6},{11,7},{24,20},{25,21},{26,22},{27,23}} | collective-permute-start | bytes 786440 | tf_op jit(solution)/shard_map/ppermute | solution.py:519
  15.0 6.7 %collective-permute-done.1.refs_3_ = bf16[32,2048]{1,0:T(8,128)(2,1)S(1)} collective-permute-done((bf16[32,2048]{1,0:T(8,128)(2,1)S(1)}, bf16[32,2048]{1,0:T(8,128)(2,1)S(1)}, u32[]{:S(2)}, u32[]{:S(2)}) %collective-permute-start.1) | collective-permute-done | bytes 131104 | tf_op jit(solution)/shard_map/ppermute | solution.py:478
  21.8 2.0 %option_partials.1 = (bf16[64,2176]{1,0:T(8,128)(2,1)S(1)}, bf16[64,2176]{1,0:T(8,128)(2,1)S(1)}) custom-call(s32[1]{0:T(128)} %bitcast.blk_ref, s32[1,64]{1,0:T(1,128)S(1)} %get-tuple-element.56.owner_ref, s32[1,64]{1,0:T(1,128)S(1)} %get-tuple-element.57.slot_ref, s32[1,64]{1,0:T(1,128)S(1)} %get-tuple-element.58.length_ref, ...), custom_call_target="tpu_custom_call" | custom-call | flops 1 | bytes 1 | tf_op jit(solution)/shard_map/option_partials/pallas_call | solution.py:413
  23.8 2.6 %collective-permute-start.9 = (bf16[64,2176]{1,0:T(8,128)(2,1)S(1)}, bf16[64,2176]{1,0:T(8,128)(2,1)S(1)}, u32[]{:S(2)}, u32[]{:S(2)}) collective-permute-start(bf16[64,2176]{1,0:T(8,128)(2,1)S(1)} %get-tuple-element.85), channel_id=1, source_target_pairs={{0,4},{4,0},{8,12},{12,8},{1,5},{5,1},{9,13},{13,9},{2,6},{6,2},{1... | collective-permute-start | bytes 835592 | tf_op jit(solution)/shard_map/ppermute | solution.py:478
  26.4 0.7 %collective-permute-start.6 = (bf16[512,256]{1,0:T(8,128)(2,1)S(1)}, bf16[512,256]{1,0:T(8,128)(2,1)S(1)}, u32[]{:S(2)}, u32[]{:S(2)}) collective-permute-start(bf16[512,256]{1,0:T(8,128)(2,1)S(1)} %collective-permute-done.4.x_ref.refs_2_), channel_id=1, source_target_pairs={{8,12},{9,13},{10,14},{11,15},{24,28},{25,29},{26,30},{27,31}} | collective-permute-start | bytes 786440 | tf_op jit(solution)/shard_map/ppermute | solution.py:526
  27.1 1.9 %collective-permute-start.3 = (bf16[256,256]{1,0:T(8,128)(2,1)S(1)}, bf16[256,256]{1,0:T(8,128)(2,1)S(1)}, u32[]{:S(2)}, u32[]{:S(2)}) collective-permute-start(bf16[256,256]{1,0:T(8,128)(2,1)S(1)} %half_rows.2), channel_id=1, source_target_pairs={{0,4},{1,5},{2,6},{3,7},{16,20},{17,21},{18,22},{19,23}} | collective-permute-start | bytes 393224 | tf_op jit(solution)/shard_map/ppermute | solution.py:522
  29.0 0.0 collective-permute-done.8.refs_2_
  29.0 0.7 %collective-permute-start.5 = (bf16[256,256]{1,0:T(8,128)(2,1)S(1)}, bf16[256,256]{1,0:T(8,128)(2,1)S(1)}, u32[]{:S(2)}, u32[]{:S(2)}) collective-permute-start(bf16[256,256]{1,0:T(8,128)(2,1)S(1)} %half_rows.3), channel_id=1, source_target_pairs={{8,4},{9,5},{10,6},{11,7},{24,20},{25,21},{26,22},{27,23}} | collective-permute-start | bytes 393224 | tf_op jit(solution)/shard_map/ppermute | solution.py:525
  29.7 3.2 %anchor_attention.2 = (bf16[512,2048]{1,0:T(8,128)(2,1)}, f32[8,128]{1,0:T(8,128)S(1)}) custom-call(s32[1]{0:T(128)} %bitcast.blk_ref, bf16[512,2048]{1,0:T(8,128)(2,1)S(1)} %get-tuple-element.49.q_ref, bf16[512,256]{1,0:T(8,128)(2,1)S(1)} %get-tuple-element.74.kv_ref.refs_0_, f32[512,1024]{1,0:T(8,128)S(1)} %get-tuple-element.75.acc_ref, ...), custom_call_target="tpu_custom_call" | custom-call | flops 1000000000 | bytes 1 | tf_op jit(solution)/shard_map/anchor_attention/pallas_call | solution.py:290
  32.9 0.3 collective-permute-done.9.b
  33.2 0.6 %merge.2 = (bf16[32,2176]{1,0:T(8,128)(2,1)S(1)}, bf16[32,2176]{1,0:T(8,128)(2,1)S(1)}) custom-call(bf16[64,2176]{1,0:T(8,128)(2,1)S(1)} %get-tuple-element.84.a, bf16[64,2176]{1,0:T(8,128)(2,1)S(1)} %collective-permute-done.9.b, f32[8,128]{1,0:T(8,128)S(1)} %get-tuple-element.86.after), custom_call_target="tpu_custom_call" | custom-call | flops 1 | bytes 1 | tf_op jit(solution)/shard_map/merge/pallas_call | solution.py:466
  33.8 3.0 %collective-permute-start.10 = (bf16[32,2176]{1,0:T(8,128)(2,1)S(1)}, bf16[32,2176]{1,0:T(8,128)(2,1)S(1)}, u32[]{:S(2)}, u32[]{:S(2)}) collective-permute-start(bf16[32,2176]{1,0:T(8,128)(2,1)S(1)} %get-tuple-element.88), channel_id=1, source_target_pairs={{0,8},{4,12},{8,0},{12,4},{1,9},{5,13},{9,1},{13,5},{2,10},{6,14},... | collective-permute-start | bytes 417800 | tf_op jit(solution)/shard_map/ppermute | solution.py:478
  36.8 3.1 %anchor_attention.3 = (bf16[512,2048]{1,0:T(8,128)(2,1)}, f32[8,128]{1,0:T(8,128)S(1)}) custom-call(s32[1]{0:T(128)} %bitcast.blk_ref, bf16[512,2048]{1,0:T(8,128)(2,1)S(1)} %get-tuple-element.49.q_ref, bf16[512,256]{1,0:T(8,128)(2,1)S(1)} %get-tuple-element.69.kv_ref.refs_1_.x_ref, ...), custom_call_target="tpu_custom_call", output_to_operand_aliasing={{0}: (10, {})} | custom-call | flops 1000000000 | bytes 1 | tf_op jit(solution)/shard_map/anchor_attention/pallas_call | solution.py:290
  39.9 2.8 %collective-permute-done.10.b = bf16[32,2176]{1,0:T(8,128)(2,1)S(1)} collective-permute-done((bf16[32,2176]{1,0:T(8,128)(2,1)S(1)}, bf16[32,2176]{1,0:T(8,128)(2,1)S(1)}, u32[]{:S(2)}, u32[]{:S(2)}) %collective-permute-start.10) | collective-permute-done | bytes 139296 | tf_op jit(solution)/shard_map/ppermute | solution.py:478
  42.7 1.0 %merge.3 = bf16[32,2048]{1,0:T(8,128)(2,1)} custom-call(bf16[32,2176]{1,0:T(8,128)(2,1)S(1)} %get-tuple-element.87.a, bf16[32,2176]{1,0:T(8,128)(2,1)S(1)} %collective-permute-done.10.b, f32[8,128]{1,0:T(8,128)S(1)} %get-tuple-element.89.after), custom_call_target="tpu_custom_call" | custom-call | flops 1 | bytes 1 | tf_op jit(solution)/shard_map/merge/pallas_call | solution.py:466
  (9 shorter events, 0.1 us)
Async XLA Ops:
  0.6 8.8 %collective-permute-start = (bf16[16,2048]{1,0:T(8,128)(2,1)}, bf16[16,2048]{1,0:T(8,128)(2,1)S(1)}, u32[]{:S(2)}, u32[]{:S(2)}) collective-permute-start(bf16[16,2048]{1,0:T(8,128)(2,1)} %refs_4_.1), channel_id=1, source_target_pairs={{0,8},{4,12},{8,0},{12,4},{1,9},{5,13},{9,1},{13,5},{2,10},{6,14},... | collective-permute-start | bytes 196616 | tf_op jit(solution)/shard_map/ppermute | solution.py:478
  5.9 7.8 %collective-permute-start.2 = (bf16[512,256]{1,0:T(8,128)(2,1)S(1)}, bf16[512,256]{1,0:T(8,128)(2,1)S(1)}, u32[]{:S(2)}, u32[]{:S(2)}) collective-permute-start(bf16[512,256]{1,0:T(8,128)(2,1)S(1)} %get-tuple-element.74.kv_ref.refs_0_), channel_id=1, source_target_pairs={{0,8},{1,9},{2,10},{3,11},{16,24},{17,25},{18,26},{19,27}} | collective-permute-start | bytes 786440 | tf_op jit(solution)/shard_map/ppermute | solution.py:505
  9.5 16.9 %collective-permute-start.4 = (bf16[512,256]{1,0:T(8,128)(2,1)S(1)}, bf16[512,256]{1,0:T(8,128)(2,1)S(1)}, u32[]{:S(2)}, u32[]{:S(2)}) collective-permute-start(bf16[512,256]{1,0:T(8,128)(2,1)S(1)} %get-tuple-element.69.kv_ref.refs_1_.x_ref), channel_id=1, source_target_pairs={{0,8},{1,9},{2,10},{3,11},{16,24},{17,25},{18,26},{19,27}} | collective-permute-start | bytes 786440 | tf_op jit(solution)/shard_map/ppermute | solution.py:513
  13.1 8.7 %collective-permute-start.1 = (bf16[32,2048]{1,0:T(8,128)(2,1)S(1)}, bf16[32,2048]{1,0:T(8,128)(2,1)S(1)}, u32[]{:S(2)}, u32[]{:S(2)}) collective-permute-start(bf16[32,2048]{1,0:T(8,128)(2,1)S(1)} %join.1.refs_2_), channel_id=1, source_target_pairs={{0,4},{4,0},{8,12},{12,8},{1,5},{5,1},{9,13},{13,9},{2,6},{6,2},{1... | collective-permute-start | bytes 393224 | tf_op jit(solution)/shard_map/ppermute | solution.py:478
  13.7 15.4 %collective-permute-start.8 = (bf16[512,256]{1,0:T(8,128)(2,1)S(1)}, bf16[512,256]{1,0:T(8,128)(2,1)S(1)}, u32[]{:S(2)}, u32[]{:S(2)}) collective-permute-start(bf16[512,256]{1,0:T(8,128)(2,1)S(1)} %collective-permute-done.2.refs_1_), channel_id=1, source_target_pairs={{8,12},{9,13},{10,14},{11,15},{24,28},{25,29},{26,30},{27,31}} | collective-permute-start | bytes 786440 | tf_op jit(solution)/shard_map/ppermute | solution.py:526
  14.4 15.4 %collective-permute-start.7 = (bf16[512,256]{1,0:T(8,128)(2,1)S(1)}, bf16[512,256]{1,0:T(8,128)(2,1)S(1)}, u32[]{:S(2)}, u32[]{:S(2)}) collective-permute-start(bf16[512,256]{1,0:T(8,128)(2,1)S(1)} %collective-permute-done.2.refs_1_), channel_id=1, source_target_pairs={{8,4},{9,5},{10,6},{11,7},{24,20},{25,21},{26,22},{27,23}} | collective-permute-start | bytes 786440 | tf_op jit(solution)/shard_map/ppermute | solution.py:519
  23.8 9.4 %collective-permute-start.9 = (bf16[64,2176]{1,0:T(8,128)(2,1)S(1)}, bf16[64,2176]{1,0:T(8,128)(2,1)S(1)}, u32[]{:S(2)}, u32[]{:S(2)}) collective-permute-start(bf16[64,2176]{1,0:T(8,128)(2,1)S(1)} %get-tuple-element.85), channel_id=1, source_target_pairs={{0,4},{4,0},{8,12},{12,8},{1,5},{5,1},{9,13},{13,9},{2,6},{6,2},{1... | collective-permute-start | bytes 835592 | tf_op jit(solution)/shard_map/ppermute | solution.py:478
  26.4 10.4 %collective-permute-start.6 = (bf16[512,256]{1,0:T(8,128)(2,1)S(1)}, bf16[512,256]{1,0:T(8,128)(2,1)S(1)}, u32[]{:S(2)}, u32[]{:S(2)}) collective-permute-start(bf16[512,256]{1,0:T(8,128)(2,1)S(1)} %collective-permute-done.4.x_ref.refs_2_), channel_id=1, source_target_pairs={{8,12},{9,13},{10,14},{11,15},{24,28},{25,29},{26,30},{27,31}} | collective-permute-start | bytes 786440 | tf_op jit(solution)/shard_map/ppermute | solution.py:526
  27.1 9.8 %collective-permute-start.3 = (bf16[256,256]{1,0:T(8,128)(2,1)S(1)}, bf16[256,256]{1,0:T(8,128)(2,1)S(1)}, u32[]{:S(2)}, u32[]{:S(2)}) collective-permute-start(bf16[256,256]{1,0:T(8,128)(2,1)S(1)} %half_rows.2), channel_id=1, source_target_pairs={{0,4},{1,5},{2,6},{3,7},{16,20},{17,21},{18,22},{19,23}} | collective-permute-start | bytes 393224 | tf_op jit(solution)/shard_map/ppermute | solution.py:522
  29.0 7.8 %collective-permute-start.5 = (bf16[256,256]{1,0:T(8,128)(2,1)S(1)}, bf16[256,256]{1,0:T(8,128)(2,1)S(1)}, u32[]{:S(2)}, u32[]{:S(2)}) collective-permute-start(bf16[256,256]{1,0:T(8,128)(2,1)S(1)} %half_rows.3), channel_id=1, source_target_pairs={{8,4},{9,5},{10,6},{11,7},{24,20},{25,21},{26,22},{27,23}} | collective-permute-start | bytes 393224 | tf_op jit(solution)/shard_map/ppermute | solution.py:525
  33.8 8.9 %collective-permute-start.10 = (bf16[32,2176]{1,0:T(8,128)(2,1)S(1)}, bf16[32,2176]{1,0:T(8,128)(2,1)S(1)}, u32[]{:S(2)}, u32[]{:S(2)}) collective-permute-start(bf16[32,2176]{1,0:T(8,128)(2,1)S(1)} %get-tuple-element.88), channel_id=1, source_target_pairs={{0,8},{4,12},{8,0},{12,4},{1,9},{5,13},{9,1},{13,5},{2,10},{6,14},... | collective-permute-start | bytes 417800 | tf_op jit(solution)/shard_map/ppermute | solution.py:478

commit v20 on v19

--- a/solution.py
+++ b/solution.py
@@ -420,7 +420,7 @@
             pltpu.VMEM((options, width), jnp.bfloat16),
         ],
         compiler_params=params(4 + options // 32),
-        cost_estimate=cost(1),
+        cost_estimate=cost(1000000000),
         name="option_partials",
     )(blk, owner, slot, length, *kvs, *queries, after)
 

time: 44 us -> 40.2 us (0.914)
  waiting for transfers between devices: 10.4 us -> 3.92 us
  starting transfers between devices: 19.9 us -> 22.7 us
    ppermute x4, waiting for transfers between devices: 9.84 us -> 2.88 us  [swap(): return lax.ppermute(x, 'blk', [(i, i ^ mask) for i in range(n)])]
    ppermute x4, starting transfers between devices: 9.77 us -> 14.3 us  [swap(): return lax.ppermute(x, 'blk', [(i, i ^ mask) for i in range(n)])]
    ppermute x1, starting transfers between devices: 3.54 us -> 2.39 us  [body(): first += [lax.ppermute(x, 'blk', [(0, 2)]) for x in kvs[1:]]]
    ppermute x1, waiting for transfers between devices: 0.01 us -> 1.02 us  [body(): first += [lax.ppermute(x, 'blk', [(0, 2)]) for x in kvs[1:]]]
    ppermute x1, starting transfers between devices: 1.93 us -> 1.3 us  [body(): near += [[lax.ppermute(x, 'blk', [(0, 1)])] for x in tops]]
    ppermute x1, waiting for transfers between devices: 0.52 us -> 0.01 us  [body(): first = [lax.ppermute(kvs[0], 'blk', [(0, 2)])]]
  transfers between devices with their start and end apart: 11 -> 11, of which waited for: 4 -> 4; matrix products, arithmetic and copies ran while one was open for 0% -> 0% of each run, Pallas kernels for 27% -> 29%
where the time goes in v20:
time: 40.2 us; the launch traced here: 40 us
  starting transfers between devices  22.7 us (56%)
  Pallas kernels  12.6 us (31%)
  waiting for transfers between devices  3.92 us (10%)
  between operations  0.8 us (2%)
    ppermute x4, starting transfers between devices, swap(): return lax.ppermute(x, 'blk', [(i, i ^ mask) for i in range(n)])  14.3 us
    pallas_call x2, Pallas kernels, anchor_attention(): pl.pallas_call(functools.partial(anchor_kernel, g, [len(group) for group...  6.23 us
    ppermute x4, waiting for transfers between devices, swap(): return lax.ppermute(x, 'blk', [(i, i ^ mask) for i in range(n)])  2.88 us
    ppermute x1, starting transfers between devices, body(): first += [lax.ppermute(x, 'blk', [(0, 2)]) for x in kvs[1:]]  2.39 us
    pallas_call x1, Pallas kernels, option_partials(): pl.pallas_call(functools.partial(option_kernel, masks, heads), out_shape=...  2.02 us
    ppermute x1, starting transfers between devices, body(): first = [lax.ppermute(kvs[0], 'blk', [(0, 2)])]  1.94 us
    pallas_call x1, Pallas kernels, first_attention(): pl.pallas_call(first_kernel, out_shape=[pltpu.VMEM((rows, GROUP * HD), jn...  1.65 us
    pallas_call x2, Pallas kernels, merge(): pl.pallas_call(functools.partial(merge_kernel, heads), out_shape=shapes,...  1.54 us
  transfers between devices with their start and end apart: 11, of which 4 were waited for; matrix products, arithmetic and copies ran while one was open for 0% of the time, Pallas kernels for 29%

profile of v20, /device:TPU:0, one launch (start us, length us, event | category | flops | bytes accessed | tf_op | source)
XLA Modules:
  0.0 40.0 jit_solution(17546385017574433027)
XLA Ops:
  0.6 4.1 %collective-permute-start = (bf16[16,2048]{1,0:T(8,128)(2,1)}, bf16[16,2048]{1,0:T(8,128)(2,1)S(1)}, u32[]{:S(2)}, u32[]{:S(2)}) collective-permute-start(bf16[16,2048]{1,0:T(8,128)(2,1)} %refs_4_.1), channel_id=1, source_target_pairs={{0,8},{4,12},{8,0},{12,4},{1,9},{5,13},{9,1},{13,5},{2,10},{6,14},... | collective-permute-start | bytes 196616 | tf_op jit(solution)/shard_map/ppermute | solution.py:478
  4.7 1.1 %parts.1 = (bf16[512,256]{1,0:T(8,128)(2,1)S(1)}, bf16[512,256]{1,0:T(8,128)(2,1)S(1)}) custom-call(bf16[512,256]{1,0:T(8,128)(2,1)} %k_ref, bf16[512,256]{1,0:T(8,128)(2,1)} %v_ref.1), custom_call_target="tpu_custom_call" | custom-call | flops 1 | bytes 1 | tf_op jit(solution)/shard_map/parts/pallas_call | solution.py:77
  5.9 1.9 %collective-permute-start.2 = (bf16[512,256]{1,0:T(8,128)(2,1)S(1)}, bf16[512,256]{1,0:T(8,128)(2,1)S(1)}, u32[]{:S(2)}, u32[]{:S(2)}) collective-permute-start(bf16[512,256]{1,0:T(8,128)(2,1)S(1)} %get-tuple-element.74.kv_ref.refs_0_), channel_id=1, source_target_pairs={{0,8},{1,9},{2,10},{3,11},{16,24},{17,25},{18,26},{19,27}} | collective-permute-start | bytes 786440 | tf_op jit(solution)/shard_map/ppermute | solution.py:505
  7.8 1.7 %local_attention.2 = (f32[512,1024]{1,0:T(8,128)S(1)}, f32[512,1024]{1,0:T(8,128)S(1)}, f32[512,1024]{1,0:T(8,128)S(1)}, bf16[512,2048]{1,0:T(8,128)(2,1)S(1)}, ...) custom-call(s32[1]{0:T(128)} %bitcast.blk_ref, ...), custom_call_target="tpu_custom_call" | custom-call | flops 2000000000 | bytes 1 | tf_op jit(solution)/shard_map/local_attention/pallas_call | solution.py:159
  9.5 0.0 collective-permute-done.refs_1_
  9.5 2.6 %collective-permute-start.1 = (bf16[32,2048]{1,0:T(8,128)(2,1)S(1)}, bf16[32,2048]{1,0:T(8,128)(2,1)S(1)}, u32[]{:S(2)}, u32[]{:S(2)}) collective-permute-start(bf16[32,2048]{1,0:T(8,128)(2,1)S(1)} %join.1.refs_2_), channel_id=1, source_target_pairs={{0,4},{4,0},{8,12},{12,8},{1,5},{5,1},{9,13},{13,9},{2,6},{6,2},{1... | collective-permute-start | bytes 393224 | tf_op jit(solution)/shard_map/ppermute | solution.py:478
  12.1 2.4 %collective-permute-start.4 = (bf16[512,256]{1,0:T(8,128)(2,1)S(1)}, bf16[512,256]{1,0:T(8,128)(2,1)S(1)}, u32[]{:S(2)}, u32[]{:S(2)}) collective-permute-start(bf16[512,256]{1,0:T(8,128)(2,1)S(1)} %get-tuple-element.69.kv_ref.refs_1_.x_ref), channel_id=1, source_target_pairs={{0,8},{1,9},{2,10},{3,11},{16,24},{17,25},{18,26},{19,27}} | collective-permute-start | bytes 786440 | tf_op jit(solution)/shard_map/ppermute | solution.py:513
  14.6 0.0 collective-permute-done.2.refs_1_
  14.6 0.7 %collective-permute-start.8 = (bf16[512,256]{1,0:T(8,128)(2,1)S(1)}, bf16[512,256]{1,0:T(8,128)(2,1)S(1)}, u32[]{:S(2)}, u32[]{:S(2)}) collective-permute-start(bf16[512,256]{1,0:T(8,128)(2,1)S(1)} %collective-permute-done.2.refs_1_), channel_id=1, source_target_pairs={{8,12},{9,13},{10,14},{11,15},{24,28},{25,29},{26,30},{27,31}} | collective-permute-start | bytes 786440 | tf_op jit(solution)/shard_map/ppermute | solution.py:526
  15.2 0.7 %collective-permute-start.7 = (bf16[512,256]{1,0:T(8,128)(2,1)S(1)}, bf16[512,256]{1,0:T(8,128)(2,1)S(1)}, u32[]{:S(2)}, u32[]{:S(2)}) collective-permute-start(bf16[512,256]{1,0:T(8,128)(2,1)S(1)} %collective-permute-done.2.refs_1_), channel_id=1, source_target_pairs={{8,4},{9,5},{10,6},{11,7},{24,20},{25,21},{26,22},{27,23}} | collective-permute-start | bytes 786440 | tf_op jit(solution)/shard_map/ppermute | solution.py:519
  15.9 1.4 %collective-permute-done.1.refs_3_ = bf16[32,2048]{1,0:T(8,128)(2,1)S(1)} collective-permute-done((bf16[32,2048]{1,0:T(8,128)(2,1)S(1)}, bf16[32,2048]{1,0:T(8,128)(2,1)S(1)}, u32[]{:S(2)}, u32[]{:S(2)}) %collective-permute-start.1) | collective-permute-done | bytes 131104 | tf_op jit(solution)/shard_map/ppermute | solution.py:478
  17.3 2.0 %option_partials.1 = (bf16[64,2176]{1,0:T(8,128)(2,1)S(1)}, bf16[64,2176]{1,0:T(8,128)(2,1)S(1)}) custom-call(s32[1]{0:T(128)} %bitcast.blk_ref, s32[1,64]{1,0:T(1,128)S(1)} %get-tuple-element.56.owner_ref, s32[1,64]{1,0:T(1,128)S(1)} %get-tuple-element.57.slot_ref, s32[1,64]{1,0:T(1,128)S(1)} %get-tuple-element.58.length_ref, ...), custom_call_target="tpu_custom_call" | custom-call | flops 1000000000 | bytes 1 | tf_op jit(solution)/shard_map/option_partials/pallas_call | solution.py:413
  19.3 2.6 %collective-permute-start.9 = (bf16[64,2176]{1,0:T(8,128)(2,1)S(1)}, bf16[64,2176]{1,0:T(8,128)(2,1)S(1)}, u32[]{:S(2)}, u32[]{:S(2)}) collective-permute-start(bf16[64,2176]{1,0:T(8,128)(2,1)S(1)} %get-tuple-element.85), channel_id=1, source_target_pairs={{0,4},{4,0},{8,12},{12,8},{1,5},{5,1},{9,13},{13,9},{2,6},{6,2},{1... | collective-permute-start | bytes 835592 | tf_op jit(solution)/shard_map/ppermute | solution.py:478
  21.9 1.0 %collective-permute-done.4.x_ref.refs_2_ = bf16[512,256]{1,0:T(8,128)(2,1)S(1)} collective-permute-done((bf16[512,256]{1,0:T(8,128)(2,1)S(1)}, bf16[512,256]{1,0:T(8,128)(2,1)S(1)}, u32[]{:S(2)}, u32[]{:S(2)}) %collective-permute-start.4) | collective-permute-done | bytes 262176 | tf_op jit(solution)/shard_map/ppermute | solution.py:513
  22.9 0.7 %collective-permute-start.6 = (bf16[512,256]{1,0:T(8,128)(2,1)S(1)}, bf16[512,256]{1,0:T(8,128)(2,1)S(1)}, u32[]{:S(2)}, u32[]{:S(2)}) collective-permute-start(bf16[512,256]{1,0:T(8,128)(2,1)S(1)} %collective-permute-done.4.x_ref.refs_2_), channel_id=1, source_target_pairs={{8,12},{9,13},{10,14},{11,15},{24,28},{25,29},{26,30},{27,31}} | collective-permute-start | bytes 786440 | tf_op jit(solution)/shard_map/ppermute | solution.py:526
  23.6 1.3 %collective-permute-start.3 = (bf16[256,256]{1,0:T(8,128)(2,1)S(1)}, bf16[256,256]{1,0:T(8,128)(2,1)S(1)}, u32[]{:S(2)}, u32[]{:S(2)}) collective-permute-start(bf16[256,256]{1,0:T(8,128)(2,1)S(1)} %half_rows.2), channel_id=1, source_target_pairs={{0,4},{1,5},{2,6},{3,7},{16,20},{17,21},{18,22},{19,23}} | collective-permute-start | bytes 393224 | tf_op jit(solution)/shard_map/ppermute | solution.py:522
  24.9 0.7 %collective-permute-start.5 = (bf16[256,256]{1,0:T(8,128)(2,1)S(1)}, bf16[256,256]{1,0:T(8,128)(2,1)S(1)}, u32[]{:S(2)}, u32[]{:S(2)}) collective-permute-start(bf16[256,256]{1,0:T(8,128)(2,1)S(1)} %half_rows.3), channel_id=1, source_target_pairs={{8,4},{9,5},{10,6},{11,7},{24,20},{25,21},{26,22},{27,23}} | collective-permute-start | bytes 393224 | tf_op jit(solution)/shard_map/ppermute | solution.py:525
  25.6 3.2 %anchor_attention.2 = (bf16[512,2048]{1,0:T(8,128)(2,1)}, f32[8,128]{1,0:T(8,128)S(1)}) custom-call(s32[1]{0:T(128)} %bitcast.blk_ref, bf16[512,2048]{1,0:T(8,128)(2,1)S(1)} %get-tuple-element.49.q_ref, bf16[512,256]{1,0:T(8,128)(2,1)S(1)} %get-tuple-element.74.kv_ref.refs_0_, f32[512,1024]{1,0:T(8,128)S(1)} %get-tuple-element.75.acc_ref, ...), custom_call_target="tpu_custom_call" | custom-call | flops 1000000000 | bytes 1 | tf_op jit(solution)/shard_map/anchor_attention/pallas_call | solution.py:290
  28.8 0.2 collective-permute-done.9.b
  29.0 0.6 %merge.2 = (bf16[32,2176]{1,0:T(8,128)(2,1)S(1)}, bf16[32,2176]{1,0:T(8,128)(2,1)S(1)}) custom-call(bf16[64,2176]{1,0:T(8,128)(2,1)S(1)} %get-tuple-element.84.a, bf16[64,2176]{1,0:T(8,128)(2,1)S(1)} %collective-permute-done.9.b, f32[8,128]{1,0:T(8,128)S(1)} %get-tuple-element.86.after), custom_call_target="tpu_custom_call" | custom-call | flops 1 | bytes 1 | tf_op jit(solution)/shard_map/merge/pallas_call | solution.py:466
  29.6 5.0 %collective-permute-start.10 = (bf16[32,2176]{1,0:T(8,128)(2,1)S(1)}, bf16[32,2176]{1,0:T(8,128)(2,1)S(1)}, u32[]{:S(2)}, u32[]{:S(2)}) collective-permute-start(bf16[32,2176]{1,0:T(8,128)(2,1)S(1)} %get-tuple-element.88), channel_id=1, source_target_pairs={{0,8},{4,12},{8,0},{12,4},{1,9},{5,13},{9,1},{13,5},{2,10},{6,14},... | collective-permute-start | bytes 417800 | tf_op jit(solution)/shard_map/ppermute | solution.py:478
  34.6 3.0 %anchor_attention.3 = (bf16[512,2048]{1,0:T(8,128)(2,1)}, f32[8,128]{1,0:T(8,128)S(1)}) custom-call(s32[1]{0:T(128)} %bitcast.blk_ref, bf16[512,2048]{1,0:T(8,128)(2,1)S(1)} %get-tuple-element.49.q_ref, bf16[512,256]{1,0:T(8,128)(2,1)S(1)} %get-tuple-element.69.kv_ref.refs_1_.x_ref, ...), custom_call_target="tpu_custom_call", output_to_operand_aliasing={{0}: (10, {})} | custom-call | flops 1000000000 | bytes 1 | tf_op jit(solution)/shard_map/anchor_attention/pallas_call | solution.py:290
  37.7 1.3 %collective-permute-done.10.b = bf16[32,2176]{1,0:T(8,128)(2,1)S(1)} collective-permute-done((bf16[32,2176]{1,0:T(8,128)(2,1)S(1)}, bf16[32,2176]{1,0:T(8,128)(2,1)S(1)}, u32[]{:S(2)}, u32[]{:S(2)}) %collective-permute-start.10) | collective-permute-done | bytes 139296 | tf_op jit(solution)/shard_map/ppermute | solution.py:478
  39.0 1.0 %merge.3 = bf16[32,2048]{1,0:T(8,128)(2,1)} custom-call(bf16[32,2176]{1,0:T(8,128)(2,1)S(1)} %get-tuple-element.87.a, bf16[32,2176]{1,0:T(8,128)(2,1)S(1)} %collective-permute-done.10.b, f32[8,128]{1,0:T(8,128)S(1)} %get-tuple-element.89.after), custom_call_target="tpu_custom_call" | custom-call | flops 1 | bytes 1 | tf_op jit(solution)/shard_map/merge/pallas_call | solution.py:466
  (9 shorter events, 0.1 us)
Async XLA Ops:
  0.6 8.8 %collective-permute-start = (bf16[16,2048]{1,0:T(8,128)(2,1)}, bf16[16,2048]{1,0:T(8,128)(2,1)S(1)}, u32[]{:S(2)}, u32[]{:S(2)}) collective-permute-start(bf16[16,2048]{1,0:T(8,128)(2,1)} %refs_4_.1), channel_id=1, source_target_pairs={{0,8},{4,12},{8,0},{12,4},{1,9},{5,13},{9,1},{13,5},{2,10},{6,14},... | collective-permute-start | bytes 196616 | tf_op jit(solution)/shard_map/ppermute | solution.py:478
  5.9 8.7 %collective-permute-start.2 = (bf16[512,256]{1,0:T(8,128)(2,1)S(1)}, bf16[512,256]{1,0:T(8,128)(2,1)S(1)}, u32[]{:S(2)}, u32[]{:S(2)}) collective-permute-start(bf16[512,256]{1,0:T(8,128)(2,1)S(1)} %get-tuple-element.74.kv_ref.refs_0_), channel_id=1, source_target_pairs={{0,8},{1,9},{2,10},{3,11},{16,24},{17,25},{18,26},{19,27}} | collective-permute-start | bytes 786440 | tf_op jit(solution)/shard_map/ppermute | solution.py:505
  9.5 7.8 %collective-permute-start.1 = (bf16[32,2048]{1,0:T(8,128)(2,1)S(1)}, bf16[32,2048]{1,0:T(8,128)(2,1)S(1)}, u32[]{:S(2)}, u32[]{:S(2)}) collective-permute-start(bf16[32,2048]{1,0:T(8,128)(2,1)S(1)} %join.1.refs_2_), channel_id=1, source_target_pairs={{0,4},{4,0},{8,12},{12,8},{1,5},{5,1},{9,13},{13,9},{2,6},{6,2},{1... | collective-permute-start | bytes 393224 | tf_op jit(solution)/shard_map/ppermute | solution.py:478
  12.1 10.8 %collective-permute-start.4 = (bf16[512,256]{1,0:T(8,128)(2,1)S(1)}, bf16[512,256]{1,0:T(8,128)(2,1)S(1)}, u32[]{:S(2)}, u32[]{:S(2)}) collective-permute-start(bf16[512,256]{1,0:T(8,128)(2,1)S(1)} %get-tuple-element.69.kv_ref.refs_1_.x_ref), channel_id=1, source_target_pairs={{0,8},{1,9},{2,10},{3,11},{16,24},{17,25},{18,26},{19,27}} | collective-permute-start | bytes 786440 | tf_op jit(solution)/shard_map/ppermute | solution.py:513
  14.6 10.4 %collective-permute-start.8 = (bf16[512,256]{1,0:T(8,128)(2,1)S(1)}, bf16[512,256]{1,0:T(8,128)(2,1)S(1)}, u32[]{:S(2)}, u32[]{:S(2)}) collective-permute-start(bf16[512,256]{1,0:T(8,128)(2,1)S(1)} %collective-permute-done.2.refs_1_), channel_id=1, source_target_pairs={{8,12},{9,13},{10,14},{11,15},{24,28},{25,29},{26,30},{27,31}} | collective-permute-start | bytes 786440 | tf_op jit(solution)/shard_map/ppermute | solution.py:526
  15.2 10.4 %collective-permute-start.7 = (bf16[512,256]{1,0:T(8,128)(2,1)S(1)}, bf16[512,256]{1,0:T(8,128)(2,1)S(1)}, u32[]{:S(2)}, u32[]{:S(2)}) collective-permute-start(bf16[512,256]{1,0:T(8,128)(2,1)S(1)} %collective-permute-done.2.refs_1_), channel_id=1, source_target_pairs={{8,4},{9,5},{10,6},{11,7},{24,20},{25,21},{26,22},{27,23}} | collective-permute-start | bytes 786440 | tf_op jit(solution)/shard_map/ppermute | solution.py:519
  19.3 9.7 %collective-permute-start.9 = (bf16[64,2176]{1,0:T(8,128)(2,1)S(1)}, bf16[64,2176]{1,0:T(8,128)(2,1)S(1)}, u32[]{:S(2)}, u32[]{:S(2)}) collective-permute-start(bf16[64,2176]{1,0:T(8,128)(2,1)S(1)} %get-tuple-element.85), channel_id=1, source_target_pairs={{0,4},{4,0},{8,12},{12,8},{1,5},{5,1},{9,13},{13,9},{2,6},{6,2},{1... | collective-permute-start | bytes 835592 | tf_op jit(solution)/shard_map/ppermute | solution.py:478
  22.9 11.7 %collective-permute-start.6 = (bf16[512,256]{1,0:T(8,128)(2,1)S(1)}, bf16[512,256]{1,0:T(8,128)(2,1)S(1)}, u32[]{:S(2)}, u32[]{:S(2)}) collective-permute-start(bf16[512,256]{1,0:T(8,128)(2,1)S(1)} %collective-permute-done.4.x_ref.refs_2_), channel_id=1, source_target_pairs={{8,12},{9,13},{10,14},{11,15},{24,28},{25,29},{26,30},{27,31}} | collective-permute-start | bytes 786440 | tf_op jit(solution)/shard_map/ppermute | solution.py:526
  23.6 11.0 %collective-permute-start.3 = (bf16[256,256]{1,0:T(8,128)(2,1)S(1)}, bf16[256,256]{1,0:T(8,128)(2,1)S(1)}, u32[]{:S(2)}, u32[]{:S(2)}) collective-permute-start(bf16[256,256]{1,0:T(8,128)(2,1)S(1)} %half_rows.2), channel_id=1, source_target_pairs={{0,4},{1,5},{2,6},{3,7},{16,20},{17,21},{18,22},{19,23}} | collective-permute-start | bytes 393224 | tf_op jit(solution)/shard_map/ppermute | solution.py:522
  24.9 9.7 %collective-permute-start.5 = (bf16[256,256]{1,0:T(8,128)(2,1)S(1)}, bf16[256,256]{1,0:T(8,128)(2,1)S(1)}, u32[]{:S(2)}, u32[]{:S(2)}) collective-permute-start(bf16[256,256]{1,0:T(8,128)(2,1)S(1)} %half_rows.3), channel_id=1, source_target_pairs={{8,4},{9,5},{10,6},{11,7},{24,20},{25,21},{26,22},{27,23}} | collective-permute-start | bytes 393224 | tf_op jit(solution)/shard_map/ppermute | solution.py:525
  29.6 9.4 %collective-permute-start.10 = (bf16[32,2176]{1,0:T(8,128)(2,1)S(1)}, bf16[32,2176]{1,0:T(8,128)(2,1)S(1)}, u32[]{:S(2)}, u32[]{:S(2)}) collective-permute-start(bf16[32,2176]{1,0:T(8,128)(2,1)S(1)} %get-tuple-element.88), channel_id=1, source_target_pairs={{0,8},{4,12},{8,0},{12,4},{1,9},{5,13},{9,1},{13,5},{2,10},{6,14},... | collective-permute-start | bytes 417800 | tf_op jit(solution)/shard_map/ppermute | solution.py:478

commit v21 on v18

--- a/solution.py
+++ b/solution.py
@@ -217,20 +217,25 @@
         ka[...] = ref[:, :HD]
         vae[:, :HD] = ref[:, HD:]
 
+    def stacked(ref, first):
+        return jnp.concatenate([ref[:, head_columns(first + j)] for j in range(PAIR)], axis=0)
+
     def scores(h):
-        return nt(q_ref[:, head_columns(g * GROUP + h)], ka[...])
+        return nt(stacked(q_ref, g * GROUP + h), ka[...])
 
     def weigh(h, s):
-        before = top_ref[:, head_columns(h)]
+        before = stacked(top_ref, h)
         top = jnp.maximum(jnp.max(s, axis=1, keepdims=True) * C2, before)
         p = [jnp.exp2(s[:, at : at + HD] * C2 - top).astype(jnp.bfloat16) for at in range(0, rows, HD)]
         return jnp.concatenate(p, axis=1), jnp.exp2(before - top)
 
-    def finish(h, total, w):
-        held = (slice(None), head_columns(h))
-        o = (total[:, :HD] + w * acc_ref[held]) * inverse(total[:, HD:] + w * sum_ref[held])
-        out[h] = o.astype(jnp.bfloat16)
-        leave(h).start()
+    def finish(first, total, w):
+        for j in range(PAIR):
+            h, mine = first + j, slice(j * rows, (j + 1) * rows)
+            held = (slice(None), head_columns(h))
+            o = (total[mine, :HD] + w[mine] * acc_ref[held]) * inverse(total[mine, HD:] + w[mine] * sum_ref[held])
+            out[h] = o.astype(jnp.bfloat16)
+            leave(h).start()
 
     @pl.when(blk > 0)
     def _():
@@ -241,16 +246,16 @@
                 pl.when(blk == i + 1)(functools.partial(take, ref))
         vae[:, HD:] = jnp.ones((rows, HD), jnp.bfloat16)
         ahead, weighed = scores(0), None
-        for h in range(GROUP + 1):
+        for h in range(0, GROUP + PAIR, PAIR):
             s = ahead
-            if h + 1 < GROUP:
-                ahead = scores(h + 1)
+            if h + PAIR < GROUP:
+                ahead = scores(h + PAIR)
             if weighed is not None:
                 total, w = nn(weighed[0], vae[...]), weighed[1]
             if h < GROUP:
                 weighed = weigh(h, s)
             if h:
-                finish(h - 1, total, w)
+                finish(h - PAIR, total, w)
 
     def emit(here, h, total, z, top):
         out[h, here, :] = (total * inverse(z)).astype(jnp.bfloat16)
@@ -291,7 +296,7 @@
             pltpu.SemaphoreType.DMA((GROUP,)),
         ],
         input_output_aliases=alias,
-        compiler_params=params(6),
+        compiler_params=params(12),
         cost_estimate=cost(1000000000),
         name="anchor_attention",
     )(*args)

time: 39.9 us -> 39.9 us (level)
  no operation moved by 1% of the time
where the time goes in v21:
time: 39.9 us; the launch traced here: 39.7 us
  Pallas kernels  19.5 us (49%)
  starting transfers between devices  11.9 us (30%)
  waiting for transfers between devices  7.55 us (19%)
  between operations  0.79 us (2%)
    pallas_call x2, Pallas kernels, anchor_attention(): pl.pallas_call(functools.partial(anchor_kernel, g, len(cands), len(alias)...  8.6 us
    ppermute x4, starting transfers between devices, swap(): return lax.ppermute(x, 'blk', [(i, i ^ mask) for i in range(n)])  6.58 us
    ppermute x4, waiting for transfers between devices, swap(): return lax.ppermute(x, 'blk', [(i, i ^ mask) for i in range(n)])  4.87 us
    pallas_call x1, Pallas kernels, first_attention(): pl.pallas_call(first_kernel, out_shape=[pltpu.VMEM((rows, GROUP * HD), jn...  3.9 us
    pallas_call x1, Pallas kernels, local_attention(): pl.pallas_call(functools.partial(local_kernel, g), out_shape=[pltpu.VMEM(...  2.27 us
    pallas_call x1, Pallas kernels, option_partials(): pl.pallas_call(functools.partial(option_kernel, masks, heads), out_shape=...  2.01 us
    pallas_call x2, Pallas kernels, merge(): pl.pallas_call(functools.partial(merge_kernel, heads), out_shape=shapes,...  1.54 us
    ppermute x1, waiting for transfers between devices, body(): near = [lax.ppermute(first[0], 'blk', [(2, 1)])]  1.48 us
  transfers between devices with their start and end apart: 10, of which 4 were waited for; matrix products, arithmetic and copies ran while one was open for 0% of the time, Pallas kernels for 47%

profile of v21, /device:TPU:12, one launch (start us, length us, event | category | flops | bytes accessed | tf_op | source)
XLA Modules:
  0.0 39.7 jit_solution(15825942454115037725)
XLA Ops:
  0.6 2.7 %collective-permute-start = (bf16[16,2048]{1,0:T(8,128)(2,1)}, bf16[16,2048]{1,0:T(8,128)(2,1)S(1)}, u32[]{:S(2)}, u32[]{:S(2)}) collective-permute-start(bf16[16,2048]{1,0:T(8,128)(2,1)} %refs_4_.1), channel_id=1, source_target_pairs={{0,8},{4,12},{8,0},{12,4},{1,9},{5,13},{9,1},{13,5},{2,10},{6,14},... | collective-permute-start | bytes 196616 | tf_op jit(solution)/shard_map/ppermute | solution.py:458
  3.3 1.1 %parts.1 = (bf16[512,256]{1,0:T(8,128)(2,1)S(1)}, bf16[512,256]{1,0:T(8,128)(2,1)S(1)}) custom-call(bf16[512,256]{1,0:T(8,128)(2,1)} %k_ref, bf16[512,256]{1,0:T(8,128)(2,1)} %v_ref.1), custom_call_target="tpu_custom_call" | custom-call | flops 1 | bytes 1 | tf_op jit(solution)/shard_map/parts/pallas_call | solution.py:77
  4.4 0.7 %collective-permute-start.2 = (bf16[512,256]{1,0:T(8,128)(2,1)S(1)}, bf16[512,256]{1,0:T(8,128)(2,1)S(1)}, u32[]{:S(2)}, u32[]{:S(2)}) collective-permute-start(bf16[512,256]{1,0:T(8,128)(2,1)S(1)} %get-tuple-element.74.kv_ref.refs_0_), channel_id=1, source_target_pairs={{0,8},{1,9},{2,10},{3,11},{16,24},{17,25},{18,26},{19,27}} | collective-permute-start | bytes 786440 | tf_op jit(solution)/shard_map/ppermute | solution.py:485
  5.1 3.9 %local_attention.2 = (f32[512,1024]{1,0:T(8,128)S(1)}, f32[512,1024]{1,0:T(8,128)S(1)}, f32[512,1024]{1,0:T(8,128)S(1)}, bf16[512,2048]{1,0:T(8,128)(2,1)S(1)}, ...) custom-call(s32[1]{0:T(128)} %bitcast.blk_ref, ...), custom_call_target="tpu_custom_call" | custom-call | flops 2000000000 | bytes 1 | tf_op jit(solution)/shard_map/local_attention/pallas_call | solution.py:159
  9.0 0.0 collective-permute-done.refs_1_
  9.0 0.1 collective-permute-start.1
  9.1 0.7 %collective-permute-start.4 = (bf16[512,256]{1,0:T(8,128)(2,1)S(1)}, bf16[512,256]{1,0:T(8,128)(2,1)S(1)}, u32[]{:S(2)}, u32[]{:S(2)}) collective-permute-start(bf16[512,256]{1,0:T(8,128)(2,1)S(1)} %get-tuple-element.69.kv_ref.refs_1_), channel_id=1, source_target_pairs={{0,8},{1,9},{2,10},{3,11},{16,24},{17,25},{18,26},{19,27}} | collective-permute-start | bytes 786440 | tf_op jit(solution)/shard_map/ppermute | solution.py:493
  9.8 2.3 %local_attention.3 = (f32[512,1024]{1,0:T(8,128)S(1)}, f32[512,1024]{1,0:T(8,128)S(1)}, f32[512,1024]{1,0:T(8,128)S(1)}) custom-call(s32[1]{0:T(128)} %bitcast.blk_ref, bf16[512,256]{1,0:T(8,128)(2,1)S(1)} %get-tuple-element.69.kv_ref.refs_1_, bf16[512,2048]{1,0:T(8,128)(2,1)S(1)} %get-tuple-element.49.q_ref), custom_call_target="tpu_custom_call" | custom-call | flops 1000000000 | bytes 1 | tf_op jit(solution)/shard_map/local_attention/pallas_call | solution.py:194
  12.1 0.7 %collective-permute-start.7 = (bf16[512,256]{1,0:T(8,128)(2,1)S(1)}, bf16[512,256]{1,0:T(8,128)(2,1)S(1)}, u32[]{:S(2)}, u32[]{:S(2)}) collective-permute-start(bf16[512,256]{1,0:T(8,128)(2,1)S(1)} %collective-permute-done.2.refs_1_), channel_id=1, source_target_pairs={{8,12},{9,13},{10,14},{11,15},{24,28},{25,29},{26,30},{27,31}} | collective-permute-start | bytes 786440 | tf_op jit(solution)/shard_map/ppermute | solution.py:503
  12.8 1.3 %collective-permute-start.6 = (bf16[512,256]{1,0:T(8,128)(2,1)S(1)}, bf16[512,256]{1,0:T(8,128)(2,1)S(1)}, u32[]{:S(2)}, u32[]{:S(2)}) collective-permute-start(bf16[512,256]{1,0:T(8,128)(2,1)S(1)} %collective-permute-done.2.refs_1_), channel_id=1, source_target_pairs={{8,4},{9,5},{10,6},{11,7},{24,20},{25,21},{26,22},{27,23}} | collective-permute-start | bytes 786440 | tf_op jit(solution)/shard_map/ppermute | solution.py:499
  14.1 3.0 %collective-permute-done.1.refs_3_ = bf16[32,2048]{1,0:T(8,128)(2,1)S(1)} collective-permute-done((bf16[32,2048]{1,0:T(8,128)(2,1)S(1)}, bf16[32,2048]{1,0:T(8,128)(2,1)S(1)}, u32[]{:S(2)}, u32[]{:S(2)}) %collective-permute-start.1) | collective-permute-done | bytes 131104 | tf_op jit(solution)/shard_map/ppermute | solution.py:458
  17.1 2.0 %option_partials.1 = (bf16[64,2176]{1,0:T(8,128)(2,1)S(1)}, bf16[64,2176]{1,0:T(8,128)(2,1)S(1)}) custom-call(s32[1]{0:T(128)} %bitcast.blk_ref, s32[1,64]{1,0:T(1,128)S(1)} %get-tuple-element.56.owner_ref, s32[1,64]{1,0:T(1,128)S(1)} %get-tuple-element.57.slot_ref, s32[1,64]{1,0:T(1,128)S(1)} %get-tuple-element.58.length_ref, ...), custom_call_target="tpu_custom_call" | custom-call | flops 1000000000 | bytes 1 | tf_op jit(solution)/shard_map/option_partials/pallas_call | solution.py:393
  19.1 0.1 collective-permute-start.8
  19.2 1.3 %collective-permute-start.3 = (bf16[512,256]{1,0:T(8,128)(2,1)S(1)}, bf16[512,256]{1,0:T(8,128)(2,1)S(1)}, u32[]{:S(2)}, u32[]{:S(2)}) collective-permute-start(bf16[512,256]{1,0:T(8,128)(2,1)S(1)} %get-tuple-element.69.kv_ref.refs_1_), channel_id=1, source_target_pairs={{0,4},{1,5},{2,6},{3,7},{16,20},{17,21},{18,22},{19,23}} | collective-permute-start | bytes 786440 | tf_op jit(solution)/shard_map/ppermute | solution.py:501
  20.5 0.0 collective-permute-done.4.refs_1_
  20.5 0.7 %collective-permute-start.5 = (bf16[512,256]{1,0:T(8,128)(2,1)S(1)}, bf16[512,256]{1,0:T(8,128)(2,1)S(1)}, u32[]{:S(2)}, u32[]{:S(2)}) collective-permute-start(bf16[512,256]{1,0:T(8,128)(2,1)S(1)} %collective-permute-done.4.refs_1_), channel_id=1, source_target_pairs={{8,12},{9,13},{10,14},{11,15},{24,28},{25,29},{26,30},{27,31}} | collective-permute-start | bytes 786440 | tf_op jit(solution)/shard_map/ppermute | solution.py:503
  21.2 1.5 %collective-permute-done.6.refs_0_ = bf16[512,256]{1,0:T(8,128)(2,1)S(1)} collective-permute-done((bf16[512,256]{1,0:T(8,128)(2,1)S(1)}, bf16[512,256]{1,0:T(8,128)(2,1)S(1)}, u32[]{:S(2)}, u32[]{:S(2)}) %collective-permute-start.6) | collective-permute-done | bytes 262176 | tf_op jit(solution)/shard_map/ppermute | solution.py:499
  22.7 4.3 %anchor_attention.2 = (bf16[512,2048]{1,0:T(8,128)(2,1)}, f32[8,128]{1,0:T(8,128)S(1)}) custom-call(s32[1]{0:T(128)} %bitcast.blk_ref, bf16[512,2048]{1,0:T(8,128)(2,1)S(1)} %get-tuple-element.49.q_ref, bf16[512,256]{1,0:T(8,128)(2,1)S(1)} %get-tuple-element.74.kv_ref.refs_0_, f32[512,1024]{1,0:T(8,128)S(1)} %get-tuple-element.75.acc_ref, ...), custom_call_target="tpu_custom_call" | custom-call | flops 1000000000 | bytes 1 | tf_op jit(solution)/shard_map/anchor_attention/pallas_call | solution.py:287
  27.0 1.8 %collective-permute-done.8.b = bf16[64,2176]{1,0:T(8,128)(2,1)S(1)} collective-permute-done((bf16[64,2176]{1,0:T(8,128)(2,1)S(1)}, bf16[64,2176]{1,0:T(8,128)(2,1)S(1)}, u32[]{:S(2)}, u32[]{:S(2)}) %collective-permute-start.8) | collective-permute-done | bytes 278560 | tf_op jit(solution)/shard_map/ppermute | solution.py:458
  28.8 0.6 %merge.2 = (bf16[32,2176]{1,0:T(8,128)(2,1)S(1)}, bf16[32,2176]{1,0:T(8,128)(2,1)S(1)}) custom-call(bf16[64,2176]{1,0:T(8,128)(2,1)S(1)} %get-tuple-element.84.a, bf16[64,2176]{1,0:T(8,128)(2,1)S(1)} %collective-permute-done.8.b, f32[8,128]{1,0:T(8,128)S(1)} %get-tuple-element.86.after), custom_call_target="tpu_custom_call" | custom-call | flops 1 | bytes 1 | tf_op jit(solution)/shard_map/merge/pallas_call | solution.py:446
  29.4 3.8 %collective-permute-start.9 = (bf16[32,2176]{1,0:T(8,128)(2,1)S(1)}, bf16[32,2176]{1,0:T(8,128)(2,1)S(1)}, u32[]{:S(2)}, u32[]{:S(2)}) collective-permute-start(bf16[32,2176]{1,0:T(8,128)(2,1)S(1)} %get-tuple-element.88), channel_id=1, source_target_pairs={{0,8},{4,12},{8,0},{12,4},{1,9},{5,13},{9,1},{13,5},{2,10},{6,14},... | collective-permute-start | bytes 417800 | tf_op jit(solution)/shard_map/ppermute | solution.py:458
  33.1 1.2 %collective-permute-done.3.refs_0_ = bf16[512,256]{1,0:T(8,128)(2,1)S(1)} collective-permute-done((bf16[512,256]{1,0:T(8,128)(2,1)S(1)}, bf16[512,256]{1,0:T(8,128)(2,1)S(1)}, u32[]{:S(2)}, u32[]{:S(2)}) %collective-permute-start.3) | collective-permute-done | bytes 262176 | tf_op jit(solution)/shard_map/ppermute | solution.py:501
  34.3 4.3 %anchor_attention.3 = (bf16[512,2048]{1,0:T(8,128)(2,1)}, f32[8,128]{1,0:T(8,128)S(1)}) custom-call(s32[1]{0:T(128)} %bitcast.blk_ref, bf16[512,2048]{1,0:T(8,128)(2,1)S(1)} %get-tuple-element.49.q_ref, bf16[512,256]{1,0:T(8,128)(2,1)S(1)} %get-tuple-element.69.kv_ref.refs_1_, ...), custom_call_target="tpu_custom_call", output_to_operand_aliasing={{0}: (9, {})} | custom-call | flops 1000000000 | bytes 1 | tf_op jit(solution)/shard_map/anchor_attention/pallas_call | solution.py:287
  38.7 1.0 %merge.3 = bf16[32,2048]{1,0:T(8,128)(2,1)} custom-call(bf16[32,2176]{1,0:T(8,128)(2,1)S(1)} %get-tuple-element.87.a, bf16[32,2176]{1,0:T(8,128)(2,1)S(1)} %collective-permute-done.9.b, f32[8,128]{1,0:T(8,128)S(1)} %get-tuple-element.89.after), custom_call_target="tpu_custom_call" | custom-call | flops 1 | bytes 1 | tf_op jit(solution)/shard_map/merge/pallas_call | solution.py:446
  (5 shorter events, 0.0 us)
Async XLA Ops:
  0.6 8.4 %collective-permute-start = (bf16[16,2048]{1,0:T(8,128)(2,1)}, bf16[16,2048]{1,0:T(8,128)(2,1)S(1)}, u32[]{:S(2)}, u32[]{:S(2)}) collective-permute-start(bf16[16,2048]{1,0:T(8,128)(2,1)} %refs_4_.1), channel_id=1, source_target_pairs={{0,8},{4,12},{8,0},{12,4},{1,9},{5,13},{9,1},{13,5},{2,10},{6,14},... | collective-permute-start | bytes 196616 | tf_op jit(solution)/shard_map/ppermute | solution.py:458
  4.4 7.7 %collective-permute-start.2 = (bf16[512,256]{1,0:T(8,128)(2,1)S(1)}, bf16[512,256]{1,0:T(8,128)(2,1)S(1)}, u32[]{:S(2)}, u32[]{:S(2)}) collective-permute-start(bf16[512,256]{1,0:T(8,128)(2,1)S(1)} %get-tuple-element.74.kv_ref.refs_0_), channel_id=1, source_target_pairs={{0,8},{1,9},{2,10},{3,11},{16,24},{17,25},{18,26},{19,27}} | collective-permute-start | bytes 786440 | tf_op jit(solution)/shard_map/ppermute | solution.py:485
  9.0 8.1 %collective-permute-start.1 = (bf16[32,2048]{1,0:T(8,128)(2,1)S(1)}, bf16[32,2048]{1,0:T(8,128)(2,1)S(1)}, u32[]{:S(2)}, u32[]{:S(2)}) collective-permute-start(bf16[32,2048]{1,0:T(8,128)(2,1)S(1)} %join.1.refs_2_), channel_id=1, source_target_pairs={{0,4},{4,0},{8,12},{12,8},{1,5},{5,1},{9,13},{13,9},{2,6},{6,2},{1... | collective-permute-start | bytes 393224 | tf_op jit(solution)/shard_map/ppermute | solution.py:458
  9.1 11.4 %collective-permute-start.4 = (bf16[512,256]{1,0:T(8,128)(2,1)S(1)}, bf16[512,256]{1,0:T(8,128)(2,1)S(1)}, u32[]{:S(2)}, u32[]{:S(2)}) collective-permute-start(bf16[512,256]{1,0:T(8,128)(2,1)S(1)} %get-tuple-element.69.kv_ref.refs_1_), channel_id=1, source_target_pairs={{0,8},{1,9},{2,10},{3,11},{16,24},{17,25},{18,26},{19,27}} | collective-permute-start | bytes 786440 | tf_op jit(solution)/shard_map/ppermute | solution.py:493
  12.1 9.1 %collective-permute-start.7 = (bf16[512,256]{1,0:T(8,128)(2,1)S(1)}, bf16[512,256]{1,0:T(8,128)(2,1)S(1)}, u32[]{:S(2)}, u32[]{:S(2)}) collective-permute-start(bf16[512,256]{1,0:T(8,128)(2,1)S(1)} %collective-permute-done.2.refs_1_), channel_id=1, source_target_pairs={{8,12},{9,13},{10,14},{11,15},{24,28},{25,29},{26,30},{27,31}} | collective-permute-start | bytes 786440 | tf_op jit(solution)/shard_map/ppermute | solution.py:503
  12.8 9.9 %collective-permute-start.6 = (bf16[512,256]{1,0:T(8,128)(2,1)S(1)}, bf16[512,256]{1,0:T(8,128)(2,1)S(1)}, u32[]{:S(2)}, u32[]{:S(2)}) collective-permute-start(bf16[512,256]{1,0:T(8,128)(2,1)S(1)} %collective-permute-done.2.refs_1_), channel_id=1, source_target_pairs={{8,4},{9,5},{10,6},{11,7},{24,20},{25,21},{26,22},{27,23}} | collective-permute-start | bytes 786440 | tf_op jit(solution)/shard_map/ppermute | solution.py:499
  19.1 9.7 %collective-permute-start.8 = (bf16[64,2176]{1,0:T(8,128)(2,1)S(1)}, bf16[64,2176]{1,0:T(8,128)(2,1)S(1)}, u32[]{:S(2)}, u32[]{:S(2)}) collective-permute-start(bf16[64,2176]{1,0:T(8,128)(2,1)S(1)} %get-tuple-element.85), channel_id=1, source_target_pairs={{0,4},{4,0},{8,12},{12,8},{1,5},{5,1},{9,13},{13,9},{2,6},{6,2},{1... | collective-permute-start | bytes 835592 | tf_op jit(solution)/shard_map/ppermute | solution.py:458
  19.2 15.1 %collective-permute-start.3 = (bf16[512,256]{1,0:T(8,128)(2,1)S(1)}, bf16[512,256]{1,0:T(8,128)(2,1)S(1)}, u32[]{:S(2)}, u32[]{:S(2)}) collective-permute-start(bf16[512,256]{1,0:T(8,128)(2,1)S(1)} %get-tuple-element.69.kv_ref.refs_1_), channel_id=1, source_target_pairs={{0,4},{1,5},{2,6},{3,7},{16,20},{17,21},{18,22},{19,23}} | collective-permute-start | bytes 786440 | tf_op jit(solution)/shard_map/ppermute | solution.py:501
  20.5 13.8 %collective-permute-start.5 = (bf16[512,256]{1,0:T(8,128)(2,1)S(1)}, bf16[512,256]{1,0:T(8,128)(2,1)S(1)}, u32[]{:S(2)}, u32[]{:S(2)}) collective-permute-start(bf16[512,256]{1,0:T(8,128)(2,1)S(1)} %collective-permute-done.4.refs_1_), channel_id=1, source_target_pairs={{8,12},{9,13},{10,14},{11,15},{24,28},{25,29},{26,30},{27,31}} | collective-permute-start | bytes 786440 | tf_op jit(solution)/shard_map/ppermute | solution.py:503
  29.4 9.3 %collective-permute-start.9 = (bf16[32,2176]{1,0:T(8,128)(2,1)S(1)}, bf16[32,2176]{1,0:T(8,128)(2,1)S(1)}, u32[]{:S(2)}, u32[]{:S(2)}) collective-permute-start(bf16[32,2176]{1,0:T(8,128)(2,1)S(1)} %get-tuple-element.88), channel_id=1, source_target_pairs={{0,8},{4,12},{8,0},{12,4},{1,9},{5,13},{9,1},{13,5},{2,10},{6,14},... | collective-permute-start | bytes 417800 | tf_op jit(solution)/shard_map/ppermute | solution.py:458
